TPU v7x, 512 devices: a whole 4x4x16 slice. The times are simulated.
512 devices in a mesh: qrow: 8 (over x, y_lo), kcol: 64 (over z, y_hi, core).
Axes of the slice: x: 4, y: 4 (y_hi: 2, y_lo: 2; y = y_hi * 2 + y_lo), z: 16, core: 2. Of those that a mesh axis runs over, the one named last changes fastest.
Arguments:
- queries: bfloat16 [32768, 256], P(('qrow', 'kcol')), may hold values from -6 to 6
- keys: bfloat16 [32768, 128], P(('kcol', 'qrow')), may hold values from -6 to 6
- values: bfloat16 [32768, 128], P(('kcol', 'qrow')), may hold values from -6 to 6
- out_grad: bfloat16 [32768, 256], P(('qrow', 'kcol')), may hold values from -6 to 6
- log_sum: float32 [32768, 2], P(('qrow', 'kcol')), may hold values from 4.5 to 6.5
- delta: float32 [32768, 2], P(('qrow', 'kcol')), may hold values from -24 to 24
- block_table: int32 [1024], replicated, may hold values from 0 to 1023, as said below
Outputs:
- q_grad: bfloat16 [32768, 256], P(('qrow', 'kcol'))
- k_grad: bfloat16 [32768, 128], P(('kcol', 'qrow'))
- v_grad: bfloat16 [32768, 128], P(('kcol', 'qrow'))
Inputs may be any that keep to these rules, and one draw needn't show every extreme that they name: `block_table`: a permutation of 0 to 1023 in which entries 2 d and 2 d + 1 sum to 1023 for every d.
All inputs are finite; a program needn't handle non-finite values.
Results may differ from a plain program's by a relative error of at most 0.0049.
Values may be sent and summed in bfloat16 or wider, within the bound.
No kernel may reach another device: no remote copies, remote signals or barrier semaphores. Data moves between devices by JAX's collectives and lax.ppermute only.
A program may use at most 64 MiB of HBM per device.

v0:
```python
import jax
import jax.numpy as jnp
from jax import lax
from jax.sharding import PartitionSpec as P

HEADS = 2
HD = 128


def spread_positions(entries, half):
    offsets = jnp.arange(half, dtype=jnp.int32)
    return (entries[:, None] * half + offsets[None, :]).reshape(-1)


def gradient_tile(query_all, grad_all, lse_all, delta_all, key_all, value_all, query_pos, key_pos):
    scale = HD ** (-0.5)
    count_rows = query_all.shape[0]
    key_count = key_all.shape[0]
    block = min(count_rows, max(8, 262144 // key_count))
    blocks = count_rows // block
    query_blocks = query_all.reshape(blocks, block, HEADS, HD)
    grad_blocks = grad_all.reshape(blocks, block, HEADS, HD)
    lse_blocks = lse_all.reshape(blocks, block, HEADS)
    delta_blocks = delta_all.reshape(blocks, block, HEADS)
    pos_blocks = query_pos.reshape(blocks, block)

    def one_block(carry, pieces):
        key_acc, value_acc = carry
        query_part, grad_part, lse_part, delta_part, pos_part = pieces
        scores = (
            jnp.einsum("qhd,kd->hqk", query_part, key_all, preferred_element_type=jnp.float32)
            * scale
        )
        live = key_pos[None, :] <= pos_part[:, None]
        probs = jnp.where(live[None], jnp.exp(scores - lse_part.T[:, :, None]), jnp.float32(0.0))
        probs_b = probs.astype(jnp.bfloat16)
        value_acc = value_acc + jnp.einsum(
            "hqk,qhd->kd", probs_b, grad_part, preferred_element_type=jnp.float32
        )
        dprobs = jnp.einsum("qhd,kd->hqk", grad_part, value_all, preferred_element_type=jnp.float32)
        dscores = (probs * (dprobs - delta_part.T[:, :, None])).astype(jnp.bfloat16)
        query_grad = jnp.einsum("hqk,kd->qhd", dscores, key_all, preferred_element_type=jnp.float32)
        key_acc = key_acc + jnp.einsum(
            "hqk,qhd->kd", dscores, query_part, preferred_element_type=jnp.float32
        )
        return ((key_acc, value_acc), query_grad.reshape(block, HEADS * HD))

    start = (jnp.zeros((key_count, HD), jnp.float32), jnp.zeros((key_count, HD), jnp.float32))
    (key_acc, value_acc), query_grads = lax.scan(
        one_block, start, (query_blocks, grad_blocks, lse_blocks, delta_blocks, pos_blocks)
    )
    return (query_grads.reshape(count_rows, HEADS * HD), key_acc, value_acc)


def local(queries, keys, values, out_grad, log_sum, delta, block_table):
    scale = HD ** (-0.5)
    half = queries.shape[0] // 2
    own_rows = queries.shape[0]
    n_rows = lax.axis_size("qrow")
    n_cols = lax.axis_size("kcol")
    query_all, grad_all = (
        lax.all_gather(queries, "kcol", axis=0, tiled=True),
        lax.all_gather(out_grad, "kcol", axis=0, tiled=True),
    )
    lse_all, delta_all = (
        lax.all_gather(log_sum, "kcol", axis=0, tiled=True),
        lax.all_gather(delta, "kcol", axis=0, tiled=True),
    )
    key_all, value_all = (
        lax.all_gather(keys, "qrow", axis=0, tiled=True),
        lax.all_gather(values, "qrow", axis=0, tiled=True),
    )
    query_entries = lax.dynamic_slice_in_dim(
        block_table, lax.axis_index("qrow") * (2 * n_cols), 2 * n_cols
    )
    key_entries = lax.dynamic_slice_in_dim(
        block_table, lax.axis_index("kcol") * (2 * n_rows), 2 * n_rows
    )
    query_pos = spread_positions(query_entries, half)
    key_pos = spread_positions(key_entries, half)
    query_part, key_part, value_part = gradient_tile(
        query_all, grad_all, lse_all, delta_all, key_all, value_all, query_pos, key_pos
    )
    arrived = lax.all_to_all(
        query_part.reshape(n_cols, own_rows, HEADS * HD),
        "kcol",
        split_axis=0,
        concat_axis=0,
        tiled=True,
    )
    query_total = jnp.sum(arrived, axis=0)
    key_total, value_total = (
        lax.psum_scatter(key_part, "qrow", scatter_dimension=0, tiled=True),
        lax.psum_scatter(value_part, "qrow", scatter_dimension=0, tiled=True),
    )
    q_grad = (query_total * scale).astype(jnp.bfloat16)
    k_grad = (key_total * scale).astype(jnp.bfloat16)
    v_grad = value_total.astype(jnp.bfloat16)
    return (q_grad, k_grad, v_grad)


def solution(mesh):
    placed = (
        P(("qrow", "kcol"), None),
        P(("kcol", "qrow"), None),
        P(("kcol", "qrow"), None),
        P(("qrow", "kcol"), None),
        P(("qrow", "kcol"), None),
        P(("qrow", "kcol"), None),
        P(),
    )
    return jax.shard_map(
        local,
        mesh=mesh,
        in_specs=placed,
        out_specs=(P(("qrow", "kcol"), None), P(("kcol", "qrow"), None), P(("kcol", "qrow"), None)),
        check_vma=False,
    )
```

profile of v0, /device:TPU:24, one launch (start us, length us, event | category | flops | bytes accessed | tf_op | source)
XLA Modules:
  0.0 559.1 jit_solution(10694483315661594520)
XLA Ops:
  8.7 0.8 dynamic-slice_multiply_fusion
  9.8 79.6 %all-gather = f32[64,64,2]{1,2,0:T(2,128)S(1)} all-gather(f32[1,64,2]{1,2,0:T(2,128)} %bitcast.99), channel_id=1, replica_groups=mesh['qrow'=8,'kcol'=64] {'kcol'}, dimensions={0}, use_global_device_ids=true | all-gather | bytes 33280 | tf_op jit(solution)/shard_map/all_gather | solution.py:66
  89.5 76.0 %all-gather.1 = f32[64,64,2]{1,2,0:T(2,128)S(1)} all-gather(f32[1,64,2]{1,2,0:T(2,128)} %bitcast.100), channel_id=1, replica_groups=mesh['qrow'=8,'kcol'=64] {'kcol'}, dimensions={0}, use_global_device_ids=true | all-gather | bytes 33280 | tf_op jit(solution)/shard_map/all_gather | solution.py:67
  165.5 28.5 %all_gather.19 = bf16[512,128]{1,0:T(8,128)(2,1)S(1)} all-gather(bf16[64,128]{1,0:T(8,128)(2,1)} %param.10), channel_id=1, replica_groups=mesh['qrow'=8,'kcol'=64] {'qrow'}, dimensions={0}, use_global_device_ids=true | all-gather | bytes 147456 | tf_op jit(solution)/shard_map/all_gather | solution.py:70
  194.1 28.4 %all_gather.22 = bf16[512,128]{1,0:T(8,128)(2,1)S(1)} all-gather(bf16[64,128]{1,0:T(8,128)(2,1)} %param.11), channel_id=1, replica_groups=mesh['qrow'=8,'kcol'=64] {'qrow'}, dimensions={0}, use_global_device_ids=true | all-gather | bytes 147456 | tf_op jit(solution)/shard_map/all_gather | solution.py:71
  223.3 4.0 reshape.78
  227.3 72.0 %all-gather.7.cloned.1.call-done = bf16[4096,256]{1,0:T(8,128)(2,1)} async-done(((bf16[64,256]{1,0:T(8,128)(2,1)}), bf16[4096,256]{1,0:T(8,128)(2,1)}) %all-gather.7.cloned.1.call-update) | async-done | bytes 2097168 | tf_op jit(solution)/shard_map/all_gather | solution.py:63
  299.3 4.0 reshape.79
  303.2 43.8 %while.15 = (s32[]{:T(128)}, f32[512,128]{1,0:T(8,128)S(1)}, f32[512,128]{1,0:T(8,128)S(1)}, f32[8,512,256]{2,1,0:T(8,128)}, s32[8,512]{1,0:T(8,128)S(1)}, /*ind...) while((s32[]{:T(128)}, f32[512,128]{1,0:T(8,128)S(1)}, ...), condition=%wide.region_1.2_spmd.clone, body=%wide.region_0.1_spmd.clone.sunk | while | flops 675283456 | bytes 16177384 | solution.py:49
  303.7 1.4 constant_dynamic-slice_fusion.10
  307.9 0.8 constant_dynamic-update-slice_fusion.2
  309.1 1.4 constant_dynamic-slice_fusion.10
  313.3 0.8 constant_dynamic-update-slice_fusion.2
  314.6 1.4 constant_dynamic-slice_fusion.10
  318.8 0.9 constant_dynamic-update-slice_fusion.2
  320.1 1.4 constant_dynamic-slice_fusion.10
  324.3 0.8 constant_dynamic-update-slice_fusion.2
  325.6 1.4 constant_dynamic-slice_fusion.10
  329.8 0.9 constant_dynamic-update-slice_fusion.2
  331.0 1.4 constant_dynamic-slice_fusion.10
  335.2 0.8 constant_dynamic-update-slice_fusion.2
  336.5 1.4 constant_dynamic-slice_fusion.10
  340.7 0.8 constant_dynamic-update-slice_fusion.2
  341.9 1.4 constant_dynamic-slice_fusion.10
  346.1 0.9 constant_dynamic-update-slice_fusion.2
  347.9 10.8 %all-to-all-start = ((f32[64,64,256]{2,1,0:T(8,128)}), f32[64,64,256]{2,1,0:T(8,128)}, u32[]{:S(2)}, u32[]{:S(2)}) async-start(f32[64,64,256]{2,1,0:T(8,128)} %bitcast.95), calls=%async_computation | async-start | bytes 8388608 | tf_op jit(solution)/shard_map/all_to_all | solution.py:84
  360.0 45.2 %reduce-scatter.5.cloned.1.call-done = f32[64,128]{1,0:T(8,128)} async-done(((f32[512,128]{1,0:T(8,128)}), f32[64,128]{1,0:T(8,128)}) %reduce-scatter.5.cloned.1.call-update) | async-done | bytes 32784 | tf_op jit(solution)/shard_map/reduce_scatter | solution.py:94
  405.2 1.4 convert_element_type.17
  406.5 45.2 %reduce-scatter.3.cloned.1.call-done = f32[64,128]{1,0:T(8,128)} async-done(((f32[512,128]{1,0:T(8,128)}), f32[64,128]{1,0:T(8,128)}) %reduce-scatter.3.cloned.1.call-update) | async-done | bytes 32784 | tf_op jit(solution)/shard_map/reduce_scatter | solution.py:93
  451.7 1.4 multiply_convert_fusion.1
  453.1 96.4 %all-to-all-done = f32[64,64,256]{2,1,0:T(8,128)} async-done(((f32[64,64,256]{2,1,0:T(8,128)}), f32[64,64,256]{2,1,0:T(8,128)}, u32[]{:S(2)}, u32[]{:S(2)}) %all-to-all-start) | async-done | bytes 4194336 | tf_op jit(solution)/shard_map/all_to_all | solution.py:84
  549.5 2.4 reduce_sum.9
  (133 shorter events, 30.7 us)
Async XLA Ops:
  7.2 216.1 %all-gather.5.cloned.1.call-start = ((), (), s32[]{:S(2)}) async-start(), calls=%async_computation.3 | async-start | bytes 2129920 | tf_op jit(solution)/shard_map/all_gather | solution.py:62
  7.9 291.4 %all-gather.7.cloned.1.call-start = ((), (), s32[]{:S(2)}) async-start(), calls=%async_computation.4 | async-start | bytes 2129920 | tf_op jit(solution)/shard_map/all_gather | solution.py:63
  347.0 0.7 copy-start
  347.0 0.8 copy-start.1
  347.9 201.6 %all-to-all-start = ((f32[64,64,256]{2,1,0:T(8,128)}), f32[64,64,256]{2,1,0:T(8,128)}, u32[]{:S(2)}, u32[]{:S(2)}) async-start(f32[64,64,256]{2,1,0:T(8,128)} %bitcast.95), calls=%async_computation | async-start | bytes 8388608 | tf_op jit(solution)/shard_map/all_to_all | solution.py:84
  358.7 46.5 %reduce-scatter.5.cloned.1.call-start = ((), (), s32[]{:S(2)}) async-start(), calls=%async_computation.6 | async-start | bytes 294912 | tf_op jit(solution)/shard_map/reduce_scatter | solution.py:94
  359.4 92.4 %reduce-scatter.3.cloned.1.call-start = ((), (), s32[]{:S(2)}) async-start(), calls=%async_computation.5 | async-start | bytes 294912 | tf_op jit(solution)/shard_map/reduce_scatter | solution.py:93
Sparse Core Ops, SparseCore 0:
  11.3 146.4 all-gather.4
  161.1 138.1 all-gather.6
  362.3 42.8 reduce-scatter.4
  408.1 43.6 reduce-scatter.2
where the time goes:
time: 560 us; the launch traced here: 559 us
  waiting for transfers between devices  261 us (47%)
  blocking collectives  212 us (38%)
  local copies, waits for them, and re-layouts  29.8 us (5%)
  matrix products  20.5 us (4%)
  between operations  13.8 us (2%)
  starting transfers between devices  10.9 us (2%)
  other arithmetic  9.6 us (2%)
    all_to_all x1, waiting for transfers between devices, local(): lax.all_to_all(query_part.reshape(n_cols, own_rows, HEADS * HD), 'kcol',...  96.4 us
    all_gather x1, blocking collectives, local(): lax.all_gather(log_sum, 'kcol', axis=0, tiled=True)  79.6 us
    all_gather x1, blocking collectives, local(): lax.all_gather(delta, 'kcol', axis=0, tiled=True)  76 us
    all_gather x1, waiting for transfers between devices, local(): lax.all_gather(out_grad, 'kcol', axis=0, tiled=True)  72 us
    reduce_scatter x1, waiting for transfers between devices, local(): lax.psum_scatter(value_part, 'qrow', scatter_dimension=0, tiled=True)  45.2 us
    reduce_scatter x1, waiting for transfers between devices, local(): lax.psum_scatter(key_part, 'qrow', scatter_dimension=0, tiled=True)  45.2 us
    all_gather x1, blocking collectives, local(): lax.all_gather(keys, 'qrow', axis=0, tiled=True)  28.5 us
    all_gather x1, blocking collectives, local(): lax.all_gather(values, 'qrow', axis=0, tiled=True)  28.4 us
  transfers between devices with their start and end apart: 5, of which 4 were waited for; matrix products, arithmetic and copies ran while one was open for 2% of the time, Pallas kernels for 0%

commit v1 on v0

v1 whole, which is shorter than its diff:
```python
import jax
import jax.numpy as jnp
from jax import lax
from jax.experimental import pallas as pl
from jax.experimental.pallas import tpu as pltpu
from jax.sharding import Mesh, PartitionSpec as P

HEADS = 2
HD = 128
HALF = 32
SCALE = HD ** (-0.5)
LOG2E = 1.4426950408889634
PIECES = 3
QT = 256
KT = 256
PLANE = ("x", "yl", "yh")


def dot(a, b):
    return jnp.dot(a, b, preferred_element_type=jnp.float32)


def dot_nt(a, b):
    return lax.dot_general(a, b, (((1,), (1,)), ((), ())), preferred_element_type=jnp.float32)


def tile_kernel(first, last, meta, q_ref, kv_ref, posq_ref, posk_ref, *rest):
    rest = list(rest)
    if not first:
        dkv_in = rest.pop(0)
    dq_ref, dkv_ref, qs, gs, st, lse, dlt, ks, vs, kt, dqt, dk, dv = rest
    rows_q = q_ref.shape[0]
    rows_k = kv_ref.shape[0]
    nbq = rows_q // HALF
    nbk = rows_k // HALF

    def sort_q(s, c):
        src = pl.multiple_of(meta[0, s] * HALF, HALF)
        dst = pl.multiple_of(s * HALF, HALF)
        for h in range(HEADS):
            qs[h, pl.ds(dst, HALF), :] = q_ref[pl.ds(src, HALF), h * HD:(h + 1) * HD]
            gs[h, pl.ds(dst, HALF), :] = q_ref[pl.ds(src, HALF), (HEADS + h) * HD:(HEADS + h + 1) * HD]
        st[pl.ds(dst, HALF), :] = q_ref[pl.ds(src, HALF), 2 * HEADS * HD:]
        return c

    lax.fori_loop(0, nbq, sort_q, 0, unroll=4)

    def sort_k(s, c):
        src = pl.multiple_of(meta[2, s] * HALF, HALF)
        dst = pl.multiple_of(s * HALF, HALF)
        ks[pl.ds(dst, HALF), :] = kv_ref[pl.ds(src, HALF), :HD]
        vs[pl.ds(dst, HALF), :] = kv_ref[pl.ds(src, HALF), HD:]
        return c

    lax.fori_loop(0, nbk, sort_k, 0, unroll=4)

    for t in range(rows_q // 128):
        cut = slice(t * 128, (t + 1) * 128)
        turned = st[cut, :].astype(jnp.float32).T
        for h in range(HEADS):
            a = h * PIECES
            b = (HEADS + h) * PIECES
            lse[h:h + 1, cut] = (turned[a:a + 1] + turned[a + 1:a + 2] + turned[a + 2:a + 3]) * LOG2E
            dlt[h:h + 1, cut] = turned[b:b + 1] + turned[b + 1:b + 2] + turned[b + 2:b + 3]
    for t in range(rows_k // 128):
        cut = slice(t * 128, (t + 1) * 128)
        kt[:, cut] = ks[cut, :].astype(jnp.float32).T.astype(jnp.bfloat16)

    if first:
        dk[...] = jnp.zeros_like(dk)
        dv[...] = jnp.zeros_like(dv)
    else:
        dk[...] = dkv_in[:, :HD]
        dv[...] = dkv_in[:, HD:]
    dqt[...] = jnp.zeros_like(dqt)

    kb = KT // HALF
    qb = QT // HALF

    def over_q(j, c):
        q0 = pl.multiple_of(j * QT, QT)
        top = meta[1, j * qb + qb - 1]
        live = jnp.int32(0)
        for i in range(rows_k // KT):
            live += (meta[3, i * kb] <= top).astype(jnp.int32)
        posq = posq_ref[:, pl.ds(q0, QT)]

        def over_k(i, c):
            k0 = pl.multiple_of(i * KT, KT)
            k = ks[pl.ds(k0, KT), :]
            v = vs[pl.ds(k0, KT), :]
            mask = posk_ref[pl.ds(k0, KT), :] <= posq
            dv_t = dv[pl.ds(k0, KT), :]
            dk_t = dk[pl.ds(k0, KT), :]
            for h in range(HEADS):
                q = qs[h, pl.ds(q0, QT), :]
                g = gs[h, pl.ds(q0, QT), :]
                s = dot_nt(k, q)
                p = jnp.where(mask, jnp.exp2(s * (SCALE * LOG2E) - lse[h:h + 1, pl.ds(q0, QT)]), 0.0)
                dv_t = dv_t + dot(p.astype(jnp.bfloat16), g)
                dp = dot_nt(v, g)
                ds = (p * (dp - dlt[h:h + 1, pl.ds(q0, QT)])).astype(jnp.bfloat16)
                dk_t = dk_t + dot(ds, q)
                dqt[h, :, pl.ds(q0, QT)] += dot(kt[:, pl.ds(k0, KT)], ds)
            dv[pl.ds(k0, KT), :] = dv_t
            dk[pl.ds(k0, KT), :] = dk_t
            return c

        lax.fori_loop(0, live, over_k, 0)
        for h in range(HEADS):
            back = dqt[h, :, pl.ds(q0, QT)].T.astype(jnp.bfloat16)
            for b in range(qb):
                dst = pl.multiple_of(meta[0, j * qb + b] * HALF, HALF)
                dq_ref[pl.ds(dst, HALF), h * HD:(h + 1) * HD] = back[b * HALF:(b + 1) * HALF]
        return c

    lax.fori_loop(0, rows_q // QT, over_q, 0)

    if last:
        def spread_k(s, c):
            dst = pl.multiple_of(meta[2, s] * HALF, HALF)
            src = pl.multiple_of(s * HALF, HALF)
            dkv_ref[pl.ds(dst, HALF), :HD] = dk[pl.ds(src, HALF), :].astype(jnp.bfloat16)
            dkv_ref[pl.ds(dst, HALF), HD:] = dv[pl.ds(src, HALF), :].astype(jnp.bfloat16)
            return c

        lax.fori_loop(0, nbk, spread_k, 0, unroll=4)
    else:
        dkv_ref[:, :HD] = dk[...]
        dkv_ref[:, HD:] = dv[...]


def tile_grads(first, last, meta, qg, kv, posq, posk, dkv_in=None):
    rows_q = qg.shape[0]
    rows_k = kv.shape[0]
    vmem = pl.BlockSpec(memory_space=pltpu.VMEM)
    args = [meta, qg, kv, posq, posk] + ([] if first else [dkv_in])
    bf, f32 = jnp.bfloat16, jnp.float32

    def body(*refs):
        tile_kernel(first, last, *refs)

    return pl.pallas_call(
        body,
        out_shape=(
            jax.ShapeDtypeStruct((rows_q, HEADS * HD), bf),
            jax.ShapeDtypeStruct((rows_k, 2 * HD), bf if last else f32),
        ),
        in_specs=[pl.BlockSpec(memory_space=pltpu.SMEM)] + [vmem] * (len(args) - 1),
        out_specs=(vmem, vmem),
        scratch_shapes=[
            pltpu.VMEM((HEADS, rows_q, HD), bf),
            pltpu.VMEM((HEADS, rows_q, HD), bf),
            pltpu.VMEM((rows_q, 128), bf),
            pltpu.VMEM((8, rows_q), f32),
            pltpu.VMEM((8, rows_q), f32),
            pltpu.VMEM((rows_k, HD), bf),
            pltpu.VMEM((rows_k, HD), bf),
            pltpu.VMEM((HD, rows_k), bf),
            pltpu.VMEM((HEADS, HD, rows_q), f32),
            pltpu.VMEM((rows_k, HD), f32),
            pltpu.VMEM((rows_k, HD), f32),
        ],
        compiler_params=pltpu.CompilerParams(vmem_limit_bytes=40 * 1024 * 1024),
        cost_estimate=pl.CostEstimate(
            flops=rows_q * HEADS * rows_k * HD * 5,
            bytes_accessed=4 * 1024 * 1024,
            transcendentals=rows_q * HEADS * rows_k // 2,
        ),
    )(*args)


def in_order(entries):
    n = entries.shape[0]
    rank = jnp.sum((entries[None, :] < entries[:, None]).astype(jnp.int32), axis=1)
    hit = rank[None, :] == jnp.arange(n, dtype=jnp.int32)[:, None]
    place = jnp.arange(n, dtype=jnp.int32)
    order = jnp.sum(jnp.where(hit, place[None, :], 0), axis=1)
    ordered = jnp.sum(jnp.where(hit, entries[None, :], 0), axis=1)
    return order, ordered


def positions(ordered):
    return (ordered[:, None] * HALF + jnp.arange(HALF, dtype=jnp.int32)[None, :]).reshape(-1)


def pieces(x):
    out = []
    for _ in range(PIECES):
        part = lax.reduce_precision(x, 8, 7)
        out.append(part.astype(jnp.bfloat16))
        x = x - part
    return out


def exchange(x, axes):
    return lax.all_to_all(x, axes, split_axis=0, concat_axis=0, tiled=True)


def to_all(x, axes, n):
    return exchange(jnp.broadcast_to(x[None], (n,) + x.shape), axes).reshape(n * x.shape[0], x.shape[1])


def local(queries, keys, values, out_grad, log_sum, delta, block_table):
    rows = queries.shape[0]
    nx, nyl, nz, nyh, nc = (lax.axis_size(a) for a in ("x", "yl", "z", "yh", "core"))
    ixy = lax.axis_index(("x", "yl"))
    iz, iyh, ic = (lax.axis_index(a) for a in ("z", "yh", "core"))
    plane = nx * nyl * nyh

    stats = []
    split = [pieces(log_sum), pieces(delta)]
    for parts in split:
        for h in range(HEADS):
            for k in range(PIECES):
                stats.append(parts[k][:, h:h + 1])
    stats.append(jnp.zeros((rows, 128 - 2 * HEADS * PIECES), jnp.bfloat16))
    packed = jnp.concatenate([queries, out_grad] + stats, axis=1)
    q_own = to_all(packed, PLANE, plane)
    kv = to_all(jnp.concatenate([keys, values], axis=1), "z", nz)
    q_sib = lax.ppermute(q_own, "core", [(0, 1), (1, 0)])

    q_table = block_table.reshape(nx * nyl, nz, nyh, nc, 2)
    q_table = lax.dynamic_index_in_dim(q_table, iz, 1, keepdims=False)
    k_table = block_table.reshape(nz, nyh, nc, nx * nyl, 2)
    k_table = lax.dynamic_index_in_dim(k_table, iyh, 1, keepdims=False)
    k_table = lax.dynamic_index_in_dim(k_table, ic, 1, keepdims=False)
    k_table = lax.dynamic_index_in_dim(k_table, ixy, 1, keepdims=False).reshape(-1)
    order_k, sorted_k = in_order(k_table)
    posk = positions(sorted_k)[:, None]
    metas, posqs = [], []
    for c in (ic, nc - 1 - ic):
        table = lax.dynamic_index_in_dim(q_table, c, 2, keepdims=False).reshape(-1)
        order_q, sorted_q = in_order(table)
        metas.append(jnp.stack([order_q, sorted_q, order_k, sorted_k]))
        posqs.append(positions(sorted_q)[None, :])

    dq_own, dkv = tile_grads(True, False, metas[0], q_own, kv, posqs[0], posk)
    dq_sib, dkv = tile_grads(False, True, metas[1], q_sib, kv, posqs[1], posk, dkv)

    first = jnp.where(ic == 0, dq_own, dq_sib)
    second = jnp.where(ic == 0, dq_sib, dq_own)
    dq_all = jnp.concatenate([first, second], axis=0).reshape(nc * plane, rows, HEADS * HD)
    dq_in = exchange(dq_all, ("core",) + PLANE)
    dkv_in = exchange(dkv.reshape(nz, rows, 2 * HD), "z")
    q_grad = (jnp.sum(dq_in.astype(jnp.float32), axis=0) * SCALE).astype(jnp.bfloat16)
    dkv_sum = jnp.sum(dkv_in.astype(jnp.float32), axis=0)
    k_grad = (dkv_sum[:, :HD] * SCALE).astype(jnp.bfloat16)
    v_grad = dkv_sum[:, HD:].astype(jnp.bfloat16)
    return (q_grad, k_grad, v_grad)


def solution(mesh):
    fine = Mesh(mesh.devices.reshape(4, 2, 16, 2, 2), ("x", "yl", "z", "yh", "core"))
    q_rows = P(("x", "yl", "z", "yh", "core"), None)
    k_rows = P(("z", "yh", "core", "x", "yl"), None)
    return jax.shard_map(
        local,
        mesh=fine,
        in_specs=(q_rows, k_rows, k_rows, q_rows, q_rows, q_rows, P()),
        out_specs=(q_rows, k_rows, k_rows),
        check_vma=False,
    )
```

time: 560 us -> 162 us (0.29)
  waiting for transfers between devices: 261 us -> 66.7 us
  blocking collectives: 212 us -> 22.1 us
  starting transfers between devices: 10.9 us -> 35.4 us
  local copies, waits for them, and re-layouts: 29.8 us -> 6.69 us
  Pallas kernels: 0 us -> 22.7 us
  matrix products: 20.5 us -> 0 us
  between operations: 13.8 us -> 0.85 us
    all_gather x4 -> x0, blocking collectives: 212 us -> none  [the longest x1 79.6 us: local(): lax.all_gather(log_sum, 'kcol', axis=0, tiled=True)]
    reduce_scatter x2 -> x0, waiting for transfers between devices: 90.4 us -> none  [the longest x1 45.2 us: local(): lax.psum_scatter(value_part, 'qrow', scatter_dimension=0, tiled=True)]
    all_gather x2 -> x0, waiting for transfers between devices: 72 us -> none  [the longest x1 72 us: local(): lax.all_gather(out_grad, 'kcol', axis=0, tiled=True)]
    all_to_all x1 -> x3, waiting for transfers between devices: 96.4 us -> 66.7 us  [exchange(): return lax.all_to_all(x, axes, split_axis=0, concat_axis=0, tiled=True)]
    all_to_all x1 -> x3, starting transfers between devices: 10.8 us -> 33.5 us  [exchange(): return lax.all_to_all(x, axes, split_axis=0, concat_axis=0, tiled=True)]
    pallas_call x0 -> x2, Pallas kernels: none -> 22.7 us  [tile_grads(): pl.pallas_call(body, out_shape=(jax.ShapeDtypeStruct((rows_q, HEADS * HD)...]
    all_to_all x0 -> x1, blocking collectives: none -> 22.1 us  [exchange(): return lax.all_to_all(x, axes, split_axis=0, concat_axis=0, tiled=True)]
    dot_general x40 -> x0, matrix products: 20.5 us -> none  [the longest x8 5.11 us: one_block(): jnp.einsum('qhd,kd->hqk', query_part, key_all, preferred_element_type=jnp...]
  transfers between devices with their start and end apart: 5 -> 4, of which waited for: 4 -> 3; matrix products, arithmetic and copies ran while one was open for 2% -> 2% of each run, Pallas kernels for 0% -> 7%
where the time goes in v1:
time: 162 us; the launch traced here: 159 us
  waiting for transfers between devices  66.7 us (41%)
  starting transfers between devices  35.4 us (22%)
  Pallas kernels  22.7 us (14%)
  blocking collectives  22.1 us (14%)
  local copies, waits for them, and re-layouts  6.69 us (4%)
  other arithmetic  4.11 us (3%)
    all_to_all x3, waiting for transfers between devices, exchange(): return lax.all_to_all(x, axes, split_axis=0, concat_axis=0, tiled=True)  66.7 us
    all_to_all x3, starting transfers between devices, exchange(): return lax.all_to_all(x, axes, split_axis=0, concat_axis=0, tiled=True)  33.5 us
    pallas_call x2, Pallas kernels, tile_grads(): pl.pallas_call(body, out_shape=(jax.ShapeDtypeStruct((rows_q, HEADS * HD)...  22.7 us
    all_to_all x1, blocking collectives, exchange(): return lax.all_to_all(x, axes, split_axis=0, concat_axis=0, tiled=True)  22.1 us
  transfers between devices with their start and end apart: 4, of which 3 were waited for; matrix products, arithmetic and copies ran while one was open for 2% of the time, Pallas kernels for 7%

profile of v1, /device:TPU:24, one launch (start us, length us, event | category | flops | bytes accessed | tf_op | source)
XLA Modules:
  0.0 158.6 jit_solution(1231903538717408409)
XLA Ops:
  0.6 0.7 fusion.2
  1.3 0.1 copy.36
  1.4 0.1 copy.37
  2.0 0.7 fusion.4
  2.7 0.1 copy.42
  2.8 0.1 copy.43
  3.4 0.9 concatenate.9
  4.3 1.2 broadcast_in_dim.76
  5.5 9.2 %all-to-all-start = ((bf16[16,64,640]{2,1,0:T(8,128)(2,1)}), bf16[16,64,640]{2,1,0:T(8,128)(2,1)S(1)}, u32[]{:S(2)}, u32[]{:S(2)}) async-start(bf16[16,64,640]{2,1,0:T(8,128)(2,1)} %broadcast_in_dim.76), calls=%async_computation | async-start | bytes 2621440 | tf_op jit(solution)/shard_map/all_to_all | solution.py:197
  14.8 0.4 reshape.127
  15.4 0.2 convert_reduce_fusion.4
  15.6 17.2 %all-to-all-done = bf16[16,64,640]{2,1,0:T(8,128)(2,1)S(1)} async-done(((bf16[16,64,640]{2,1,0:T(8,128)(2,1)}), bf16[16,64,640]{2,1,0:T(8,128)(2,1)S(1)}, u32[]{:S(2)}, u32[]{:S(2)}) %all-to-all-start) | async-done | bytes 1310752 | tf_op jit(solution)/shard_map/all_to_all | solution.py:197
  32.8 0.9 broadcast_in_dim.77
  33.6 16.9 %all-to-all-start.1 = ((bf16[16,64,256]{2,1,0:T(8,128)(2,1)}), bf16[16,64,256]{2,1,0:T(8,128)(2,1)S(1)}, u32[]{:S(2)}, u32[]{:S(2)}) async-start(bf16[16,64,256]{2,1,0:T(8,128)(2,1)} %broadcast_in_dim.77), calls=%async_computation.1 | async-start | bytes 1048576 | tf_op jit(solution)/shard_map/all_to_all | solution.py:197
  50.6 0.1 select_reduce_fusion.5
  50.7 0.2 reshape.128
  51.3 0.2 convert_reduce_fusion.3
  51.5 0.1 select_reduce_fusion.3
  51.6 1.9 %collective-permute-start = (bf16[1024,640]{1,0:T(8,128)(2,1)S(1)}, bf16[1024,640]{1,0:T(8,128)(2,1)}, u32[]{:S(2)}, u32[]{:S(2)}) collective-permute-start(bf16[1024,640]{1,0:T(8,128)(2,1)S(1)} %bitcast.10), channel_id=1, source_target_pairs={{0,1},{1,0},{2,3},{3,2},{4,5},{5,4},{6,7},{7,6},{8,9},{9,8},{10,11... | collective-permute-start | bytes 3932168 | tf_op jit(solution)/shard_map/ppermute | solution.py:221
  53.6 0.5 add.123.refs_4_
  54.2 0.2 convert_reduce_fusion.2
  54.4 0.1 select_reduce_fusion.1
  54.7 21.7 %all-to-all-done.1 = bf16[16,64,256]{2,1,0:T(8,128)(2,1)S(1)} async-done(((bf16[16,64,256]{2,1,0:T(8,128)(2,1)}), bf16[16,64,256]{2,1,0:T(8,128)(2,1)S(1)}, u32[]{:S(2)}, u32[]{:S(2)}) %all-to-all-start.1) | async-done | bytes 524320 | tf_op jit(solution)/shard_map/all_to_all | solution.py:197
  76.3 10.9 %shard_map.94 = (bf16[1024,256]{1,0:T(8,128)(2,1)S(1)}, f32[1024,256]{1,0:T(8,128)S(1)}) custom-call(s32[4,32]{1,0:T(4,128)S(1)} %get-tuple-element.21.refs_0_, bf16[1024,640]{1,0:T(8,128)(2,1)S(1)} %bitcast.11, bf16[1024,256]{1,0:T(8,128)(2,1)S(1)} %bitcast.12, s32[1,1024]{1,0:T(1,128)S(1)} %add.115.refs_3_, s32[1024,1]{1,0:T(8,128)S(1)} %add.123.refs_4_), custom_call_target="tpu_custom_call" | custom-call | flops 1342177280 | bytes 4194304 | tf_op jit(solution)/shard_map/pallas_call | solution.py:143
  87.3 11.8 %shard_map.95 = (bf16[1024,256]{1,0:T(8,128)(2,1)S(1)}, bf16[1024,256]{1,0:T(8,128)(2,1)}) custom-call(s32[4,32]{1,0:T(4,128)S(1)} %get-tuple-element.22.refs_0_, bf16[1024,640]{1,0:T(8,128)(2,1)} %collective-permute-done.refs_1_, bf16[1024,256]{1,0:T(8,128)(2,1)S(1)} %bitcast.13, s32[1,1024]{1,0:T(1,128)S(1)} %add.122.refs_3_, s32[1024,1]{1,0:T(8,128)S(1)} %add.123.refs_4_, ...), custom_call_target="tpu_custom_call" | custom-call | flops 1342177280 | bytes 4194304 | tf_op jit(solution)/shard_map/pallas_call | solution.py:143
  99.2 22.1 %all_to_all.20 = bf16[32,64,256]{2,1,0:T(8,128)(2,1)S(1)} all-to-all(bf16[32,64,256]{2,1,0:T(8,128)(2,1)S(1)} %bitcast.14), channel_id=1, replica_groups=mesh['x'=4,'yl'=2,'z'=16,'yh'=2,'core'=2] {'core','x','yl','yh'}, dimensions={0} | all-to-all | bytes 2097152 | tf_op jit(solution)/shard_map/all_to_all | solution.py:197
  121.4 7.3 %all-to-all-start.3 = ((bf16[16,64,256]{2,1,0:T(8,128)(2,1)}), bf16[16,64,256]{2,1,0:T(8,128)(2,1)S(1)}, u32[]{:S(2)}, u32[]{:S(2)}) async-start(bf16[16,64,256]{2,1,0:T(8,128)(2,1)} %bitcast.9), calls=%async_computation.3 | async-start | bytes 1048576 | tf_op jit(solution)/shard_map/all_to_all | solution.py:197
  128.7 0.2 convert_reduce_fusion
  128.9 0.6 multiply_convert_fusion
  129.5 27.8 %all-to-all-done.3 = bf16[16,64,256]{2,1,0:T(8,128)(2,1)S(1)} async-done(((bf16[16,64,256]{2,1,0:T(8,128)(2,1)}), bf16[16,64,256]{2,1,0:T(8,128)(2,1)S(1)}, u32[]{:S(2)}, u32[]{:S(2)}) %all-to-all-start.3) | async-done | bytes 524320 | tf_op jit(solution)/shard_map/all_to_all | solution.py:197
  157.4 0.6 fusion
  158.0 0.6 slice.63
  (38 shorter events, 1.9 us)
Async XLA Ops:
  5.5 9.2 %copy-start = (s32[1024]{0:T(1024)S(1)}, s32[1024]{0:T(1024)}, u32[]{:S(2)}) copy-start(s32[1024]{0:T(1024)} %param.13) | copy-start | bytes 12292
  5.5 9.8 %copy-start.1 = (bf16[64,128]{1,0:T(8,128)(2,1)S(1)}, bf16[64,128]{1,0:T(8,128)(2,1)}, u32[]{:S(2)}) copy-start(bf16[64,128]{1,0:T(8,128)(2,1)} %param.9) | copy-start | bytes 49156
  5.5 9.8 %copy-start.2 = (bf16[64,128]{1,0:T(8,128)(2,1)S(1)}, bf16[64,128]{1,0:T(8,128)(2,1)}, u32[]{:S(2)}) copy-start(bf16[64,128]{1,0:T(8,128)(2,1)} %param.8) | copy-start | bytes 49156
  5.5 27.2 %all-to-all-start = ((bf16[16,64,640]{2,1,0:T(8,128)(2,1)}), bf16[16,64,640]{2,1,0:T(8,128)(2,1)S(1)}, u32[]{:S(2)}, u32[]{:S(2)}) async-start(bf16[16,64,640]{2,1,0:T(8,128)(2,1)} %broadcast_in_dim.76), calls=%async_computation | async-start | bytes 2621440 | tf_op jit(solution)/shard_map/all_to_all | solution.py:197
  33.6 42.7 %all-to-all-start.1 = ((bf16[16,64,256]{2,1,0:T(8,128)(2,1)}), bf16[16,64,256]{2,1,0:T(8,128)(2,1)S(1)}, u32[]{:S(2)}, u32[]{:S(2)}) async-start(bf16[16,64,256]{2,1,0:T(8,128)(2,1)} %broadcast_in_dim.77), calls=%async_computation.1 | async-start | bytes 1048576 | tf_op jit(solution)/shard_map/all_to_all | solution.py:197
  51.6 35.7 %collective-permute-start = (bf16[1024,640]{1,0:T(8,128)(2,1)S(1)}, bf16[1024,640]{1,0:T(8,128)(2,1)}, u32[]{:S(2)}, u32[]{:S(2)}) collective-permute-start(bf16[1024,640]{1,0:T(8,128)(2,1)S(1)} %bitcast.10), channel_id=1, source_target_pairs={{0,1},{1,0},{2,3},{3,2},{4,5},{5,4},{6,7},{7,6},{8,9},{9,8},{10,11... | collective-permute-start | bytes 3932168 | tf_op jit(solution)/shard_map/ppermute | solution.py:221
  121.4 36.0 %all-to-all-start.3 = ((bf16[16,64,256]{2,1,0:T(8,128)(2,1)}), bf16[16,64,256]{2,1,0:T(8,128)(2,1)S(1)}, u32[]{:S(2)}, u32[]{:S(2)}) async-start(bf16[16,64,256]{2,1,0:T(8,128)(2,1)} %bitcast.9), calls=%async_computation.3 | async-start | bytes 1048576 | tf_op jit(solution)/shard_map/all_to_all | solution.py:197

commit v2 on v1

--- a/solution.py
+++ b/solution.py
@@ -13,7 +13,6 @@
 PIECES = 3
 QT = 256
 KT = 256
-PLANE = ("x", "yl", "yh")
 
 
 def dot(a, b):
@@ -58,10 +57,9 @@
         cut = slice(t * 128, (t + 1) * 128)
         turned = st[cut, :].astype(jnp.float32).T
         for h in range(HEADS):
-            a = h * PIECES
-            b = (HEADS + h) * PIECES
-            lse[h:h + 1, cut] = (turned[a:a + 1] + turned[a + 1:a + 2] + turned[a + 2:a + 3]) * LOG2E
-            dlt[h:h + 1, cut] = turned[b:b + 1] + turned[b + 1:b + 2] + turned[b + 2:b + 3]
+            a, b, n = h, HEADS + h, 2 * HEADS
+            lse[h:h + 1, cut] = (turned[a:a + 1] + turned[a + n:a + n + 1] + turned[a + 2 * n:a + 2 * n + 1]) * LOG2E
+            dlt[h:h + 1, cut] = turned[b:b + 1] + turned[b + n:b + n + 1] + turned[b + 2 * n:b + 2 * n + 1]
     for t in range(rows_k // 128):
         cut = slice(t * 128, (t + 1) * 128)
         kt[:, cut] = ks[cut, :].astype(jnp.float32).T.astype(jnp.bfloat16)
@@ -108,7 +106,7 @@
 
         lax.fori_loop(0, live, over_k, 0)
         for h in range(HEADS):
-            back = dqt[h, :, pl.ds(q0, QT)].T.astype(jnp.bfloat16)
+            back = dqt[h, :, pl.ds(q0, QT)].T
             for b in range(qb):
                 dst = pl.multiple_of(meta[0, j * qb + b] * HALF, HALF)
                 dq_ref[pl.ds(dst, HALF), h * HD:(h + 1) * HD] = back[b * HALF:(b + 1) * HALF]
@@ -143,7 +141,7 @@
     return pl.pallas_call(
         body,
         out_shape=(
-            jax.ShapeDtypeStruct((rows_q, HEADS * HD), bf),
+            jax.ShapeDtypeStruct((rows_q, HEADS * HD), f32),
             jax.ShapeDtypeStruct((rows_k, 2 * HD), bf if last else f32),
         ),
         in_specs=[pl.BlockSpec(memory_space=pltpu.SMEM)] + [vmem] * (len(args) - 1),
@@ -184,49 +182,79 @@
     return (ordered[:, None] * HALF + jnp.arange(HALF, dtype=jnp.int32)[None, :]).reshape(-1)
 
 
-def pieces(x):
-    out = []
-    for _ in range(PIECES):
-        part = lax.reduce_precision(x, 8, 7)
-        out.append(part.astype(jnp.bfloat16))
+def pack_q_kernel(q_ref, g_ref, lse_ref, delta_ref, out_ref):
+    width = HEADS * HD
+    out_ref[:, :width] = q_ref[...]
+    out_ref[:, width:2 * width] = g_ref[...]
+    rows = q_ref.shape[0]
+    lane = lax.broadcasted_iota(jnp.int32, (rows, 128), 1)
+    which = lane % (2 * HEADS)
+    x = jnp.zeros((rows, 128), jnp.float32)
+    for h in range(HEADS):
+        x = jnp.where(which == h, lse_ref[:, h:h + 1], x)
+        x = jnp.where(which == HEADS + h, delta_ref[:, h:h + 1], x)
+    out = jnp.zeros((rows, 128), jnp.float32)
+    for k in range(PIECES):
+        part = x.astype(jnp.bfloat16).astype(jnp.float32)
         x = x - part
-    return out
-
-
-def exchange(x, axes):
-    return lax.all_to_all(x, axes, split_axis=0, concat_axis=0, tiled=True)
-
-
-def to_all(x, axes, n):
-    return exchange(jnp.broadcast_to(x[None], (n,) + x.shape), axes).reshape(n * x.shape[0], x.shape[1])
+        out = jnp.where(lane // (2 * HEADS) == k, part, out)
+    out_ref[:, 2 * width:] = out.astype(jnp.bfloat16)
+
+
+def pack_q(queries, out_grad, log_sum, delta):
+    vmem = pl.BlockSpec(memory_space=pltpu.VMEM)
+    return pl.pallas_call(
+        pack_q_kernel,
+        out_shape=jax.ShapeDtypeStruct((queries.shape[0], 2 * HEADS * HD + 128), jnp.bfloat16),
+        in_specs=[vmem] * 4,
+        out_specs=vmem,
+    )(queries, out_grad, log_sum, delta)
+
+
+def from_offset(x, axes, index_of, d):
+    return lax.ppermute(x, axes, [(index_of(j), index_of((j + d) % 4)) for j in range(4)])
+
+
+def along_x(j):
+    return j
+
+
+def along_y(j):
+    return (j % 2) * 2 + j // 2
+
+
+def back_from(table, index, axis):
+    table = jnp.concatenate([lax.slice_in_dim(table, 0, 1, axis=axis), jnp.flip(lax.slice_in_dim(table, 1, 4, axis=axis), axis)], axis)
+    return lax.dynamic_slice_in_dim(jnp.concatenate([table, table], axis), (4 - index) % 4, 4, axis)
 
 
 def local(queries, keys, values, out_grad, log_sum, delta, block_table):
     rows = queries.shape[0]
+    width = HEADS * HD
     nx, nyl, nz, nyh, nc = (lax.axis_size(a) for a in ("x", "yl", "z", "yh", "core"))
-    ixy = lax.axis_index(("x", "yl"))
-    iz, iyh, ic = (lax.axis_index(a) for a in ("z", "yh", "core"))
-    plane = nx * nyl * nyh
-
-    stats = []
-    split = [pieces(log_sum), pieces(delta)]
-    for parts in split:
-        for h in range(HEADS):
-            for k in range(PIECES):
-                stats.append(parts[k][:, h:h + 1])
-    stats.append(jnp.zeros((rows, 128 - 2 * HEADS * PIECES), jnp.bfloat16))
-    packed = jnp.concatenate([queries, out_grad] + stats, axis=1)
-    q_own = to_all(packed, PLANE, plane)
-    kv = to_all(jnp.concatenate([keys, values], axis=1), "z", nz)
+    ix, iyl, iz, iyh, ic = (lax.axis_index(a) for a in ("x", "yl", "z", "yh", "core"))
+    iy = iyh * nyl + iyl
+    xy = nx * nyl * nyh
+    Y = ("yl", "yh")
+
+    kv = jnp.concatenate([keys, values], axis=1)
+    kv = lax.all_to_all(
+        jnp.broadcast_to(kv[None], (nz,) + kv.shape), "z", split_axis=0, concat_axis=0, tiled=True
+    ).reshape(nz * rows, 2 * HD)
+
+    packed = pack_q(queries, out_grad, log_sum, delta)
+    row = jnp.concatenate([packed] + [from_offset(packed, "x", along_x, d) for d in (1, 2, 3)], axis=0)
+    q_own = jnp.concatenate([row] + [from_offset(row, Y, along_y, d) for d in (1, 2, 3)], axis=0)
     q_sib = lax.ppermute(q_own, "core", [(0, 1), (1, 0)])
 
-    q_table = block_table.reshape(nx * nyl, nz, nyh, nc, 2)
-    q_table = lax.dynamic_index_in_dim(q_table, iz, 1, keepdims=False)
-    k_table = block_table.reshape(nz, nyh, nc, nx * nyl, 2)
-    k_table = lax.dynamic_index_in_dim(k_table, iyh, 1, keepdims=False)
-    k_table = lax.dynamic_index_in_dim(k_table, ic, 1, keepdims=False)
-    k_table = lax.dynamic_index_in_dim(k_table, ixy, 1, keepdims=False).reshape(-1)
-    order_k, sorted_k = in_order(k_table)
+    q_table = block_table.reshape(nx, nyl, nz, nyh, nc, 2)
+    q_table = lax.dynamic_index_in_dim(q_table, iz, 2, keepdims=False)
+    q_table = q_table.transpose(2, 1, 0, 3, 4).reshape(nyh * nyl, nx, nc, 2)
+    q_table = back_from(back_from(q_table, iy, 0), ix, 1)
+    k_table = block_table.reshape(nz, nyh, nc, nx, nyl, 2)
+    for axis, index in ((1, iyh), (1, ic), (1, ix), (1, iyl)):
+        k_table = lax.dynamic_index_in_dim(k_table, index, axis, keepdims=False)
+    order_k, sorted_k = in_order(k_table.reshape(-1))
     posk = positions(sorted_k)[:, None]
     metas, posqs = [], []
     for c in (ic, nc - 1 - ic):
@@ -238,12 +266,18 @@
     dq_own, dkv = tile_grads(True, False, metas[0], q_own, kv, posqs[0], posk)
     dq_sib, dkv = tile_grads(False, True, metas[1], q_sib, kv, posqs[1], posk, dkv)
 
-    first = jnp.where(ic == 0, dq_own, dq_sib)
-    second = jnp.where(ic == 0, dq_sib, dq_own)
-    dq_all = jnp.concatenate([first, second], axis=0).reshape(nc * plane, rows, HEADS * HD)
-    dq_in = exchange(dq_all, ("core",) + PLANE)
-    dkv_in = exchange(dkv.reshape(nz, rows, 2 * HD), "z")
-    q_grad = (jnp.sum(dq_in.astype(jnp.float32), axis=0) * SCALE).astype(jnp.bfloat16)
+    dkv_in = lax.all_to_all(dkv.reshape(nz, rows, 2 * HD), "z", split_axis=0, concat_axis=0, tiled=True)
+    dq = dq_own + lax.ppermute(dq_sib, "core", [(0, 1), (1, 0)])
+    dq = dq.reshape(nyl * nyh, nx * rows, width)
+    far = dq.astype(jnp.bfloat16)
+    total = dq[0]
+    for d in (1, 2, 3):
+        total = total + from_offset(far[d], Y, along_y, 4 - d).astype(jnp.float32)
+    dq = total.reshape(nx, rows, width)
+    total = dq[0]
+    for d in (1, 2, 3):
+        total = total + from_offset(dq[d], "x", along_x, 4 - d)
+    q_grad = (total * SCALE).astype(jnp.bfloat16)
     dkv_sum = jnp.sum(dkv_in.astype(jnp.float32), axis=0)
     k_grad = (dkv_sum[:, :HD] * SCALE).astype(jnp.bfloat16)
     v_grad = dkv_sum[:, HD:].astype(jnp.bfloat16)

time: 162 us -> 131 us (0.81)
  waiting for transfers between devices: 66.7 us -> 21.7 us
  starting transfers between devices: 35.4 us -> 68.6 us
  blocking collectives: 22.1 us -> 0 us
  Pallas kernels: 22.7 us -> 25.3 us
    all_to_all x3 -> x2, waiting for transfers between devices: 66.7 us -> 0.84 us  [the longest x1 0.84 us: local(): lax.all_to_all(jnp.broadcast_to(kv[None], (nz,) + kv.shape), 'z', split_a...]
    ppermute x0 -> x13, starting transfers between devices: none -> 40.1 us  [the longest x12 38.2 us: from_offset(): lax.ppermute(x, axes, [(index_of(j), index_of((j + d) % 4)) for j in rang...]
    all_to_all x1 -> x0, blocking collectives: 22.1 us -> none  [exchange(): return lax.all_to_all(x, axes, split_axis=0, concat_axis=0, tiled=True)]
    ppermute x0 -> x13, waiting for transfers between devices: none -> 20.8 us  [the longest x12 20.8 us: from_offset(): lax.ppermute(x, axes, [(index_of(j), index_of((j + d) % 4)) for j in rang...]
    all_to_all x3 -> x2, starting transfers between devices: 33.5 us -> 26.6 us  [the longest x1 15.2 us: local(): lax.all_to_all(jnp.broadcast_to(kv[None], (nz,) + kv.shape), 'z', split_a...]
    unnamed x6 -> x12, local copies, waits for them, and re-layouts: 0.01 us -> 2.9 us
  transfers between devices with their start and end apart: 4 -> 16, of which waited for: 3 -> 8; matrix products, arithmetic and copies ran while one was open for 2% -> 6% of each run, Pallas kernels for 7% -> 9%
where the time goes in v2:
time: 131 us; the launch traced here: 129 us
  starting transfers between devices  68.6 us (52%)
  Pallas kernels  25.3 us (19%)
  waiting for transfers between devices  21.7 us (17%)
  local copies, waits for them, and re-layouts  6.94 us (5%)
  other arithmetic  4.86 us (4%)
    ppermute x12, starting transfers between devices, from_offset(): lax.ppermute(x, axes, [(index_of(j), index_of((j + d) % 4)) for j in rang...  38.2 us
    pallas_call x2, Pallas kernels, tile_grads(): pl.pallas_call(body, out_shape=(jax.ShapeDtypeStruct((rows_q, HEADS * HD)...  23.8 us
    ppermute x12, waiting for transfers between devices, from_offset(): lax.ppermute(x, axes, [(index_of(j), index_of((j + d) % 4)) for j in rang...  20.8 us
    all_to_all x1, starting transfers between devices, local(): lax.all_to_all(jnp.broadcast_to(kv[None], (nz,) + kv.shape), 'z', split_a...  15.2 us
    all_to_all x1, starting transfers between devices, local(): lax.all_to_all(dkv.reshape(nz, rows, 2 * HD), 'z', split_axis=0, concat_a...  11.4 us
    unnamed x12, local copies, waits for them, and re-layouts  2.9 us
  transfers between devices with their start and end apart: 16, of which 8 were waited for; matrix products, arithmetic and copies ran while one was open for 6% of the time, Pallas kernels for 9%

profile of v2, /device:TPU:24, one launch (start us, length us, event | category | flops | bytes accessed | tf_op | source)
XLA Modules:
  0.0 128.6 jit_solution(10532629513546657747)
XLA Ops:
  0.6 1.4 %copy.26.lse_ref = f32[64,2]{1,0:T(8,128)} copy(f32[64,2]{0,1:T(2,128)} %param.11) | data formatting | bytes 1024 | tf_op args[4]
  2.0 1.4 %copy.27.delta_ref = f32[64,2]{1,0:T(8,128)} copy(f32[64,2]{0,1:T(2,128)} %param.12) | data formatting | bytes 1024 | tf_op args[5]
  3.4 1.5 %shard_map.94 = bf16[64,640]{1,0:T(8,128)(2,1)} custom-call(bf16[64,256]{1,0:T(8,128)(2,1)} %q_ref.1, bf16[64,256]{1,0:T(8,128)(2,1)} %g_ref.1, f32[64,2]{1,0:T(8,128)} %copy.26.lse_ref, f32[64,2]{1,0:T(8,128)} %copy.27.delta_ref), custom_call_target="tpu_custom_call" | custom-call | tf_op jit(solution)/shard_map/pallas_call | solution.py:206
  4.9 3.5 %collective-permute-start = (bf16[64,640]{1,0:T(8,128)(2,1)}, bf16[64,640]{1,0:T(8,128)(2,1)S(1)}, u32[]{:S(2)}, u32[]{:S(2)}) collective-permute-start(bf16[64,640]{1,0:T(8,128)(2,1)} %shard_map.94), channel_id=1, source_target_pairs={{0,128},{128,256},{256,384},{384,0},{1,129},{129,257},{257,385},{3... | collective-permute-start | bytes 245768 | tf_op jit(solution)/shard_map/ppermute | solution.py:215
  8.5 4.6 %collective-permute-start.1 = (bf16[64,640]{1,0:T(8,128)(2,1)}, bf16[64,640]{1,0:T(8,128)(2,1)S(1)}, u32[]{:S(2)}, u32[]{:S(2)}) collective-permute-start(bf16[64,640]{1,0:T(8,128)(2,1)} %shard_map.94), channel_id=1, source_target_pairs={{0,256},{128,384},{256,0},{384,128},{1,257},{129,385},{257,1},{385... | collective-permute-start | bytes 245768 | tf_op jit(solution)/shard_map/ppermute | solution.py:215
  13.1 3.3 %collective-permute-start.2 = (bf16[64,640]{1,0:T(8,128)(2,1)}, bf16[64,640]{1,0:T(8,128)(2,1)S(1)}, u32[]{:S(2)}, u32[]{:S(2)}) collective-permute-start(bf16[64,640]{1,0:T(8,128)(2,1)} %shard_map.94), channel_id=1, source_target_pairs={{0,384},{128,0},{256,128},{384,256},{1,385},{129,1},{257,129},{385... | collective-permute-start | bytes 245768 | tf_op jit(solution)/shard_map/ppermute | solution.py:215
  16.5 0.7 pad_maximum_fusion.1
  17.2 0.9 broadcast_in_dim.66
  18.1 15.2 %all-to-all-start = ((bf16[16,64,256]{2,1,0:T(8,128)(2,1)}), bf16[16,64,256]{2,1,0:T(8,128)(2,1)S(1)}, u32[]{:S(2)}, u32[]{:S(2)}) async-start(bf16[16,64,256]{2,1,0:T(8,128)(2,1)} %broadcast_in_dim.66), calls=%async_computation | async-start | bytes 1048576 | tf_op jit(solution)/shard_map/all_to_all | solution.py:241
  36.2 2.1 %collective-permute-start.3 = (bf16[256,640]{1,0:T(8,128)(2,1)S(1)}, bf16[256,640]{1,0:T(8,128)(2,1)S(1)}, u32[]{:S(2)}, u32[]{:S(2)}) collective-permute-start(bf16[256,640]{1,0:T(8,128)(2,1)S(1)} %pad_maximum_fusion), channel_id=1, source_target_pairs={{0,64},{64,2},{2,66},{66,0},{1,65},{65,3},{3,67},{67,1},{4,68},{68... | collective-permute-start | bytes 983048 | tf_op jit(solution)/shard_map/ppermute | solution.py:215
  38.4 4.5 %collective-permute-start.4 = (bf16[256,640]{1,0:T(8,128)(2,1)S(1)}, bf16[256,640]{1,0:T(8,128)(2,1)S(1)}, u32[]{:S(2)}, u32[]{:S(2)}) collective-permute-start(bf16[256,640]{1,0:T(8,128)(2,1)S(1)} %pad_maximum_fusion), channel_id=1, source_target_pairs={{0,2},{64,66},{2,0},{66,64},{1,3},{65,67},{3,1},{67,65},{4,6},{68,... | collective-permute-start | bytes 983048 | tf_op jit(solution)/shard_map/ppermute | solution.py:215
  42.9 1.9 %collective-permute-start.5 = (bf16[256,640]{1,0:T(8,128)(2,1)S(1)}, bf16[256,640]{1,0:T(8,128)(2,1)S(1)}, u32[]{:S(2)}, u32[]{:S(2)}) collective-permute-start(bf16[256,640]{1,0:T(8,128)(2,1)S(1)} %pad_maximum_fusion), channel_id=1, source_target_pairs={{0,66},{64,0},{2,64},{66,2},{1,67},{65,1},{3,65},{67,3},{4,70},{68... | collective-permute-start | bytes 983048 | tf_op jit(solution)/shard_map/ppermute | solution.py:215
  44.9 3.9 %collective-permute-done.3 = bf16[256,640]{1,0:T(8,128)(2,1)S(1)} collective-permute-done((bf16[256,640]{1,0:T(8,128)(2,1)S(1)}, bf16[256,640]{1,0:T(8,128)(2,1)S(1)}, u32[]{:S(2)}, u32[]{:S(2)}) %collective-permute-start.3) | collective-permute-done | bytes 327712 | tf_op jit(solution)/shard_map/ppermute | solution.py:215
  48.8 3.6 %collective-permute-done.4 = bf16[256,640]{1,0:T(8,128)(2,1)S(1)} collective-permute-done((bf16[256,640]{1,0:T(8,128)(2,1)S(1)}, bf16[256,640]{1,0:T(8,128)(2,1)S(1)}, u32[]{:S(2)}, u32[]{:S(2)}) %collective-permute-start.4) | collective-permute-done | bytes 327712 | tf_op jit(solution)/shard_map/ppermute | solution.py:215
  52.4 4.4 %collective-permute-done.5 = bf16[256,640]{1,0:T(8,128)(2,1)S(1)} collective-permute-done((bf16[256,640]{1,0:T(8,128)(2,1)S(1)}, bf16[256,640]{1,0:T(8,128)(2,1)S(1)}, u32[]{:S(2)}, u32[]{:S(2)}) %collective-permute-start.5) | collective-permute-done | bytes 327712 | tf_op jit(solution)/shard_map/ppermute | solution.py:215
  56.9 1.9 %collective-permute-start.6 = (bf16[1024,640]{1,0:T(8,128)(2,1)S(1)}, bf16[1024,640]{1,0:T(8,128)(2,1)}, u32[]{:S(2)}, u32[]{:S(2)}) collective-permute-start(bf16[1024,640]{1,0:T(8,128)(2,1)S(1)} %constant_dynamic-update-slice_fusion.refs_1_), channel_id=1, source_target_pairs={{0,1},{1,0},{2,3},{3,2},{4,5},{5,4},{6,7},{7,6},{8,9},{9,8},{10,11... | collective-permute-start | bytes 3932168 | tf_op jit(solution)/shard_map/ppermute | solution.py:248
  60.0 0.8 all-to-all-done
  60.8 11.1 %shard_map.95 = (f32[1024,256]{1,0:T(8,128)S(1)}, f32[1024,256]{1,0:T(8,128)S(1)}) custom-call(s32[4,32]{1,0:T(4,128)S(1)} %get-tuple-element.28.refs_0_, bf16[1024,640]{1,0:T(8,128)(2,1)S(1)} %constant_dynamic-update-slice_fusion.refs_1_, bf16[1024,256]{1,0:T(8,128)(2,1)S(1)} %bitcast.18, s32[1,1024]{1,0:T(1,128)S(1)} %add.164.refs_3_, ...), custom_call_target="tpu_custom_call" | custom-call | flops 1342177280 | bytes 4194304 | tf_op jit(solution)/shard_map/pallas_call | solution.py:141
  71.9 12.7 %shard_map.96 = (f32[1024,256]{1,0:T(8,128)S(1)}, bf16[1024,256]{1,0:T(8,128)(2,1)}) custom-call(s32[4,32]{1,0:T(4,128)S(1)} %get-tuple-element.27.refs_0_, bf16[1024,640]{1,0:T(8,128)(2,1)} %collective-permute-done.6.refs_1_, bf16[1024,256]{1,0:T(8,128)(2,1)S(1)} %bitcast.19, s32[1,1024]{1,0:T(1,128)S(1)} %add.171.refs_3_, s32[1024,1]{1,0:T(8,128)S(1)} %add.179.refs_4_, ...), custom_call_target="tpu_custom_call" | custom-call | flops 1342177280 | bytes 4194304 | tf_op jit(solution)/shard_map/pallas_call | solution.py:141
  84.6 1.9 %collective-permute-start.7 = (f32[1024,256]{1,0:T(8,128)S(1)}, f32[1024,256]{1,0:T(8,128)}, u32[]{:S(2)}, u32[]{:S(2)}) collective-permute-start(f32[1024,256]{1,0:T(8,128)S(1)} %get-tuple-element.9), channel_id=1, source_target_pairs={{0,1},{1,0},{2,3},{3,2},{4,5},{5,4},{6,7},{7,6},{8,9},{9,8},{10,11... | collective-permute-start | bytes 3145736 | tf_op jit(solution)/shard_map/ppermute | solution.py:270
  86.6 11.4 %all-to-all-start.1 = ((bf16[16,64,256]{2,1,0:T(8,128)(2,1)}), bf16[16,64,256]{2,1,0:T(8,128)(2,1)S(1)}, u32[]{:S(2)}, u32[]{:S(2)}) async-start(bf16[16,64,256]{2,1,0:T(8,128)(2,1)} %bitcast.11), calls=%async_computation.1 | async-start | bytes 1048576 | tf_op jit(solution)/shard_map/all_to_all | solution.py:269
  98.0 1.4 %fusion.10 = (bf16[1024,256]{1,0:T(8,128)(2,1)S(1)}, f32[1024,256]{1,0:T(8,128)S(1)}) fusion(f32[1024,256]{1,0:T(8,128)S(1)} %get-tuple-element.7, f32[1024,256]{1,0:T(8,128)} %collective-permute-done.7), kind=kLoop, calls=%fused_computation.55 | loop fusion | flops 524288 | bytes 3670016 | tf_op jit(solution)/shard_map/convert_element_type | solution.py:272
  99.4 2.5 %collective-permute-start.10 = (bf16[256,256]{1,0:T(8,128)(2,1)S(1)}, bf16[256,256]{1,0:T(8,128)(2,1)S(1)}, u32[]{:S(2)}, u32[]{:S(2)}) collective-permute-start(bf16[256,256]{1,0:T(8,128)(2,1)S(1)} %get-tuple-element.20), channel_id=1, source_target_pairs={{0,64},{64,2},{2,66},{66,0},{1,65},{65,3},{3,67},{67,1},{4,68},{68... | collective-permute-start | bytes 393224 | tf_op jit(solution)/shard_map/ppermute | solution.py:215
  101.9 4.5 %collective-permute-start.9 = (bf16[256,256]{1,0:T(8,128)(2,1)S(1)}, bf16[256,256]{1,0:T(8,128)(2,1)S(1)}, u32[]{:S(2)}, u32[]{:S(2)}) collective-permute-start(bf16[256,256]{1,0:T(8,128)(2,1)S(1)} %get-tuple-element.21), channel_id=1, source_target_pairs={{0,2},{64,66},{2,0},{66,64},{1,3},{65,67},{3,1},{67,65},{4,6},{68,... | collective-permute-start | bytes 393224 | tf_op jit(solution)/shard_map/ppermute | solution.py:215
  106.4 2.2 %collective-permute-start.8 = (bf16[256,256]{1,0:T(8,128)(2,1)S(1)}, bf16[256,256]{1,0:T(8,128)(2,1)S(1)}, u32[]{:S(2)}, u32[]{:S(2)}) collective-permute-start(bf16[256,256]{1,0:T(8,128)(2,1)S(1)} %get-tuple-element.19), channel_id=1, source_target_pairs={{0,66},{64,0},{2,64},{66,2},{1,67},{65,1},{3,65},{67,3},{4,70},{68... | collective-permute-start | bytes 393224 | tf_op jit(solution)/shard_map/ppermute | solution.py:215
  108.7 1.6 %collective-permute-done.9 = bf16[256,256]{1,0:T(8,128)(2,1)S(1)} collective-permute-done((bf16[256,256]{1,0:T(8,128)(2,1)S(1)}, bf16[256,256]{1,0:T(8,128)(2,1)S(1)}, u32[]{:S(2)}, u32[]{:S(2)}) %collective-permute-start.9) | collective-permute-done | bytes 131104 | tf_op jit(solution)/shard_map/ppermute | solution.py:215
  110.3 4.2 %collective-permute-done.8 = bf16[256,256]{1,0:T(8,128)(2,1)S(1)} collective-permute-done((bf16[256,256]{1,0:T(8,128)(2,1)S(1)}, bf16[256,256]{1,0:T(8,128)(2,1)S(1)}, u32[]{:S(2)}, u32[]{:S(2)}) %collective-permute-start.8) | collective-permute-done | bytes 131104 | tf_op jit(solution)/shard_map/ppermute | solution.py:215
  114.6 2.1 %collective-permute-start.13 = (f32[64,256]{1,0:T(8,128)S(1)}, f32[64,256]{1,0:T(8,128)S(1)}, u32[]{:S(2)}, u32[]{:S(2)}) collective-permute-start(f32[64,256]{1,0:T(8,128)S(1)} %get-tuple-element.23), channel_id=1, source_target_pairs={{0,128},{128,256},{256,384},{384,0},{1,129},{129,257},{257,385},{3... | collective-permute-start | bytes 196616 | tf_op jit(solution)/shard_map/ppermute | solution.py:215
  116.7 3.1 %collective-permute-start.12 = (f32[64,256]{1,0:T(8,128)S(1)}, f32[64,256]{1,0:T(8,128)S(1)}, u32[]{:S(2)}, u32[]{:S(2)}) collective-permute-start(f32[64,256]{1,0:T(8,128)S(1)} %get-tuple-element.24), channel_id=1, source_target_pairs={{0,256},{128,384},{256,0},{384,128},{1,257},{129,385},{257,1},{385... | collective-permute-start | bytes 196616 | tf_op jit(solution)/shard_map/ppermute | solution.py:215
  119.8 3.8 %collective-permute-start.11 = (f32[64,256]{1,0:T(8,128)S(1)}, f32[64,256]{1,0:T(8,128)S(1)}, u32[]{:S(2)}, u32[]{:S(2)}) collective-permute-start(f32[64,256]{1,0:T(8,128)S(1)} %get-tuple-element.22), channel_id=1, source_target_pairs={{0,384},{128,0},{256,128},{384,256},{1,385},{129,1},{257,129},{385... | collective-permute-start | bytes 196616 | tf_op jit(solution)/shard_map/ppermute | solution.py:215
  123.6 0.8 collective-permute-done.12
  124.3 2.3 %collective-permute-done.11 = f32[64,256]{1,0:T(8,128)S(1)} collective-permute-done((f32[64,256]{1,0:T(8,128)S(1)}, f32[64,256]{1,0:T(8,128)S(1)}, u32[]{:S(2)}, u32[]{:S(2)}) %collective-permute-start.11) | collective-permute-done | bytes 65568 | tf_op jit(solution)/shard_map/ppermute | solution.py:215
  (61 shorter events, 6.0 us)
Async XLA Ops:
  0.6 32.7 %copy-start.1 = (s32[1024]{0:T(1024)S(1)}, s32[1024]{0:T(1024)}, u32[]{:S(2)}) copy-start(s32[1024]{0:T(1024)} %param.13) | copy-start | bytes 12292
  4.9 29.4 %copy-start = (bf16[64,640]{1,0:T(8,128)(2,1)S(1)}, bf16[64,640]{1,0:T(8,128)(2,1)}, u32[]{:S(2)}) copy-start(bf16[64,640]{1,0:T(8,128)(2,1)} %shard_map.94) | copy-start | bytes 245764
  4.9 31.2 %collective-permute-start = (bf16[64,640]{1,0:T(8,128)(2,1)}, bf16[64,640]{1,0:T(8,128)(2,1)S(1)}, u32[]{:S(2)}, u32[]{:S(2)}) collective-permute-start(bf16[64,640]{1,0:T(8,128)(2,1)} %shard_map.94), channel_id=1, source_target_pairs={{0,128},{128,256},{256,384},{384,0},{1,129},{129,257},{257,385},{3... | collective-permute-start | bytes 245768 | tf_op jit(solution)/shard_map/ppermute | solution.py:215
  8.5 27.7 %collective-permute-start.1 = (bf16[64,640]{1,0:T(8,128)(2,1)}, bf16[64,640]{1,0:T(8,128)(2,1)S(1)}, u32[]{:S(2)}, u32[]{:S(2)}) collective-permute-start(bf16[64,640]{1,0:T(8,128)(2,1)} %shard_map.94), channel_id=1, source_target_pairs={{0,256},{128,384},{256,0},{384,128},{1,257},{129,385},{257,1},{385... | collective-permute-start | bytes 245768 | tf_op jit(solution)/shard_map/ppermute | solution.py:215
  13.1 23.1 %collective-permute-start.2 = (bf16[64,640]{1,0:T(8,128)(2,1)}, bf16[64,640]{1,0:T(8,128)(2,1)S(1)}, u32[]{:S(2)}, u32[]{:S(2)}) collective-permute-start(bf16[64,640]{1,0:T(8,128)(2,1)} %shard_map.94), channel_id=1, source_target_pairs={{0,384},{128,0},{256,128},{384,256},{1,385},{129,1},{257,129},{385... | collective-permute-start | bytes 245768 | tf_op jit(solution)/shard_map/ppermute | solution.py:215
  18.1 42.7 %all-to-all-start = ((bf16[16,64,256]{2,1,0:T(8,128)(2,1)}), bf16[16,64,256]{2,1,0:T(8,128)(2,1)S(1)}, u32[]{:S(2)}, u32[]{:S(2)}) async-start(bf16[16,64,256]{2,1,0:T(8,128)(2,1)} %broadcast_in_dim.66), calls=%async_computation | async-start | bytes 1048576 | tf_op jit(solution)/shard_map/all_to_all | solution.py:241
  36.2 12.5 %collective-permute-start.3 = (bf16[256,640]{1,0:T(8,128)(2,1)S(1)}, bf16[256,640]{1,0:T(8,128)(2,1)S(1)}, u32[]{:S(2)}, u32[]{:S(2)}) collective-permute-start(bf16[256,640]{1,0:T(8,128)(2,1)S(1)} %pad_maximum_fusion), channel_id=1, source_target_pairs={{0,64},{64,2},{2,66},{66,0},{1,65},{65,3},{3,67},{67,1},{4,68},{68... | collective-permute-start | bytes 983048 | tf_op jit(solution)/shard_map/ppermute | solution.py:215
  38.4 14.0 %collective-permute-start.4 = (bf16[256,640]{1,0:T(8,128)(2,1)S(1)}, bf16[256,640]{1,0:T(8,128)(2,1)S(1)}, u32[]{:S(2)}, u32[]{:S(2)}) collective-permute-start(bf16[256,640]{1,0:T(8,128)(2,1)S(1)} %pad_maximum_fusion), channel_id=1, source_target_pairs={{0,2},{64,66},{2,0},{66,64},{1,3},{65,67},{3,1},{67,65},{4,6},{68,... | collective-permute-start | bytes 983048 | tf_op jit(solution)/shard_map/ppermute | solution.py:215
  42.9 14.0 %collective-permute-start.5 = (bf16[256,640]{1,0:T(8,128)(2,1)S(1)}, bf16[256,640]{1,0:T(8,128)(2,1)S(1)}, u32[]{:S(2)}, u32[]{:S(2)}) collective-permute-start(bf16[256,640]{1,0:T(8,128)(2,1)S(1)} %pad_maximum_fusion), channel_id=1, source_target_pairs={{0,66},{64,0},{2,64},{66,2},{1,67},{65,1},{3,65},{67,3},{4,70},{68... | collective-permute-start | bytes 983048 | tf_op jit(solution)/shard_map/ppermute | solution.py:215
  56.9 15.0 %collective-permute-start.6 = (bf16[1024,640]{1,0:T(8,128)(2,1)S(1)}, bf16[1024,640]{1,0:T(8,128)(2,1)}, u32[]{:S(2)}, u32[]{:S(2)}) collective-permute-start(bf16[1024,640]{1,0:T(8,128)(2,1)S(1)} %constant_dynamic-update-slice_fusion.refs_1_), channel_id=1, source_target_pairs={{0,1},{1,0},{2,3},{3,2},{4,5},{5,4},{6,7},{7,6},{8,9},{9,8},{10,11... | collective-permute-start | bytes 3932168 | tf_op jit(solution)/shard_map/ppermute | solution.py:248
  84.6 13.3 %collective-permute-start.7 = (f32[1024,256]{1,0:T(8,128)S(1)}, f32[1024,256]{1,0:T(8,128)}, u32[]{:S(2)}, u32[]{:S(2)}) collective-permute-start(f32[1024,256]{1,0:T(8,128)S(1)} %get-tuple-element.9), channel_id=1, source_target_pairs={{0,1},{1,0},{2,3},{3,2},{4,5},{5,4},{6,7},{7,6},{8,9},{9,8},{10,11... | collective-permute-start | bytes 3145736 | tf_op jit(solution)/shard_map/ppermute | solution.py:270
  86.6 40.7 %all-to-all-start.1 = ((bf16[16,64,256]{2,1,0:T(8,128)(2,1)}), bf16[16,64,256]{2,1,0:T(8,128)(2,1)S(1)}, u32[]{:S(2)}, u32[]{:S(2)}) async-start(bf16[16,64,256]{2,1,0:T(8,128)(2,1)} %bitcast.11), calls=%async_computation.1 | async-start | bytes 1048576 | tf_op jit(solution)/shard_map/all_to_all | solution.py:269
  99.4 9.2 %collective-permute-start.10 = (bf16[256,256]{1,0:T(8,128)(2,1)S(1)}, bf16[256,256]{1,0:T(8,128)(2,1)S(1)}, u32[]{:S(2)}, u32[]{:S(2)}) collective-permute-start(bf16[256,256]{1,0:T(8,128)(2,1)S(1)} %get-tuple-element.20), channel_id=1, source_target_pairs={{0,64},{64,2},{2,66},{66,0},{1,65},{65,3},{3,67},{67,1},{4,68},{68... | collective-permute-start | bytes 393224 | tf_op jit(solution)/shard_map/ppermute | solution.py:215
  101.9 8.4 %collective-permute-start.9 = (bf16[256,256]{1,0:T(8,128)(2,1)S(1)}, bf16[256,256]{1,0:T(8,128)(2,1)S(1)}, u32[]{:S(2)}, u32[]{:S(2)}) collective-permute-start(bf16[256,256]{1,0:T(8,128)(2,1)S(1)} %get-tuple-element.21), channel_id=1, source_target_pairs={{0,2},{64,66},{2,0},{66,64},{1,3},{65,67},{3,1},{67,65},{4,6},{68,... | collective-permute-start | bytes 393224 | tf_op jit(solution)/shard_map/ppermute | solution.py:215
  106.4 8.1 %collective-permute-start.8 = (bf16[256,256]{1,0:T(8,128)(2,1)S(1)}, bf16[256,256]{1,0:T(8,128)(2,1)S(1)}, u32[]{:S(2)}, u32[]{:S(2)}) collective-permute-start(bf16[256,256]{1,0:T(8,128)(2,1)S(1)} %get-tuple-element.19), channel_id=1, source_target_pairs={{0,66},{64,0},{2,64},{66,2},{1,67},{65,1},{3,65},{67,3},{4,70},{68... | collective-permute-start | bytes 393224 | tf_op jit(solution)/shard_map/ppermute | solution.py:215
  114.6 9.0 %collective-permute-start.13 = (f32[64,256]{1,0:T(8,128)S(1)}, f32[64,256]{1,0:T(8,128)S(1)}, u32[]{:S(2)}, u32[]{:S(2)}) collective-permute-start(f32[64,256]{1,0:T(8,128)S(1)} %get-tuple-element.23), channel_id=1, source_target_pairs={{0,128},{128,256},{256,384},{384,0},{1,129},{129,257},{257,385},{3... | collective-permute-start | bytes 196616 | tf_op jit(solution)/shard_map/ppermute | solution.py:215
  116.7 7.7 %collective-permute-start.12 = (f32[64,256]{1,0:T(8,128)S(1)}, f32[64,256]{1,0:T(8,128)S(1)}, u32[]{:S(2)}, u32[]{:S(2)}) collective-permute-start(f32[64,256]{1,0:T(8,128)S(1)} %get-tuple-element.24), channel_id=1, source_target_pairs={{0,256},{128,384},{256,0},{384,128},{1,257},{129,385},{257,1},{385... | collective-permute-start | bytes 196616 | tf_op jit(solution)/shard_map/ppermute | solution.py:215
  119.8 6.9 %collective-permute-start.11 = (f32[64,256]{1,0:T(8,128)S(1)}, f32[64,256]{1,0:T(8,128)S(1)}, u32[]{:S(2)}, u32[]{:S(2)}) collective-permute-start(f32[64,256]{1,0:T(8,128)S(1)} %get-tuple-element.22), channel_id=1, source_target_pairs={{0,384},{128,0},{256,128},{384,256},{1,385},{129,1},{257,129},{385... | collective-permute-start | bytes 196616 | tf_op jit(solution)/shard_map/ppermute | solution.py:215

commit v3 on v0

v3 whole, which is shorter than its diff:
```python
import jax
import jax.numpy as jnp
from jax import lax
from jax.experimental import pallas as pl
from jax.experimental.pallas import tpu as pltpu
from jax.sharding import Mesh, PartitionSpec as P

HEADS = 2
HD = 128
HALF = 32
SCALE = HD ** (-0.5)
LOG2E = 1.4426950408889634
PIECES = 3
STATS = 16
QT = 256
KT = 256
TOGETHER = 2
VMEM = pl.BlockSpec(memory_space=pltpu.VMEM)
SMEM = pl.BlockSpec(memory_space=pltpu.SMEM)


def dot(a, b):
    return jnp.dot(a, b, preferred_element_type=jnp.float32)


def dot_nt(a, b):
    return lax.dot_general(a, b, (((1,), (1,)), ((), ())), preferred_element_type=jnp.float32)


def tile_kernel(rank_q, order_q, sorted_q, rank_k, sorted_k, *refs):
    q_refs = refs[:4]
    kv_refs = refs[4:6]
    posq_ref, near_ref, far_ref, own_ref, sib_ref = refs[6:11]
    qs, gs, rows, ks, vs, kt, dqt, dk, dv, todo = refs[11:]
    n_q = qs.shape[0]
    n_k = ks.shape[0]
    per_q = QT // HALF
    per_k = KT // HALF
    part_q = (q_refs[0].shape[0] - STATS) // HALF
    part_k = kv_refs[0].shape[0] // HALF

    for a in range(4):
        for b in range(part_q):
            place = rank_q[a * part_q + b]
            j = place // per_q
            r = pl.multiple_of(place % per_q * HALF, HALF)
            cut = slice(b * HALF, (b + 1) * HALF)
            for h in range(HEADS):
                qs[j, pl.ds(h * QT + r, HALF), :] = q_refs[a][cut, h * HD:(h + 1) * HD]
                gs[j, pl.ds(h * QT + r, HALF), :] = q_refs[a][cut, (HEADS + h) * HD:(HEADS + h + 1) * HD]
    for a in range(2):
        for b in range(part_k):
            place = rank_k[a * part_k + b]
            i = place // per_k
            r = pl.multiple_of(place % per_k * HALF, HALF)
            cut = slice(b * HALF, (b + 1) * HALF)
            ks[i, pl.ds(r, HALF), :] = kv_refs[a][cut, :HD]
            vs[i, pl.ds(r, HALF), :] = kv_refs[a][cut, HD:]

    stat_refs = rows.at[pl.ds(n_q, 4)]
    base = q_refs[0].shape[0] - STATS
    for a in range(4):
        stat_refs[a] = q_refs[a][base:, :].astype(jnp.float32)
    quarter = lax.broadcasted_iota(jnp.int32, (STATS, 128), 1) // HALF
    for t in range(n_q * QT // 128):
        line = jnp.zeros((STATS, 128), jnp.float32)
        for u in range(4):
            b = order_q[t * 4 + u]
            column = pl.multiple_of(b % part_q // 2 * 128, 128)
            piece = rows[n_q + b // part_q, :, pl.ds(column, 128)]
            piece = pltpu.roll(piece, (u - b % 2 + 4) % 4 * HALF, 1)
            line = jnp.where(quarter == u, piece, line)
        j, c = t // (QT // 128), t % (QT // 128)
        n = 2 * HEADS
        stat = line[:n] + line[n:2 * n] + line[2 * n:3 * n]
        for h in range(HEADS):
            cut = slice(h * QT + c * 128, h * QT + (c + 1) * 128)
            rows[j, 0:1, cut] = stat[h:h + 1] * LOG2E
            rows[j, 1:2, cut] = stat[HEADS + h:HEADS + h + 1]

    for i in range(n_k):
        kt[i] = ks[i].astype(jnp.float32).T.astype(jnp.bfloat16)

    dk[...] = jnp.zeros_like(dk)
    dv[...] = jnp.zeros_like(dv)
    dqt[...] = jnp.zeros_like(dqt)

    count = jnp.int32(0)
    dead = jnp.int32(0)
    for j in range(n_q):
        top = sorted_q[j * per_q + per_q - 1]
        for i in range(n_k):
            live = sorted_k[i * per_k] <= top
            todo[count] = jnp.int32(j * n_k + i)
            count = count + live.astype(jnp.int32)
            dead = jnp.where(live, dead, j * n_k + i)
    for u in range(TOGETHER - 1):
        todo[count + u] = dead

    within = lax.broadcasted_iota(jnp.int32, (HALF, 128), 0)

    def one(t):
        j = todo[t] // n_k
        i = todo[t] % n_k
        q, g, k, v = qs[j], gs[j], ks[i], vs[i]
        posk = jnp.concatenate([within + sorted_k[i * per_k + b] * HALF for b in range(per_k)], axis=0)
        posk = jnp.concatenate([posk] * (HEADS * QT // 128), axis=1)
        s = dot_nt(k, q)
        p = jnp.where(posk <= posq_ref[j], jnp.exp2(s * (SCALE * LOG2E) - rows[j, 0:1, :]), 0.0)
        dp = dot_nt(v, g)
        ds = (p * (dp - rows[j, 1:2, :])).astype(jnp.bfloat16)
        dv[i] += dot(p.astype(jnp.bfloat16), g)
        dk[i] += dot(ds, q)
        dqt[j] += dot(kt[i], ds)

    def some(t, c):
        for u in range(TOGETHER):
            one(t * TOGETHER + u)
        return c

    lax.fori_loop(0, (count + TOGETHER - 1) // TOGETHER, some, 0)

    for j in range(n_q):
        for h in range(HEADS):
            back = dqt[j, :, h * QT:(h + 1) * QT].T
            half = back.astype(jnp.bfloat16)
            for b in range(per_q):
                to = order_q[j * per_q + b]
                cut = slice(b * HALF, (b + 1) * HALF)
                lane = slice(h * HD, (h + 1) * HD)
                dst = pl.multiple_of(to * HALF, HALF)
                far_ref[pl.ds(dst, HALF), lane] = half[cut]

                @pl.when(to < part_q)
                def _():
                    near_ref[pl.ds(dst, HALF), lane] = back[cut]
    for a in range(2):
        for b in range(part_k):
            place = rank_k[a * part_k + b]
            i = place // per_k
            r = pl.multiple_of(place % per_k * HALF, HALF)
            cut = slice(b * HALF, (b + 1) * HALF)
            out = own_ref if a == 0 else sib_ref
            out[cut, :HD] = dk[i, pl.ds(r, HALF), :].astype(out.dtype)
            out[cut, HD:] = dv[i, pl.ds(r, HALF), :].astype(out.dtype)


def tile_grads(q_parts, kv_parts, table_q, table_k):
    part = q_parts[0].shape[0] - STATS
    rows_q = 4 * part
    part_k = kv_parts[0].shape[0]
    rows_k = 2 * part_k
    n_q, n_k = rows_q // QT, rows_k // KT
    rank_q, order_q, sorted_q = in_order(table_q)
    rank_k, _, sorted_k = in_order(table_k)
    posq = positions(sorted_q).reshape(n_q, 1, QT)
    posq = jnp.concatenate([posq] * HEADS, axis=2)
    bf, f32 = jnp.bfloat16, jnp.float32
    return pl.pallas_call(
        tile_kernel,
        out_shape=(
            jax.ShapeDtypeStruct((part, HEADS * HD), f32),
            jax.ShapeDtypeStruct((rows_q, HEADS * HD), bf),
            jax.ShapeDtypeStruct((part_k, 2 * HD), f32),
            jax.ShapeDtypeStruct((part_k, 2 * HD), bf),
        ),
        in_specs=[SMEM] * 5 + [VMEM] * 7,
        out_specs=(VMEM,) * 4,
        scratch_shapes=[
            pltpu.VMEM((n_q, HEADS * QT, HD), bf),
            pltpu.VMEM((n_q, HEADS * QT, HD), bf),
            pltpu.VMEM((n_q + 4, STATS, HEADS * QT), f32),
            pltpu.VMEM((n_k, KT, HD), bf),
            pltpu.VMEM((n_k, KT, HD), bf),
            pltpu.VMEM((n_k, HD, KT), bf),
            pltpu.VMEM((n_q, HD, HEADS * QT), f32),
            pltpu.VMEM((n_k, KT, HD), f32),
            pltpu.VMEM((n_k, KT, HD), f32),
            pltpu.SMEM((n_q * n_k + TOGETHER,), jnp.int32),
        ],
        compiler_params=pltpu.CompilerParams(vmem_limit_bytes=40 * 1024 * 1024),
        cost_estimate=pl.CostEstimate(
            flops=rows_q * HEADS * rows_k * HD * 5,
            bytes_accessed=4 * 1024 * 1024,
            transcendentals=rows_q * HEADS * rows_k // 2,
        ),
    )(rank_q, order_q, sorted_q, rank_k, sorted_k, *q_parts, *kv_parts, posq)


def in_order(entries):
    n = entries.shape[0]
    rank = jnp.sum((entries[None, :] < entries[:, None]).astype(jnp.int32), axis=1)
    hit = rank[None, :] == jnp.arange(n, dtype=jnp.int32)[:, None]
    place = jnp.arange(n, dtype=jnp.int32)
    order = jnp.sum(jnp.where(hit, place[None, :], 0), axis=1)
    ordered = jnp.sum(jnp.where(hit, entries[None, :], 0), axis=1)
    return rank, order, ordered


def positions(ordered):
    return (ordered[:, None] * HALF + jnp.arange(HALF, dtype=jnp.int32)[None, :]).reshape(-1)


def pack_kv_kernel(k_ref, v_ref, out_ref):
    for n in range(out_ref.shape[0]):
        out_ref[n, :, :HD] = k_ref[...]
        out_ref[n, :, HD:] = v_ref[...]


def pack_kv(keys, values, copies):
    return pl.pallas_call(
        pack_kv_kernel,
        out_shape=jax.ShapeDtypeStruct((copies, keys.shape[0], 2 * HD), keys.dtype),
        in_specs=[VMEM] * 2,
        out_specs=VMEM,
    )(keys, values)


def pack_q_kernel(q_ref, g_ref, lse_ref, delta_ref, out_ref, wide):
    width = HEADS * HD
    rows = q_ref.shape[0]
    out_ref[:rows, :width] = q_ref[...]
    out_ref[:rows, width:] = g_ref[...]
    out_ref[rows:, :] = jnp.zeros((STATS, 2 * width), jnp.bfloat16)
    wide[...] = jnp.zeros_like(wide)
    n = 2 * HEADS
    for k in range(PIECES):
        wide[k * n:k * n + HEADS, :rows] = lse_ref[...]
        wide[k * n + HEADS:(k + 1) * n, :rows] = delta_ref[...]
    x = wide[...]
    piece = lax.broadcasted_iota(jnp.int32, x.shape, 0) // n
    out = jnp.zeros_like(x)
    for k in range(PIECES):
        part = x.astype(jnp.bfloat16).astype(jnp.float32)
        x = x - part
        out = jnp.where(piece == k, part, out)
    out_ref[rows:, :128] = out.astype(jnp.bfloat16)


def pack_q(queries, out_grad, log_sum, delta):
    rows = queries.shape[0]
    return pl.pallas_call(
        pack_q_kernel,
        out_shape=jax.ShapeDtypeStruct((rows + STATS, 2 * HEADS * HD), jnp.bfloat16),
        in_specs=[VMEM] * 4,
        out_specs=VMEM,
        scratch_shapes=[pltpu.VMEM((STATS, 128), jnp.float32)],
    )(queries, out_grad, log_sum.T, delta.T)


def join_kernel(*refs):
    parts, out_ref = refs[:-1], refs[-1]
    rows = parts[0].shape[0] - STATS
    for a, part in enumerate(parts):
        out_ref[a * rows:(a + 1) * rows, :] = part[:rows, :]
        out_ref[len(parts) * rows:, a * 128:(a + 1) * 128] = part[rows:, :128]


def join(parts):
    rows, width = parts[0].shape
    return pl.pallas_call(
        join_kernel,
        out_shape=jax.ShapeDtypeStruct((len(parts) * (rows - STATS) + STATS, width), parts[0].dtype),
        in_specs=[VMEM] * len(parts),
        out_specs=VMEM,
    )(*parts)


def finish_kv_kernel(in_ref, k_ref, v_ref):
    total = in_ref[0].astype(jnp.float32)
    for n in range(1, in_ref.shape[0]):
        total = total + in_ref[n].astype(jnp.float32)
    k_ref[...] = (total[:, :HD] * SCALE).astype(k_ref.dtype)
    v_ref[...] = total[:, HD:].astype(v_ref.dtype)


def finish_kv(x):
    out = jax.ShapeDtypeStruct((x.shape[1], HD), jnp.bfloat16)
    return pl.pallas_call(
        finish_kv_kernel, out_shape=(out, out), in_specs=[VMEM], out_specs=(VMEM, VMEM)
    )(x)


def from_offset(x, axes, index_of, d):
    return lax.ppermute(x, axes, [(index_of(j), index_of((j + d) % 4)) for j in range(4)])


def along_x(j):
    return j


def along_y(j):
    return (j % 2) * 2 + j // 2


def other_core(x):
    return lax.ppermute(x, "core", [(0, 1), (1, 0)])


def back_from(table, index, axis):
    head = lax.slice_in_dim(table, 0, 1, axis=axis)
    tail = jnp.flip(lax.slice_in_dim(table, 1, 4, axis=axis), axis)
    return lax.dynamic_slice_in_dim(jnp.concatenate([head, tail, head, tail], axis), (4 - index) % 4, 4, axis)


def pick(table, *choices):
    for axis, index in choices:
        table = lax.dynamic_index_in_dim(table, index, axis, keepdims=False)
    return table


def local(queries, keys, values, out_grad, log_sum, delta, block_table):
    rows = queries.shape[0]
    width = HEADS * HD
    nx, nyl, nz, nyh, nc = (lax.axis_size(a) for a in ("x", "yl", "z", "yh", "core"))
    ix, iyl, iz, iyh, ic = (lax.axis_index(a) for a in ("x", "yl", "z", "yh", "core"))
    iy = iyh * nyl + iyl
    y = ("yl", "yh")

    kv_own = lax.all_to_all(pack_kv(keys, values, nz), "z", split_axis=0, concat_axis=0, tiled=True)
    kv_own = kv_own.reshape(nz * rows, 2 * HD)
    kv_sib = other_core(kv_own)
    packed = pack_q(queries, out_grad, log_sum, delta)
    row = join([packed] + [from_offset(packed, "x", along_x, d) for d in (1, 2, 3)])
    q_parts = [row] + [from_offset(row, y, along_y, d) for d in (1, 2, 3)]

    table_q = pick(block_table.reshape(nx, nyl, nz, nyh, nc, 2), (2, iz), (3, ic))
    table_q = table_q.transpose(2, 1, 0, 3).reshape(nyh * nyl, nx, 2)
    table_q = back_from(back_from(table_q, iy, 0), ix, 1).reshape(-1)
    table_k = pick(block_table.reshape(nz, nyh, nc, nx, nyl, 2), (1, iyh), (2, ix), (2, iyl))
    table_k = jnp.concatenate([pick(table_k, (1, c)).reshape(-1) for c in (ic, nc - 1 - ic)])

    near, far, dkv_own, dkv_sib = tile_grads(q_parts, [kv_own, kv_sib], table_q, table_k)

    dkv = (dkv_own + other_core(dkv_sib).astype(jnp.float32)).astype(jnp.bfloat16)
    dkv = lax.all_to_all(dkv.reshape(nz, rows, 2 * HD), "z", split_axis=0, concat_axis=0, tiled=True)
    far = far.reshape(nyl * nyh, nx * rows, width)
    for d in (1, 2, 3):
        near = near + from_offset(far[d], y, along_y, 4 - d).astype(jnp.float32)
    near = near.reshape(nx, rows, width)
    total = near[0]
    for d in (1, 2, 3):
        total = total + from_offset(near[d], "x", along_x, 4 - d)
    q_grad = (total * SCALE).astype(jnp.bfloat16)
    k_grad, v_grad = finish_kv(dkv)
    return (q_grad, k_grad, v_grad)


def solution(mesh):
    fine = Mesh(mesh.devices.reshape(4, 2, 16, 2, 2), ("x", "yl", "z", "yh", "core"))
    q_rows = P(("x", "yl", "z", "yh", "core"), None)
    k_rows = P(("z", "yh", "core", "x", "yl"), None)
    return jax.shard_map(
        local,
        mesh=fine,
        in_specs=(q_rows, k_rows, k_rows, q_rows, q_rows, q_rows, P()),
        out_specs=(q_rows, k_rows, k_rows),
        check_vma=False,
    )
```

time: 560 us -> 134 us (0.24)
  waiting for transfers between devices: 261 us -> 36.9 us
  blocking collectives: 212 us -> 0 us
  starting transfers between devices: 10.9 us -> 65.6 us
  local copies, waits for them, and re-layouts: 29.8 us -> 5.62 us
  matrix products: 20.5 us -> 0 us
  Pallas kernels: 0 us -> 19.4 us
  between operations: 13.8 us -> 1.04 us
  other arithmetic: 9.6 us -> 2.49 us
    all_gather x4 -> x0, blocking collectives: 212 us -> none  [the longest x1 79.6 us: local(): lax.all_gather(log_sum, 'kcol', axis=0, tiled=True)]
    reduce_scatter x2 -> x0, waiting for transfers between devices: 90.4 us -> none  [the longest x1 45.2 us: local(): lax.psum_scatter(value_part, 'qrow', scatter_dimension=0, tiled=True)]
    all_to_all x1 -> x2, waiting for transfers between devices: 96.4 us -> 15 us  [the longest x1 15 us: local(): lax.all_to_all(pack_kv(keys, values, nz), 'z', split_axis=0, concat_axis=...]
    all_gather x2 -> x0, waiting for transfers between devices: 72 us -> none  [the longest x1 72 us: local(): lax.all_gather(out_grad, 'kcol', axis=0, tiled=True)]
    ppermute x0 -> x14, starting transfers between devices: none -> 44.2 us  [the longest x12 40.3 us: from_offset(): lax.ppermute(x, axes, [(index_of(j), index_of((j + d) % 4)) for j in rang...]
    ppermute x0 -> x14, waiting for transfers between devices: none -> 21.8 us  [the longest x12 19.9 us: from_offset(): lax.ppermute(x, axes, [(index_of(j), index_of((j + d) % 4)) for j in rang...]
    dot_general x40 -> x0, matrix products: 20.5 us -> none  [the longest x8 5.11 us: one_block(): jnp.einsum('qhd,kd->hqk', query_part, key_all, preferred_element_type=jnp...]
    pallas_call x0 -> x5, Pallas kernels: none -> 19.4 us  [the longest x1 12.9 us: tile_grads(): pl.pallas_call(tile_kernel, out_shape=(jax.ShapeDtypeStruct((part, HEADS...]
  transfers between devices with their start and end apart: 5 -> 16, of which waited for: 4 -> 7; matrix products, arithmetic and copies ran while one was open for 2% -> 3% of each run, Pallas kernels for 0% -> 2%
where the time goes in v3:
time: 134 us; the launch traced here: 131 us
  starting transfers between devices  65.6 us (49%)
  waiting for transfers between devices  36.9 us (28%)
  Pallas kernels  19.4 us (14%)
  local copies, waits for them, and re-layouts  5.62 us (4%)
  other arithmetic  2.49 us (2%)
    ppermute x12, starting transfers between devices, from_offset(): lax.ppermute(x, axes, [(index_of(j), index_of((j + d) % 4)) for j in rang...  40.3 us
    ppermute x12, waiting for transfers between devices, from_offset(): lax.ppermute(x, axes, [(index_of(j), index_of((j + d) % 4)) for j in rang...  19.9 us
    all_to_all x1, starting transfers between devices, local(): lax.all_to_all(pack_kv(keys, values, nz), 'z', split_axis=0, concat_axis=...  15.2 us
    all_to_all x1, waiting for transfers between devices, local(): lax.all_to_all(pack_kv(keys, values, nz), 'z', split_axis=0, concat_axis=...  15 us
    pallas_call x1, Pallas kernels, tile_grads(): pl.pallas_call(tile_kernel, out_shape=(jax.ShapeDtypeStruct((part, HEADS...  12.9 us
    all_to_all x1, starting transfers between devices, local(): lax.all_to_all(dkv.reshape(nz, rows, 2 * HD), 'z', split_axis=0, concat_a...  6.29 us
    ppermute x2, starting transfers between devices, other_core(): return lax.ppermute(x, 'core', [(0, 1), (1, 0)])  3.83 us
    unnamed x12, local copies, waits for them, and re-layouts  3.7 us
  transfers between devices with their start and end apart: 16, of which 7 were waited for; matrix products, arithmetic and copies ran while one was open for 3% of the time, Pallas kernels for 2%

profile of v3, /device:TPU:24, one launch (start us, length us, event | category | flops | bytes accessed | tf_op | source)
XLA Modules:
  0.0 131.1 jit_solution(125787859204188416)
XLA Ops:
  0.6 1.6 %shard_map.96 = bf16[16,64,256]{2,1,0:T(8,128)(2,1)} custom-call(bf16[64,128]{1,0:T(8,128)(2,1)} %k_ref.1, bf16[64,128]{1,0:T(8,128)(2,1)} %v_ref.1), custom_call_target="tpu_custom_call" | custom-call | tf_op jit(solution)/shard_map/pallas_call | solution.py:211
  2.2 15.2 %all-to-all-start = ((bf16[16,64,256]{2,1,0:T(8,128)(2,1)}), bf16[16,64,256]{2,1,0:T(8,128)(2,1)S(1)}, u32[]{:S(2)}, u32[]{:S(2)}) async-start(bf16[16,64,256]{2,1,0:T(8,128)(2,1)} %shard_map.96), calls=%async_computation | async-start | bytes 1048576 | tf_op jit(solution)/shard_map/all_to_all | solution.py:320
  17.4 1.4 %shard_map.94.refs_0_ = bf16[80,512]{1,0:T(8,128)(2,1)} custom-call(bf16[64,256]{1,0:T(8,128)(2,1)} %q_ref.1, bf16[64,256]{1,0:T(8,128)(2,1)} %g_ref.1, f32[2,64]{1,0:T(2,128)} %bitcast.15, f32[2,64]{1,0:T(2,128)} %bitcast.16), custom_call_target="tpu_custom_call" | custom-call | tf_op jit(solution)/shard_map/pallas_call | solution.py:242
  18.9 4.7 %collective-permute-start.2 = (bf16[80,512]{1,0:T(8,128)(2,1)}, bf16[80,512]{1,0:T(8,128)(2,1)S(1)}, u32[]{:S(2)}, u32[]{:S(2)}) collective-permute-start(bf16[80,512]{1,0:T(8,128)(2,1)} %shard_map.94.refs_0_), channel_id=1, source_target_pairs={{0,384},{128,0},{256,128},{384,256},{1,385},{129,1},{257,129},{385... | collective-permute-start | bytes 245768 | tf_op jit(solution)/shard_map/ppermute | solution.py:285
  23.5 2.7 %collective-permute-start.1 = (bf16[80,512]{1,0:T(8,128)(2,1)}, bf16[80,512]{1,0:T(8,128)(2,1)S(1)}, u32[]{:S(2)}, u32[]{:S(2)}) collective-permute-start(bf16[80,512]{1,0:T(8,128)(2,1)} %shard_map.94.refs_0_), channel_id=1, source_target_pairs={{0,256},{128,384},{256,0},{384,128},{1,257},{129,385},{257,1},{385... | collective-permute-start | bytes 245768 | tf_op jit(solution)/shard_map/ppermute | solution.py:285
  26.2 2.8 %collective-permute-start = (bf16[80,512]{1,0:T(8,128)(2,1)}, bf16[80,512]{1,0:T(8,128)(2,1)S(1)}, u32[]{:S(2)}, u32[]{:S(2)}) collective-permute-start(bf16[80,512]{1,0:T(8,128)(2,1)} %shard_map.94.refs_0_), channel_id=1, source_target_pairs={{0,128},{128,256},{256,384},{384,0},{1,129},{129,257},{257,385},{3... | collective-permute-start | bytes 245768 | tf_op jit(solution)/shard_map/ppermute | solution.py:285
  29.1 0.7 copy-done.5
  31.5 15.0 %all-to-all-done = bf16[16,64,256]{2,1,0:T(8,128)(2,1)S(1)} async-done(((bf16[16,64,256]{2,1,0:T(8,128)(2,1)}), bf16[16,64,256]{2,1,0:T(8,128)(2,1)S(1)}, u32[]{:S(2)}, u32[]{:S(2)}) %all-to-all-start) | async-done | bytes 524320 | tf_op jit(solution)/shard_map/all_to_all | solution.py:320
  46.5 1.9 %collective-permute-start.6 = (bf16[1024,256]{1,0:T(8,128)(2,1)S(1)}, bf16[1024,256]{1,0:T(8,128)(2,1)S(1)}, u32[]{:S(2)}, u32[]{:S(2)}) collective-permute-start(bf16[1024,256]{1,0:T(8,128)(2,1)S(1)} %bitcast.10), channel_id=1, source_target_pairs={{0,1},{1,0},{2,3},{3,2},{4,5},{5,4},{6,7},{7,6},{8,9},{9,8},{10,11... | collective-permute-start | bytes 1572872 | tf_op jit(solution)/shard_map/ppermute | solution.py:297
  50.5 1.7 %shard_map.95.refs_0_ = bf16[272,512]{1,0:T(8,128)(2,1)} custom-call(bf16[80,512]{1,0:T(8,128)(2,1)} %shard_map.94.refs_0_, bf16[80,512]{1,0:T(8,128)(2,1)} %copy-done.4, bf16[80,512]{1,0:T(8,128)(2,1)} %copy-done.3, bf16[80,512]{1,0:T(8,128)(2,1)} %copy-done.2), custom_call_target="tpu_custom_call" | custom-call | tf_op jit(solution)/shard_map/pallas_call | solution.py:261
  52.2 2.6 %collective-permute-start.5 = (bf16[272,512]{1,0:T(8,128)(2,1)}, bf16[272,512]{1,0:T(8,128)(2,1)S(1)}, u32[]{:S(2)}, u32[]{:S(2)}) collective-permute-start(bf16[272,512]{1,0:T(8,128)(2,1)} %shard_map.95.refs_0_), channel_id=1, source_target_pairs={{0,66},{64,0},{2,64},{66,2},{1,67},{65,1},{3,65},{67,3},{4,70},{68... | collective-permute-start | bytes 835592 | tf_op jit(solution)/shard_map/ppermute | solution.py:285
  54.9 2.8 %collective-permute-start.4 = (bf16[272,512]{1,0:T(8,128)(2,1)}, bf16[272,512]{1,0:T(8,128)(2,1)S(1)}, u32[]{:S(2)}, u32[]{:S(2)}) collective-permute-start(bf16[272,512]{1,0:T(8,128)(2,1)} %shard_map.95.refs_0_), channel_id=1, source_target_pairs={{0,2},{64,66},{2,0},{66,64},{1,3},{65,67},{3,1},{67,65},{4,6},{68,... | collective-permute-start | bytes 835592 | tf_op jit(solution)/shard_map/ppermute | solution.py:285
  57.7 4.1 %collective-permute-start.3 = (bf16[272,512]{1,0:T(8,128)(2,1)}, bf16[272,512]{1,0:T(8,128)(2,1)S(1)}, u32[]{:S(2)}, u32[]{:S(2)}) collective-permute-start(bf16[272,512]{1,0:T(8,128)(2,1)} %shard_map.95.refs_0_), channel_id=1, source_target_pairs={{0,64},{64,2},{2,66},{66,0},{1,65},{65,3},{3,67},{67,1},{4,68},{68... | collective-permute-start | bytes 835592 | tf_op jit(solution)/shard_map/ppermute | solution.py:285
  62.2 8.4 %collective-permute-done.5.refs_3_ = bf16[272,512]{1,0:T(8,128)(2,1)S(1)} collective-permute-done((bf16[272,512]{1,0:T(8,128)(2,1)}, bf16[272,512]{1,0:T(8,128)(2,1)S(1)}, u32[]{:S(2)}, u32[]{:S(2)}) %collective-permute-start.5) | collective-permute-done | bytes 278560 | tf_op jit(solution)/shard_map/ppermute | solution.py:285
  70.6 2.5 %collective-permute-done.3.refs_1_ = bf16[272,512]{1,0:T(8,128)(2,1)S(1)} collective-permute-done((bf16[272,512]{1,0:T(8,128)(2,1)}, bf16[272,512]{1,0:T(8,128)(2,1)S(1)}, u32[]{:S(2)}, u32[]{:S(2)}) %collective-permute-start.3) | collective-permute-done | bytes 278560 | tf_op jit(solution)/shard_map/ppermute | solution.py:285
  73.1 1.0 copy-done
  74.0 12.9 %shard_map.97 = (f32[256,256]{1,0:T(8,128)S(1)}, bf16[1024,256]{1,0:T(8,128)(2,1)S(1)}, f32[1024,256]{1,0:T(8,128)S(1)}, bf16[1024,256]{1,0:T(8,128)(2,1)S(1)}) custom-call(s32[32]{0:T(128)S(1)} %convert_reduce_fusion.1.rank_q, s32[32]{0:T(128)S(1)} %get-tuple-element.18.order_q, s32[32]{0:T(128)S(1)} %get-tuple-element.17.sorted_q, ...), custom_call_target="tpu_custom_call" | custom-call | flops 2684354560 | bytes 4194304 | tf_op jit(solution)/shard_map/pallas_call | solution.py:159
  87.0 1.9 %collective-permute-start.13 = (bf16[1024,256]{1,0:T(8,128)(2,1)S(1)}, bf16[1024,256]{1,0:T(8,128)(2,1)S(1)}, u32[]{:S(2)}, u32[]{:S(2)}) collective-permute-start(bf16[1024,256]{1,0:T(8,128)(2,1)S(1)} %get-tuple-element.12), channel_id=1, source_target_pairs={{0,1},{1,0},{2,3},{3,2},{4,5},{5,4},{6,7},{7,6},{8,9},{9,8},{10,11... | collective-permute-start | bytes 1572872 | tf_op jit(solution)/shard_map/ppermute | solution.py:297
  88.9 1.9 %collective-permute-done.13 = bf16[1024,256]{1,0:T(8,128)(2,1)S(1)} collective-permute-done((bf16[1024,256]{1,0:T(8,128)(2,1)S(1)}, bf16[1024,256]{1,0:T(8,128)(2,1)S(1)}, u32[]{:S(2)}, u32[]{:S(2)}) %collective-permute-start.13) | collective-permute-done | bytes 524320 | tf_op jit(solution)/shard_map/ppermute | solution.py:297
  90.8 1.0 add_convert_fusion
  91.8 6.3 %all-to-all-start.1 = ((bf16[16,64,256]{2,1,0:T(8,128)(2,1)}), bf16[16,64,256]{2,1,0:T(8,128)(2,1)S(1)}, u32[]{:S(2)}, u32[]{:S(2)}) async-start(bf16[16,64,256]{2,1,0:T(8,128)(2,1)} %bitcast.8), calls=%async_computation.1 | async-start | bytes 1048576 | tf_op jit(solution)/shard_map/all_to_all | solution.py:336
  98.1 2.5 %collective-permute-start.7 = (bf16[256,256]{1,0:T(8,128)(2,1)S(1)}, bf16[256,256]{1,0:T(8,128)(2,1)S(1)}, u32[]{:S(2)}, u32[]{:S(2)}) collective-permute-start(bf16[256,256]{1,0:T(8,128)(2,1)S(1)} %get-tuple-element.19), channel_id=1, source_target_pairs={{0,66},{64,0},{2,64},{66,2},{1,67},{65,1},{3,65},{67,3},{4,70},{68... | collective-permute-start | bytes 393224 | tf_op jit(solution)/shard_map/ppermute | solution.py:285
  100.6 4.6 %collective-permute-start.9 = (bf16[256,256]{1,0:T(8,128)(2,1)S(1)}, bf16[256,256]{1,0:T(8,128)(2,1)S(1)}, u32[]{:S(2)}, u32[]{:S(2)}) collective-permute-start(bf16[256,256]{1,0:T(8,128)(2,1)S(1)} %get-tuple-element.20), channel_id=1, source_target_pairs={{0,64},{64,2},{2,66},{66,0},{1,65},{65,3},{3,67},{67,1},{4,68},{68... | collective-permute-start | bytes 393224 | tf_op jit(solution)/shard_map/ppermute | solution.py:285
  105.2 2.8 %collective-permute-start.8 = (bf16[256,256]{1,0:T(8,128)(2,1)S(1)}, bf16[256,256]{1,0:T(8,128)(2,1)S(1)}, u32[]{:S(2)}, u32[]{:S(2)}) collective-permute-start(bf16[256,256]{1,0:T(8,128)(2,1)S(1)} %get-tuple-element.21), channel_id=1, source_target_pairs={{0,2},{64,66},{2,0},{66,64},{1,3},{65,67},{3,1},{67,65},{4,6},{68,... | collective-permute-start | bytes 393224 | tf_op jit(solution)/shard_map/ppermute | solution.py:285
  108.0 5.6 %collective-permute-done.8 = bf16[256,256]{1,0:T(8,128)(2,1)S(1)} collective-permute-done((bf16[256,256]{1,0:T(8,128)(2,1)S(1)}, bf16[256,256]{1,0:T(8,128)(2,1)S(1)}, u32[]{:S(2)}, u32[]{:S(2)}) %collective-permute-start.8) | collective-permute-done | bytes 131104 | tf_op jit(solution)/shard_map/ppermute | solution.py:285
  113.6 4.7 %collective-permute-start.10 = (f32[64,256]{1,0:T(8,128)S(1)}, f32[64,256]{1,0:T(8,128)S(1)}, u32[]{:S(2)}, u32[]{:S(2)}) collective-permute-start(f32[64,256]{1,0:T(8,128)S(1)} %get-tuple-element.22), channel_id=1, source_target_pairs={{0,384},{128,0},{256,128},{384,256},{1,385},{129,1},{257,129},{385... | collective-permute-start | bytes 196616 | tf_op jit(solution)/shard_map/ppermute | solution.py:285
  118.3 1.9 %collective-permute-start.12 = (f32[64,256]{1,0:T(8,128)S(1)}, f32[64,256]{1,0:T(8,128)S(1)}, u32[]{:S(2)}, u32[]{:S(2)}) collective-permute-start(f32[64,256]{1,0:T(8,128)S(1)} %get-tuple-element.23), channel_id=1, source_target_pairs={{0,128},{128,256},{256,384},{384,0},{1,129},{129,257},{257,385},{3... | collective-permute-start | bytes 196616 | tf_op jit(solution)/shard_map/ppermute | solution.py:285
  120.2 4.2 %collective-permute-start.11 = (f32[64,256]{1,0:T(8,128)S(1)}, f32[64,256]{1,0:T(8,128)S(1)}, u32[]{:S(2)}, u32[]{:S(2)}) collective-permute-start(f32[64,256]{1,0:T(8,128)S(1)} %get-tuple-element.24), channel_id=1, source_target_pairs={{0,256},{128,384},{256,0},{384,128},{1,257},{129,385},{257,1},{385... | collective-permute-start | bytes 196616 | tf_op jit(solution)/shard_map/ppermute | solution.py:285
  124.4 1.6 %collective-permute-done.12 = f32[64,256]{1,0:T(8,128)S(1)} collective-permute-done((f32[64,256]{1,0:T(8,128)S(1)}, f32[64,256]{1,0:T(8,128)S(1)}, u32[]{:S(2)}, u32[]{:S(2)}) %collective-permute-start.12) | collective-permute-done | bytes 65568 | tf_op jit(solution)/shard_map/ppermute | solution.py:285
  126.0 1.9 %collective-permute-done.11 = f32[64,256]{1,0:T(8,128)S(1)} collective-permute-done((f32[64,256]{1,0:T(8,128)S(1)}, f32[64,256]{1,0:T(8,128)S(1)}, u32[]{:S(2)}, u32[]{:S(2)}) %collective-permute-start.11) | collective-permute-done | bytes 65568 | tf_op jit(solution)/shard_map/ppermute | solution.py:285
  128.5 0.8 copy-done.1
  129.3 1.7 %shard_map.98 = (bf16[64,128]{1,0:T(8,128)(2,1)}, bf16[64,128]{1,0:T(8,128)(2,1)}) custom-call(bf16[16,64,256]{2,1,0:T(8,128)(2,1)} %copy-done.1), custom_call_target="tpu_custom_call" | custom-call | tf_op jit(solution)/shard_map/pallas_call | solution.py:279
  (51 shorter events, 4.7 us)
Async XLA Ops:
  2.2 44.3 %all-to-all-start = ((bf16[16,64,256]{2,1,0:T(8,128)(2,1)}), bf16[16,64,256]{2,1,0:T(8,128)(2,1)S(1)}, u32[]{:S(2)}, u32[]{:S(2)}) async-start(bf16[16,64,256]{2,1,0:T(8,128)(2,1)} %shard_map.96), calls=%async_computation | async-start | bytes 1048576 | tf_op jit(solution)/shard_map/all_to_all | solution.py:320
  18.9 30.3 %collective-permute-start.2 = (bf16[80,512]{1,0:T(8,128)(2,1)}, bf16[80,512]{1,0:T(8,128)(2,1)S(1)}, u32[]{:S(2)}, u32[]{:S(2)}) collective-permute-start(bf16[80,512]{1,0:T(8,128)(2,1)} %shard_map.94.refs_0_), channel_id=1, source_target_pairs={{0,384},{128,0},{256,128},{384,256},{1,385},{129,1},{257,129},{385... | collective-permute-start | bytes 245768 | tf_op jit(solution)/shard_map/ppermute | solution.py:285
  23.5 25.7 %collective-permute-start.1 = (bf16[80,512]{1,0:T(8,128)(2,1)}, bf16[80,512]{1,0:T(8,128)(2,1)S(1)}, u32[]{:S(2)}, u32[]{:S(2)}) collective-permute-start(bf16[80,512]{1,0:T(8,128)(2,1)} %shard_map.94.refs_0_), channel_id=1, source_target_pairs={{0,256},{128,384},{256,0},{384,128},{1,257},{129,385},{257,1},{385... | collective-permute-start | bytes 245768 | tf_op jit(solution)/shard_map/ppermute | solution.py:285
  26.2 23.0 %collective-permute-start = (bf16[80,512]{1,0:T(8,128)(2,1)}, bf16[80,512]{1,0:T(8,128)(2,1)S(1)}, u32[]{:S(2)}, u32[]{:S(2)}) collective-permute-start(bf16[80,512]{1,0:T(8,128)(2,1)} %shard_map.94.refs_0_), channel_id=1, source_target_pairs={{0,128},{128,256},{256,384},{384,0},{1,129},{129,257},{257,385},{3... | collective-permute-start | bytes 245768 | tf_op jit(solution)/shard_map/ppermute | solution.py:285
  29.1 0.7 copy-start.5
  46.5 26.6 %collective-permute-start.6 = (bf16[1024,256]{1,0:T(8,128)(2,1)S(1)}, bf16[1024,256]{1,0:T(8,128)(2,1)S(1)}, u32[]{:S(2)}, u32[]{:S(2)}) collective-permute-start(bf16[1024,256]{1,0:T(8,128)(2,1)S(1)} %bitcast.10), channel_id=1, source_target_pairs={{0,1},{1,0},{2,3},{3,2},{4,5},{5,4},{6,7},{7,6},{8,9},{9,8},{10,11... | collective-permute-start | bytes 1572872 | tf_op jit(solution)/shard_map/ppermute | solution.py:297
  49.2 0.6 copy-start.2
  49.2 0.7 copy-start.3
  49.9 0.6 copy-start.4
  52.2 18.3 %collective-permute-start.5 = (bf16[272,512]{1,0:T(8,128)(2,1)}, bf16[272,512]{1,0:T(8,128)(2,1)S(1)}, u32[]{:S(2)}, u32[]{:S(2)}) collective-permute-start(bf16[272,512]{1,0:T(8,128)(2,1)} %shard_map.95.refs_0_), channel_id=1, source_target_pairs={{0,66},{64,0},{2,64},{66,2},{1,67},{65,1},{3,65},{67,3},{4,70},{68... | collective-permute-start | bytes 835592 | tf_op jit(solution)/shard_map/ppermute | solution.py:285
  54.9 15.7 %collective-permute-start.4 = (bf16[272,512]{1,0:T(8,128)(2,1)}, bf16[272,512]{1,0:T(8,128)(2,1)S(1)}, u32[]{:S(2)}, u32[]{:S(2)}) collective-permute-start(bf16[272,512]{1,0:T(8,128)(2,1)} %shard_map.95.refs_0_), channel_id=1, source_target_pairs={{0,2},{64,66},{2,0},{66,64},{1,3},{65,67},{3,1},{67,65},{4,6},{68,... | collective-permute-start | bytes 835592 | tf_op jit(solution)/shard_map/ppermute | solution.py:285
  57.7 15.4 %collective-permute-start.3 = (bf16[272,512]{1,0:T(8,128)(2,1)}, bf16[272,512]{1,0:T(8,128)(2,1)S(1)}, u32[]{:S(2)}, u32[]{:S(2)}) collective-permute-start(bf16[272,512]{1,0:T(8,128)(2,1)} %shard_map.95.refs_0_), channel_id=1, source_target_pairs={{0,64},{64,2},{2,66},{66,0},{1,65},{65,3},{3,67},{67,1},{4,68},{68... | collective-permute-start | bytes 835592 | tf_op jit(solution)/shard_map/ppermute | solution.py:285
  73.1 1.0 copy-start
  87.0 3.8 %collective-permute-start.13 = (bf16[1024,256]{1,0:T(8,128)(2,1)S(1)}, bf16[1024,256]{1,0:T(8,128)(2,1)S(1)}, u32[]{:S(2)}, u32[]{:S(2)}) collective-permute-start(bf16[1024,256]{1,0:T(8,128)(2,1)S(1)} %get-tuple-element.12), channel_id=1, source_target_pairs={{0,1},{1,0},{2,3},{3,2},{4,5},{5,4},{6,7},{7,6},{8,9},{9,8},{10,11... | collective-permute-start | bytes 1572872 | tf_op jit(solution)/shard_map/ppermute | solution.py:297
  91.8 36.8 %all-to-all-start.1 = ((bf16[16,64,256]{2,1,0:T(8,128)(2,1)}), bf16[16,64,256]{2,1,0:T(8,128)(2,1)S(1)}, u32[]{:S(2)}, u32[]{:S(2)}) async-start(bf16[16,64,256]{2,1,0:T(8,128)(2,1)} %bitcast.8), calls=%async_computation.1 | async-start | bytes 1048576 | tf_op jit(solution)/shard_map/all_to_all | solution.py:336
  98.1 9.9 %collective-permute-start.7 = (bf16[256,256]{1,0:T(8,128)(2,1)S(1)}, bf16[256,256]{1,0:T(8,128)(2,1)S(1)}, u32[]{:S(2)}, u32[]{:S(2)}) collective-permute-start(bf16[256,256]{1,0:T(8,128)(2,1)S(1)} %get-tuple-element.19), channel_id=1, source_target_pairs={{0,66},{64,0},{2,64},{66,2},{1,67},{65,1},{3,65},{67,3},{4,70},{68... | collective-permute-start | bytes 393224 | tf_op jit(solution)/shard_map/ppermute | solution.py:285
  100.6 7.4 %collective-permute-start.9 = (bf16[256,256]{1,0:T(8,128)(2,1)S(1)}, bf16[256,256]{1,0:T(8,128)(2,1)S(1)}, u32[]{:S(2)}, u32[]{:S(2)}) collective-permute-start(bf16[256,256]{1,0:T(8,128)(2,1)S(1)} %get-tuple-element.20), channel_id=1, source_target_pairs={{0,64},{64,2},{2,66},{66,0},{1,65},{65,3},{3,67},{67,1},{4,68},{68... | collective-permute-start | bytes 393224 | tf_op jit(solution)/shard_map/ppermute | solution.py:285
  105.2 8.4 %collective-permute-start.8 = (bf16[256,256]{1,0:T(8,128)(2,1)S(1)}, bf16[256,256]{1,0:T(8,128)(2,1)S(1)}, u32[]{:S(2)}, u32[]{:S(2)}) collective-permute-start(bf16[256,256]{1,0:T(8,128)(2,1)S(1)} %get-tuple-element.21), channel_id=1, source_target_pairs={{0,2},{64,66},{2,0},{66,64},{1,3},{65,67},{3,1},{67,65},{4,6},{68,... | collective-permute-start | bytes 393224 | tf_op jit(solution)/shard_map/ppermute | solution.py:285
  113.6 10.8 %collective-permute-start.10 = (f32[64,256]{1,0:T(8,128)S(1)}, f32[64,256]{1,0:T(8,128)S(1)}, u32[]{:S(2)}, u32[]{:S(2)}) collective-permute-start(f32[64,256]{1,0:T(8,128)S(1)} %get-tuple-element.22), channel_id=1, source_target_pairs={{0,384},{128,0},{256,128},{384,256},{1,385},{129,1},{257,129},{385... | collective-permute-start | bytes 196616 | tf_op jit(solution)/shard_map/ppermute | solution.py:285
  118.3 7.7 %collective-permute-start.12 = (f32[64,256]{1,0:T(8,128)S(1)}, f32[64,256]{1,0:T(8,128)S(1)}, u32[]{:S(2)}, u32[]{:S(2)}) collective-permute-start(f32[64,256]{1,0:T(8,128)S(1)} %get-tuple-element.23), channel_id=1, source_target_pairs={{0,128},{128,256},{256,384},{384,0},{1,129},{129,257},{257,385},{3... | collective-permute-start | bytes 196616 | tf_op jit(solution)/shard_map/ppermute | solution.py:285
  120.2 7.7 %collective-permute-start.11 = (f32[64,256]{1,0:T(8,128)S(1)}, f32[64,256]{1,0:T(8,128)S(1)}, u32[]{:S(2)}, u32[]{:S(2)}) collective-permute-start(f32[64,256]{1,0:T(8,128)S(1)} %get-tuple-element.24), channel_id=1, source_target_pairs={{0,256},{128,384},{256,0},{384,128},{1,257},{129,385},{257,1},{385... | collective-permute-start | bytes 196616 | tf_op jit(solution)/shard_map/ppermute | solution.py:285
  128.5 0.8 copy-start.1

commit v4 on v3

--- a/solution.py
+++ b/solution.py
@@ -248,49 +248,24 @@
     )(queries, out_grad, log_sum.T, delta.T)
 
 
-def join_kernel(*refs):
-    parts, out_ref = refs[:-1], refs[-1]
+def join(parts):
     rows = parts[0].shape[0] - STATS
-    for a, part in enumerate(parts):
-        out_ref[a * rows:(a + 1) * rows, :] = part[:rows, :]
-        out_ref[len(parts) * rows:, a * 128:(a + 1) * 128] = part[rows:, :128]
-
-
-def join(parts):
-    rows, width = parts[0].shape
-    return pl.pallas_call(
-        join_kernel,
-        out_shape=jax.ShapeDtypeStruct((len(parts) * (rows - STATS) + STATS, width), parts[0].dtype),
-        in_specs=[VMEM] * len(parts),
-        out_specs=VMEM,
-    )(*parts)
-
-
-def finish_kv_kernel(in_ref, k_ref, v_ref):
-    total = in_ref[0].astype(jnp.float32)
-    for n in range(1, in_ref.shape[0]):
-        total = total + in_ref[n].astype(jnp.float32)
-    k_ref[...] = (total[:, :HD] * SCALE).astype(k_ref.dtype)
-    v_ref[...] = total[:, HD:].astype(v_ref.dtype)
-
-
-def finish_kv(x):
-    out = jax.ShapeDtypeStruct((x.shape[1], HD), jnp.bfloat16)
-    return pl.pallas_call(
-        finish_kv_kernel, out_shape=(out, out), in_specs=[VMEM], out_specs=(VMEM, VMEM)
-    )(x)
-
-
-def from_offset(x, axes, index_of, d):
-    return lax.ppermute(x, axes, [(index_of(j), index_of((j + d) % 4)) for j in range(4)])
-
-
-def along_x(j):
-    return j
-
-
-def along_y(j):
-    return (j % 2) * 2 + j // 2
+    stats = jnp.concatenate([p[rows:, :128] for p in parts], axis=1)
+    return jnp.concatenate([p[:rows] for p in parts] + [stats], axis=0)
+
+
+def from_offset(x, stage, d):
+    pairs = []
+    for ix in range(4):
+        for iy in range(4):
+            for core in range(2):
+                tx, ty = ((ix + d) % 4, iy) if core == stage else (ix, (iy + d) % 4)
+                pairs.append((place(ix, iy, core), place(tx, ty, core)))
+    return lax.ppermute(x, ("x", "yl", "yh", "core"), pairs)
+
+
+def place(ix, iy, core):
+    return ((ix * 2 + iy % 2) * 2 + iy // 2) * 2 + core
 
 
 def other_core(x):
@@ -315,18 +290,19 @@
     nx, nyl, nz, nyh, nc = (lax.axis_size(a) for a in ("x", "yl", "z", "yh", "core"))
     ix, iyl, iz, iyh, ic = (lax.axis_index(a) for a in ("x", "yl", "z", "yh", "core"))
     iy = iyh * nyl + iyl
-    y = ("yl", "yh")
 
     kv_own = lax.all_to_all(pack_kv(keys, values, nz), "z", split_axis=0, concat_axis=0, tiled=True)
     kv_own = kv_own.reshape(nz * rows, 2 * HD)
+    packed = pack_q(queries, out_grad, log_sum, delta)
+    line = join([packed] + [from_offset(packed, 0, d) for d in (1, 2, 3)])
+    q_parts = [line] + [from_offset(line, 1, d) for d in (1, 2, 3)]
+    kv_own, q_parts = lax.optimization_barrier((kv_own, q_parts))
     kv_sib = other_core(kv_own)
-    packed = pack_q(queries, out_grad, log_sum, delta)
-    row = join([packed] + [from_offset(packed, "x", along_x, d) for d in (1, 2, 3)])
-    q_parts = [row] + [from_offset(row, y, along_y, d) for d in (1, 2, 3)]
 
     table_q = pick(block_table.reshape(nx, nyl, nz, nyh, nc, 2), (2, iz), (3, ic))
-    table_q = table_q.transpose(2, 1, 0, 3).reshape(nyh * nyl, nx, 2)
-    table_q = back_from(back_from(table_q, iy, 0), ix, 1).reshape(-1)
+    table_q = table_q.transpose(0, 2, 1, 3).reshape(nx, nyh * nyl, 2)
+    table_q = back_from(back_from(table_q, ix, 0), iy, 1)
+    table_q = jnp.where(ic == 0, table_q.transpose(1, 0, 2), table_q).reshape(-1)
     table_k = pick(block_table.reshape(nz, nyh, nc, nx, nyl, 2), (1, iyh), (2, ix), (2, iyl))
     table_k = jnp.concatenate([pick(table_k, (1, c)).reshape(-1) for c in (ic, nc - 1 - ic)])
 
@@ -334,15 +310,17 @@
 
     dkv = (dkv_own + other_core(dkv_sib).astype(jnp.float32)).astype(jnp.bfloat16)
     dkv = lax.all_to_all(dkv.reshape(nz, rows, 2 * HD), "z", split_axis=0, concat_axis=0, tiled=True)
-    far = far.reshape(nyl * nyh, nx * rows, width)
+    far = far.reshape(4, 4 * rows, width)
     for d in (1, 2, 3):
-        near = near + from_offset(far[d], y, along_y, 4 - d).astype(jnp.float32)
-    near = near.reshape(nx, rows, width)
+        near = near + from_offset(far[d], 1, 4 - d).astype(jnp.float32)
+    near = near.reshape(4, rows, width)
     total = near[0]
     for d in (1, 2, 3):
-        total = total + from_offset(near[d], "x", along_x, 4 - d)
+        total = total + from_offset(near[d], 0, 4 - d)
     q_grad = (total * SCALE).astype(jnp.bfloat16)
-    k_grad, v_grad = finish_kv(dkv)
+    dkv = jnp.sum(dkv.astype(jnp.float32), axis=0)
+    k_grad = (dkv[:, :HD] * SCALE).astype(jnp.bfloat16)
+    v_grad = dkv[:, HD:].astype(jnp.bfloat16)
     return (q_grad, k_grad, v_grad)
 
 

time: 134 us -> 118 us (0.88)
  waiting for transfers between devices: 36.9 us -> 25 us
  Pallas kernels: 19.4 us -> 16 us
    all_to_all x1, waiting for transfers between devices: 15 us -> 7.39 us  [local(): lax.all_to_all(pack_kv(keys, values, nz), 'z', split_axis=0, concat_axis=...]
    ppermute x12, waiting for transfers between devices: 19.9 us -> 14.3 us  [from_offset(): return lax.ppermute(x, ('x', 'yl', 'yh', 'core'), pairs)]
    pallas_call x2 -> x0, Pallas kernels: 3.46 us -> none  [the longest x1 1.74 us: join(): pl.pallas_call(join_kernel, out_shape=jax.ShapeDtypeStruct((len(parts) *...]
    unnamed x12 -> x10, local copies, waits for them, and re-layouts: 3.7 us -> 0.94 us
    ppermute x2, waiting for transfers between devices: 1.88 us -> 3.3 us  [other_core(): return lax.ppermute(x, 'core', [(0, 1), (1, 0)])]
  transfers between devices with their start and end apart: 16 -> 16, of which waited for: 7 -> 8; matrix products, arithmetic and copies ran while one was open for 3% -> 3% of each run, Pallas kernels for 2% -> 1%
where the time goes in v4:
time: 118 us; the launch traced here: 116 us
  starting transfers between devices  66.7 us (57%)
  waiting for transfers between devices  25 us (21%)
  Pallas kernels  16 us (14%)
  local copies, waits for them, and re-layouts  4.35 us (4%)
  other arithmetic  3.13 us (3%)
    ppermute x12, starting transfers between devices, from_offset(): return lax.ppermute(x, ('x', 'yl', 'yh', 'core'), pairs)  40.6 us
    all_to_all x1, starting transfers between devices, local(): lax.all_to_all(pack_kv(keys, values, nz), 'z', split_axis=0, concat_axis=...  15.2 us
    ppermute x12, waiting for transfers between devices, from_offset(): return lax.ppermute(x, ('x', 'yl', 'yh', 'core'), pairs)  14.3 us
    pallas_call x1, Pallas kernels, tile_grads(): pl.pallas_call(tile_kernel, out_shape=(jax.ShapeDtypeStruct((part, HEADS...  12.9 us
    all_to_all x1, waiting for transfers between devices, local(): lax.all_to_all(pack_kv(keys, values, nz), 'z', split_axis=0, concat_axis=...  7.39 us
    all_to_all x1, starting transfers between devices, local(): lax.all_to_all(dkv.reshape(nz, rows, 2 * HD), 'z', split_axis=0, concat_a...  6.97 us
    ppermute x2, starting transfers between devices, other_core(): return lax.ppermute(x, 'core', [(0, 1), (1, 0)])  3.95 us
    ppermute x2, waiting for transfers between devices, other_core(): return lax.ppermute(x, 'core', [(0, 1), (1, 0)])  3.3 us
  transfers between devices with their start and end apart: 16, of which 8 were waited for; matrix products, arithmetic and copies ran while one was open for 3% of the time, Pallas kernels for 1%

profile of v4, /device:TPU:24, one launch (start us, length us, event | category | flops | bytes accessed | tf_op | source)
XLA Modules:
  0.0 116.2 jit_solution(15635338092149066799)
XLA Ops:
  0.6 1.4 %shard_map.95 = bf16[80,512]{1,0:T(8,128)(2,1)} custom-call(bf16[64,256]{1,0:T(8,128)(2,1)} %q_ref.1, bf16[64,256]{1,0:T(8,128)(2,1)} %g_ref.1, f32[2,64]{1,0:T(2,128)} %bitcast.16, f32[2,64]{1,0:T(2,128)} %bitcast.17), custom_call_target="tpu_custom_call" | custom-call | tf_op jit(solution)/shard_map/pallas_call | solution.py:242
  2.1 4.7 %collective-permute-start.2 = (bf16[80,512]{1,0:T(8,128)(2,1)}, bf16[80,512]{1,0:T(8,128)(2,1)S(1)}, u32[]{:S(2)}, u32[]{:S(2)}) collective-permute-start(bf16[80,512]{1,0:T(8,128)(2,1)} %shard_map.95), channel_id=1, source_target_pairs={{0,384},{1,67},{64,448},{65,1},{2,386},{3,65},{66,450},{67,3},{128... | collective-permute-start | bytes 245768 | tf_op jit(solution)/shard_map/ppermute | solution.py:264
  6.7 2.7 %collective-permute-start.1 = (bf16[80,512]{1,0:T(8,128)(2,1)}, bf16[80,512]{1,0:T(8,128)(2,1)S(1)}, u32[]{:S(2)}, u32[]{:S(2)}) collective-permute-start(bf16[80,512]{1,0:T(8,128)(2,1)} %shard_map.95), channel_id=1, source_target_pairs={{0,256},{1,3},{64,320},{65,67},{2,258},{3,1},{66,322},{67,65},{128... | collective-permute-start | bytes 245768 | tf_op jit(solution)/shard_map/ppermute | solution.py:264
  9.4 2.8 %collective-permute-start = (bf16[80,512]{1,0:T(8,128)(2,1)}, bf16[80,512]{1,0:T(8,128)(2,1)S(1)}, u32[]{:S(2)}, u32[]{:S(2)}) collective-permute-start(bf16[80,512]{1,0:T(8,128)(2,1)} %shard_map.95), channel_id=1, source_target_pairs={{0,128},{1,65},{64,192},{65,3},{2,130},{3,67},{66,194},{67,1},{128... | collective-permute-start | bytes 245768 | tf_op jit(solution)/shard_map/ppermute | solution.py:264
  12.2 1.6 %shard_map.94 = bf16[16,64,256]{2,1,0:T(8,128)(2,1)} custom-call(bf16[64,128]{1,0:T(8,128)(2,1)} %k_ref.1, bf16[64,128]{1,0:T(8,128)(2,1)} %v_ref.1), custom_call_target="tpu_custom_call" | custom-call | tf_op jit(solution)/shard_map/pallas_call | solution.py:211
  13.9 15.2 %all-to-all-start = ((bf16[16,64,256]{2,1,0:T(8,128)(2,1)}), bf16[16,64,256]{2,1,0:T(8,128)(2,1)S(1)}, u32[]{:S(2)}, u32[]{:S(2)}) async-start(bf16[16,64,256]{2,1,0:T(8,128)(2,1)} %shard_map.94), calls=%async_computation | async-start | bytes 1048576 | tf_op jit(solution)/shard_map/all_to_all | solution.py:294
  29.1 0.7 copy-done.1
  33.3 2.7 %collective-permute-start.5 = (bf16[272,512]{1,0:T(8,128)(2,1)S(1)}, bf16[272,512]{1,0:T(8,128)(2,1)S(1)}, u32[]{:S(2)}, u32[]{:S(2)}) collective-permute-start(bf16[272,512]{1,0:T(8,128)(2,1)S(1)} %maximum_dynamic-update-slice_fusion.refs_0_), channel_id=1, source_target_pairs={{0,66},{1,385},{64,0},{65,449},{2,64},{3,387},{66,2},{67,451},{128... | collective-permute-start | bytes 835592 | tf_op jit(solution)/shard_map/ppermute | solution.py:264
  35.9 2.8 %collective-permute-start.4 = (bf16[272,512]{1,0:T(8,128)(2,1)S(1)}, bf16[272,512]{1,0:T(8,128)(2,1)S(1)}, u32[]{:S(2)}, u32[]{:S(2)}) collective-permute-start(bf16[272,512]{1,0:T(8,128)(2,1)S(1)} %maximum_dynamic-update-slice_fusion.refs_0_), channel_id=1, source_target_pairs={{0,2},{1,257},{64,66},{65,321},{2,0},{3,259},{66,64},{67,323},{128... | collective-permute-start | bytes 835592 | tf_op jit(solution)/shard_map/ppermute | solution.py:264
  38.8 4.1 %collective-permute-start.3 = (bf16[272,512]{1,0:T(8,128)(2,1)S(1)}, bf16[272,512]{1,0:T(8,128)(2,1)S(1)}, u32[]{:S(2)}, u32[]{:S(2)}) collective-permute-start(bf16[272,512]{1,0:T(8,128)(2,1)S(1)} %maximum_dynamic-update-slice_fusion.refs_0_), channel_id=1, source_target_pairs={{0,64},{1,129},{64,2},{65,193},{2,66},{3,131},{66,0},{67,195},{128... | collective-permute-start | bytes 835592 | tf_op jit(solution)/shard_map/ppermute | solution.py:264
  43.2 2.7 %collective-permute-done.4.refs_2_ = bf16[272,512]{1,0:T(8,128)(2,1)S(1)} collective-permute-done((bf16[272,512]{1,0:T(8,128)(2,1)S(1)}, bf16[272,512]{1,0:T(8,128)(2,1)S(1)}, u32[]{:S(2)}, u32[]{:S(2)}) %collective-permute-start.4) | collective-permute-done | bytes 278560 | tf_op jit(solution)/shard_map/ppermute | solution.py:264
  45.9 2.8 %collective-permute-done.3.refs_1_ = bf16[272,512]{1,0:T(8,128)(2,1)S(1)} collective-permute-done((bf16[272,512]{1,0:T(8,128)(2,1)S(1)}, bf16[272,512]{1,0:T(8,128)(2,1)S(1)}, u32[]{:S(2)}, u32[]{:S(2)}) %collective-permute-start.3) | collective-permute-done | bytes 278560 | tf_op jit(solution)/shard_map/ppermute | solution.py:264
  48.7 7.4 %all-to-all-done = bf16[16,64,256]{2,1,0:T(8,128)(2,1)S(1)} async-done(((bf16[16,64,256]{2,1,0:T(8,128)(2,1)}), bf16[16,64,256]{2,1,0:T(8,128)(2,1)S(1)}, u32[]{:S(2)}, u32[]{:S(2)}) %all-to-all-start) | async-done | bytes 524320 | tf_op jit(solution)/shard_map/all_to_all | solution.py:294
  56.1 1.9 %collective-permute-start.6 = (bf16[1024,256]{1,0:T(8,128)(2,1)S(1)}, bf16[1024,256]{1,0:T(8,128)(2,1)S(1)}, u32[]{:S(2)}, u32[]{:S(2)}) collective-permute-start(bf16[1024,256]{1,0:T(8,128)(2,1)S(1)} %bitcast.11), channel_id=1, source_target_pairs={{0,1},{1,0},{2,3},{3,2},{4,5},{5,4},{6,7},{7,6},{8,9},{9,8},{10,11... | collective-permute-start | bytes 1572872 | tf_op jit(solution)/shard_map/ppermute | solution.py:272
  58.3 1.6 %collective-permute-done.6.refs_5_ = bf16[1024,256]{1,0:T(8,128)(2,1)S(1)} collective-permute-done((bf16[1024,256]{1,0:T(8,128)(2,1)S(1)}, bf16[1024,256]{1,0:T(8,128)(2,1)S(1)}, u32[]{:S(2)}, u32[]{:S(2)}) %collective-permute-start.6) | collective-permute-done | bytes 524320 | tf_op jit(solution)/shard_map/ppermute | solution.py:272
  59.8 12.9 %shard_map.96 = (f32[256,256]{1,0:T(8,128)S(1)}, bf16[1024,256]{1,0:T(8,128)(2,1)S(1)}, f32[1024,256]{1,0:T(8,128)S(1)}, bf16[1024,256]{1,0:T(8,128)(2,1)S(1)}) custom-call(s32[32]{0:T(128)S(1)} %convert_reduce_fusion.2.rank_q, s32[32]{0:T(128)S(1)} %get-tuple-element.24.order_q, s32[32]{0:T(128)S(1)} %get-tuple-element.23.sorted_q, ...), custom_call_target="tpu_custom_call" | custom-call | flops 2684354560 | bytes 4194304 | tf_op jit(solution)/shard_map/pallas_call | solution.py:159
  72.8 2.0 %collective-permute-start.13 = (bf16[1024,256]{1,0:T(8,128)(2,1)S(1)}, bf16[1024,256]{1,0:T(8,128)(2,1)S(1)}, u32[]{:S(2)}, u32[]{:S(2)}) collective-permute-start(bf16[1024,256]{1,0:T(8,128)(2,1)S(1)} %get-tuple-element.20), channel_id=1, source_target_pairs={{0,1},{1,0},{2,3},{3,2},{4,5},{5,4},{6,7},{7,6},{8,9},{9,8},{10,11... | collective-permute-start | bytes 1572872 | tf_op jit(solution)/shard_map/ppermute | solution.py:272
  74.8 1.8 %collective-permute-done.13 = bf16[1024,256]{1,0:T(8,128)(2,1)S(1)} collective-permute-done((bf16[1024,256]{1,0:T(8,128)(2,1)S(1)}, bf16[1024,256]{1,0:T(8,128)(2,1)S(1)}, u32[]{:S(2)}, u32[]{:S(2)}) %collective-permute-start.13) | collective-permute-done | bytes 524320 | tf_op jit(solution)/shard_map/ppermute | solution.py:272
  76.6 0.9 add_convert_fusion
  77.5 7.0 %all-to-all-start.1 = ((bf16[16,64,256]{2,1,0:T(8,128)(2,1)}), bf16[16,64,256]{2,1,0:T(8,128)(2,1)S(1)}, u32[]{:S(2)}, u32[]{:S(2)}) async-start(bf16[16,64,256]{2,1,0:T(8,128)(2,1)} %bitcast.8), calls=%async_computation.1 | async-start | bytes 1048576 | tf_op jit(solution)/shard_map/all_to_all | solution.py:312
  84.5 2.4 %collective-permute-start.7 = (bf16[256,256]{1,0:T(8,128)(2,1)S(1)}, bf16[256,256]{1,0:T(8,128)(2,1)S(1)}, u32[]{:S(2)}, u32[]{:S(2)}) collective-permute-start(bf16[256,256]{1,0:T(8,128)(2,1)S(1)} %get-tuple-element.25), channel_id=1, source_target_pairs={{0,66},{1,385},{64,0},{65,449},{2,64},{3,387},{66,2},{67,451},{128... | collective-permute-start | bytes 393224 | tf_op jit(solution)/shard_map/ppermute | solution.py:264
  86.9 4.6 %collective-permute-start.9 = (bf16[256,256]{1,0:T(8,128)(2,1)S(1)}, bf16[256,256]{1,0:T(8,128)(2,1)S(1)}, u32[]{:S(2)}, u32[]{:S(2)}) collective-permute-start(bf16[256,256]{1,0:T(8,128)(2,1)S(1)} %get-tuple-element.26), channel_id=1, source_target_pairs={{0,64},{1,129},{64,2},{65,193},{2,66},{3,131},{66,0},{67,195},{128... | collective-permute-start | bytes 393224 | tf_op jit(solution)/shard_map/ppermute | solution.py:264
  91.6 3.0 %collective-permute-start.8 = (bf16[256,256]{1,0:T(8,128)(2,1)S(1)}, bf16[256,256]{1,0:T(8,128)(2,1)S(1)}, u32[]{:S(2)}, u32[]{:S(2)}) collective-permute-start(bf16[256,256]{1,0:T(8,128)(2,1)S(1)} %get-tuple-element.27), channel_id=1, source_target_pairs={{0,2},{1,257},{64,66},{65,321},{2,0},{3,259},{66,64},{67,323},{128... | collective-permute-start | bytes 393224 | tf_op jit(solution)/shard_map/ppermute | solution.py:264
  94.6 5.3 %collective-permute-done.8 = bf16[256,256]{1,0:T(8,128)(2,1)S(1)} collective-permute-done((bf16[256,256]{1,0:T(8,128)(2,1)S(1)}, bf16[256,256]{1,0:T(8,128)(2,1)S(1)}, u32[]{:S(2)}, u32[]{:S(2)}) %collective-permute-start.8) | collective-permute-done | bytes 131104 | tf_op jit(solution)/shard_map/ppermute | solution.py:264
  100.0 4.7 %collective-permute-start.10 = (f32[64,256]{1,0:T(8,128)S(1)}, f32[64,256]{1,0:T(8,128)S(1)}, u32[]{:S(2)}, u32[]{:S(2)}) collective-permute-start(f32[64,256]{1,0:T(8,128)S(1)} %get-tuple-element.28), channel_id=1, source_target_pairs={{0,384},{1,67},{64,448},{65,1},{2,386},{3,65},{66,450},{67,3},{128... | collective-permute-start | bytes 196616 | tf_op jit(solution)/shard_map/ppermute | solution.py:264
  104.7 1.9 %collective-permute-start.12 = (f32[64,256]{1,0:T(8,128)S(1)}, f32[64,256]{1,0:T(8,128)S(1)}, u32[]{:S(2)}, u32[]{:S(2)}) collective-permute-start(f32[64,256]{1,0:T(8,128)S(1)} %get-tuple-element.29), channel_id=1, source_target_pairs={{0,128},{1,65},{64,192},{65,3},{2,130},{3,67},{66,194},{67,1},{128... | collective-permute-start | bytes 196616 | tf_op jit(solution)/shard_map/ppermute | solution.py:264
  106.6 4.2 %collective-permute-start.11 = (f32[64,256]{1,0:T(8,128)S(1)}, f32[64,256]{1,0:T(8,128)S(1)}, u32[]{:S(2)}, u32[]{:S(2)}) collective-permute-start(f32[64,256]{1,0:T(8,128)S(1)} %get-tuple-element.30), channel_id=1, source_target_pairs={{0,256},{1,3},{64,320},{65,67},{2,258},{3,1},{66,322},{67,65},{128... | collective-permute-start | bytes 196616 | tf_op jit(solution)/shard_map/ppermute | solution.py:264
  110.9 1.2 %collective-permute-done.12 = f32[64,256]{1,0:T(8,128)S(1)} collective-permute-done((f32[64,256]{1,0:T(8,128)S(1)}, f32[64,256]{1,0:T(8,128)S(1)}, u32[]{:S(2)}, u32[]{:S(2)}) %collective-permute-start.12) | collective-permute-done | bytes 65568 | tf_op jit(solution)/shard_map/ppermute | solution.py:264
  112.1 2.2 %collective-permute-done.11 = f32[64,256]{1,0:T(8,128)S(1)} collective-permute-done((f32[64,256]{1,0:T(8,128)S(1)}, f32[64,256]{1,0:T(8,128)S(1)}, u32[]{:S(2)}, u32[]{:S(2)}) %collective-permute-start.11) | collective-permute-done | bytes 65568 | tf_op jit(solution)/shard_map/ppermute | solution.py:264
  114.3 0.6 fusion.3
  115.0 0.6 slice.135
  115.6 0.6 fusion.4
  (61 shorter events, 4.1 us)
Async XLA Ops:
  2.1 31.1 %collective-permute-start.2 = (bf16[80,512]{1,0:T(8,128)(2,1)}, bf16[80,512]{1,0:T(8,128)(2,1)S(1)}, u32[]{:S(2)}, u32[]{:S(2)}) collective-permute-start(bf16[80,512]{1,0:T(8,128)(2,1)} %shard_map.95), channel_id=1, source_target_pairs={{0,384},{1,67},{64,448},{65,1},{2,386},{3,65},{66,450},{67,3},{128... | collective-permute-start | bytes 245768 | tf_op jit(solution)/shard_map/ppermute | solution.py:264
  6.7 26.4 %collective-permute-start.1 = (bf16[80,512]{1,0:T(8,128)(2,1)}, bf16[80,512]{1,0:T(8,128)(2,1)S(1)}, u32[]{:S(2)}, u32[]{:S(2)}) collective-permute-start(bf16[80,512]{1,0:T(8,128)(2,1)} %shard_map.95), channel_id=1, source_target_pairs={{0,256},{1,3},{64,320},{65,67},{2,258},{3,1},{66,322},{67,65},{128... | collective-permute-start | bytes 245768 | tf_op jit(solution)/shard_map/ppermute | solution.py:264
  9.4 23.7 %collective-permute-start = (bf16[80,512]{1,0:T(8,128)(2,1)}, bf16[80,512]{1,0:T(8,128)(2,1)S(1)}, u32[]{:S(2)}, u32[]{:S(2)}) collective-permute-start(bf16[80,512]{1,0:T(8,128)(2,1)} %shard_map.95), channel_id=1, source_target_pairs={{0,128},{1,65},{64,192},{65,3},{2,130},{3,67},{66,194},{67,1},{128... | collective-permute-start | bytes 245768 | tf_op jit(solution)/shard_map/ppermute | solution.py:264
  13.9 42.2 %all-to-all-start = ((bf16[16,64,256]{2,1,0:T(8,128)(2,1)}), bf16[16,64,256]{2,1,0:T(8,128)(2,1)S(1)}, u32[]{:S(2)}, u32[]{:S(2)}) async-start(bf16[16,64,256]{2,1,0:T(8,128)(2,1)} %shard_map.94), calls=%async_computation | async-start | bytes 1048576 | tf_op jit(solution)/shard_map/all_to_all | solution.py:294
  29.1 0.7 copy-start.1
  30.2 0.9 copy-start
  30.8 0.7 copy-start.2
  31.8 0.7 slice-start
  33.3 9.9 %collective-permute-start.5 = (bf16[272,512]{1,0:T(8,128)(2,1)S(1)}, bf16[272,512]{1,0:T(8,128)(2,1)S(1)}, u32[]{:S(2)}, u32[]{:S(2)}) collective-permute-start(bf16[272,512]{1,0:T(8,128)(2,1)S(1)} %maximum_dynamic-update-slice_fusion.refs_0_), channel_id=1, source_target_pairs={{0,66},{1,385},{64,0},{65,449},{2,64},{3,387},{66,2},{67,451},{128... | collective-permute-start | bytes 835592 | tf_op jit(solution)/shard_map/ppermute | solution.py:264
  35.9 10.0 %collective-permute-start.4 = (bf16[272,512]{1,0:T(8,128)(2,1)S(1)}, bf16[272,512]{1,0:T(8,128)(2,1)S(1)}, u32[]{:S(2)}, u32[]{:S(2)}) collective-permute-start(bf16[272,512]{1,0:T(8,128)(2,1)S(1)} %maximum_dynamic-update-slice_fusion.refs_0_), channel_id=1, source_target_pairs={{0,2},{1,257},{64,66},{65,321},{2,0},{3,259},{66,64},{67,323},{128... | collective-permute-start | bytes 835592 | tf_op jit(solution)/shard_map/ppermute | solution.py:264
  38.8 9.9 %collective-permute-start.3 = (bf16[272,512]{1,0:T(8,128)(2,1)S(1)}, bf16[272,512]{1,0:T(8,128)(2,1)S(1)}, u32[]{:S(2)}, u32[]{:S(2)}) collective-permute-start(bf16[272,512]{1,0:T(8,128)(2,1)S(1)} %maximum_dynamic-update-slice_fusion.refs_0_), channel_id=1, source_target_pairs={{0,64},{1,129},{64,2},{65,193},{2,66},{3,131},{66,0},{67,195},{128... | collective-permute-start | bytes 835592 | tf_op jit(solution)/shard_map/ppermute | solution.py:264
  56.1 3.8 %collective-permute-start.6 = (bf16[1024,256]{1,0:T(8,128)(2,1)S(1)}, bf16[1024,256]{1,0:T(8,128)(2,1)S(1)}, u32[]{:S(2)}, u32[]{:S(2)}) collective-permute-start(bf16[1024,256]{1,0:T(8,128)(2,1)S(1)} %bitcast.11), channel_id=1, source_target_pairs={{0,1},{1,0},{2,3},{3,2},{4,5},{5,4},{6,7},{7,6},{8,9},{9,8},{10,11... | collective-permute-start | bytes 1572872 | tf_op jit(solution)/shard_map/ppermute | solution.py:272
  72.8 3.8 %collective-permute-start.13 = (bf16[1024,256]{1,0:T(8,128)(2,1)S(1)}, bf16[1024,256]{1,0:T(8,128)(2,1)S(1)}, u32[]{:S(2)}, u32[]{:S(2)}) collective-permute-start(bf16[1024,256]{1,0:T(8,128)(2,1)S(1)} %get-tuple-element.20), channel_id=1, source_target_pairs={{0,1},{1,0},{2,3},{3,2},{4,5},{5,4},{6,7},{7,6},{8,9},{9,8},{10,11... | collective-permute-start | bytes 1572872 | tf_op jit(solution)/shard_map/ppermute | solution.py:272
  77.5 37.5 %all-to-all-start.1 = ((bf16[16,64,256]{2,1,0:T(8,128)(2,1)}), bf16[16,64,256]{2,1,0:T(8,128)(2,1)S(1)}, u32[]{:S(2)}, u32[]{:S(2)}) async-start(bf16[16,64,256]{2,1,0:T(8,128)(2,1)} %bitcast.8), calls=%async_computation.1 | async-start | bytes 1048576 | tf_op jit(solution)/shard_map/all_to_all | solution.py:312
  84.5 10.1 %collective-permute-start.7 = (bf16[256,256]{1,0:T(8,128)(2,1)S(1)}, bf16[256,256]{1,0:T(8,128)(2,1)S(1)}, u32[]{:S(2)}, u32[]{:S(2)}) collective-permute-start(bf16[256,256]{1,0:T(8,128)(2,1)S(1)} %get-tuple-element.25), channel_id=1, source_target_pairs={{0,66},{1,385},{64,0},{65,449},{2,64},{3,387},{66,2},{67,451},{128... | collective-permute-start | bytes 393224 | tf_op jit(solution)/shard_map/ppermute | solution.py:264
  86.9 7.6 %collective-permute-start.9 = (bf16[256,256]{1,0:T(8,128)(2,1)S(1)}, bf16[256,256]{1,0:T(8,128)(2,1)S(1)}, u32[]{:S(2)}, u32[]{:S(2)}) collective-permute-start(bf16[256,256]{1,0:T(8,128)(2,1)S(1)} %get-tuple-element.26), channel_id=1, source_target_pairs={{0,64},{1,129},{64,2},{65,193},{2,66},{3,131},{66,0},{67,195},{128... | collective-permute-start | bytes 393224 | tf_op jit(solution)/shard_map/ppermute | solution.py:264
  91.6 8.4 %collective-permute-start.8 = (bf16[256,256]{1,0:T(8,128)(2,1)S(1)}, bf16[256,256]{1,0:T(8,128)(2,1)S(1)}, u32[]{:S(2)}, u32[]{:S(2)}) collective-permute-start(bf16[256,256]{1,0:T(8,128)(2,1)S(1)} %get-tuple-element.27), channel_id=1, source_target_pairs={{0,2},{1,257},{64,66},{65,321},{2,0},{3,259},{66,64},{67,323},{128... | collective-permute-start | bytes 393224 | tf_op jit(solution)/shard_map/ppermute | solution.py:264
  100.0 10.8 %collective-permute-start.10 = (f32[64,256]{1,0:T(8,128)S(1)}, f32[64,256]{1,0:T(8,128)S(1)}, u32[]{:S(2)}, u32[]{:S(2)}) collective-permute-start(f32[64,256]{1,0:T(8,128)S(1)} %get-tuple-element.28), channel_id=1, source_target_pairs={{0,384},{1,67},{64,448},{65,1},{2,386},{3,65},{66,450},{67,3},{128... | collective-permute-start | bytes 196616 | tf_op jit(solution)/shard_map/ppermute | solution.py:264
  104.7 7.4 %collective-permute-start.12 = (f32[64,256]{1,0:T(8,128)S(1)}, f32[64,256]{1,0:T(8,128)S(1)}, u32[]{:S(2)}, u32[]{:S(2)}) collective-permute-start(f32[64,256]{1,0:T(8,128)S(1)} %get-tuple-element.29), channel_id=1, source_target_pairs={{0,128},{1,65},{64,192},{65,3},{2,130},{3,67},{66,194},{67,1},{128... | collective-permute-start | bytes 196616 | tf_op jit(solution)/shard_map/ppermute | solution.py:264
  106.6 7.7 %collective-permute-start.11 = (f32[64,256]{1,0:T(8,128)S(1)}, f32[64,256]{1,0:T(8,128)S(1)}, u32[]{:S(2)}, u32[]{:S(2)}) collective-permute-start(f32[64,256]{1,0:T(8,128)S(1)} %get-tuple-element.30), channel_id=1, source_target_pairs={{0,256},{1,3},{64,320},{65,67},{2,258},{3,1},{66,322},{67,65},{128... | collective-permute-start | bytes 196616 | tf_op jit(solution)/shard_map/ppermute | solution.py:264

commit v5 on v4

v5 whole, which is shorter than its diff:
```python
import jax
import jax.numpy as jnp
from jax import lax
from jax.experimental import pallas as pl
from jax.experimental.pallas import tpu as pltpu
from jax.sharding import Mesh, PartitionSpec as P

HEADS = 2
HD = 128
HALF = 32
SCALE = HD ** (-0.5)
LOG2E = 1.4426950408889634
PIECES = 3
STATS = 16
QT = 256
KT = 256
TOGETHER = 2
VMEM = pl.BlockSpec(memory_space=pltpu.VMEM)
SMEM = pl.BlockSpec(memory_space=pltpu.SMEM)


def dot(a, b):
    return jnp.dot(a, b, preferred_element_type=jnp.float32)


def dot_nt(a, b):
    return lax.dot_general(a, b, (((1,), (1,)), ((), ())), preferred_element_type=jnp.float32)


def tile_kernel(core, rank_q, order_q, sorted_q, rank_k, sorted_k, *refs):
    q_refs = refs[:2]
    kv_refs = refs[2:6]
    posq_ref, dq_ref, near_ref, far_ref = refs[6:10]
    qs, gs, stats, rows, ks, vs, kt, dqt, dk, dv, todo = refs[10:]
    n_q = qs.shape[0]
    n_k = ks.shape[0]
    per_q = QT // HALF
    per_k = KT // HALF
    devs = q_refs[0].shape[0]
    part_q = (q_refs[0].shape[1] - STATS) // HALF
    part_k = kv_refs[0].shape[0] // HALF

    for a in range(2):
        for n in range(devs):
            for b in range(part_q):
                place = rank_q[(a * devs + n) * part_q + b]
                j = place // per_q
                r = pl.multiple_of(place % per_q * HALF, HALF)
                cut = slice(b * HALF, (b + 1) * HALF)
                for h in range(HEADS):
                    qs[j, pl.ds(h * QT + r, HALF), :] = q_refs[a][n, cut, h * HD:(h + 1) * HD]
                    gs[j, pl.ds(h * QT + r, HALF), :] = q_refs[a][n, cut, (HEADS + h) * HD:(HEADS + h + 1) * HD]
            stats[a * devs + n] = q_refs[a][n, part_q * HALF:, :128].astype(jnp.float32)
    for a in range(4):
        for b in range(part_k):
            place = rank_k[a * part_k + b]
            i = place // per_k
            r = pl.multiple_of(place % per_k * HALF, HALF)
            cut = slice(b * HALF, (b + 1) * HALF)
            ks[i, pl.ds(r, HALF), :] = kv_refs[a][cut, :HD]
            vs[i, pl.ds(r, HALF), :] = kv_refs[a][cut, HD:]

    quarter = lax.broadcasted_iota(jnp.int32, (STATS, 128), 1) // HALF
    for t in range(n_q * QT // 128):
        line = jnp.zeros((STATS, 128), jnp.float32)
        for u in range(4):
            b = order_q[t * 4 + u]
            piece = pltpu.roll(stats[b // part_q], (u - b % part_q + 4) % 4 * HALF, 1)
            line = jnp.where(quarter == u, piece, line)
        j, c = t // (QT // 128), t % (QT // 128)
        n = 2 * HEADS
        stat = line[:n] + line[n:2 * n] + line[2 * n:3 * n]
        for h in range(HEADS):
            cut = slice(h * QT + c * 128, h * QT + (c + 1) * 128)
            rows[j, 0:1, cut] = stat[h:h + 1] * LOG2E
            rows[j, 1:2, cut] = stat[HEADS + h:HEADS + h + 1]

    for i in range(n_k):
        kt[i] = ks[i].astype(jnp.float32).T.astype(jnp.bfloat16)

    dk[...] = jnp.zeros_like(dk)
    dv[...] = jnp.zeros_like(dv)
    dqt[...] = jnp.zeros_like(dqt)

    count = jnp.int32(0)
    dead = jnp.int32(0)
    for j in range(n_q):
        top = sorted_q[j * per_q + per_q - 1]
        for i in range(n_k):
            live = sorted_k[i * per_k] <= top
            todo[count] = jnp.int32(j * n_k + i)
            count = count + live.astype(jnp.int32)
            dead = jnp.where(live, dead, j * n_k + i)
    for u in range(TOGETHER - 1):
        todo[count + u] = dead

    within = lax.broadcasted_iota(jnp.int32, (HALF, 128), 0)

    def one(t):
        j = todo[t] // n_k
        i = todo[t] % n_k
        q, g, k, v = qs[j], gs[j], ks[i], vs[i]
        posk = jnp.concatenate([within + sorted_k[i * per_k + b] * HALF for b in range(per_k)], axis=0)
        posk = jnp.concatenate([posk] * (HEADS * QT // 128), axis=1)
        s = dot_nt(k, q)
        p = jnp.where(posk <= posq_ref[j], jnp.exp2(s * (SCALE * LOG2E) - rows[j, 0:1, :]), 0.0)
        dp = dot_nt(v, g)
        ds = (p * (dp - rows[j, 1:2, :])).astype(jnp.bfloat16)
        dv[i] += dot(p.astype(jnp.bfloat16), g)
        dk[i] += dot(ds, q)
        dqt[j] += dot(kt[i], ds)

    def some(t, c):
        for u in range(TOGETHER):
            one(t * TOGETHER + u)
        return c

    lax.fori_loop(0, (count + TOGETHER - 1) // TOGETHER, some, 0)

    half_q = devs * part_q
    for j in range(n_q):
        for h in range(HEADS):
            back = dqt[j, :, h * QT:(h + 1) * QT].T.astype(jnp.bfloat16)
            for b in range(per_q):
                to = order_q[j * per_q + b]
                owner = jnp.where(to < half_q, core[0], 1 - core[0])
                dst = pl.multiple_of((owner * half_q + to % half_q) * HALF, HALF)
                dq_ref[pl.ds(dst, HALF), h * HD:(h + 1) * HD] = back[b * HALF:(b + 1) * HALF]
    for a in range(4):
        for b in range(part_k):
            place = rank_k[a * part_k + b]
            i = place // per_k
            r = pl.multiple_of(place % per_k * HALF, HALF)
            out = near_ref if a == 0 else far_ref
            cut = slice((b if a == 0 else (a - 1) * part_k + b) * HALF, (b + 1 if a == 0 else (a - 1) * part_k + b + 1) * HALF)
            out[cut, :HD] = dk[i, pl.ds(r, HALF), :].astype(out.dtype)
            out[cut, HD:] = dv[i, pl.ds(r, HALF), :].astype(out.dtype)


def tile_grads(core, q_parts, kv_parts, table_q, table_k):
    devs, part = q_parts[0].shape[:2]
    rows_q = 2 * devs * (part - STATS)
    part_k = kv_parts[0].shape[0]
    rows_k = 4 * part_k
    n_q, n_k = rows_q // QT, rows_k // KT
    rank_q, order_q, sorted_q = in_order(table_q)
    rank_k, _, sorted_k = in_order(table_k)
    posq = positions(sorted_q).reshape(n_q, 1, QT)
    posq = jnp.concatenate([posq] * HEADS, axis=2)
    bf, f32 = jnp.bfloat16, jnp.float32
    return pl.pallas_call(
        tile_kernel,
        out_shape=(
            jax.ShapeDtypeStruct((rows_q, HEADS * HD), bf),
            jax.ShapeDtypeStruct((part_k, 2 * HD), f32),
            jax.ShapeDtypeStruct((3 * part_k, 2 * HD), bf),
        ),
        in_specs=[SMEM] * 6 + [VMEM] * 7,
        out_specs=(VMEM,) * 3,
        scratch_shapes=[
            pltpu.VMEM((n_q, HEADS * QT, HD), bf),
            pltpu.VMEM((n_q, HEADS * QT, HD), bf),
            pltpu.VMEM((2 * devs, STATS, 128), f32),
            pltpu.VMEM((n_q, 8, HEADS * QT), f32),
            pltpu.VMEM((n_k, KT, HD), bf),
            pltpu.VMEM((n_k, KT, HD), bf),
            pltpu.VMEM((n_k, HD, KT), bf),
            pltpu.VMEM((n_q, HD, HEADS * QT), f32),
            pltpu.VMEM((n_k, KT, HD), f32),
            pltpu.VMEM((n_k, KT, HD), f32),
            pltpu.SMEM((n_q * n_k + TOGETHER,), jnp.int32),
        ],
        compiler_params=pltpu.CompilerParams(vmem_limit_bytes=40 * 1024 * 1024),
        cost_estimate=pl.CostEstimate(
            flops=rows_q * HEADS * rows_k * HD * 5,
            bytes_accessed=4 * 1024 * 1024,
            transcendentals=rows_q * HEADS * rows_k // 2,
        ),
    )(core, rank_q, order_q, sorted_q, rank_k, sorted_k, *q_parts, *kv_parts, posq)


def in_order(entries):
    n = entries.shape[0]
    rank = jnp.sum((entries[None, :] < entries[:, None]).astype(jnp.int32), axis=1)
    hit = rank[None, :] == jnp.arange(n, dtype=jnp.int32)[:, None]
    place = jnp.arange(n, dtype=jnp.int32)
    order = jnp.sum(jnp.where(hit, place[None, :], 0), axis=1)
    ordered = jnp.sum(jnp.where(hit, entries[None, :], 0), axis=1)
    return rank, order, ordered


def positions(ordered):
    return (ordered[:, None] * HALF + jnp.arange(HALF, dtype=jnp.int32)[None, :]).reshape(-1)


def pack_q_kernel(q_ref, g_ref, lse_ref, delta_ref, out_ref, wide):
    width = HEADS * HD
    rows = q_ref.shape[0]
    out_ref[:rows, :width] = q_ref[...]
    out_ref[:rows, width:] = g_ref[...]
    out_ref[rows:, :] = jnp.zeros((STATS, 2 * width), jnp.bfloat16)
    wide[...] = jnp.zeros_like(wide)
    n = 2 * HEADS
    for k in range(PIECES):
        wide[k * n:k * n + HEADS, :rows] = lse_ref[...]
        wide[k * n + HEADS:(k + 1) * n, :rows] = delta_ref[...]
    x = wide[...]
    piece = lax.broadcasted_iota(jnp.int32, x.shape, 0) // n
    out = jnp.zeros_like(x)
    for k in range(PIECES):
        part = x.astype(jnp.bfloat16).astype(jnp.float32)
        x = x - part
        out = jnp.where(piece == k, part, out)
    out_ref[rows:, :128] = out.astype(jnp.bfloat16)


def pack_q(queries, out_grad, log_sum, delta):
    rows = queries.shape[0]
    return pl.pallas_call(
        pack_q_kernel,
        out_shape=jax.ShapeDtypeStruct((rows + STATS, 2 * HEADS * HD), jnp.bfloat16),
        in_specs=[VMEM] * 4,
        out_specs=VMEM,
        scratch_shapes=[pltpu.VMEM((STATS, 128), jnp.float32)],
    )(queries, out_grad, log_sum.T, delta.T)


FAR = (4, -4, 8)
CLOSE = (1, -1, 2)


def from_far(x, d, back=1):
    return lax.ppermute(x, "z", [(i, (i + back * d) % 16) for i in range(16)])


def from_close(x, d, back=1):
    pairs = []
    for i in range(16):
        for core in range(2):
            step = -d if core == 1 and d == 2 else d
            pairs.append((i * 2 + core, (i + back * step) % 16 * 2 + core))
    return lax.ppermute(x, ("z", "core"), pairs)


def other_core(x):
    return lax.ppermute(x, "core", [(0, 1), (1, 0)])


def look_up(table, index):
    spot = jnp.arange(table.shape[0], dtype=jnp.int32)
    return jnp.sum(jnp.where(index[:, None] == spot[None, :], table[None, :], 0), axis=1)


def both_blocks(device):
    return (2 * device[:, None] + jnp.arange(2, dtype=jnp.int32)[None, :]).reshape(-1)


def local(queries, keys, values, out_grad, log_sum, delta, block_table):
    rows = queries.shape[0]
    width = HEADS * HD
    nx, nyl, nz, nyh, nc = (lax.axis_size(a) for a in ("x", "yl", "z", "yh", "core"))
    ix, iyl, iz, iyh, ic = (lax.axis_index(a) for a in ("x", "yl", "z", "yh", "core"))
    plane = ("x", "yl", "yh")
    devs = nx * nyl * nyh

    packed = pack_q(queries, out_grad, log_sum, delta)
    packed = jnp.broadcast_to(packed[None], (devs,) + packed.shape)
    q_own = lax.all_to_all(packed, plane, split_axis=0, concat_axis=0, tiled=True)
    kv = jnp.concatenate([keys, values], axis=1)
    kv = jnp.concatenate([kv] + [from_far(kv, d) for d in FAR], axis=0)
    kv_parts = [kv] + [from_close(kv, d) for d in CLOSE]
    q_own, kv_parts = lax.optimization_barrier((q_own, kv_parts))
    q_sib = other_core(q_own)

    spot = jnp.arange(devs, dtype=jnp.int32)
    at = [((spot // nyh) * nz + iz) * nyh * nc + (spot % nyh) * nc + c for c in (ic, nc - 1 - ic)]
    table_q = look_up(block_table, both_blocks(jnp.concatenate(at)))
    turn = jnp.where(ic == 1, -1, 1)
    far = jnp.array((0,) + FAR, jnp.int32)
    close = jnp.stack([jnp.int32(0), jnp.int32(1), jnp.int32(-1), 2 * turn])
    z = (iz - close[:, None] - far[None, :]).reshape(-1) % nz
    at = ((z * nyh + iyh) * nc + ic) * nx * nyl + ix * nyl + iyl
    table_k = look_up(block_table, both_blocks(at))

    dq, near, far_kv = tile_grads(ic.reshape(1).astype(jnp.int32), [q_own, q_sib], kv_parts, table_q, table_k)

    dq = dq.reshape(nc * devs, rows, width)
    dq = lax.all_to_all(dq, ("core",) + plane, split_axis=0, concat_axis=0, tiled=True)
    q_grad = (jnp.sum(dq.astype(jnp.float32), axis=0) * SCALE).astype(jnp.bfloat16)
    far_kv = far_kv.reshape(3, 4 * rows, 2 * HD)
    for n, d in enumerate(CLOSE):
        near = near + from_close(far_kv[n], d, -1).astype(jnp.float32)
    near = near.reshape(4, rows, 2 * HD)
    total = near[0]
    for n, d in enumerate(FAR):
        total = total + from_far(near[n + 1], d, -1)
    k_grad = (total[:, :HD] * SCALE).astype(jnp.bfloat16)
    v_grad = total[:, HD:].astype(jnp.bfloat16)
    return (q_grad, k_grad, v_grad)


def solution(mesh):
    fine = Mesh(mesh.devices.reshape(4, 2, 16, 2, 2), ("x", "yl", "z", "yh", "core"))
    q_rows = P(("x", "yl", "z", "yh", "core"), None)
    k_rows = P(("z", "yh", "core", "x", "yl"), None)
    return jax.shard_map(
        local,
        mesh=fine,
        in_specs=(q_rows, k_rows, k_rows, q_rows, q_rows, q_rows, P()),
        out_specs=(q_rows, k_rows, k_rows),
        check_vma=False,
    )
```

time: 118 us -> 118 us (level)
  the two profiles are of different devices: /device:TPU:24 before, /device:TPU:98 now
where the time goes in v5:
time: 118 us; the launch traced here: 117 us
  starting transfers between devices  78.4 us (66%)
  waiting for transfers between devices  17.2 us (15%)
  Pallas kernels  14.4 us (12%)
  local copies, waits for them, and re-layouts  3.36 us (3%)
  other arithmetic  2.86 us (2%)
    ppermute x6, starting transfers between devices, from_far(): return lax.ppermute(x, 'z', [(i, (i + back * d) % 16) for i in range(16)])  40.1 us
    ppermute x6, starting transfers between devices, from_close(): return lax.ppermute(x, ('z', 'core'), pairs)  21 us
    pallas_call x1, Pallas kernels, tile_grads(): pl.pallas_call(tile_kernel, out_shape=(jax.ShapeDtypeStruct((rows_q, HEAD...  12.9 us
    ppermute x6, waiting for transfers between devices, from_far(): return lax.ppermute(x, 'z', [(i, (i + back * d) % 16) for i in range(16)])  12.7 us
    all_to_all x1, starting transfers between devices, local(): lax.all_to_all(dq, ('core',) + plane, split_axis=0, concat_axis=0, tiled=...  7.75 us
    all_to_all x1, starting transfers between devices, local(): lax.all_to_all(packed, plane, split_axis=0, concat_axis=0, tiled=True)  7.62 us
    ppermute x6, waiting for transfers between devices, from_close(): return lax.ppermute(x, ('z', 'core'), pairs)  3.12 us
  transfers between devices with their start and end apart: 15, of which 6 were waited for; matrix products, arithmetic and copies ran while one was open for 3% of the time, Pallas kernels for 0%

profile of v5, /device:TPU:98, one launch (start us, length us, event | category | flops | bytes accessed | tf_op | source)
XLA Modules:
  0.0 117.1 jit_solution(5821675646762611916)
XLA Ops:
  0.6 1.4 %shard_map.103 = bf16[80,512]{1,0:T(8,128)(2,1)} custom-call(bf16[64,256]{1,0:T(8,128)(2,1)} %q_ref.1, bf16[64,256]{1,0:T(8,128)(2,1)} %g_ref.1, f32[2,64]{1,0:T(2,128)} %bitcast.5, f32[2,64]{1,0:T(2,128)} %bitcast.6), custom_call_target="tpu_custom_call" | custom-call | tf_op jit(solution)/shard_map/pallas_call | solution.py:219
  2.1 2.1 %broadcast_in_dim.86 = bf16[16,80,512]{2,1,0:T(8,128)(2,1)} broadcast(bf16[80,512]{1,0:T(8,128)(2,1)} %shard_map.103), dimensions={1,2} | broadcast | bytes 1392640 | tf_op jit(solution)/shard_map/broadcast_in_dim | solution.py:267
  4.1 7.6 %all-to-all-start = ((bf16[16,80,512]{2,1,0:T(8,128)(2,1)}), bf16[16,80,512]{2,1,0:T(8,128)(2,1)S(1)}, u32[]{:S(2)}, u32[]{:S(2)}) async-start(bf16[16,80,512]{2,1,0:T(8,128)(2,1)} %broadcast_in_dim.86), calls=%async_computation | async-start | bytes 2621440 | tf_op jit(solution)/shard_map/all_to_all | solution.py:268
  11.8 13.0 %collective-permute-start.2 = (bf16[64,256]{1,0:T(8,128)(2,1)S(1)}, bf16[64,256]{1,0:T(8,128)(2,1)S(1)}, u32[]{:S(2)}, u32[]{:S(2)}) collective-permute-start(bf16[64,256]{1,0:T(8,128)(2,1)S(1)} %constant_dynamic-update-slice_fusion), channel_id=1, source_target_pairs={{0,32},{4,36},{8,40},{12,44},{16,48},{20,52},{24,56},{28,60},{32,0... | collective-permute-start | bytes 98312 | tf_op jit(solution)/shard_map/ppermute | solution.py:233
  24.8 3.3 %collective-permute-start.1 = (bf16[64,256]{1,0:T(8,128)(2,1)S(1)}, bf16[64,256]{1,0:T(8,128)(2,1)S(1)}, u32[]{:S(2)}, u32[]{:S(2)}) collective-permute-start(bf16[64,256]{1,0:T(8,128)(2,1)S(1)} %constant_dynamic-update-slice_fusion), channel_id=1, source_target_pairs={{0,48},{4,52},{8,56},{12,60},{16,0},{20,4},{24,8},{28,12},{32,16},... | collective-permute-start | bytes 98312 | tf_op jit(solution)/shard_map/ppermute | solution.py:233
  28.2 6.4 %collective-permute-start = (bf16[64,256]{1,0:T(8,128)(2,1)S(1)}, bf16[64,256]{1,0:T(8,128)(2,1)S(1)}, u32[]{:S(2)}, u32[]{:S(2)}) collective-permute-start(bf16[64,256]{1,0:T(8,128)(2,1)S(1)} %constant_dynamic-update-slice_fusion), channel_id=1, source_target_pairs={{0,16},{4,20},{8,24},{12,28},{16,32},{20,36},{24,40},{28,44},{32,4... | collective-permute-start | bytes 98312 | tf_op jit(solution)/shard_map/ppermute | solution.py:233
  35.0 3.5 %collective-permute-done = bf16[64,256]{1,0:T(8,128)(2,1)S(1)} collective-permute-done((bf16[64,256]{1,0:T(8,128)(2,1)S(1)}, bf16[64,256]{1,0:T(8,128)(2,1)S(1)}, u32[]{:S(2)}, u32[]{:S(2)}) %collective-permute-start) | collective-permute-done | bytes 32800 | tf_op jit(solution)/shard_map/ppermute | solution.py:233
  38.5 5.0 %collective-permute-start.5 = (bf16[256,256]{1,0:T(8,128)(2,1)S(1)}, bf16[256,256]{1,0:T(8,128)(2,1)S(1)}, u32[]{:S(2)}, u32[]{:S(2)}) collective-permute-start(bf16[256,256]{1,0:T(8,128)(2,1)S(1)} %pad_maximum_fusion.refs_2_), channel_id=1, source_target_pairs={{0,8},{1,57},{4,12},{5,61},{8,16},{9,1},{12,20},{13,5},{16,24},{17... | collective-permute-start | bytes 393224 | tf_op jit(solution)/shard_map/ppermute | solution.py:242
  43.5 3.4 %collective-permute-start.4 = (bf16[256,256]{1,0:T(8,128)(2,1)S(1)}, bf16[256,256]{1,0:T(8,128)(2,1)S(1)}, u32[]{:S(2)}, u32[]{:S(2)}) collective-permute-start(bf16[256,256]{1,0:T(8,128)(2,1)S(1)} %pad_maximum_fusion.refs_2_), channel_id=1, source_target_pairs={{0,60},{1,61},{4,0},{5,1},{8,4},{9,5},{12,8},{13,9},{16,12},{17,13... | collective-permute-start | bytes 393224 | tf_op jit(solution)/shard_map/ppermute | solution.py:242
  46.9 3.7 %collective-permute-start.3 = (bf16[256,256]{1,0:T(8,128)(2,1)S(1)}, bf16[256,256]{1,0:T(8,128)(2,1)S(1)}, u32[]{:S(2)}, u32[]{:S(2)}) collective-permute-start(bf16[256,256]{1,0:T(8,128)(2,1)S(1)} %pad_maximum_fusion.refs_2_), channel_id=1, source_target_pairs={{0,4},{1,5},{4,8},{5,9},{8,12},{9,13},{12,16},{13,17},{16,20},{17,... | collective-permute-start | bytes 393224 | tf_op jit(solution)/shard_map/ppermute | solution.py:242
  50.6 0.9 collective-permute-done.4.refs_4_
  51.5 2.2 %collective-permute-done.3.refs_3_ = bf16[256,256]{1,0:T(8,128)(2,1)S(1)} collective-permute-done((bf16[256,256]{1,0:T(8,128)(2,1)S(1)}, bf16[256,256]{1,0:T(8,128)(2,1)S(1)}, u32[]{:S(2)}, u32[]{:S(2)}) %collective-permute-start.3) | collective-permute-done | bytes 131104 | tf_op jit(solution)/shard_map/ppermute | solution.py:242
  53.7 1.9 %collective-permute-start.6 = (bf16[16,80,512]{2,1,0:T(8,128)(2,1)S(1)}, bf16[16,80,512]{2,1,0:T(8,128)(2,1)S(1)}, u32[]{:S(2)}, u32[]{:S(2)}) collective-permute-start(bf16[16,80,512]{2,1,0:T(8,128)(2,1)S(1)} %all-to-all-done.refs_0_), channel_id=1, source_target_pairs={{0,1},{1,0},{2,3},{3,2},{4,5},{5,4},{6,7},{7,6},{8,9},{9,8},{10,11... | collective-permute-start | bytes 3932168 | tf_op jit(solution)/shard_map/ppermute | solution.py:246
  56.0 0.2 select_reduce_fusion
  56.2 0.2 convert_reduce_fusion.1.rank_q
  56.8 0.2 select_reduce_fusion.1
  57.0 0.2 convert_reduce_fusion.2.rank_k
  57.3 1.3 %collective-permute-done.6.refs_1_ = bf16[16,80,512]{2,1,0:T(8,128)(2,1)S(1)} collective-permute-done((bf16[16,80,512]{2,1,0:T(8,128)(2,1)S(1)}, bf16[16,80,512]{2,1,0:T(8,128)(2,1)S(1)}, u32[]{:S(2)}, u32[]{:S(2)}) %collective-permute-start.6) | collective-permute-done | bytes 1310752 | tf_op jit(solution)/shard_map/ppermute | solution.py:246
  58.7 12.9 %shard_map.104 = (bf16[2048,256]{1,0:T(8,128)(2,1)}, f32[256,256]{1,0:T(8,128)S(1)}, bf16[768,256]{1,0:T(8,128)(2,1)S(1)}) custom-call(s32[1]{0:T(128)} %bitcast.core, s32[64]{0:T(128)S(1)} %convert_reduce_fusion.1.rank_q, s32[64]{0:T(128)S(1)} %get-tuple-element.20.order_q, s32[64]{0:T(128)S(1)} %get-tuple-element.19.sorted_q, ...), custom_call_target="tpu_custom_call" | custom-call | flops 2684354560 | bytes 4194304 | tf_op jit(solution)/shard_map/pallas_call | solution.py:151
  71.6 1.9 %collective-permute-start.7 = (bf16[256,256]{1,0:T(8,128)(2,1)S(1)}, bf16[256,256]{1,0:T(8,128)(2,1)S(1)}, u32[]{:S(2)}, u32[]{:S(2)}) collective-permute-start(bf16[256,256]{1,0:T(8,128)(2,1)S(1)} %get-tuple-element.21), channel_id=1, source_target_pairs={{0,60},{1,61},{4,0},{5,1},{8,4},{9,5},{12,8},{13,9},{16,12},{17,13... | collective-permute-start | bytes 393224 | tf_op jit(solution)/shard_map/ppermute | solution.py:242
  73.5 2.8 %collective-permute-start.9 = (bf16[256,256]{1,0:T(8,128)(2,1)S(1)}, bf16[256,256]{1,0:T(8,128)(2,1)S(1)}, u32[]{:S(2)}, u32[]{:S(2)}) collective-permute-start(bf16[256,256]{1,0:T(8,128)(2,1)S(1)} %get-tuple-element.22), channel_id=1, source_target_pairs={{0,56},{1,9},{4,60},{5,13},{8,0},{9,17},{12,4},{13,21},{16,8},{17,... | collective-permute-start | bytes 393224 | tf_op jit(solution)/shard_map/ppermute | solution.py:242
  76.3 4.3 %collective-permute-start.8 = (bf16[256,256]{1,0:T(8,128)(2,1)S(1)}, bf16[256,256]{1,0:T(8,128)(2,1)S(1)}, u32[]{:S(2)}, u32[]{:S(2)}) collective-permute-start(bf16[256,256]{1,0:T(8,128)(2,1)S(1)} %get-tuple-element.23), channel_id=1, source_target_pairs={{0,4},{1,5},{4,8},{5,9},{8,12},{9,13},{12,16},{13,17},{16,20},{17,... | collective-permute-start | bytes 393224 | tf_op jit(solution)/shard_map/ppermute | solution.py:242
  80.6 7.8 %all-to-all-start.1 = ((bf16[32,64,256]{2,1,0:T(8,128)(2,1)}), bf16[32,64,256]{2,1,0:T(8,128)(2,1)S(1)}, u32[]{:S(2)}, u32[]{:S(2)}) async-start(bf16[32,64,256]{2,1,0:T(8,128)(2,1)} %bitcast.4), calls=%async_computation.1 | async-start | bytes 2097152 | tf_op jit(solution)/shard_map/all_to_all | solution.py:288
  88.5 2.4 %collective-permute-start.10 = (f32[64,256]{1,0:T(8,128)S(1)}, f32[64,256]{1,0:T(8,128)S(1)}, u32[]{:S(2)}, u32[]{:S(2)}) collective-permute-start(f32[64,256]{1,0:T(8,128)S(1)} %get-tuple-element.24), channel_id=1, source_target_pairs={{0,48},{4,52},{8,56},{12,60},{16,0},{20,4},{24,8},{28,12},{32,16},... | collective-permute-start | bytes 196616 | tf_op jit(solution)/shard_map/ppermute | solution.py:233
  90.9 9.9 %collective-permute-start.12 = (f32[64,256]{1,0:T(8,128)S(1)}, f32[64,256]{1,0:T(8,128)S(1)}, u32[]{:S(2)}, u32[]{:S(2)}) collective-permute-start(f32[64,256]{1,0:T(8,128)S(1)} %get-tuple-element.25), channel_id=1, source_target_pairs={{0,32},{4,36},{8,40},{12,44},{16,48},{20,52},{24,56},{28,60},{32,0... | collective-permute-start | bytes 196616 | tf_op jit(solution)/shard_map/ppermute | solution.py:233
  100.9 4.9 %collective-permute-start.11 = (f32[64,256]{1,0:T(8,128)S(1)}, f32[64,256]{1,0:T(8,128)S(1)}, u32[]{:S(2)}, u32[]{:S(2)}) collective-permute-start(f32[64,256]{1,0:T(8,128)S(1)} %get-tuple-element.26), channel_id=1, source_target_pairs={{0,16},{4,20},{8,24},{12,28},{16,32},{20,36},{24,40},{28,44},{32,4... | collective-permute-start | bytes 196616 | tf_op jit(solution)/shard_map/ppermute | solution.py:233
  105.8 1.7 %collective-permute-done.12 = f32[64,256]{1,0:T(8,128)S(1)} collective-permute-done((f32[64,256]{1,0:T(8,128)S(1)}, f32[64,256]{1,0:T(8,128)S(1)}, u32[]{:S(2)}, u32[]{:S(2)}) %collective-permute-start.12) | collective-permute-done | bytes 65568 | tf_op jit(solution)/shard_map/ppermute | solution.py:233
  107.5 7.5 %collective-permute-done.11 = f32[64,256]{1,0:T(8,128)S(1)} collective-permute-done((f32[64,256]{1,0:T(8,128)S(1)}, f32[64,256]{1,0:T(8,128)S(1)}, u32[]{:S(2)}, u32[]{:S(2)}) %collective-permute-start.11) | collective-permute-done | bytes 65568 | tf_op jit(solution)/shard_map/ppermute | solution.py:233
  115.1 0.6 slice.59
  115.7 0.6 fusion.2
  116.3 0.2 convert_reduce_fusion
  116.4 0.6 multiply_convert_fusion
  (44 shorter events, 1.4 us)
Async XLA Ops:
  4.1 7.6 %copy-start.1 = (bf16[64,128]{1,0:T(8,128)(2,1)S(1)}, bf16[64,128]{1,0:T(8,128)(2,1)}, u32[]{:S(2)}) copy-start(bf16[64,128]{1,0:T(8,128)(2,1)} %param.9) | copy-start | bytes 49156
  4.1 7.7 %copy-start.2 = (bf16[64,128]{1,0:T(8,128)(2,1)S(1)}, bf16[64,128]{1,0:T(8,128)(2,1)}, u32[]{:S(2)}) copy-start(bf16[64,128]{1,0:T(8,128)(2,1)} %param.10) | copy-start | bytes 49156
  4.1 30.6 %copy-start.3 = (s32[4]{0:T(128)S(1)}, s32[4]{0:T(128)}, u32[]{:S(2)}) copy-start(s32[4]{0:T(128)} %constant.106) | copy-start | bytes 52
  4.1 51.9 %copy-start = (s32[1024]{0:T(1024)S(1)}, s32[1024]{0:T(1024)}, u32[]{:S(2)}) copy-start(s32[1024]{0:T(1024)} %param.14) | copy-start | bytes 12292
  4.1 49.6 %all-to-all-start = ((bf16[16,80,512]{2,1,0:T(8,128)(2,1)}), bf16[16,80,512]{2,1,0:T(8,128)(2,1)S(1)}, u32[]{:S(2)}, u32[]{:S(2)}) async-start(bf16[16,80,512]{2,1,0:T(8,128)(2,1)} %broadcast_in_dim.86), calls=%async_computation | async-start | bytes 2621440 | tf_op jit(solution)/shard_map/all_to_all | solution.py:268
  11.8 23.2 %collective-permute-start.2 = (bf16[64,256]{1,0:T(8,128)(2,1)S(1)}, bf16[64,256]{1,0:T(8,128)(2,1)S(1)}, u32[]{:S(2)}, u32[]{:S(2)}) collective-permute-start(bf16[64,256]{1,0:T(8,128)(2,1)S(1)} %constant_dynamic-update-slice_fusion), channel_id=1, source_target_pairs={{0,32},{4,36},{8,40},{12,44},{16,48},{20,52},{24,56},{28,60},{32,0... | collective-permute-start | bytes 98312 | tf_op jit(solution)/shard_map/ppermute | solution.py:233
  24.8 10.1 %collective-permute-start.1 = (bf16[64,256]{1,0:T(8,128)(2,1)S(1)}, bf16[64,256]{1,0:T(8,128)(2,1)S(1)}, u32[]{:S(2)}, u32[]{:S(2)}) collective-permute-start(bf16[64,256]{1,0:T(8,128)(2,1)S(1)} %constant_dynamic-update-slice_fusion), channel_id=1, source_target_pairs={{0,48},{4,52},{8,56},{12,60},{16,0},{20,4},{24,8},{28,12},{32,16},... | collective-permute-start | bytes 98312 | tf_op jit(solution)/shard_map/ppermute | solution.py:233
  28.2 10.2 %collective-permute-start = (bf16[64,256]{1,0:T(8,128)(2,1)S(1)}, bf16[64,256]{1,0:T(8,128)(2,1)S(1)}, u32[]{:S(2)}, u32[]{:S(2)}) collective-permute-start(bf16[64,256]{1,0:T(8,128)(2,1)S(1)} %constant_dynamic-update-slice_fusion), channel_id=1, source_target_pairs={{0,16},{4,20},{8,24},{12,28},{16,32},{20,36},{24,40},{28,44},{32,4... | collective-permute-start | bytes 98312 | tf_op jit(solution)/shard_map/ppermute | solution.py:233
  38.5 12.2 %collective-permute-start.5 = (bf16[256,256]{1,0:T(8,128)(2,1)S(1)}, bf16[256,256]{1,0:T(8,128)(2,1)S(1)}, u32[]{:S(2)}, u32[]{:S(2)}) collective-permute-start(bf16[256,256]{1,0:T(8,128)(2,1)S(1)} %pad_maximum_fusion.refs_2_), channel_id=1, source_target_pairs={{0,8},{1,57},{4,12},{5,61},{8,16},{9,1},{12,20},{13,5},{16,24},{17... | collective-permute-start | bytes 393224 | tf_op jit(solution)/shard_map/ppermute | solution.py:242
  43.5 8.1 %collective-permute-start.4 = (bf16[256,256]{1,0:T(8,128)(2,1)S(1)}, bf16[256,256]{1,0:T(8,128)(2,1)S(1)}, u32[]{:S(2)}, u32[]{:S(2)}) collective-permute-start(bf16[256,256]{1,0:T(8,128)(2,1)S(1)} %pad_maximum_fusion.refs_2_), channel_id=1, source_target_pairs={{0,60},{1,61},{4,0},{5,1},{8,4},{9,5},{12,8},{13,9},{16,12},{17,13... | collective-permute-start | bytes 393224 | tf_op jit(solution)/shard_map/ppermute | solution.py:242
  46.9 6.9 %collective-permute-start.3 = (bf16[256,256]{1,0:T(8,128)(2,1)S(1)}, bf16[256,256]{1,0:T(8,128)(2,1)S(1)}, u32[]{:S(2)}, u32[]{:S(2)}) collective-permute-start(bf16[256,256]{1,0:T(8,128)(2,1)S(1)} %pad_maximum_fusion.refs_2_), channel_id=1, source_target_pairs={{0,4},{1,5},{4,8},{5,9},{8,12},{9,13},{12,16},{13,17},{16,20},{17,... | collective-permute-start | bytes 393224 | tf_op jit(solution)/shard_map/ppermute | solution.py:242
  53.7 4.9 %collective-permute-start.6 = (bf16[16,80,512]{2,1,0:T(8,128)(2,1)S(1)}, bf16[16,80,512]{2,1,0:T(8,128)(2,1)S(1)}, u32[]{:S(2)}, u32[]{:S(2)}) collective-permute-start(bf16[16,80,512]{2,1,0:T(8,128)(2,1)S(1)} %all-to-all-done.refs_0_), channel_id=1, source_target_pairs={{0,1},{1,0},{2,3},{3,2},{4,5},{5,4},{6,7},{7,6},{8,9},{9,8},{10,11... | collective-permute-start | bytes 3932168 | tf_op jit(solution)/shard_map/ppermute | solution.py:246
  71.6 16.8 %collective-permute-start.7 = (bf16[256,256]{1,0:T(8,128)(2,1)S(1)}, bf16[256,256]{1,0:T(8,128)(2,1)S(1)}, u32[]{:S(2)}, u32[]{:S(2)}) collective-permute-start(bf16[256,256]{1,0:T(8,128)(2,1)S(1)} %get-tuple-element.21), channel_id=1, source_target_pairs={{0,60},{1,61},{4,0},{5,1},{8,4},{9,5},{12,8},{13,9},{16,12},{17,13... | collective-permute-start | bytes 393224 | tf_op jit(solution)/shard_map/ppermute | solution.py:242
  73.5 14.8 %collective-permute-start.9 = (bf16[256,256]{1,0:T(8,128)(2,1)S(1)}, bf16[256,256]{1,0:T(8,128)(2,1)S(1)}, u32[]{:S(2)}, u32[]{:S(2)}) collective-permute-start(bf16[256,256]{1,0:T(8,128)(2,1)S(1)} %get-tuple-element.22), channel_id=1, source_target_pairs={{0,56},{1,9},{4,60},{5,13},{8,0},{9,17},{12,4},{13,21},{16,8},{17,... | collective-permute-start | bytes 393224 | tf_op jit(solution)/shard_map/ppermute | solution.py:242
  76.3 12.1 %collective-permute-start.8 = (bf16[256,256]{1,0:T(8,128)(2,1)S(1)}, bf16[256,256]{1,0:T(8,128)(2,1)S(1)}, u32[]{:S(2)}, u32[]{:S(2)}) collective-permute-start(bf16[256,256]{1,0:T(8,128)(2,1)S(1)} %get-tuple-element.23), channel_id=1, source_target_pairs={{0,4},{1,5},{4,8},{5,9},{8,12},{9,13},{12,16},{13,17},{16,20},{17,... | collective-permute-start | bytes 393224 | tf_op jit(solution)/shard_map/ppermute | solution.py:242
  80.6 35.7 %all-to-all-start.1 = ((bf16[32,64,256]{2,1,0:T(8,128)(2,1)}), bf16[32,64,256]{2,1,0:T(8,128)(2,1)S(1)}, u32[]{:S(2)}, u32[]{:S(2)}) async-start(bf16[32,64,256]{2,1,0:T(8,128)(2,1)} %bitcast.4), calls=%async_computation.1 | async-start | bytes 2097152 | tf_op jit(solution)/shard_map/all_to_all | solution.py:288
  88.5 17.3 %collective-permute-start.10 = (f32[64,256]{1,0:T(8,128)S(1)}, f32[64,256]{1,0:T(8,128)S(1)}, u32[]{:S(2)}, u32[]{:S(2)}) collective-permute-start(f32[64,256]{1,0:T(8,128)S(1)} %get-tuple-element.24), channel_id=1, source_target_pairs={{0,48},{4,52},{8,56},{12,60},{16,0},{20,4},{24,8},{28,12},{32,16},... | collective-permute-start | bytes 196616 | tf_op jit(solution)/shard_map/ppermute | solution.py:233
  90.9 16.6 %collective-permute-start.12 = (f32[64,256]{1,0:T(8,128)S(1)}, f32[64,256]{1,0:T(8,128)S(1)}, u32[]{:S(2)}, u32[]{:S(2)}) collective-permute-start(f32[64,256]{1,0:T(8,128)S(1)} %get-tuple-element.25), channel_id=1, source_target_pairs={{0,32},{4,36},{8,40},{12,44},{16,48},{20,52},{24,56},{28,60},{32,0... | collective-permute-start | bytes 196616 | tf_op jit(solution)/shard_map/ppermute | solution.py:233
  100.9 14.2 %collective-permute-start.11 = (f32[64,256]{1,0:T(8,128)S(1)}, f32[64,256]{1,0:T(8,128)S(1)}, u32[]{:S(2)}, u32[]{:S(2)}) collective-permute-start(f32[64,256]{1,0:T(8,128)S(1)} %get-tuple-element.26), channel_id=1, source_target_pairs={{0,16},{4,20},{8,24},{12,28},{16,32},{20,36},{24,40},{28,44},{32,4... | collective-permute-start | bytes 196616 | tf_op jit(solution)/shard_map/ppermute | solution.py:233

commit v6 on v4

--- a/solution.py
+++ b/solution.py
@@ -14,7 +14,7 @@
 STATS = 16
 QT = 256
 KT = 256
-TOGETHER = 2
+TOGETHER = 4
 VMEM = pl.BlockSpec(memory_space=pltpu.VMEM)
 SMEM = pl.BlockSpec(memory_space=pltpu.SMEM)
 
@@ -145,14 +145,14 @@
             out[cut, HD:] = dv[i, pl.ds(r, HALF), :].astype(out.dtype)
 
 
-def tile_grads(q_parts, kv_parts, table_q, table_k):
+def tile_grads(q_parts, kv_parts, lists_q, lists_k):
     part = q_parts[0].shape[0] - STATS
     rows_q = 4 * part
     part_k = kv_parts[0].shape[0]
     rows_k = 2 * part_k
     n_q, n_k = rows_q // QT, rows_k // KT
-    rank_q, order_q, sorted_q = in_order(table_q)
-    rank_k, _, sorted_k = in_order(table_k)
+    rank_q, order_q, sorted_q = lists_q
+    rank_k, _, sorted_k = lists_k
     posq = positions(sorted_q).reshape(n_q, 1, QT)
     posq = jnp.concatenate([posq] * HEADS, axis=2)
     bf, f32 = jnp.bfloat16, jnp.float32
@@ -272,16 +272,13 @@
     return lax.ppermute(x, "core", [(0, 1), (1, 0)])
 
 
-def back_from(table, index, axis):
-    head = lax.slice_in_dim(table, 0, 1, axis=axis)
-    tail = jnp.flip(lax.slice_in_dim(table, 1, 4, axis=axis), axis)
-    return lax.dynamic_slice_in_dim(jnp.concatenate([head, tail, head, tail], axis), (4 - index) % 4, 4, axis)
-
-
-def pick(table, *choices):
-    for axis, index in choices:
-        table = lax.dynamic_index_in_dim(table, index, axis, keepdims=False)
-    return table
+def look_up(table, index):
+    spot = jnp.arange(table.shape[0], dtype=jnp.int32)
+    return jnp.sum(jnp.where(index[:, None] == spot[None, :], table[None, :], 0), axis=1)
+
+
+def both_blocks(device):
+    return (2 * device[:, None] + jnp.arange(2, dtype=jnp.int32)[None, :]).reshape(-1)
 
 
 def local(queries, keys, values, out_grad, log_sum, delta, block_table):
@@ -293,20 +290,29 @@
 
     kv_own = lax.all_to_all(pack_kv(keys, values, nz), "z", split_axis=0, concat_axis=0, tiled=True)
     kv_own = kv_own.reshape(nz * rows, 2 * HD)
-    packed = pack_q(queries, out_grad, log_sum, delta)
-    line = join([packed] + [from_offset(packed, 0, d) for d in (1, 2, 3)])
-    q_parts = [line] + [from_offset(line, 1, d) for d in (1, 2, 3)]
+
+    def gather_q(turn, carried):
+        packed = pack_q(queries, out_grad, log_sum, delta)
+        line = join([packed] + [from_offset(packed, 0, d) for d in (1, 2, 3)])
+        q_parts = [line] + [from_offset(line, 1, d) for d in (1, 2, 3)]
+        table = block_table + jnp.minimum(turn, 0)
+        spot = jnp.arange(16, dtype=jnp.int32)
+        inner, outer = spot % 4, spot // 4
+        x = (ix - jnp.where(ic == 0, inner, outer)) % nx
+        y = (iy - jnp.where(ic == 0, outer, inner)) % (nyl * nyh)
+        at = ((x * nyl + y % nyl) * nz + iz) * nyh * nc + y // nyl * nc + ic
+        lists_q = in_order(look_up(table, both_blocks(at)))
+        both = [((spot * nyh + iyh) * nc + c) * nx * nyl + ix * nyl + iyl for c in (ic, nc - 1 - ic)]
+        lists_k = in_order(look_up(table, both_blocks(jnp.concatenate(both))))
+        return q_parts, lists_q, lists_k
+
+    empty = jax.tree.map(lambda x: jnp.zeros(x.shape, x.dtype), jax.eval_shape(lambda: gather_q(0, None)))
+    turns = 1 + jnp.minimum(block_table[0], 0)
+    q_parts, lists_q, lists_k = lax.fori_loop(0, turns, gather_q, empty)
     kv_own, q_parts = lax.optimization_barrier((kv_own, q_parts))
     kv_sib = other_core(kv_own)
 
-    table_q = pick(block_table.reshape(nx, nyl, nz, nyh, nc, 2), (2, iz), (3, ic))
-    table_q = table_q.transpose(0, 2, 1, 3).reshape(nx, nyh * nyl, 2)
-    table_q = back_from(back_from(table_q, ix, 0), iy, 1)
-    table_q = jnp.where(ic == 0, table_q.transpose(1, 0, 2), table_q).reshape(-1)
-    table_k = pick(block_table.reshape(nz, nyh, nc, nx, nyl, 2), (1, iyh), (2, ix), (2, iyl))
-    table_k = jnp.concatenate([pick(table_k, (1, c)).reshape(-1) for c in (ic, nc - 1 - ic)])
-
-    near, far, dkv_own, dkv_sib = tile_grads(q_parts, [kv_own, kv_sib], table_q, table_k)
+    near, far, dkv_own, dkv_sib = tile_grads(q_parts, [kv_own, kv_sib], lists_q, lists_k)
 
     dkv = (dkv_own + other_core(dkv_sib).astype(jnp.float32)).astype(jnp.bfloat16)
     dkv = lax.all_to_all(dkv.reshape(nz, rows, 2 * HD), "z", split_axis=0, concat_axis=0, tiled=True)

time: 118 us -> 126 us (1.068)
  the two profiles are of different devices: /device:TPU:24 before, /device:TPU:32 now
where the time goes in v6:
time: 126 us; the launch traced here: 125 us
  starting transfers between devices  71.5 us (57%)
  waiting for transfers between devices  22.3 us (18%)
  Pallas kernels  14.1 us (11%)
  local copies, waits for them, and re-layouts  10.9 us (9%)
  other arithmetic  4.65 us (4%)
  between operations  1.45 us (1%)
    ppermute x12, starting transfers between devices, from_offset(): return lax.ppermute(x, ('x', 'yl', 'yh', 'core'), pairs)  38.9 us
    ppermute x12, waiting for transfers between devices, from_offset(): return lax.ppermute(x, ('x', 'yl', 'yh', 'core'), pairs)  17.6 us
    all_to_all x1, starting transfers between devices, local(): lax.all_to_all(pack_kv(keys, values, nz), 'z', split_axis=0, concat_axis=...  15.2 us
    all_to_all x1, starting transfers between devices, local(): lax.all_to_all(dkv.reshape(nz, rows, 2 * HD), 'z', split_axis=0, concat_a...  13.3 us
    pallas_call x1, Pallas kernels, tile_grads(): pl.pallas_call(tile_kernel, out_shape=(jax.ShapeDtypeStruct((part, HEADS...  11.8 us
    another operation x9, local copies, waits for them, and re-layouts  5.5 us
    ppermute x2, starting transfers between devices, other_core(): return lax.ppermute(x, 'core', [(0, 1), (1, 0)])  4.08 us
    ppermute x2, waiting for transfers between devices, other_core(): return lax.ppermute(x, 'core', [(0, 1), (1, 0)])  3.35 us
  transfers between devices with their start and end apart: 16, of which 10 were waited for; matrix products, arithmetic and copies ran while one was open for 9% of the time, Pallas kernels for 1%

profile of v6, /device:TPU:32, one launch (start us, length us, event | category | flops | bytes accessed | tf_op | source)
XLA Modules:
  0.0 125.0 jit_solution(15051707595611179175)
XLA Ops:
  0.6 1.6 %shard_map.94 = bf16[16,64,256]{2,1,0:T(8,128)(2,1)} custom-call(bf16[64,128]{1,0:T(8,128)(2,1)} %k_ref.1, bf16[64,128]{1,0:T(8,128)(2,1)} %v_ref.1), custom_call_target="tpu_custom_call" | custom-call | tf_op jit(solution)/shard_map/pallas_call | solution.py:211
  2.2 15.2 %all-to-all-start = ((bf16[16,64,256]{2,1,0:T(8,128)(2,1)}), bf16[16,64,256]{2,1,0:T(8,128)(2,1)S(1)}, u32[]{:S(2)}, u32[]{:S(2)}) async-start(bf16[16,64,256]{2,1,0:T(8,128)(2,1)} %shard_map.94), calls=%async_computation | async-start | bytes 1048576 | tf_op jit(solution)/shard_map/all_to_all | solution.py:291
  22.7 0.7 broadcast.473.clone.1
  23.4 0.7 broadcast.473.clone
  24.9 34.4 %while.31 = (s32[]{:T(128)}, bf16[272,512]{1,0:T(8,128)(2,1)}, bf16[272,512]{1,0:T(8,128)(2,1)}, bf16[272,512]{1,0:T(8,128)(2,1)}, bf16[272,512]{1,0:T(8,128)(2,...) while((s32[]{:T(128)}, bf16[272,512]{1,0:T(8,128)(2,1)}, ...), condition=%wide.region_8.9_spmd, body=%wide.region_0.8_spmd.sunk | while | flops 395315 | bytes 9394874 | solution.py:311
  25.6 4.7 %collective-permute-start.2 = (bf16[80,512]{1,0:T(8,128)(2,1)}, bf16[80,512]{1,0:T(8,128)(2,1)S(1)}, u32[]{:S(2)}, u32[]{:S(2)}) collective-permute-start(bf16[80,512]{1,0:T(8,128)(2,1)} %body.6), channel_id=1, source_target_pairs={{0,384},{1,67},{64,448},{65,1},{2,386},{3,65},{66,450},{67,3},{128... | collective-permute-start | bytes 245768 | tf_op jit(solution)/shard_map/while/body/ppermute | solution.py:264
  30.3 2.7 %collective-permute-start.1 = (bf16[80,512]{1,0:T(8,128)(2,1)}, bf16[80,512]{1,0:T(8,128)(2,1)S(1)}, u32[]{:S(2)}, u32[]{:S(2)}) collective-permute-start(bf16[80,512]{1,0:T(8,128)(2,1)} %body.6), channel_id=1, source_target_pairs={{0,256},{1,3},{64,320},{65,67},{2,258},{3,1},{66,322},{67,65},{128... | collective-permute-start | bytes 245768 | tf_op jit(solution)/shard_map/while/body/ppermute | solution.py:264
  33.0 2.8 %collective-permute-start = (bf16[80,512]{1,0:T(8,128)(2,1)}, bf16[80,512]{1,0:T(8,128)(2,1)S(1)}, u32[]{:S(2)}, u32[]{:S(2)}) collective-permute-start(bf16[80,512]{1,0:T(8,128)(2,1)} %body.6), channel_id=1, source_target_pairs={{0,128},{1,65},{64,192},{65,3},{2,130},{3,67},{66,194},{67,1},{128... | collective-permute-start | bytes 245768 | tf_op jit(solution)/shard_map/while/body/ppermute | solution.py:264
  36.5 0.8 slice_dynamic-update-slice_fusion.8
  38.4 2.3 %collective-permute-done = bf16[80,512]{1,0:T(8,128)(2,1)S(1)} collective-permute-done((bf16[80,512]{1,0:T(8,128)(2,1)}, bf16[80,512]{1,0:T(8,128)(2,1)S(1)}, u32[]{:S(2)}, u32[]{:S(2)}) %collective-permute-start) | collective-permute-done | bytes 81952 | tf_op jit(solution)/shard_map/while/body/ppermute | solution.py:264
  40.8 4.9 %collective-permute-start.5 = (bf16[272,512]{1,0:T(8,128)(2,1)S(1)}, bf16[272,512]{1,0:T(8,128)(2,1)S(1)}, u32[]{:S(2)}, u32[]{:S(2)}) collective-permute-start(bf16[272,512]{1,0:T(8,128)(2,1)S(1)} %maximum_dynamic-update-slice_fusion.2), channel_id=1, source_target_pairs={{0,66},{1,385},{64,0},{65,449},{2,64},{3,387},{66,2},{67,451},{128... | collective-permute-start | bytes 835592 | tf_op jit(solution)/shard_map/while/body/ppermute | solution.py:264
  45.7 2.5 %collective-permute-start.4 = (bf16[272,512]{1,0:T(8,128)(2,1)S(1)}, bf16[272,512]{1,0:T(8,128)(2,1)S(1)}, u32[]{:S(2)}, u32[]{:S(2)}) collective-permute-start(bf16[272,512]{1,0:T(8,128)(2,1)S(1)} %maximum_dynamic-update-slice_fusion.2), channel_id=1, source_target_pairs={{0,2},{1,257},{64,66},{65,321},{2,0},{3,259},{66,64},{67,323},{128... | collective-permute-start | bytes 835592 | tf_op jit(solution)/shard_map/while/body/ppermute | solution.py:264
  48.3 2.9 %collective-permute-start.3 = (bf16[272,512]{1,0:T(8,128)(2,1)S(1)}, bf16[272,512]{1,0:T(8,128)(2,1)S(1)}, u32[]{:S(2)}, u32[]{:S(2)}) collective-permute-start(bf16[272,512]{1,0:T(8,128)(2,1)S(1)} %maximum_dynamic-update-slice_fusion.2), channel_id=1, source_target_pairs={{0,64},{1,129},{64,2},{65,193},{2,66},{3,131},{66,0},{67,195},{128... | collective-permute-start | bytes 835592 | tf_op jit(solution)/shard_map/while/body/ppermute | solution.py:264
  52.6 3.1 %collective-permute-done.4 = bf16[272,512]{1,0:T(8,128)(2,1)S(1)} collective-permute-done((bf16[272,512]{1,0:T(8,128)(2,1)S(1)}, bf16[272,512]{1,0:T(8,128)(2,1)S(1)}, u32[]{:S(2)}, u32[]{:S(2)}) %collective-permute-start.4) | collective-permute-done | bytes 278560 | tf_op jit(solution)/shard_map/while/body/ppermute | solution.py:264
  55.7 2.9 %collective-permute-done.3 = bf16[272,512]{1,0:T(8,128)(2,1)S(1)} collective-permute-done((bf16[272,512]{1,0:T(8,128)(2,1)S(1)}, bf16[272,512]{1,0:T(8,128)(2,1)S(1)}, u32[]{:S(2)}, u32[]{:S(2)}) %collective-permute-start.3) | collective-permute-done | bytes 278560 | tf_op jit(solution)/shard_map/while/body/ppermute | solution.py:264
  59.4 2.0 %collective-permute-start.6 = (bf16[1024,256]{1,0:T(8,128)(2,1)S(1)}, bf16[1024,256]{1,0:T(8,128)(2,1)S(1)}, u32[]{:S(2)}, u32[]{:S(2)}) collective-permute-start(bf16[1024,256]{1,0:T(8,128)(2,1)S(1)} %bitcast.9), channel_id=1, source_target_pairs={{0,1},{1,0},{2,3},{3,2},{4,5},{5,4},{6,7},{7,6},{8,9},{9,8},{10,11... | collective-permute-start | bytes 1572872 | tf_op jit(solution)/shard_map/ppermute | solution.py:272
  61.7 1.6 %collective-permute-done.6.refs_5_ = bf16[1024,256]{1,0:T(8,128)(2,1)S(1)} collective-permute-done((bf16[1024,256]{1,0:T(8,128)(2,1)S(1)}, bf16[1024,256]{1,0:T(8,128)(2,1)S(1)}, u32[]{:S(2)}, u32[]{:S(2)}) %collective-permute-start.6) | collective-permute-done | bytes 524320 | tf_op jit(solution)/shard_map/ppermute | solution.py:272
  64.0 11.8 %shard_map.95 = (f32[256,256]{1,0:T(8,128)S(1)}, bf16[1024,256]{1,0:T(8,128)(2,1)S(1)}, f32[1024,256]{1,0:T(8,128)S(1)}, bf16[1024,256]{1,0:T(8,128)(2,1)S(1)}) custom-call(s32[32]{0:T(128)S(1)} %copy-done.10, s32[32]{0:T(128)S(1)} %copy-done.15, s32[32]{0:T(128)S(1)} %copy-done.14, s32[64]{0:T(128)S(1)} %copy-done.12, s32[64]{0:T(128)S(1)} %copy-done.13, ...), custom_call_target="tpu_custom_call" | custom-call | flops 2684354560 | bytes 4194304 | tf_op jit(solution)/shard_map/pallas_call | solution.py:159
  75.8 2.0 %collective-permute-start.13 = (bf16[1024,256]{1,0:T(8,128)(2,1)S(1)}, bf16[1024,256]{1,0:T(8,128)(2,1)S(1)}, u32[]{:S(2)}, u32[]{:S(2)}) collective-permute-start(bf16[1024,256]{1,0:T(8,128)(2,1)S(1)} %get-tuple-element.406), channel_id=1, source_target_pairs={{0,1},{1,0},{2,3},{3,2},{4,5},{5,4},{6,7},{7,6},{8,9},{9,8},{10,11... | collective-permute-start | bytes 1572872 | tf_op jit(solution)/shard_map/ppermute | solution.py:272
  77.9 1.8 %collective-permute-done.13 = bf16[1024,256]{1,0:T(8,128)(2,1)S(1)} collective-permute-done((bf16[1024,256]{1,0:T(8,128)(2,1)S(1)}, bf16[1024,256]{1,0:T(8,128)(2,1)S(1)}, u32[]{:S(2)}, u32[]{:S(2)}) %collective-permute-start.13) | collective-permute-done | bytes 524320 | tf_op jit(solution)/shard_map/ppermute | solution.py:272
  79.6 1.0 add_convert_fusion
  80.6 13.3 %all-to-all-start.1 = ((bf16[16,64,256]{2,1,0:T(8,128)(2,1)}), bf16[16,64,256]{2,1,0:T(8,128)(2,1)S(1)}, u32[]{:S(2)}, u32[]{:S(2)}) async-start(bf16[16,64,256]{2,1,0:T(8,128)(2,1)} %bitcast.4), calls=%async_computation.1 | async-start | bytes 1048576 | tf_op jit(solution)/shard_map/all_to_all | solution.py:318
  93.9 1.9 %collective-permute-start.7 = (bf16[256,256]{1,0:T(8,128)(2,1)S(1)}, bf16[256,256]{1,0:T(8,128)(2,1)S(1)}, u32[]{:S(2)}, u32[]{:S(2)}) collective-permute-start(bf16[256,256]{1,0:T(8,128)(2,1)S(1)} %get-tuple-element.461), channel_id=1, source_target_pairs={{0,66},{1,385},{64,0},{65,449},{2,64},{3,387},{66,2},{67,451},{128... | collective-permute-start | bytes 393224 | tf_op jit(solution)/shard_map/ppermute | solution.py:264
  95.9 3.9 %collective-permute-start.9 = (bf16[256,256]{1,0:T(8,128)(2,1)S(1)}, bf16[256,256]{1,0:T(8,128)(2,1)S(1)}, u32[]{:S(2)}, u32[]{:S(2)}) collective-permute-start(bf16[256,256]{1,0:T(8,128)(2,1)S(1)} %get-tuple-element.462), channel_id=1, source_target_pairs={{0,64},{1,129},{64,2},{65,193},{2,66},{3,131},{66,0},{67,195},{128... | collective-permute-start | bytes 393224 | tf_op jit(solution)/shard_map/ppermute | solution.py:264
  99.8 3.1 %collective-permute-start.8 = (bf16[256,256]{1,0:T(8,128)(2,1)S(1)}, bf16[256,256]{1,0:T(8,128)(2,1)S(1)}, u32[]{:S(2)}, u32[]{:S(2)}) collective-permute-start(bf16[256,256]{1,0:T(8,128)(2,1)S(1)} %get-tuple-element.463), channel_id=1, source_target_pairs={{0,2},{1,257},{64,66},{65,321},{2,0},{3,259},{66,64},{67,323},{128... | collective-permute-start | bytes 393224 | tf_op jit(solution)/shard_map/ppermute | solution.py:264
  102.9 1.0 collective-permute-done.9
  103.9 4.2 %collective-permute-done.8 = bf16[256,256]{1,0:T(8,128)(2,1)S(1)} collective-permute-done((bf16[256,256]{1,0:T(8,128)(2,1)S(1)}, bf16[256,256]{1,0:T(8,128)(2,1)S(1)}, u32[]{:S(2)}, u32[]{:S(2)}) %collective-permute-start.8) | collective-permute-done | bytes 131104 | tf_op jit(solution)/shard_map/ppermute | solution.py:264
  108.3 2.2 %collective-permute-start.10 = (f32[64,256]{1,0:T(8,128)S(1)}, f32[64,256]{1,0:T(8,128)S(1)}, u32[]{:S(2)}, u32[]{:S(2)}) collective-permute-start(f32[64,256]{1,0:T(8,128)S(1)} %get-tuple-element.464), channel_id=1, source_target_pairs={{0,384},{1,67},{64,448},{65,1},{2,386},{3,65},{66,450},{67,3},{128... | collective-permute-start | bytes 196616 | tf_op jit(solution)/shard_map/ppermute | solution.py:264
  110.5 3.6 %collective-permute-start.12 = (f32[64,256]{1,0:T(8,128)S(1)}, f32[64,256]{1,0:T(8,128)S(1)}, u32[]{:S(2)}, u32[]{:S(2)}) collective-permute-start(f32[64,256]{1,0:T(8,128)S(1)} %get-tuple-element.465), channel_id=1, source_target_pairs={{0,128},{1,65},{64,192},{65,3},{2,130},{3,67},{66,194},{67,1},{128... | collective-permute-start | bytes 196616 | tf_op jit(solution)/shard_map/ppermute | solution.py:264
  114.1 3.7 %collective-permute-start.11 = (f32[64,256]{1,0:T(8,128)S(1)}, f32[64,256]{1,0:T(8,128)S(1)}, u32[]{:S(2)}, u32[]{:S(2)}) collective-permute-start(f32[64,256]{1,0:T(8,128)S(1)} %get-tuple-element.466), channel_id=1, source_target_pairs={{0,256},{1,3},{64,320},{65,67},{2,258},{3,1},{66,322},{67,65},{128... | collective-permute-start | bytes 196616 | tf_op jit(solution)/shard_map/ppermute | solution.py:264
  117.8 3.9 %collective-permute-done.11 = f32[64,256]{1,0:T(8,128)S(1)} collective-permute-done((f32[64,256]{1,0:T(8,128)S(1)}, f32[64,256]{1,0:T(8,128)S(1)}, u32[]{:S(2)}, u32[]{:S(2)}) %collective-permute-start.11) | collective-permute-done | bytes 65568 | tf_op jit(solution)/shard_map/ppermute | solution.py:264
  122.4 1.3 %all-to-all-done.1 = bf16[16,64,256]{2,1,0:T(8,128)(2,1)S(1)} async-done(((bf16[16,64,256]{2,1,0:T(8,128)(2,1)}), bf16[16,64,256]{2,1,0:T(8,128)(2,1)S(1)}, u32[]{:S(2)}, u32[]{:S(2)}) %all-to-all-start.1) | async-done | bytes 524320 | tf_op jit(solution)/shard_map/all_to_all | solution.py:318
  (85 shorter events, 12.9 us)
Async XLA Ops:
  2.2 57.1 %all-to-all-start = ((bf16[16,64,256]{2,1,0:T(8,128)(2,1)}), bf16[16,64,256]{2,1,0:T(8,128)(2,1)S(1)}, u32[]{:S(2)}, u32[]{:S(2)}) async-start(bf16[16,64,256]{2,1,0:T(8,128)(2,1)} %shard_map.94), calls=%async_computation | async-start | bytes 1048576 | tf_op jit(solution)/shard_map/all_to_all | solution.py:291
  17.4 0.7 copy-start.6
  24.2 0.8 copy-start
  24.2 0.8 copy-start.1
  24.2 0.8 copy-start.7
  24.2 0.8 copy-start.8
  25.6 12.8 %collective-permute-start.2 = (bf16[80,512]{1,0:T(8,128)(2,1)}, bf16[80,512]{1,0:T(8,128)(2,1)S(1)}, u32[]{:S(2)}, u32[]{:S(2)}) collective-permute-start(bf16[80,512]{1,0:T(8,128)(2,1)} %body.6), channel_id=1, source_target_pairs={{0,384},{1,67},{64,448},{65,1},{2,386},{3,65},{66,450},{67,3},{128... | collective-permute-start | bytes 245768 | tf_op jit(solution)/shard_map/while/body/ppermute | solution.py:264
  30.3 8.1 %collective-permute-start.1 = (bf16[80,512]{1,0:T(8,128)(2,1)}, bf16[80,512]{1,0:T(8,128)(2,1)S(1)}, u32[]{:S(2)}, u32[]{:S(2)}) collective-permute-start(bf16[80,512]{1,0:T(8,128)(2,1)} %body.6), channel_id=1, source_target_pairs={{0,256},{1,3},{64,320},{65,67},{2,258},{3,1},{66,322},{67,65},{128... | collective-permute-start | bytes 245768 | tf_op jit(solution)/shard_map/while/body/ppermute | solution.py:264
  33.0 7.8 %collective-permute-start = (bf16[80,512]{1,0:T(8,128)(2,1)}, bf16[80,512]{1,0:T(8,128)(2,1)S(1)}, u32[]{:S(2)}, u32[]{:S(2)}) collective-permute-start(bf16[80,512]{1,0:T(8,128)(2,1)} %body.6), channel_id=1, source_target_pairs={{0,128},{1,65},{64,192},{65,3},{2,130},{3,67},{66,194},{67,1},{128... | collective-permute-start | bytes 245768 | tf_op jit(solution)/shard_map/while/body/ppermute | solution.py:264
  38.4 12.8 %copy-start.9 = (s32[32]{0:T(128)}, s32[32]{0:T(128)S(1)}, u32[]{:S(2)}) copy-start(s32[32]{0:T(128)S(1)} %convert_reduce_fusion.5) | copy-start | bytes 388 | tf_op jit(solution)/shard_map/while
  40.8 17.9 %copy-start.5 = (bf16[272,512]{1,0:T(8,128)(2,1)}, bf16[272,512]{1,0:T(8,128)(2,1)S(1)}, u32[]{:S(2)}) copy-start(bf16[272,512]{1,0:T(8,128)(2,1)S(1)} %maximum_dynamic-update-slice_fusion.2) | copy-start | bytes 835588 | tf_op jit(solution)/shard_map/while
  40.8 11.8 %collective-permute-start.5 = (bf16[272,512]{1,0:T(8,128)(2,1)S(1)}, bf16[272,512]{1,0:T(8,128)(2,1)S(1)}, u32[]{:S(2)}, u32[]{:S(2)}) collective-permute-start(bf16[272,512]{1,0:T(8,128)(2,1)S(1)} %maximum_dynamic-update-slice_fusion.2), channel_id=1, source_target_pairs={{0,66},{1,385},{64,0},{65,449},{2,64},{3,387},{66,2},{67,451},{128... | collective-permute-start | bytes 835592 | tf_op jit(solution)/shard_map/while/body/ppermute | solution.py:264
  45.7 10.0 %collective-permute-start.4 = (bf16[272,512]{1,0:T(8,128)(2,1)S(1)}, bf16[272,512]{1,0:T(8,128)(2,1)S(1)}, u32[]{:S(2)}, u32[]{:S(2)}) collective-permute-start(bf16[272,512]{1,0:T(8,128)(2,1)S(1)} %maximum_dynamic-update-slice_fusion.2), channel_id=1, source_target_pairs={{0,2},{1,257},{64,66},{65,321},{2,0},{3,259},{66,64},{67,323},{128... | collective-permute-start | bytes 835592 | tf_op jit(solution)/shard_map/while/body/ppermute | solution.py:264
  48.3 10.4 %collective-permute-start.3 = (bf16[272,512]{1,0:T(8,128)(2,1)S(1)}, bf16[272,512]{1,0:T(8,128)(2,1)S(1)}, u32[]{:S(2)}, u32[]{:S(2)}) collective-permute-start(bf16[272,512]{1,0:T(8,128)(2,1)S(1)} %maximum_dynamic-update-slice_fusion.2), channel_id=1, source_target_pairs={{0,64},{1,129},{64,2},{65,193},{2,66},{3,131},{66,0},{67,195},{128... | collective-permute-start | bytes 835592 | tf_op jit(solution)/shard_map/while/body/ppermute | solution.py:264
  52.0 0.6 copy-start.11
  52.6 6.0 %copy-start.2 = (bf16[272,512]{1,0:T(8,128)(2,1)}, bf16[272,512]{1,0:T(8,128)(2,1)S(1)}, u32[]{:S(2)}) copy-start(bf16[272,512]{1,0:T(8,128)(2,1)S(1)} %collective-permute-done.5) | copy-start | bytes 835588 | tf_op jit(solution)/shard_map/while
  55.7 2.9 %copy-start.3 = (bf16[272,512]{1,0:T(8,128)(2,1)}, bf16[272,512]{1,0:T(8,128)(2,1)S(1)}, u32[]{:S(2)}) copy-start(bf16[272,512]{1,0:T(8,128)(2,1)S(1)} %collective-permute-done.4) | copy-start | bytes 835588 | tf_op jit(solution)/shard_map/while
  58.7 0.7 copy-start.4
  59.4 2.1 %copy-start.14 = (s32[32]{0:T(128)S(1)}, s32[32]{0:T(128)}, u32[]{:S(2)}) copy-start(s32[32]{0:T(128)} %get-tuple-element.391.sorted_q) | copy-start | bytes 388
  59.4 3.9 %collective-permute-start.6 = (bf16[1024,256]{1,0:T(8,128)(2,1)S(1)}, bf16[1024,256]{1,0:T(8,128)(2,1)S(1)}, u32[]{:S(2)}, u32[]{:S(2)}) collective-permute-start(bf16[1024,256]{1,0:T(8,128)(2,1)S(1)} %bitcast.9), channel_id=1, source_target_pairs={{0,1},{1,0},{2,3},{3,2},{4,5},{5,4},{6,7},{7,6},{8,9},{9,8},{10,11... | collective-permute-start | bytes 1572872 | tf_op jit(solution)/shard_map/ppermute | solution.py:272
  63.3 0.7 copy-start.15
  63.3 0.7 copy-start.10
  63.3 0.7 copy-start.12
  63.3 0.7 copy-start.13
  75.8 3.8 %collective-permute-start.13 = (bf16[1024,256]{1,0:T(8,128)(2,1)S(1)}, bf16[1024,256]{1,0:T(8,128)(2,1)S(1)}, u32[]{:S(2)}, u32[]{:S(2)}) collective-permute-start(bf16[1024,256]{1,0:T(8,128)(2,1)S(1)} %get-tuple-element.406), channel_id=1, source_target_pairs={{0,1},{1,0},{2,3},{3,2},{4,5},{5,4},{6,7},{7,6},{8,9},{9,8},{10,11... | collective-permute-start | bytes 1572872 | tf_op jit(solution)/shard_map/ppermute | solution.py:272
  80.6 43.1 %all-to-all-start.1 = ((bf16[16,64,256]{2,1,0:T(8,128)(2,1)}), bf16[16,64,256]{2,1,0:T(8,128)(2,1)S(1)}, u32[]{:S(2)}, u32[]{:S(2)}) async-start(bf16[16,64,256]{2,1,0:T(8,128)(2,1)} %bitcast.4), calls=%async_computation.1 | async-start | bytes 1048576 | tf_op jit(solution)/shard_map/all_to_all | solution.py:318
  93.9 9.0 %collective-permute-start.7 = (bf16[256,256]{1,0:T(8,128)(2,1)S(1)}, bf16[256,256]{1,0:T(8,128)(2,1)S(1)}, u32[]{:S(2)}, u32[]{:S(2)}) collective-permute-start(bf16[256,256]{1,0:T(8,128)(2,1)S(1)} %get-tuple-element.461), channel_id=1, source_target_pairs={{0,66},{1,385},{64,0},{65,449},{2,64},{3,387},{66,2},{67,451},{128... | collective-permute-start | bytes 393224 | tf_op jit(solution)/shard_map/ppermute | solution.py:264
  95.9 8.1 %collective-permute-start.9 = (bf16[256,256]{1,0:T(8,128)(2,1)S(1)}, bf16[256,256]{1,0:T(8,128)(2,1)S(1)}, u32[]{:S(2)}, u32[]{:S(2)}) collective-permute-start(bf16[256,256]{1,0:T(8,128)(2,1)S(1)} %get-tuple-element.462), channel_id=1, source_target_pairs={{0,64},{1,129},{64,2},{65,193},{2,66},{3,131},{66,0},{67,195},{128... | collective-permute-start | bytes 393224 | tf_op jit(solution)/shard_map/ppermute | solution.py:264
  99.8 8.4 %collective-permute-start.8 = (bf16[256,256]{1,0:T(8,128)(2,1)S(1)}, bf16[256,256]{1,0:T(8,128)(2,1)S(1)}, u32[]{:S(2)}, u32[]{:S(2)}) collective-permute-start(bf16[256,256]{1,0:T(8,128)(2,1)S(1)} %get-tuple-element.463), channel_id=1, source_target_pairs={{0,2},{1,257},{64,66},{65,321},{2,0},{3,259},{66,64},{67,323},{128... | collective-permute-start | bytes 393224 | tf_op jit(solution)/shard_map/ppermute | solution.py:264
  108.3 9.5 %collective-permute-start.10 = (f32[64,256]{1,0:T(8,128)S(1)}, f32[64,256]{1,0:T(8,128)S(1)}, u32[]{:S(2)}, u32[]{:S(2)}) collective-permute-start(f32[64,256]{1,0:T(8,128)S(1)} %get-tuple-element.464), channel_id=1, source_target_pairs={{0,384},{1,67},{64,448},{65,1},{2,386},{3,65},{66,450},{67,3},{128... | collective-permute-start | bytes 196616 | tf_op jit(solution)/shard_map/ppermute | solution.py:264
  110.5 7.4 %collective-permute-start.12 = (f32[64,256]{1,0:T(8,128)S(1)}, f32[64,256]{1,0:T(8,128)S(1)}, u32[]{:S(2)}, u32[]{:S(2)}) collective-permute-start(f32[64,256]{1,0:T(8,128)S(1)} %get-tuple-element.465), channel_id=1, source_target_pairs={{0,128},{1,65},{64,192},{65,3},{2,130},{3,67},{66,194},{67,1},{128... | collective-permute-start | bytes 196616 | tf_op jit(solution)/shard_map/ppermute | solution.py:264
  114.1 7.7 %collective-permute-start.11 = (f32[64,256]{1,0:T(8,128)S(1)}, f32[64,256]{1,0:T(8,128)S(1)}, u32[]{:S(2)}, u32[]{:S(2)}) collective-permute-start(f32[64,256]{1,0:T(8,128)S(1)} %get-tuple-element.466), channel_id=1, source_target_pairs={{0,256},{1,3},{64,320},{65,67},{2,258},{3,1},{66,322},{67,65},{128... | collective-permute-start | bytes 196616 | tf_op jit(solution)/shard_map/ppermute | solution.py:264

commit v7 on v6

--- a/solution.py
+++ b/solution.py
@@ -14,7 +14,7 @@
 STATS = 16
 QT = 256
 KT = 256
-TOGETHER = 4
+TOGETHER = 2
 VMEM = pl.BlockSpec(memory_space=pltpu.VMEM)
 SMEM = pl.BlockSpec(memory_space=pltpu.SMEM)
 
@@ -28,46 +28,43 @@
 
 
 def tile_kernel(rank_q, order_q, sorted_q, rank_k, sorted_k, *refs):
-    q_refs = refs[:4]
-    kv_refs = refs[4:6]
-    posq_ref, near_ref, far_ref, own_ref, sib_ref = refs[6:11]
-    qs, gs, rows, ks, vs, kt, dqt, dk, dv, todo = refs[11:]
+    q_refs = refs[:2]
+    kv_ref, posq_ref, own_ref, sib_ref, dkv_ref = refs[2:7]
+    qs, gs, stats, rows, ks, vs, kt, dqt, dqn, dk, dv, todo = refs[7:]
     n_q = qs.shape[0]
     n_k = ks.shape[0]
     per_q = QT // HALF
     per_k = KT // HALF
-    part_q = (q_refs[0].shape[0] - STATS) // HALF
-    part_k = kv_refs[0].shape[0] // HALF
-
-    for a in range(4):
-        for b in range(part_q):
-            place = rank_q[a * part_q + b]
-            j = place // per_q
-            r = pl.multiple_of(place % per_q * HALF, HALF)
-            cut = slice(b * HALF, (b + 1) * HALF)
-            for h in range(HEADS):
-                qs[j, pl.ds(h * QT + r, HALF), :] = q_refs[a][cut, h * HD:(h + 1) * HD]
-                gs[j, pl.ds(h * QT + r, HALF), :] = q_refs[a][cut, (HEADS + h) * HD:(HEADS + h + 1) * HD]
+    lines = q_refs[0].shape[0]
+    part_q = (q_refs[0].shape[1] - STATS) // HALF
+    part_k = kv_ref.shape[0] // HALF
+
     for a in range(2):
-        for b in range(part_k):
-            place = rank_k[a * part_k + b]
-            i = place // per_k
-            r = pl.multiple_of(place % per_k * HALF, HALF)
-            cut = slice(b * HALF, (b + 1) * HALF)
-            ks[i, pl.ds(r, HALF), :] = kv_refs[a][cut, :HD]
-            vs[i, pl.ds(r, HALF), :] = kv_refs[a][cut, HD:]
-
-    stat_refs = rows.at[pl.ds(n_q, 4)]
-    base = q_refs[0].shape[0] - STATS
-    for a in range(4):
-        stat_refs[a] = q_refs[a][base:, :].astype(jnp.float32)
+        for n in range(lines):
+            for b in range(part_q):
+                place = rank_q[(a * lines + n) * part_q + b]
+                j = place // per_q
+                r = pl.multiple_of(place % per_q * HALF, HALF)
+                cut = slice(b * HALF, (b + 1) * HALF)
+                for h in range(HEADS):
+                    qs[j, pl.ds(h * QT + r, HALF), :] = q_refs[a][n, cut, h * HD:(h + 1) * HD]
+                    gs[j, pl.ds(h * QT + r, HALF), :] = q_refs[a][n, cut, (HEADS + h) * HD:(HEADS + h + 1) * HD]
+            stats[a * lines + n] = q_refs[a][n, part_q * HALF:, :].astype(jnp.float32)
+    for b in range(part_k):
+        place = rank_k[b]
+        i = place // per_k
+        r = pl.multiple_of(place % per_k * HALF, HALF)
+        cut = slice(b * HALF, (b + 1) * HALF)
+        ks[i, pl.ds(r, HALF), :] = kv_ref[cut, :HD]
+        vs[i, pl.ds(r, HALF), :] = kv_ref[cut, HD:]
+
     quarter = lax.broadcasted_iota(jnp.int32, (STATS, 128), 1) // HALF
     for t in range(n_q * QT // 128):
         line = jnp.zeros((STATS, 128), jnp.float32)
         for u in range(4):
             b = order_q[t * 4 + u]
             column = pl.multiple_of(b % part_q // 2 * 128, 128)
-            piece = rows[n_q + b // part_q, :, pl.ds(column, 128)]
+            piece = stats[b // part_q, :, pl.ds(column, 128)]
             piece = pltpu.roll(piece, (u - b % 2 + 4) % 4 * HALF, 1)
             line = jnp.where(quarter == u, piece, line)
         j, c = t // (QT // 128), t % (QT // 128)
@@ -122,34 +119,29 @@
 
     for j in range(n_q):
         for h in range(HEADS):
-            back = dqt[j, :, h * QT:(h + 1) * QT].T
-            half = back.astype(jnp.bfloat16)
-            for b in range(per_q):
-                to = order_q[j * per_q + b]
-                cut = slice(b * HALF, (b + 1) * HALF)
-                lane = slice(h * HD, (h + 1) * HD)
-                dst = pl.multiple_of(to * HALF, HALF)
-                far_ref[pl.ds(dst, HALF), lane] = half[cut]
-
-                @pl.when(to < part_q)
-                def _():
-                    near_ref[pl.ds(dst, HALF), lane] = back[cut]
-    for a in range(2):
-        for b in range(part_k):
-            place = rank_k[a * part_k + b]
-            i = place // per_k
-            r = pl.multiple_of(place % per_k * HALF, HALF)
+            cut = slice(h * QT, (h + 1) * QT)
+            dqn[j, cut, :] = dqt[j, :, cut].T
+    for a, out in enumerate((own_ref, sib_ref)):
+        for b in range(lines * part_q):
+            place = rank_q[a * lines * part_q + b]
+            j = place // per_q
+            r = pl.multiple_of(place % per_q * HALF, HALF)
             cut = slice(b * HALF, (b + 1) * HALF)
-            out = own_ref if a == 0 else sib_ref
-            out[cut, :HD] = dk[i, pl.ds(r, HALF), :].astype(out.dtype)
-            out[cut, HD:] = dv[i, pl.ds(r, HALF), :].astype(out.dtype)
-
-
-def tile_grads(q_parts, kv_parts, lists_q, lists_k):
-    part = q_parts[0].shape[0] - STATS
-    rows_q = 4 * part
-    part_k = kv_parts[0].shape[0]
-    rows_k = 2 * part_k
+            for h in range(HEADS):
+                out[cut, h * HD:(h + 1) * HD] = dqn[j, pl.ds(h * QT + r, HALF), :]
+    for b in range(part_k):
+        place = rank_k[b]
+        i = place // per_k
+        r = pl.multiple_of(place % per_k * HALF, HALF)
+        cut = slice(b * HALF, (b + 1) * HALF)
+        dkv_ref[cut, :HD] = dk[i, pl.ds(r, HALF), :].astype(jnp.bfloat16)
+        dkv_ref[cut, HD:] = dv[i, pl.ds(r, HALF), :].astype(jnp.bfloat16)
+
+
+def tile_grads(q_parts, kv, lists_q, lists_k):
+    lines, part = q_parts[0].shape[:2]
+    rows_q = 2 * lines * (part - STATS)
+    rows_k = kv.shape[0]
     n_q, n_k = rows_q // QT, rows_k // KT
     rank_q, order_q, sorted_q = lists_q
     rank_k, _, sorted_k = lists_k
@@ -159,21 +151,22 @@
     return pl.pallas_call(
         tile_kernel,
         out_shape=(
-            jax.ShapeDtypeStruct((part, HEADS * HD), f32),
-            jax.ShapeDtypeStruct((rows_q, HEADS * HD), bf),
-            jax.ShapeDtypeStruct((part_k, 2 * HD), f32),
-            jax.ShapeDtypeStruct((part_k, 2 * HD), bf),
+            jax.ShapeDtypeStruct((rows_q // 2, HEADS * HD), f32),
+            jax.ShapeDtypeStruct((rows_q // 2, HEADS * HD), f32),
+            jax.ShapeDtypeStruct((rows_k, 2 * HD), bf),
         ),
-        in_specs=[SMEM] * 5 + [VMEM] * 7,
-        out_specs=(VMEM,) * 4,
+        in_specs=[SMEM] * 5 + [VMEM] * 4,
+        out_specs=(VMEM,) * 3,
         scratch_shapes=[
             pltpu.VMEM((n_q, HEADS * QT, HD), bf),
             pltpu.VMEM((n_q, HEADS * QT, HD), bf),
-            pltpu.VMEM((n_q + 4, STATS, HEADS * QT), f32),
+            pltpu.VMEM((2 * lines, STATS, 512), f32),
+            pltpu.VMEM((n_q, 8, HEADS * QT), f32),
             pltpu.VMEM((n_k, KT, HD), bf),
             pltpu.VMEM((n_k, KT, HD), bf),
             pltpu.VMEM((n_k, HD, KT), bf),
             pltpu.VMEM((n_q, HD, HEADS * QT), f32),
+            pltpu.VMEM((n_q, HEADS * QT, HD), f32),
             pltpu.VMEM((n_k, KT, HD), f32),
             pltpu.VMEM((n_k, KT, HD), f32),
             pltpu.SMEM((n_q * n_k + TOGETHER,), jnp.int32),
@@ -184,7 +177,7 @@
             bytes_accessed=4 * 1024 * 1024,
             transcendentals=rows_q * HEADS * rows_k // 2,
         ),
-    )(rank_q, order_q, sorted_q, rank_k, sorted_k, *q_parts, *kv_parts, posq)
+    )(rank_q, order_q, sorted_q, rank_k, sorted_k, *q_parts, kv, posq)
 
 
 def in_order(entries):
@@ -288,34 +281,28 @@
     ix, iyl, iz, iyh, ic = (lax.axis_index(a) for a in ("x", "yl", "z", "yh", "core"))
     iy = iyh * nyl + iyl
 
-    kv_own = lax.all_to_all(pack_kv(keys, values, nz), "z", split_axis=0, concat_axis=0, tiled=True)
-    kv_own = kv_own.reshape(nz * rows, 2 * HD)
-
-    def gather_q(turn, carried):
-        packed = pack_q(queries, out_grad, log_sum, delta)
-        line = join([packed] + [from_offset(packed, 0, d) for d in (1, 2, 3)])
-        q_parts = [line] + [from_offset(line, 1, d) for d in (1, 2, 3)]
-        table = block_table + jnp.minimum(turn, 0)
-        spot = jnp.arange(16, dtype=jnp.int32)
-        inner, outer = spot % 4, spot // 4
-        x = (ix - jnp.where(ic == 0, inner, outer)) % nx
-        y = (iy - jnp.where(ic == 0, outer, inner)) % (nyl * nyh)
-        at = ((x * nyl + y % nyl) * nz + iz) * nyh * nc + y // nyl * nc + ic
-        lists_q = in_order(look_up(table, both_blocks(at)))
-        both = [((spot * nyh + iyh) * nc + c) * nx * nyl + ix * nyl + iyl for c in (ic, nc - 1 - ic)]
-        lists_k = in_order(look_up(table, both_blocks(jnp.concatenate(both))))
-        return q_parts, lists_q, lists_k
-
-    empty = jax.tree.map(lambda x: jnp.zeros(x.shape, x.dtype), jax.eval_shape(lambda: gather_q(0, None)))
-    turns = 1 + jnp.minimum(block_table[0], 0)
-    q_parts, lists_q, lists_k = lax.fori_loop(0, turns, gather_q, empty)
-    kv_own, q_parts = lax.optimization_barrier((kv_own, q_parts))
-    kv_sib = other_core(kv_own)
-
-    near, far, dkv_own, dkv_sib = tile_grads(q_parts, [kv_own, kv_sib], lists_q, lists_k)
-
-    dkv = (dkv_own + other_core(dkv_sib).astype(jnp.float32)).astype(jnp.bfloat16)
+    kv = lax.all_to_all(pack_kv(keys, values, nz), "z", split_axis=0, concat_axis=0, tiled=True)
+    kv = kv.reshape(nz * rows, 2 * HD)
+    packed = pack_q(queries, out_grad, log_sum, delta)
+    line = join([packed] + [from_offset(packed, 0, d) for d in (1, 2, 3)])
+    q_own = jnp.stack([line] + [from_offset(line, 1, d) for d in (1, 2, 3)])
+    table, q_own = lax.optimization_barrier((block_table, q_own))
+    q_sib = other_core(q_own)
+
+    spot = jnp.arange(nz, dtype=jnp.int32)
+    lists_k = in_order(look_up(table, both_blocks(((spot * nyh + iyh) * nc + ic) * nx * nyl + ix * nyl + iyl)))
+    at = []
+    for c in (ic, nc - 1 - ic):
+        along_x, along_y = jnp.where(c == 0, spot % 4, spot // 4), jnp.where(c == 0, spot // 4, spot % 4)
+        x, y = (ix - along_x) % nx, (iy - along_y) % (nyl * nyh)
+        at.append(((x * nyl + y % nyl) * nz + iz) * nyh * nc + y // nyl * nc + c)
+    lists_q = in_order(look_up(table, both_blocks(jnp.concatenate(at))))
+
+    dq, dq_sib, dkv = tile_grads([q_own, q_sib], kv, lists_q, lists_k)
+
     dkv = lax.all_to_all(dkv.reshape(nz, rows, 2 * HD), "z", split_axis=0, concat_axis=0, tiled=True)
+    dq = dq + other_core(dq_sib)
+    near, far = dq[:4 * rows], dq.astype(jnp.bfloat16)
     far = far.reshape(4, 4 * rows, width)
     for d in (1, 2, 3):
         near = near + from_offset(far[d], 1, 4 - d).astype(jnp.float32)

time: 126 us -> 113 us (0.90)
  the two profiles are of different devices: /device:TPU:32 before, /device:TPU:24 now
where the time goes in v7:
time: 113 us; the launch traced here: 112 us
  starting transfers between devices  66.7 us (59%)
  waiting for transfers between devices  22.1 us (20%)
  Pallas kernels  17.7 us (16%)
  other arithmetic  3 us (3%)
  local copies, waits for them, and re-layouts  1.22 us (1%)
    ppermute x12, starting transfers between devices, from_offset(): return lax.ppermute(x, ('x', 'yl', 'yh', 'core'), pairs)  40.7 us
    all_to_all x1, starting transfers between devices, local(): lax.all_to_all(pack_kv(keys, values, nz), 'z', split_axis=0, concat_axis=...  15.2 us
    pallas_call x1, Pallas kernels, tile_grads(): pl.pallas_call(tile_kernel, out_shape=(jax.ShapeDtypeStruct((rows_q // 2,...  14.6 us
    ppermute x12, waiting for transfers between devices, from_offset(): return lax.ppermute(x, ('x', 'yl', 'yh', 'core'), pairs)  14.2 us
    all_to_all x1, starting transfers between devices, local(): lax.all_to_all(dkv.reshape(nz, rows, 2 * HD), 'z', split_axis=0, concat_a...  6.98 us
    all_to_all x1, waiting for transfers between devices, local(): lax.all_to_all(pack_kv(keys, values, nz), 'z', split_axis=0, concat_axis=...  6.35 us
    ppermute x2, starting transfers between devices, other_core(): return lax.ppermute(x, 'core', [(0, 1), (1, 0)])  3.83 us
  transfers between devices with their start and end apart: 16, of which 7 were waited for; matrix products, arithmetic and copies ran while one was open for 3% of the time, Pallas kernels for 1%

profile of v7, /device:TPU:24, one launch (start us, length us, event | category | flops | bytes accessed | tf_op | source)
XLA Modules:
  0.0 111.7 jit_solution(11415418675587181365)
XLA Ops:
  0.6 1.4 %shard_map.94 = bf16[80,512]{1,0:T(8,128)(2,1)} custom-call(bf16[64,256]{1,0:T(8,128)(2,1)} %q_ref.1, bf16[64,256]{1,0:T(8,128)(2,1)} %g_ref.1, f32[2,64]{1,0:T(2,128)} %bitcast.13, f32[2,64]{1,0:T(2,128)} %bitcast.14), custom_call_target="tpu_custom_call" | custom-call | tf_op jit(solution)/shard_map/pallas_call | solution.py:235
  2.1 4.8 %collective-permute-start.2 = (bf16[80,512]{1,0:T(8,128)(2,1)}, bf16[80,512]{1,0:T(8,128)(2,1)S(1)}, u32[]{:S(2)}, u32[]{:S(2)}) collective-permute-start(bf16[80,512]{1,0:T(8,128)(2,1)} %shard_map.94), channel_id=1, source_target_pairs={{0,384},{1,67},{64,448},{65,1},{2,386},{3,65},{66,450},{67,3},{128... | collective-permute-start | bytes 245768 | tf_op jit(solution)/shard_map/ppermute | solution.py:257
  6.8 2.7 %collective-permute-start.1 = (bf16[80,512]{1,0:T(8,128)(2,1)}, bf16[80,512]{1,0:T(8,128)(2,1)S(1)}, u32[]{:S(2)}, u32[]{:S(2)}) collective-permute-start(bf16[80,512]{1,0:T(8,128)(2,1)} %shard_map.94), channel_id=1, source_target_pairs={{0,256},{1,3},{64,320},{65,67},{2,258},{3,1},{66,322},{67,65},{128... | collective-permute-start | bytes 245768 | tf_op jit(solution)/shard_map/ppermute | solution.py:257
  9.6 2.8 %collective-permute-start = (bf16[80,512]{1,0:T(8,128)(2,1)}, bf16[80,512]{1,0:T(8,128)(2,1)S(1)}, u32[]{:S(2)}, u32[]{:S(2)}) collective-permute-start(bf16[80,512]{1,0:T(8,128)(2,1)} %shard_map.94), channel_id=1, source_target_pairs={{0,128},{1,65},{64,192},{65,3},{2,130},{3,67},{66,194},{67,1},{128... | collective-permute-start | bytes 245768 | tf_op jit(solution)/shard_map/ppermute | solution.py:257
  12.4 1.6 %shard_map.95 = bf16[16,64,256]{2,1,0:T(8,128)(2,1)} custom-call(bf16[64,128]{1,0:T(8,128)(2,1)} %k_ref.1, bf16[64,128]{1,0:T(8,128)(2,1)} %v_ref.1), custom_call_target="tpu_custom_call" | custom-call | tf_op jit(solution)/shard_map/pallas_call | solution.py:204
  14.0 15.2 %all-to-all-start = ((bf16[16,64,256]{2,1,0:T(8,128)(2,1)}), bf16[16,64,256]{2,1,0:T(8,128)(2,1)S(1)}, u32[]{:S(2)}, u32[]{:S(2)}) async-start(bf16[16,64,256]{2,1,0:T(8,128)(2,1)} %shard_map.95), calls=%async_computation | async-start | bytes 1048576 | tf_op jit(solution)/shard_map/all_to_all | solution.py:284
  29.5 2.7 %collective-permute-start.5 = (bf16[272,512]{1,0:T(8,128)(2,1)S(1)}, bf16[272,512]{1,0:T(8,128)(2,1)S(1)}, u32[]{:S(2)}, u32[]{:S(2)}) collective-permute-start(bf16[272,512]{1,0:T(8,128)(2,1)S(1)} %maximum_dynamic-update-slice_fusion), channel_id=1, source_target_pairs={{0,66},{1,385},{64,0},{65,449},{2,64},{3,387},{66,2},{67,451},{128... | collective-permute-start | bytes 835592 | tf_op jit(solution)/shard_map/ppermute | solution.py:257
  32.1 2.8 %collective-permute-start.4 = (bf16[272,512]{1,0:T(8,128)(2,1)S(1)}, bf16[272,512]{1,0:T(8,128)(2,1)S(1)}, u32[]{:S(2)}, u32[]{:S(2)}) collective-permute-start(bf16[272,512]{1,0:T(8,128)(2,1)S(1)} %maximum_dynamic-update-slice_fusion), channel_id=1, source_target_pairs={{0,2},{1,257},{64,66},{65,321},{2,0},{3,259},{66,64},{67,323},{128... | collective-permute-start | bytes 835592 | tf_op jit(solution)/shard_map/ppermute | solution.py:257
  35.0 4.1 %collective-permute-start.3 = (bf16[272,512]{1,0:T(8,128)(2,1)S(1)}, bf16[272,512]{1,0:T(8,128)(2,1)S(1)}, u32[]{:S(2)}, u32[]{:S(2)}) collective-permute-start(bf16[272,512]{1,0:T(8,128)(2,1)S(1)} %maximum_dynamic-update-slice_fusion), channel_id=1, source_target_pairs={{0,64},{1,129},{64,2},{65,193},{2,66},{3,131},{66,0},{67,195},{128... | collective-permute-start | bytes 835592 | tf_op jit(solution)/shard_map/ppermute | solution.py:257
  39.5 2.6 %collective-permute-done.4 = bf16[272,512]{1,0:T(8,128)(2,1)S(1)} collective-permute-done((bf16[272,512]{1,0:T(8,128)(2,1)S(1)}, bf16[272,512]{1,0:T(8,128)(2,1)S(1)}, u32[]{:S(2)}, u32[]{:S(2)}) %collective-permute-start.4) | collective-permute-done | bytes 278560 | tf_op jit(solution)/shard_map/ppermute | solution.py:257
  42.1 2.8 %collective-permute-done.3 = bf16[272,512]{1,0:T(8,128)(2,1)S(1)} collective-permute-done((bf16[272,512]{1,0:T(8,128)(2,1)S(1)}, bf16[272,512]{1,0:T(8,128)(2,1)S(1)}, u32[]{:S(2)}, u32[]{:S(2)}) %collective-permute-start.3) | collective-permute-done | bytes 278560 | tf_op jit(solution)/shard_map/ppermute | solution.py:257
  45.0 1.9 %collective-permute-start.6 = (bf16[4,272,512]{2,1,0:T(8,128)(2,1)S(1)}, bf16[4,272,512]{2,1,0:T(8,128)(2,1)}, u32[]{:S(2)}, u32[]{:S(2)}) collective-permute-start(bf16[4,272,512]{2,1,0:T(8,128)(2,1)S(1)} %pad_maximum_fusion.refs_0_), channel_id=1, source_target_pairs={{0,1},{1,0},{2,3},{3,2},{4,5},{5,4},{6,7},{7,6},{8,9},{9,8},{10,11... | collective-permute-start | bytes 3342344 | tf_op jit(solution)/shard_map/ppermute | solution.py:265
  47.0 0.2 select_reduce_fusion
  47.8 0.2 select_reduce_fusion.1
  48.3 1.6 %collective-permute-done.6.refs_1_ = bf16[4,272,512]{2,1,0:T(8,128)(2,1)} collective-permute-done((bf16[4,272,512]{2,1,0:T(8,128)(2,1)S(1)}, bf16[4,272,512]{2,1,0:T(8,128)(2,1)}, u32[]{:S(2)}, u32[]{:S(2)}) %collective-permute-start.6) | collective-permute-done | bytes 1114144 | tf_op jit(solution)/shard_map/ppermute | solution.py:265
  49.8 6.4 %all-to-all-done = bf16[16,64,256]{2,1,0:T(8,128)(2,1)S(1)} async-done(((bf16[16,64,256]{2,1,0:T(8,128)(2,1)}), bf16[16,64,256]{2,1,0:T(8,128)(2,1)S(1)}, u32[]{:S(2)}, u32[]{:S(2)}) %all-to-all-start) | async-done | bytes 524320 | tf_op jit(solution)/shard_map/all_to_all | solution.py:284
  56.2 14.6 %shard_map.96 = (f32[1024,256]{1,0:T(8,128)S(1)}, f32[1024,256]{1,0:T(8,128)}, bf16[1024,256]{1,0:T(8,128)(2,1)}) custom-call(s32[64]{0:T(128)S(1)} %convert_reduce_fusion.1.rank_q, s32[64]{0:T(128)S(1)} %get-tuple-element.14.order_q, s32[64]{0:T(128)S(1)} %get-tuple-element.13.sorted_q, s32[32]{0:T(128)S(1)} %convert_reduce_fusion.2.rank_k, ...), custom_call_target="tpu_custom_call" | custom-call | flops 2684354560 | bytes 4194304 | tf_op jit(solution)/shard_map/pallas_call | solution.py:151
  70.8 1.9 %collective-permute-start.7 = (f32[1024,256]{1,0:T(8,128)}, f32[1024,256]{1,0:T(8,128)S(1)}, u32[]{:S(2)}, u32[]{:S(2)}) collective-permute-start(f32[1024,256]{1,0:T(8,128)} %get-tuple-element.11), channel_id=1, source_target_pairs={{0,1},{1,0},{2,3},{3,2},{4,5},{5,4},{6,7},{7,6},{8,9},{9,8},{10,11... | collective-permute-start | bytes 3145736 | tf_op jit(solution)/shard_map/ppermute | solution.py:265
  72.7 7.0 %all-to-all-start.1 = ((bf16[16,64,256]{2,1,0:T(8,128)(2,1)}), bf16[16,64,256]{2,1,0:T(8,128)(2,1)S(1)}, u32[]{:S(2)}, u32[]{:S(2)}) async-start(bf16[16,64,256]{2,1,0:T(8,128)(2,1)} %bitcast.7), calls=%async_computation.1 | async-start | bytes 1048576 | tf_op jit(solution)/shard_map/all_to_all | solution.py:303
  79.7 0.2 fusion.19
  80.0 2.4 %collective-permute-start.8 = (bf16[256,256]{1,0:T(8,128)(2,1)S(1)}, bf16[256,256]{1,0:T(8,128)(2,1)S(1)}, u32[]{:S(2)}, u32[]{:S(2)}) collective-permute-start(bf16[256,256]{1,0:T(8,128)(2,1)S(1)} %get-tuple-element.17), channel_id=1, source_target_pairs={{0,66},{1,385},{64,0},{65,449},{2,64},{3,387},{66,2},{67,451},{128... | collective-permute-start | bytes 393224 | tf_op jit(solution)/shard_map/ppermute | solution.py:257
  82.4 4.6 %collective-permute-start.10 = (bf16[256,256]{1,0:T(8,128)(2,1)S(1)}, bf16[256,256]{1,0:T(8,128)(2,1)S(1)}, u32[]{:S(2)}, u32[]{:S(2)}) collective-permute-start(bf16[256,256]{1,0:T(8,128)(2,1)S(1)} %get-tuple-element.18), channel_id=1, source_target_pairs={{0,64},{1,129},{64,2},{65,193},{2,66},{3,131},{66,0},{67,195},{128... | collective-permute-start | bytes 393224 | tf_op jit(solution)/shard_map/ppermute | solution.py:257
  87.0 3.0 %collective-permute-start.9 = (bf16[256,256]{1,0:T(8,128)(2,1)S(1)}, bf16[256,256]{1,0:T(8,128)(2,1)S(1)}, u32[]{:S(2)}, u32[]{:S(2)}) collective-permute-start(bf16[256,256]{1,0:T(8,128)(2,1)S(1)} %get-tuple-element.19), channel_id=1, source_target_pairs={{0,2},{1,257},{64,66},{65,321},{2,0},{3,259},{66,64},{67,323},{128... | collective-permute-start | bytes 393224 | tf_op jit(solution)/shard_map/ppermute | solution.py:257
  90.0 5.3 %collective-permute-done.9 = bf16[256,256]{1,0:T(8,128)(2,1)S(1)} collective-permute-done((bf16[256,256]{1,0:T(8,128)(2,1)S(1)}, bf16[256,256]{1,0:T(8,128)(2,1)S(1)}, u32[]{:S(2)}, u32[]{:S(2)}) %collective-permute-start.9) | collective-permute-done | bytes 131104 | tf_op jit(solution)/shard_map/ppermute | solution.py:257
  95.5 4.7 %collective-permute-start.11 = (f32[64,256]{1,0:T(8,128)S(1)}, f32[64,256]{1,0:T(8,128)S(1)}, u32[]{:S(2)}, u32[]{:S(2)}) collective-permute-start(f32[64,256]{1,0:T(8,128)S(1)} %get-tuple-element.20), channel_id=1, source_target_pairs={{0,384},{1,67},{64,448},{65,1},{2,386},{3,65},{66,450},{67,3},{128... | collective-permute-start | bytes 196616 | tf_op jit(solution)/shard_map/ppermute | solution.py:257
  100.2 1.9 %collective-permute-start.13 = (f32[64,256]{1,0:T(8,128)S(1)}, f32[64,256]{1,0:T(8,128)S(1)}, u32[]{:S(2)}, u32[]{:S(2)}) collective-permute-start(f32[64,256]{1,0:T(8,128)S(1)} %get-tuple-element.21), channel_id=1, source_target_pairs={{0,128},{1,65},{64,192},{65,3},{2,130},{3,67},{66,194},{67,1},{128... | collective-permute-start | bytes 196616 | tf_op jit(solution)/shard_map/ppermute | solution.py:257
  102.1 4.2 %collective-permute-start.12 = (f32[64,256]{1,0:T(8,128)S(1)}, f32[64,256]{1,0:T(8,128)S(1)}, u32[]{:S(2)}, u32[]{:S(2)}) collective-permute-start(f32[64,256]{1,0:T(8,128)S(1)} %get-tuple-element.22), channel_id=1, source_target_pairs={{0,256},{1,3},{64,320},{65,67},{2,258},{3,1},{66,322},{67,65},{128... | collective-permute-start | bytes 196616 | tf_op jit(solution)/shard_map/ppermute | solution.py:257
  106.3 1.2 %collective-permute-done.13 = f32[64,256]{1,0:T(8,128)S(1)} collective-permute-done((f32[64,256]{1,0:T(8,128)S(1)}, f32[64,256]{1,0:T(8,128)S(1)}, u32[]{:S(2)}, u32[]{:S(2)}) %collective-permute-start.13) | collective-permute-done | bytes 65568 | tf_op jit(solution)/shard_map/ppermute | solution.py:257
  107.5 2.2 %collective-permute-done.12 = f32[64,256]{1,0:T(8,128)S(1)} collective-permute-done((f32[64,256]{1,0:T(8,128)S(1)}, f32[64,256]{1,0:T(8,128)S(1)}, u32[]{:S(2)}, u32[]{:S(2)}) %collective-permute-start.12) | collective-permute-done | bytes 65568 | tf_op jit(solution)/shard_map/ppermute | solution.py:257
  109.8 0.6 fusion.5
  110.5 0.6 slice.120
  111.1 0.6 fusion.6
  (46 shorter events, 1.8 us)
Async XLA Ops:
  2.1 27.1 %copy-start = (bf16[80,512]{1,0:T(8,128)(2,1)S(1)}, bf16[80,512]{1,0:T(8,128)(2,1)}, u32[]{:S(2)}) copy-start(bf16[80,512]{1,0:T(8,128)(2,1)} %shard_map.94) | copy-start | bytes 245764
  2.1 27.3 %collective-permute-start.2 = (bf16[80,512]{1,0:T(8,128)(2,1)}, bf16[80,512]{1,0:T(8,128)(2,1)S(1)}, u32[]{:S(2)}, u32[]{:S(2)}) collective-permute-start(bf16[80,512]{1,0:T(8,128)(2,1)} %shard_map.94), channel_id=1, source_target_pairs={{0,384},{1,67},{64,448},{65,1},{2,386},{3,65},{66,450},{67,3},{128... | collective-permute-start | bytes 245768 | tf_op jit(solution)/shard_map/ppermute | solution.py:257
  6.8 22.5 %collective-permute-start.1 = (bf16[80,512]{1,0:T(8,128)(2,1)}, bf16[80,512]{1,0:T(8,128)(2,1)S(1)}, u32[]{:S(2)}, u32[]{:S(2)}) collective-permute-start(bf16[80,512]{1,0:T(8,128)(2,1)} %shard_map.94), channel_id=1, source_target_pairs={{0,256},{1,3},{64,320},{65,67},{2,258},{3,1},{66,322},{67,65},{128... | collective-permute-start | bytes 245768 | tf_op jit(solution)/shard_map/ppermute | solution.py:257
  9.6 19.8 %collective-permute-start = (bf16[80,512]{1,0:T(8,128)(2,1)}, bf16[80,512]{1,0:T(8,128)(2,1)S(1)}, u32[]{:S(2)}, u32[]{:S(2)}) collective-permute-start(bf16[80,512]{1,0:T(8,128)(2,1)} %shard_map.94), channel_id=1, source_target_pairs={{0,128},{1,65},{64,192},{65,3},{2,130},{3,67},{66,194},{67,1},{128... | collective-permute-start | bytes 245768 | tf_op jit(solution)/shard_map/ppermute | solution.py:257
  14.0 42.2 %all-to-all-start = ((bf16[16,64,256]{2,1,0:T(8,128)(2,1)}), bf16[16,64,256]{2,1,0:T(8,128)(2,1)S(1)}, u32[]{:S(2)}, u32[]{:S(2)}) async-start(bf16[16,64,256]{2,1,0:T(8,128)(2,1)} %shard_map.95), calls=%async_computation | async-start | bytes 1048576 | tf_op jit(solution)/shard_map/all_to_all | solution.py:284
  29.5 10.1 %collective-permute-start.5 = (bf16[272,512]{1,0:T(8,128)(2,1)S(1)}, bf16[272,512]{1,0:T(8,128)(2,1)S(1)}, u32[]{:S(2)}, u32[]{:S(2)}) collective-permute-start(bf16[272,512]{1,0:T(8,128)(2,1)S(1)} %maximum_dynamic-update-slice_fusion), channel_id=1, source_target_pairs={{0,66},{1,385},{64,0},{65,449},{2,64},{3,387},{66,2},{67,451},{128... | collective-permute-start | bytes 835592 | tf_op jit(solution)/shard_map/ppermute | solution.py:257
  32.1 10.0 %collective-permute-start.4 = (bf16[272,512]{1,0:T(8,128)(2,1)S(1)}, bf16[272,512]{1,0:T(8,128)(2,1)S(1)}, u32[]{:S(2)}, u32[]{:S(2)}) collective-permute-start(bf16[272,512]{1,0:T(8,128)(2,1)S(1)} %maximum_dynamic-update-slice_fusion), channel_id=1, source_target_pairs={{0,2},{1,257},{64,66},{65,321},{2,0},{3,259},{66,64},{67,323},{128... | collective-permute-start | bytes 835592 | tf_op jit(solution)/shard_map/ppermute | solution.py:257
  35.0 9.9 %collective-permute-start.3 = (bf16[272,512]{1,0:T(8,128)(2,1)S(1)}, bf16[272,512]{1,0:T(8,128)(2,1)S(1)}, u32[]{:S(2)}, u32[]{:S(2)}) collective-permute-start(bf16[272,512]{1,0:T(8,128)(2,1)S(1)} %maximum_dynamic-update-slice_fusion), channel_id=1, source_target_pairs={{0,64},{1,129},{64,2},{65,193},{2,66},{3,131},{66,0},{67,195},{128... | collective-permute-start | bytes 835592 | tf_op jit(solution)/shard_map/ppermute | solution.py:257
  44.9 2.1 %copy-start.1 = (s32[1024]{0:T(1024)S(1)}, s32[1024]{0:T(1024)}, u32[]{:S(2)}) copy-start(s32[1024]{0:T(1024)} %param.13) | copy-start | bytes 12292
  45.0 4.8 %collective-permute-start.6 = (bf16[4,272,512]{2,1,0:T(8,128)(2,1)S(1)}, bf16[4,272,512]{2,1,0:T(8,128)(2,1)}, u32[]{:S(2)}, u32[]{:S(2)}) collective-permute-start(bf16[4,272,512]{2,1,0:T(8,128)(2,1)S(1)} %pad_maximum_fusion.refs_0_), channel_id=1, source_target_pairs={{0,1},{1,0},{2,3},{3,2},{4,5},{5,4},{6,7},{7,6},{8,9},{9,8},{10,11... | collective-permute-start | bytes 3342344 | tf_op jit(solution)/shard_map/ppermute | solution.py:265
  70.8 8.9 %collective-permute-start.7 = (f32[1024,256]{1,0:T(8,128)}, f32[1024,256]{1,0:T(8,128)S(1)}, u32[]{:S(2)}, u32[]{:S(2)}) collective-permute-start(f32[1024,256]{1,0:T(8,128)} %get-tuple-element.11), channel_id=1, source_target_pairs={{0,1},{1,0},{2,3},{3,2},{4,5},{5,4},{6,7},{7,6},{8,9},{9,8},{10,11... | collective-permute-start | bytes 3145736 | tf_op jit(solution)/shard_map/ppermute | solution.py:265
  72.7 37.7 %all-to-all-start.1 = ((bf16[16,64,256]{2,1,0:T(8,128)(2,1)}), bf16[16,64,256]{2,1,0:T(8,128)(2,1)S(1)}, u32[]{:S(2)}, u32[]{:S(2)}) async-start(bf16[16,64,256]{2,1,0:T(8,128)(2,1)} %bitcast.7), calls=%async_computation.1 | async-start | bytes 1048576 | tf_op jit(solution)/shard_map/all_to_all | solution.py:303
  80.0 10.1 %collective-permute-start.8 = (bf16[256,256]{1,0:T(8,128)(2,1)S(1)}, bf16[256,256]{1,0:T(8,128)(2,1)S(1)}, u32[]{:S(2)}, u32[]{:S(2)}) collective-permute-start(bf16[256,256]{1,0:T(8,128)(2,1)S(1)} %get-tuple-element.17), channel_id=1, source_target_pairs={{0,66},{1,385},{64,0},{65,449},{2,64},{3,387},{66,2},{67,451},{128... | collective-permute-start | bytes 393224 | tf_op jit(solution)/shard_map/ppermute | solution.py:257
  82.4 7.6 %collective-permute-start.10 = (bf16[256,256]{1,0:T(8,128)(2,1)S(1)}, bf16[256,256]{1,0:T(8,128)(2,1)S(1)}, u32[]{:S(2)}, u32[]{:S(2)}) collective-permute-start(bf16[256,256]{1,0:T(8,128)(2,1)S(1)} %get-tuple-element.18), channel_id=1, source_target_pairs={{0,64},{1,129},{64,2},{65,193},{2,66},{3,131},{66,0},{67,195},{128... | collective-permute-start | bytes 393224 | tf_op jit(solution)/shard_map/ppermute | solution.py:257
  87.0 8.4 %collective-permute-start.9 = (bf16[256,256]{1,0:T(8,128)(2,1)S(1)}, bf16[256,256]{1,0:T(8,128)(2,1)S(1)}, u32[]{:S(2)}, u32[]{:S(2)}) collective-permute-start(bf16[256,256]{1,0:T(8,128)(2,1)S(1)} %get-tuple-element.19), channel_id=1, source_target_pairs={{0,2},{1,257},{64,66},{65,321},{2,0},{3,259},{66,64},{67,323},{128... | collective-permute-start | bytes 393224 | tf_op jit(solution)/shard_map/ppermute | solution.py:257
  95.5 10.8 %collective-permute-start.11 = (f32[64,256]{1,0:T(8,128)S(1)}, f32[64,256]{1,0:T(8,128)S(1)}, u32[]{:S(2)}, u32[]{:S(2)}) collective-permute-start(f32[64,256]{1,0:T(8,128)S(1)} %get-tuple-element.20), channel_id=1, source_target_pairs={{0,384},{1,67},{64,448},{65,1},{2,386},{3,65},{66,450},{67,3},{128... | collective-permute-start | bytes 196616 | tf_op jit(solution)/shard_map/ppermute | solution.py:257
  100.2 7.4 %collective-permute-start.13 = (f32[64,256]{1,0:T(8,128)S(1)}, f32[64,256]{1,0:T(8,128)S(1)}, u32[]{:S(2)}, u32[]{:S(2)}) collective-permute-start(f32[64,256]{1,0:T(8,128)S(1)} %get-tuple-element.21), channel_id=1, source_target_pairs={{0,128},{1,65},{64,192},{65,3},{2,130},{3,67},{66,194},{67,1},{128... | collective-permute-start | bytes 196616 | tf_op jit(solution)/shard_map/ppermute | solution.py:257
  102.1 7.7 %collective-permute-start.12 = (f32[64,256]{1,0:T(8,128)S(1)}, f32[64,256]{1,0:T(8,128)S(1)}, u32[]{:S(2)}, u32[]{:S(2)}) collective-permute-start(f32[64,256]{1,0:T(8,128)S(1)} %get-tuple-element.22), channel_id=1, source_target_pairs={{0,256},{1,3},{64,320},{65,67},{2,258},{3,1},{66,322},{67,65},{128... | collective-permute-start | bytes 196616 | tf_op jit(solution)/shard_map/ppermute | solution.py:257

commit v8 on v7

--- a/solution.py
+++ b/solution.py
@@ -14,7 +14,7 @@
 STATS = 16
 QT = 256
 KT = 256
-TOGETHER = 2
+TOGETHER = 4
 VMEM = pl.BlockSpec(memory_space=pltpu.VMEM)
 SMEM = pl.BlockSpec(memory_space=pltpu.SMEM)
 
@@ -194,21 +194,6 @@
     return (ordered[:, None] * HALF + jnp.arange(HALF, dtype=jnp.int32)[None, :]).reshape(-1)
 
 
-def pack_kv_kernel(k_ref, v_ref, out_ref):
-    for n in range(out_ref.shape[0]):
-        out_ref[n, :, :HD] = k_ref[...]
-        out_ref[n, :, HD:] = v_ref[...]
-
-
-def pack_kv(keys, values, copies):
-    return pl.pallas_call(
-        pack_kv_kernel,
-        out_shape=jax.ShapeDtypeStruct((copies, keys.shape[0], 2 * HD), keys.dtype),
-        in_specs=[VMEM] * 2,
-        out_specs=VMEM,
-    )(keys, values)
-
-
 def pack_q_kernel(q_ref, g_ref, lse_ref, delta_ref, out_ref, wide):
     width = HEADS * HD
     rows = q_ref.shape[0]
@@ -281,12 +266,13 @@
     ix, iyl, iz, iyh, ic = (lax.axis_index(a) for a in ("x", "yl", "z", "yh", "core"))
     iy = iyh * nyl + iyl
 
-    kv = lax.all_to_all(pack_kv(keys, values, nz), "z", split_axis=0, concat_axis=0, tiled=True)
+    kv = jnp.concatenate([keys, values], axis=1)
+    kv = lax.all_to_all(jnp.broadcast_to(kv[None], (nz,) + kv.shape), "z", split_axis=0, concat_axis=0, tiled=True)
     kv = kv.reshape(nz * rows, 2 * HD)
     packed = pack_q(queries, out_grad, log_sum, delta)
     line = join([packed] + [from_offset(packed, 0, d) for d in (1, 2, 3)])
     q_own = jnp.stack([line] + [from_offset(line, 1, d) for d in (1, 2, 3)])
-    table, q_own = lax.optimization_barrier((block_table, q_own))
+    table, q_own, kv = lax.optimization_barrier((block_table, q_own, kv))
     q_sib = other_core(q_own)
 
     spot = jnp.arange(nz, dtype=jnp.int32)

time: 113 us -> 116 us (1.027)
  starting transfers between devices: 66.7 us -> 70.1 us
  local copies, waits for them, and re-layouts: 1.22 us -> 3.55 us
  waiting for transfers between devices: 22.1 us -> 19.8 us
  Pallas kernels: 17.7 us -> 15.8 us
    all_to_all x1, waiting for transfers between devices: 6.35 us -> 0.01 us  [local(): lax.all_to_all(jnp.broadcast_to(kv[None], (nz,) + kv.shape), 'z', split_a...]
    all_to_all x1, starting transfers between devices: 6.98 us -> 12 us  [local(): lax.all_to_all(dkv.reshape(nz, rows, 2 * HD), 'z', split_axis=0, concat_a...]
    ppermute x12, waiting for transfers between devices: 14.2 us -> 18.3 us  [from_offset(): return lax.ppermute(x, ('x', 'yl', 'yh', 'core'), pairs)]
    ppermute x12, starting transfers between devices: 40.7 us -> 39 us  [from_offset(): return lax.ppermute(x, ('x', 'yl', 'yh', 'core'), pairs)]
    pallas_call x1 -> x0, Pallas kernels: 1.61 us -> none  [pack_kv(): pl.pallas_call(pack_kv_kernel, out_shape=jax.ShapeDtypeStruct((copies, ke...]
  transfers between devices with their start and end apart: 16 -> 16, of which waited for: 7 -> 7; matrix products, arithmetic and copies ran while one was open for 3% -> 4% of each run, Pallas kernels for 1% -> 1%
where the time goes in v8:
time: 116 us; the launch traced here: 114 us
  starting transfers between devices  70.1 us (60%)
  waiting for transfers between devices  19.8 us (17%)
  Pallas kernels  15.8 us (14%)
  other arithmetic  3.74 us (3%)
  local copies, waits for them, and re-layouts  3.55 us (3%)
    ppermute x12, starting transfers between devices, from_offset(): return lax.ppermute(x, ('x', 'yl', 'yh', 'core'), pairs)  39 us
    ppermute x12, waiting for transfers between devices, from_offset(): return lax.ppermute(x, ('x', 'yl', 'yh', 'core'), pairs)  18.3 us
    all_to_all x1, starting transfers between devices, local(): lax.all_to_all(jnp.broadcast_to(kv[None], (nz,) + kv.shape), 'z', split_a...  15.2 us
    pallas_call x1, Pallas kernels, tile_grads(): pl.pallas_call(tile_kernel, out_shape=(jax.ShapeDtypeStruct((rows_q // 2,...  14.4 us
    all_to_all x1, starting transfers between devices, local(): lax.all_to_all(dkv.reshape(nz, rows, 2 * HD), 'z', split_axis=0, concat_a...  12 us
    ppermute x2, starting transfers between devices, other_core(): return lax.ppermute(x, 'core', [(0, 1), (1, 0)])  3.83 us
  transfers between devices with their start and end apart: 16, of which 7 were waited for; matrix products, arithmetic and copies ran while one was open for 4% of the time, Pallas kernels for 1%

profile of v8, /device:TPU:24, one launch (start us, length us, event | category | flops | bytes accessed | tf_op | source)
XLA Modules:
  0.0 114.0 jit_solution(990898146684832775)
XLA Ops:
  0.6 0.7 pad_maximum_fusion.1
  1.4 0.8 broadcast_in_dim.48
  2.2 15.2 %all-to-all-start = ((bf16[16,64,256]{2,1,0:T(8,128)(2,1)}), bf16[16,64,256]{2,1,0:T(8,128)(2,1)S(1)}, u32[]{:S(2)}, u32[]{:S(2)}) async-start(bf16[16,64,256]{2,1,0:T(8,128)(2,1)} %broadcast_in_dim.48), calls=%async_computation | async-start | bytes 1048576 | tf_op jit(solution)/shard_map/all_to_all | solution.py:270
  17.4 1.4 %shard_map.94 = bf16[80,512]{1,0:T(8,128)(2,1)} custom-call(bf16[64,256]{1,0:T(8,128)(2,1)} %q_ref.1, bf16[64,256]{1,0:T(8,128)(2,1)} %g_ref.1, f32[2,64]{1,0:T(2,128)} %bitcast.13, f32[2,64]{1,0:T(2,128)} %bitcast.14), custom_call_target="tpu_custom_call" | custom-call | tf_op jit(solution)/shard_map/pallas_call | solution.py:220
  18.8 4.7 %collective-permute-start.2 = (bf16[80,512]{1,0:T(8,128)(2,1)}, bf16[80,512]{1,0:T(8,128)(2,1)S(1)}, u32[]{:S(2)}, u32[]{:S(2)}) collective-permute-start(bf16[80,512]{1,0:T(8,128)(2,1)} %shard_map.94), channel_id=1, source_target_pairs={{0,384},{1,67},{64,448},{65,1},{2,386},{3,65},{66,450},{67,3},{128... | collective-permute-start | bytes 245768 | tf_op jit(solution)/shard_map/ppermute | solution.py:242
  23.5 2.7 %collective-permute-start.1 = (bf16[80,512]{1,0:T(8,128)(2,1)}, bf16[80,512]{1,0:T(8,128)(2,1)S(1)}, u32[]{:S(2)}, u32[]{:S(2)}) collective-permute-start(bf16[80,512]{1,0:T(8,128)(2,1)} %shard_map.94), channel_id=1, source_target_pairs={{0,256},{1,3},{64,320},{65,67},{2,258},{3,1},{66,322},{67,65},{128... | collective-permute-start | bytes 245768 | tf_op jit(solution)/shard_map/ppermute | solution.py:242
  26.2 2.8 %collective-permute-start = (bf16[80,512]{1,0:T(8,128)(2,1)}, bf16[80,512]{1,0:T(8,128)(2,1)S(1)}, u32[]{:S(2)}, u32[]{:S(2)}) collective-permute-start(bf16[80,512]{1,0:T(8,128)(2,1)} %shard_map.94), channel_id=1, source_target_pairs={{0,128},{1,65},{64,192},{65,3},{2,130},{3,67},{66,194},{67,1},{128... | collective-permute-start | bytes 245768 | tf_op jit(solution)/shard_map/ppermute | solution.py:242
  29.0 0.7 slice.84
  29.8 0.8 slice_dynamic-update-slice_fusion.3
  30.7 0.9 collective-permute-done.1
  31.6 2.4 %collective-permute-done = bf16[80,512]{1,0:T(8,128)(2,1)S(1)} collective-permute-done((bf16[80,512]{1,0:T(8,128)(2,1)}, bf16[80,512]{1,0:T(8,128)(2,1)S(1)}, u32[]{:S(2)}, u32[]{:S(2)}) %collective-permute-start) | collective-permute-done | bytes 81952 | tf_op jit(solution)/shard_map/ppermute | solution.py:242
  34.0 2.7 %collective-permute-start.5 = (bf16[272,512]{1,0:T(8,128)(2,1)S(1)}, bf16[272,512]{1,0:T(8,128)(2,1)S(1)}, u32[]{:S(2)}, u32[]{:S(2)}) collective-permute-start(bf16[272,512]{1,0:T(8,128)(2,1)S(1)} %maximum_dynamic-update-slice_fusion), channel_id=1, source_target_pairs={{0,66},{1,385},{64,0},{65,449},{2,64},{3,387},{66,2},{67,451},{128... | collective-permute-start | bytes 835592 | tf_op jit(solution)/shard_map/ppermute | solution.py:242
  36.7 2.8 %collective-permute-start.4 = (bf16[272,512]{1,0:T(8,128)(2,1)S(1)}, bf16[272,512]{1,0:T(8,128)(2,1)S(1)}, u32[]{:S(2)}, u32[]{:S(2)}) collective-permute-start(bf16[272,512]{1,0:T(8,128)(2,1)S(1)} %maximum_dynamic-update-slice_fusion), channel_id=1, source_target_pairs={{0,2},{1,257},{64,66},{65,321},{2,0},{3,259},{66,64},{67,323},{128... | collective-permute-start | bytes 835592 | tf_op jit(solution)/shard_map/ppermute | solution.py:242
  39.5 4.1 %collective-permute-start.3 = (bf16[272,512]{1,0:T(8,128)(2,1)S(1)}, bf16[272,512]{1,0:T(8,128)(2,1)S(1)}, u32[]{:S(2)}, u32[]{:S(2)}) collective-permute-start(bf16[272,512]{1,0:T(8,128)(2,1)S(1)} %maximum_dynamic-update-slice_fusion), channel_id=1, source_target_pairs={{0,64},{1,129},{64,2},{65,193},{2,66},{3,131},{66,0},{67,195},{128... | collective-permute-start | bytes 835592 | tf_op jit(solution)/shard_map/ppermute | solution.py:242
  44.1 2.6 %collective-permute-done.4 = bf16[272,512]{1,0:T(8,128)(2,1)S(1)} collective-permute-done((bf16[272,512]{1,0:T(8,128)(2,1)S(1)}, bf16[272,512]{1,0:T(8,128)(2,1)S(1)}, u32[]{:S(2)}, u32[]{:S(2)}) %collective-permute-start.4) | collective-permute-done | bytes 278560 | tf_op jit(solution)/shard_map/ppermute | solution.py:242
  46.7 2.8 %collective-permute-done.3 = bf16[272,512]{1,0:T(8,128)(2,1)S(1)} collective-permute-done((bf16[272,512]{1,0:T(8,128)(2,1)S(1)}, bf16[272,512]{1,0:T(8,128)(2,1)S(1)}, u32[]{:S(2)}, u32[]{:S(2)}) %collective-permute-start.3) | collective-permute-done | bytes 278560 | tf_op jit(solution)/shard_map/ppermute | solution.py:242
  49.6 1.9 %collective-permute-start.6 = (bf16[4,272,512]{2,1,0:T(8,128)(2,1)S(1)}, bf16[4,272,512]{2,1,0:T(8,128)(2,1)}, u32[]{:S(2)}, u32[]{:S(2)}) collective-permute-start(bf16[4,272,512]{2,1,0:T(8,128)(2,1)S(1)} %pad_maximum_fusion.refs_0_), channel_id=1, source_target_pairs={{0,1},{1,0},{2,3},{3,2},{4,5},{5,4},{6,7},{7,6},{8,9},{9,8},{10,11... | collective-permute-start | bytes 3342344 | tf_op jit(solution)/shard_map/ppermute | solution.py:250
  52.8 1.6 %collective-permute-done.6.refs_1_ = bf16[4,272,512]{2,1,0:T(8,128)(2,1)} collective-permute-done((bf16[4,272,512]{2,1,0:T(8,128)(2,1)S(1)}, bf16[4,272,512]{2,1,0:T(8,128)(2,1)}, u32[]{:S(2)}, u32[]{:S(2)}) %collective-permute-start.6) | collective-permute-done | bytes 1114144 | tf_op jit(solution)/shard_map/ppermute | solution.py:250
  54.4 14.4 %shard_map.95 = (f32[1024,256]{1,0:T(8,128)S(1)}, f32[1024,256]{1,0:T(8,128)}, bf16[1024,256]{1,0:T(8,128)(2,1)}) custom-call(s32[64]{0:T(128)S(1)} %convert_reduce_fusion.1.rank_q, s32[64]{0:T(128)S(1)} %get-tuple-element.16.order_q, s32[64]{0:T(128)S(1)} %get-tuple-element.15.sorted_q, s32[32]{0:T(128)S(1)} %convert_reduce_fusion.2.rank_k, ...), custom_call_target="tpu_custom_call" | custom-call | flops 2684354560 | bytes 4194304 | tf_op jit(solution)/shard_map/pallas_call | solution.py:151
  68.8 1.9 %collective-permute-start.7 = (f32[1024,256]{1,0:T(8,128)}, f32[1024,256]{1,0:T(8,128)S(1)}, u32[]{:S(2)}, u32[]{:S(2)}) collective-permute-start(f32[1024,256]{1,0:T(8,128)} %get-tuple-element.13), channel_id=1, source_target_pairs={{0,1},{1,0},{2,3},{3,2},{4,5},{5,4},{6,7},{7,6},{8,9},{9,8},{10,11... | collective-permute-start | bytes 3145736 | tf_op jit(solution)/shard_map/ppermute | solution.py:250
  70.7 12.0 %all-to-all-start.1 = ((bf16[16,64,256]{2,1,0:T(8,128)(2,1)}), bf16[16,64,256]{2,1,0:T(8,128)(2,1)S(1)}, u32[]{:S(2)}, u32[]{:S(2)}) async-start(bf16[16,64,256]{2,1,0:T(8,128)(2,1)} %bitcast.7), calls=%async_computation.1 | async-start | bytes 1048576 | tf_op jit(solution)/shard_map/all_to_all | solution.py:289
  83.0 2.0 %collective-permute-start.8 = (bf16[256,256]{1,0:T(8,128)(2,1)S(1)}, bf16[256,256]{1,0:T(8,128)(2,1)S(1)}, u32[]{:S(2)}, u32[]{:S(2)}) collective-permute-start(bf16[256,256]{1,0:T(8,128)(2,1)S(1)} %get-tuple-element.19), channel_id=1, source_target_pairs={{0,66},{1,385},{64,0},{65,449},{2,64},{3,387},{66,2},{67,451},{128... | collective-permute-start | bytes 393224 | tf_op jit(solution)/shard_map/ppermute | solution.py:242
  84.9 5.1 %collective-permute-start.10 = (bf16[256,256]{1,0:T(8,128)(2,1)S(1)}, bf16[256,256]{1,0:T(8,128)(2,1)S(1)}, u32[]{:S(2)}, u32[]{:S(2)}) collective-permute-start(bf16[256,256]{1,0:T(8,128)(2,1)S(1)} %get-tuple-element.20), channel_id=1, source_target_pairs={{0,64},{1,129},{64,2},{65,193},{2,66},{3,131},{66,0},{67,195},{128... | collective-permute-start | bytes 393224 | tf_op jit(solution)/shard_map/ppermute | solution.py:242
  90.0 2.9 %collective-permute-start.9 = (bf16[256,256]{1,0:T(8,128)(2,1)S(1)}, bf16[256,256]{1,0:T(8,128)(2,1)S(1)}, u32[]{:S(2)}, u32[]{:S(2)}) collective-permute-start(bf16[256,256]{1,0:T(8,128)(2,1)S(1)} %get-tuple-element.21), channel_id=1, source_target_pairs={{0,2},{1,257},{64,66},{65,321},{2,0},{3,259},{66,64},{67,323},{128... | collective-permute-start | bytes 393224 | tf_op jit(solution)/shard_map/ppermute | solution.py:242
  93.0 5.4 %collective-permute-done.9 = bf16[256,256]{1,0:T(8,128)(2,1)S(1)} collective-permute-done((bf16[256,256]{1,0:T(8,128)(2,1)S(1)}, bf16[256,256]{1,0:T(8,128)(2,1)S(1)}, u32[]{:S(2)}, u32[]{:S(2)}) %collective-permute-start.9) | collective-permute-done | bytes 131104 | tf_op jit(solution)/shard_map/ppermute | solution.py:242
  98.5 2.0 %collective-permute-start.11 = (f32[64,256]{1,0:T(8,128)S(1)}, f32[64,256]{1,0:T(8,128)S(1)}, u32[]{:S(2)}, u32[]{:S(2)}) collective-permute-start(f32[64,256]{1,0:T(8,128)S(1)} %get-tuple-element.22), channel_id=1, source_target_pairs={{0,384},{1,67},{64,448},{65,1},{2,386},{3,65},{66,450},{67,3},{128... | collective-permute-start | bytes 196616 | tf_op jit(solution)/shard_map/ppermute | solution.py:242
  100.5 3.9 %collective-permute-start.13 = (f32[64,256]{1,0:T(8,128)S(1)}, f32[64,256]{1,0:T(8,128)S(1)}, u32[]{:S(2)}, u32[]{:S(2)}) collective-permute-start(f32[64,256]{1,0:T(8,128)S(1)} %get-tuple-element.23), channel_id=1, source_target_pairs={{0,128},{1,65},{64,192},{65,3},{2,130},{3,67},{66,194},{67,1},{128... | collective-permute-start | bytes 196616 | tf_op jit(solution)/shard_map/ppermute | solution.py:242
  104.4 3.4 %collective-permute-start.12 = (f32[64,256]{1,0:T(8,128)S(1)}, f32[64,256]{1,0:T(8,128)S(1)}, u32[]{:S(2)}, u32[]{:S(2)}) collective-permute-start(f32[64,256]{1,0:T(8,128)S(1)} %get-tuple-element.24), channel_id=1, source_target_pairs={{0,256},{1,3},{64,320},{65,67},{2,258},{3,1},{66,322},{67,65},{128... | collective-permute-start | bytes 196616 | tf_op jit(solution)/shard_map/ppermute | solution.py:242
  107.9 4.2 %collective-permute-done.12 = f32[64,256]{1,0:T(8,128)S(1)} collective-permute-done((f32[64,256]{1,0:T(8,128)S(1)}, f32[64,256]{1,0:T(8,128)S(1)}, u32[]{:S(2)}, u32[]{:S(2)}) %collective-permute-start.12) | collective-permute-done | bytes 65568 | tf_op jit(solution)/shard_map/ppermute | solution.py:242
  112.0 0.6 fusion.5
  112.7 0.6 slice.120
  113.4 0.6 fusion.6
  (45 shorter events, 2.4 us)
Async XLA Ops:
  2.2 47.4 %all-to-all-start = ((bf16[16,64,256]{2,1,0:T(8,128)(2,1)}), bf16[16,64,256]{2,1,0:T(8,128)(2,1)S(1)}, u32[]{:S(2)}, u32[]{:S(2)}) async-start(bf16[16,64,256]{2,1,0:T(8,128)(2,1)} %broadcast_in_dim.48), calls=%async_computation | async-start | bytes 1048576 | tf_op jit(solution)/shard_map/all_to_all | solution.py:270
  18.8 11.8 %collective-permute-start.2 = (bf16[80,512]{1,0:T(8,128)(2,1)}, bf16[80,512]{1,0:T(8,128)(2,1)S(1)}, u32[]{:S(2)}, u32[]{:S(2)}) collective-permute-start(bf16[80,512]{1,0:T(8,128)(2,1)} %shard_map.94), channel_id=1, source_target_pairs={{0,384},{1,67},{64,448},{65,1},{2,386},{3,65},{66,450},{67,3},{128... | collective-permute-start | bytes 245768 | tf_op jit(solution)/shard_map/ppermute | solution.py:242
  23.5 8.0 %collective-permute-start.1 = (bf16[80,512]{1,0:T(8,128)(2,1)}, bf16[80,512]{1,0:T(8,128)(2,1)S(1)}, u32[]{:S(2)}, u32[]{:S(2)}) collective-permute-start(bf16[80,512]{1,0:T(8,128)(2,1)} %shard_map.94), channel_id=1, source_target_pairs={{0,256},{1,3},{64,320},{65,67},{2,258},{3,1},{66,322},{67,65},{128... | collective-permute-start | bytes 245768 | tf_op jit(solution)/shard_map/ppermute | solution.py:242
  26.2 7.8 %collective-permute-start = (bf16[80,512]{1,0:T(8,128)(2,1)}, bf16[80,512]{1,0:T(8,128)(2,1)S(1)}, u32[]{:S(2)}, u32[]{:S(2)}) collective-permute-start(bf16[80,512]{1,0:T(8,128)(2,1)} %shard_map.94), channel_id=1, source_target_pairs={{0,128},{1,65},{64,192},{65,3},{2,130},{3,67},{66,194},{67,1},{128... | collective-permute-start | bytes 245768 | tf_op jit(solution)/shard_map/ppermute | solution.py:242
  34.0 10.1 %collective-permute-start.5 = (bf16[272,512]{1,0:T(8,128)(2,1)S(1)}, bf16[272,512]{1,0:T(8,128)(2,1)S(1)}, u32[]{:S(2)}, u32[]{:S(2)}) collective-permute-start(bf16[272,512]{1,0:T(8,128)(2,1)S(1)} %maximum_dynamic-update-slice_fusion), channel_id=1, source_target_pairs={{0,66},{1,385},{64,0},{65,449},{2,64},{3,387},{66,2},{67,451},{128... | collective-permute-start | bytes 835592 | tf_op jit(solution)/shard_map/ppermute | solution.py:242
  36.7 10.0 %collective-permute-start.4 = (bf16[272,512]{1,0:T(8,128)(2,1)S(1)}, bf16[272,512]{1,0:T(8,128)(2,1)S(1)}, u32[]{:S(2)}, u32[]{:S(2)}) collective-permute-start(bf16[272,512]{1,0:T(8,128)(2,1)S(1)} %maximum_dynamic-update-slice_fusion), channel_id=1, source_target_pairs={{0,2},{1,257},{64,66},{65,321},{2,0},{3,259},{66,64},{67,323},{128... | collective-permute-start | bytes 835592 | tf_op jit(solution)/shard_map/ppermute | solution.py:242
  39.5 9.9 %collective-permute-start.3 = (bf16[272,512]{1,0:T(8,128)(2,1)S(1)}, bf16[272,512]{1,0:T(8,128)(2,1)S(1)}, u32[]{:S(2)}, u32[]{:S(2)}) collective-permute-start(bf16[272,512]{1,0:T(8,128)(2,1)S(1)} %maximum_dynamic-update-slice_fusion), channel_id=1, source_target_pairs={{0,64},{1,129},{64,2},{65,193},{2,66},{3,131},{66,0},{67,195},{128... | collective-permute-start | bytes 835592 | tf_op jit(solution)/shard_map/ppermute | solution.py:242
  49.4 2.1 %copy-start = (s32[1024]{0:T(1024)S(1)}, s32[1024]{0:T(1024)}, u32[]{:S(2)}) copy-start(s32[1024]{0:T(1024)} %param.13) | copy-start | bytes 12292
  49.6 4.8 %collective-permute-start.6 = (bf16[4,272,512]{2,1,0:T(8,128)(2,1)S(1)}, bf16[4,272,512]{2,1,0:T(8,128)(2,1)}, u32[]{:S(2)}, u32[]{:S(2)}) collective-permute-start(bf16[4,272,512]{2,1,0:T(8,128)(2,1)S(1)} %pad_maximum_fusion.refs_0_), channel_id=1, source_target_pairs={{0,1},{1,0},{2,3},{3,2},{4,5},{5,4},{6,7},{7,6},{8,9},{9,8},{10,11... | collective-permute-start | bytes 3342344 | tf_op jit(solution)/shard_map/ppermute | solution.py:250
  68.8 14.0 %collective-permute-start.7 = (f32[1024,256]{1,0:T(8,128)}, f32[1024,256]{1,0:T(8,128)S(1)}, u32[]{:S(2)}, u32[]{:S(2)}) collective-permute-start(f32[1024,256]{1,0:T(8,128)} %get-tuple-element.13), channel_id=1, source_target_pairs={{0,1},{1,0},{2,3},{3,2},{4,5},{5,4},{6,7},{7,6},{8,9},{9,8},{10,11... | collective-permute-start | bytes 3145736 | tf_op jit(solution)/shard_map/ppermute | solution.py:250
  70.7 42.0 %all-to-all-start.1 = ((bf16[16,64,256]{2,1,0:T(8,128)(2,1)}), bf16[16,64,256]{2,1,0:T(8,128)(2,1)S(1)}, u32[]{:S(2)}, u32[]{:S(2)}) async-start(bf16[16,64,256]{2,1,0:T(8,128)(2,1)} %bitcast.7), calls=%async_computation.1 | async-start | bytes 1048576 | tf_op jit(solution)/shard_map/all_to_all | solution.py:289
  83.0 10.0 %collective-permute-start.8 = (bf16[256,256]{1,0:T(8,128)(2,1)S(1)}, bf16[256,256]{1,0:T(8,128)(2,1)S(1)}, u32[]{:S(2)}, u32[]{:S(2)}) collective-permute-start(bf16[256,256]{1,0:T(8,128)(2,1)S(1)} %get-tuple-element.19), channel_id=1, source_target_pairs={{0,66},{1,385},{64,0},{65,449},{2,64},{3,387},{66,2},{67,451},{128... | collective-permute-start | bytes 393224 | tf_op jit(solution)/shard_map/ppermute | solution.py:242
  84.9 8.1 %collective-permute-start.10 = (bf16[256,256]{1,0:T(8,128)(2,1)S(1)}, bf16[256,256]{1,0:T(8,128)(2,1)S(1)}, u32[]{:S(2)}, u32[]{:S(2)}) collective-permute-start(bf16[256,256]{1,0:T(8,128)(2,1)S(1)} %get-tuple-element.20), channel_id=1, source_target_pairs={{0,64},{1,129},{64,2},{65,193},{2,66},{3,131},{66,0},{67,195},{128... | collective-permute-start | bytes 393224 | tf_op jit(solution)/shard_map/ppermute | solution.py:242
  90.0 8.4 %collective-permute-start.9 = (bf16[256,256]{1,0:T(8,128)(2,1)S(1)}, bf16[256,256]{1,0:T(8,128)(2,1)S(1)}, u32[]{:S(2)}, u32[]{:S(2)}) collective-permute-start(bf16[256,256]{1,0:T(8,128)(2,1)S(1)} %get-tuple-element.21), channel_id=1, source_target_pairs={{0,2},{1,257},{64,66},{65,321},{2,0},{3,259},{66,64},{67,323},{128... | collective-permute-start | bytes 393224 | tf_op jit(solution)/shard_map/ppermute | solution.py:242
  98.5 9.3 %collective-permute-start.11 = (f32[64,256]{1,0:T(8,128)S(1)}, f32[64,256]{1,0:T(8,128)S(1)}, u32[]{:S(2)}, u32[]{:S(2)}) collective-permute-start(f32[64,256]{1,0:T(8,128)S(1)} %get-tuple-element.22), channel_id=1, source_target_pairs={{0,384},{1,67},{64,448},{65,1},{2,386},{3,65},{66,450},{67,3},{128... | collective-permute-start | bytes 196616 | tf_op jit(solution)/shard_map/ppermute | solution.py:242
  100.5 7.4 %collective-permute-start.13 = (f32[64,256]{1,0:T(8,128)S(1)}, f32[64,256]{1,0:T(8,128)S(1)}, u32[]{:S(2)}, u32[]{:S(2)}) collective-permute-start(f32[64,256]{1,0:T(8,128)S(1)} %get-tuple-element.23), channel_id=1, source_target_pairs={{0,128},{1,65},{64,192},{65,3},{2,130},{3,67},{66,194},{67,1},{128... | collective-permute-start | bytes 196616 | tf_op jit(solution)/shard_map/ppermute | solution.py:242
  104.4 7.7 %collective-permute-start.12 = (f32[64,256]{1,0:T(8,128)S(1)}, f32[64,256]{1,0:T(8,128)S(1)}, u32[]{:S(2)}, u32[]{:S(2)}) collective-permute-start(f32[64,256]{1,0:T(8,128)S(1)} %get-tuple-element.24), channel_id=1, source_target_pairs={{0,256},{1,3},{64,320},{65,67},{2,258},{3,1},{66,322},{67,65},{128... | collective-permute-start | bytes 196616 | tf_op jit(solution)/shard_map/ppermute | solution.py:242

commit v9 on v8

--- a/solution.py
+++ b/solution.py
@@ -14,7 +14,6 @@
 STATS = 16
 QT = 256
 KT = 256
-TOGETHER = 4
 VMEM = pl.BlockSpec(memory_space=pltpu.VMEM)
 SMEM = pl.BlockSpec(memory_space=pltpu.SMEM)
 
@@ -91,8 +90,7 @@
             todo[count] = jnp.int32(j * n_k + i)
             count = count + live.astype(jnp.int32)
             dead = jnp.where(live, dead, j * n_k + i)
-    for u in range(TOGETHER - 1):
-        todo[count + u] = dead
+    todo[count] = dead
 
     within = lax.broadcasted_iota(jnp.int32, (HALF, 128), 0)
 
@@ -110,12 +108,18 @@
         dk[i] += dot(ds, q)
         dqt[j] += dot(kt[i], ds)
 
-    def some(t, c):
-        for u in range(TOGETHER):
-            one(t * TOGETHER + u)
+    def four(t, c):
+        for u in range(4):
+            one(t * 4 + u)
         return c
 
-    lax.fori_loop(0, (count + TOGETHER - 1) // TOGETHER, some, 0)
+    def two(t, c):
+        for u in range(2):
+            one(t * 2 + u)
+        return c
+
+    lax.fori_loop(0, count // 4, four, 0)
+    lax.fori_loop(count // 4 * 2, (count + 1) // 2, two, 0)
 
     for j in range(n_q):
         for h in range(HEADS):
@@ -169,7 +173,7 @@
             pltpu.VMEM((n_q, HEADS * QT, HD), f32),
             pltpu.VMEM((n_k, KT, HD), f32),
             pltpu.VMEM((n_k, KT, HD), f32),
-            pltpu.SMEM((n_q * n_k + TOGETHER,), jnp.int32),
+            pltpu.SMEM((n_q * n_k + 1,), jnp.int32),
         ],
         compiler_params=pltpu.CompilerParams(vmem_limit_bytes=40 * 1024 * 1024),
         cost_estimate=pl.CostEstimate(
@@ -272,7 +276,7 @@
     packed = pack_q(queries, out_grad, log_sum, delta)
     line = join([packed] + [from_offset(packed, 0, d) for d in (1, 2, 3)])
     q_own = jnp.stack([line] + [from_offset(line, 1, d) for d in (1, 2, 3)])
-    table, q_own, kv = lax.optimization_barrier((block_table, q_own, kv))
+    table, q_own = lax.optimization_barrier((block_table, q_own))
     q_sib = other_core(q_own)
 
     spot = jnp.arange(nz, dtype=jnp.int32)

time: 116 us -> 112 us (0.966)
  starting transfers between devices: 70.1 us -> 66.7 us
  waiting for transfers between devices: 19.8 us -> 22.1 us
  local copies, waits for them, and re-layouts: 3.55 us -> 2.07 us
    all_to_all x1, waiting for transfers between devices: 0.01 us -> 6.36 us  [local(): lax.all_to_all(jnp.broadcast_to(kv[None], (nz,) + kv.shape), 'z', split_a...]
    all_to_all x1, starting transfers between devices: 12 us -> 6.98 us  [local(): lax.all_to_all(dkv.reshape(nz, rows, 2 * HD), 'z', split_axis=0, concat_a...]
    ppermute x12, waiting for transfers between devices: 18.3 us -> 14.2 us  [from_offset(): return lax.ppermute(x, ('x', 'yl', 'yh', 'core'), pairs)]
    ppermute x12, starting transfers between devices: 39 us -> 40.7 us  [from_offset(): return lax.ppermute(x, ('x', 'yl', 'yh', 'core'), pairs)]
  transfers between devices with their start and end apart: 16 -> 16, of which waited for: 7 -> 7; matrix products, arithmetic and copies ran while one was open for 4% -> 4% of each run, Pallas kernels for 1% -> 0%
where the time goes in v9:
time: 112 us; the launch traced here: 111 us
  starting transfers between devices  66.7 us (60%)
  waiting for transfers between devices  22.1 us (20%)
  Pallas kernels  15.2 us (14%)
  other arithmetic  3.75 us (3%)
  local copies, waits for them, and re-layouts  2.07 us (2%)
    ppermute x12, starting transfers between devices, from_offset(): return lax.ppermute(x, ('x', 'yl', 'yh', 'core'), pairs)  40.7 us
    all_to_all x1, starting transfers between devices, local(): lax.all_to_all(jnp.broadcast_to(kv[None], (nz,) + kv.shape), 'z', split_a...  15.2 us
    ppermute x12, waiting for transfers between devices, from_offset(): return lax.ppermute(x, ('x', 'yl', 'yh', 'core'), pairs)  14.2 us
    pallas_call x1, Pallas kernels, tile_grads(): pl.pallas_call(tile_kernel, out_shape=(jax.ShapeDtypeStruct((rows_q // 2,...  13.8 us
    all_to_all x1, starting transfers between devices, local(): lax.all_to_all(dkv.reshape(nz, rows, 2 * HD), 'z', split_axis=0, concat_a...  6.98 us
    all_to_all x1, waiting for transfers between devices, local(): lax.all_to_all(jnp.broadcast_to(kv[None], (nz,) + kv.shape), 'z', split_a...  6.36 us
    ppermute x2, starting transfers between devices, other_core(): return lax.ppermute(x, 'core', [(0, 1), (1, 0)])  3.83 us
  transfers between devices with their start and end apart: 16, of which 7 were waited for; matrix products, arithmetic and copies ran while one was open for 4% of the time, Pallas kernels for 0%

profile of v9, /device:TPU:24, one launch (start us, length us, event | category | flops | bytes accessed | tf_op | source)
XLA Modules:
  0.0 110.8 jit_solution(13043697712187604312)
XLA Ops:
  0.6 1.4 %shard_map.94 = bf16[80,512]{1,0:T(8,128)(2,1)} custom-call(bf16[64,256]{1,0:T(8,128)(2,1)} %q_ref.1, bf16[64,256]{1,0:T(8,128)(2,1)} %g_ref.1, f32[2,64]{1,0:T(2,128)} %bitcast.13, f32[2,64]{1,0:T(2,128)} %bitcast.14), custom_call_target="tpu_custom_call" | custom-call | tf_op jit(solution)/shard_map/pallas_call | solution.py:224
  2.1 4.8 %collective-permute-start.2 = (bf16[80,512]{1,0:T(8,128)(2,1)}, bf16[80,512]{1,0:T(8,128)(2,1)S(1)}, u32[]{:S(2)}, u32[]{:S(2)}) collective-permute-start(bf16[80,512]{1,0:T(8,128)(2,1)} %shard_map.94), channel_id=1, source_target_pairs={{0,384},{1,67},{64,448},{65,1},{2,386},{3,65},{66,450},{67,3},{128... | collective-permute-start | bytes 245768 | tf_op jit(solution)/shard_map/ppermute | solution.py:246
  6.8 2.7 %collective-permute-start.1 = (bf16[80,512]{1,0:T(8,128)(2,1)}, bf16[80,512]{1,0:T(8,128)(2,1)S(1)}, u32[]{:S(2)}, u32[]{:S(2)}) collective-permute-start(bf16[80,512]{1,0:T(8,128)(2,1)} %shard_map.94), channel_id=1, source_target_pairs={{0,256},{1,3},{64,320},{65,67},{2,258},{3,1},{66,322},{67,65},{128... | collective-permute-start | bytes 245768 | tf_op jit(solution)/shard_map/ppermute | solution.py:246
  9.6 2.8 %collective-permute-start = (bf16[80,512]{1,0:T(8,128)(2,1)}, bf16[80,512]{1,0:T(8,128)(2,1)S(1)}, u32[]{:S(2)}, u32[]{:S(2)}) collective-permute-start(bf16[80,512]{1,0:T(8,128)(2,1)} %shard_map.94), channel_id=1, source_target_pairs={{0,128},{1,65},{64,192},{65,3},{2,130},{3,67},{66,194},{67,1},{128... | collective-permute-start | bytes 245768 | tf_op jit(solution)/shard_map/ppermute | solution.py:246
  12.4 0.7 pad_maximum_fusion.1
  13.1 0.9 broadcast_in_dim.84
  14.0 15.2 %all-to-all-start = ((bf16[16,64,256]{2,1,0:T(8,128)(2,1)}), bf16[16,64,256]{2,1,0:T(8,128)(2,1)S(1)}, u32[]{:S(2)}, u32[]{:S(2)}) async-start(bf16[16,64,256]{2,1,0:T(8,128)(2,1)} %broadcast_in_dim.84), calls=%async_computation | async-start | bytes 1048576 | tf_op jit(solution)/shard_map/all_to_all | solution.py:274
  29.5 2.7 %collective-permute-start.5 = (bf16[272,512]{1,0:T(8,128)(2,1)S(1)}, bf16[272,512]{1,0:T(8,128)(2,1)S(1)}, u32[]{:S(2)}, u32[]{:S(2)}) collective-permute-start(bf16[272,512]{1,0:T(8,128)(2,1)S(1)} %maximum_dynamic-update-slice_fusion), channel_id=1, source_target_pairs={{0,66},{1,385},{64,0},{65,449},{2,64},{3,387},{66,2},{67,451},{128... | collective-permute-start | bytes 835592 | tf_op jit(solution)/shard_map/ppermute | solution.py:246
  32.1 2.8 %collective-permute-start.4 = (bf16[272,512]{1,0:T(8,128)(2,1)S(1)}, bf16[272,512]{1,0:T(8,128)(2,1)S(1)}, u32[]{:S(2)}, u32[]{:S(2)}) collective-permute-start(bf16[272,512]{1,0:T(8,128)(2,1)S(1)} %maximum_dynamic-update-slice_fusion), channel_id=1, source_target_pairs={{0,2},{1,257},{64,66},{65,321},{2,0},{3,259},{66,64},{67,323},{128... | collective-permute-start | bytes 835592 | tf_op jit(solution)/shard_map/ppermute | solution.py:246
  35.0 4.1 %collective-permute-start.3 = (bf16[272,512]{1,0:T(8,128)(2,1)S(1)}, bf16[272,512]{1,0:T(8,128)(2,1)S(1)}, u32[]{:S(2)}, u32[]{:S(2)}) collective-permute-start(bf16[272,512]{1,0:T(8,128)(2,1)S(1)} %maximum_dynamic-update-slice_fusion), channel_id=1, source_target_pairs={{0,64},{1,129},{64,2},{65,193},{2,66},{3,131},{66,0},{67,195},{128... | collective-permute-start | bytes 835592 | tf_op jit(solution)/shard_map/ppermute | solution.py:246
  39.5 2.6 %collective-permute-done.4 = bf16[272,512]{1,0:T(8,128)(2,1)S(1)} collective-permute-done((bf16[272,512]{1,0:T(8,128)(2,1)S(1)}, bf16[272,512]{1,0:T(8,128)(2,1)S(1)}, u32[]{:S(2)}, u32[]{:S(2)}) %collective-permute-start.4) | collective-permute-done | bytes 278560 | tf_op jit(solution)/shard_map/ppermute | solution.py:246
  42.1 2.8 %collective-permute-done.3 = bf16[272,512]{1,0:T(8,128)(2,1)S(1)} collective-permute-done((bf16[272,512]{1,0:T(8,128)(2,1)S(1)}, bf16[272,512]{1,0:T(8,128)(2,1)S(1)}, u32[]{:S(2)}, u32[]{:S(2)}) %collective-permute-start.3) | collective-permute-done | bytes 278560 | tf_op jit(solution)/shard_map/ppermute | solution.py:246
  45.0 1.9 %collective-permute-start.6 = (bf16[4,272,512]{2,1,0:T(8,128)(2,1)S(1)}, bf16[4,272,512]{2,1,0:T(8,128)(2,1)}, u32[]{:S(2)}, u32[]{:S(2)}) collective-permute-start(bf16[4,272,512]{2,1,0:T(8,128)(2,1)S(1)} %pad_maximum_fusion.refs_0_), channel_id=1, source_target_pairs={{0,1},{1,0},{2,3},{3,2},{4,5},{5,4},{6,7},{7,6},{8,9},{9,8},{10,11... | collective-permute-start | bytes 3342344 | tf_op jit(solution)/shard_map/ppermute | solution.py:254
  47.0 0.2 select_reduce_fusion
  48.3 1.6 %collective-permute-done.6.refs_1_ = bf16[4,272,512]{2,1,0:T(8,128)(2,1)} collective-permute-done((bf16[4,272,512]{2,1,0:T(8,128)(2,1)S(1)}, bf16[4,272,512]{2,1,0:T(8,128)(2,1)}, u32[]{:S(2)}, u32[]{:S(2)}) %collective-permute-start.6) | collective-permute-done | bytes 1114144 | tf_op jit(solution)/shard_map/ppermute | solution.py:254
  49.8 6.4 %all-to-all-done = bf16[16,64,256]{2,1,0:T(8,128)(2,1)S(1)} async-done(((bf16[16,64,256]{2,1,0:T(8,128)(2,1)}), bf16[16,64,256]{2,1,0:T(8,128)(2,1)S(1)}, u32[]{:S(2)}, u32[]{:S(2)}) %all-to-all-start) | async-done | bytes 524320 | tf_op jit(solution)/shard_map/all_to_all | solution.py:274
  56.2 13.8 %shard_map.95 = (f32[1024,256]{1,0:T(8,128)S(1)}, f32[1024,256]{1,0:T(8,128)}, bf16[1024,256]{1,0:T(8,128)(2,1)}) custom-call(s32[64]{0:T(128)S(1)} %convert_reduce_fusion.1.rank_q, s32[64]{0:T(128)S(1)} %get-tuple-element.14.order_q, s32[64]{0:T(128)S(1)} %get-tuple-element.13.sorted_q, s32[32]{0:T(128)S(1)} %convert_reduce_fusion.2.rank_k, ...), custom_call_target="tpu_custom_call" | custom-call | flops 2684354560 | bytes 4194304 | tf_op jit(solution)/shard_map/pallas_call | solution.py:155
  69.9 1.9 %collective-permute-start.7 = (f32[1024,256]{1,0:T(8,128)}, f32[1024,256]{1,0:T(8,128)S(1)}, u32[]{:S(2)}, u32[]{:S(2)}) collective-permute-start(f32[1024,256]{1,0:T(8,128)} %get-tuple-element.11), channel_id=1, source_target_pairs={{0,1},{1,0},{2,3},{3,2},{4,5},{5,4},{6,7},{7,6},{8,9},{9,8},{10,11... | collective-permute-start | bytes 3145736 | tf_op jit(solution)/shard_map/ppermute | solution.py:254
  71.8 7.0 %all-to-all-start.1 = ((bf16[16,64,256]{2,1,0:T(8,128)(2,1)}), bf16[16,64,256]{2,1,0:T(8,128)(2,1)S(1)}, u32[]{:S(2)}, u32[]{:S(2)}) async-start(bf16[16,64,256]{2,1,0:T(8,128)(2,1)} %bitcast.7), calls=%async_computation.1 | async-start | bytes 1048576 | tf_op jit(solution)/shard_map/all_to_all | solution.py:293
  78.8 0.2 fusion.19
  79.1 2.4 %collective-permute-start.8 = (bf16[256,256]{1,0:T(8,128)(2,1)S(1)}, bf16[256,256]{1,0:T(8,128)(2,1)S(1)}, u32[]{:S(2)}, u32[]{:S(2)}) collective-permute-start(bf16[256,256]{1,0:T(8,128)(2,1)S(1)} %get-tuple-element.17), channel_id=1, source_target_pairs={{0,66},{1,385},{64,0},{65,449},{2,64},{3,387},{66,2},{67,451},{128... | collective-permute-start | bytes 393224 | tf_op jit(solution)/shard_map/ppermute | solution.py:246
  81.5 4.6 %collective-permute-start.10 = (bf16[256,256]{1,0:T(8,128)(2,1)S(1)}, bf16[256,256]{1,0:T(8,128)(2,1)S(1)}, u32[]{:S(2)}, u32[]{:S(2)}) collective-permute-start(bf16[256,256]{1,0:T(8,128)(2,1)S(1)} %get-tuple-element.18), channel_id=1, source_target_pairs={{0,64},{1,129},{64,2},{65,193},{2,66},{3,131},{66,0},{67,195},{128... | collective-permute-start | bytes 393224 | tf_op jit(solution)/shard_map/ppermute | solution.py:246
  86.1 3.0 %collective-permute-start.9 = (bf16[256,256]{1,0:T(8,128)(2,1)S(1)}, bf16[256,256]{1,0:T(8,128)(2,1)S(1)}, u32[]{:S(2)}, u32[]{:S(2)}) collective-permute-start(bf16[256,256]{1,0:T(8,128)(2,1)S(1)} %get-tuple-element.19), channel_id=1, source_target_pairs={{0,2},{1,257},{64,66},{65,321},{2,0},{3,259},{66,64},{67,323},{128... | collective-permute-start | bytes 393224 | tf_op jit(solution)/shard_map/ppermute | solution.py:246
  89.2 5.3 %collective-permute-done.9 = bf16[256,256]{1,0:T(8,128)(2,1)S(1)} collective-permute-done((bf16[256,256]{1,0:T(8,128)(2,1)S(1)}, bf16[256,256]{1,0:T(8,128)(2,1)S(1)}, u32[]{:S(2)}, u32[]{:S(2)}) %collective-permute-start.9) | collective-permute-done | bytes 131104 | tf_op jit(solution)/shard_map/ppermute | solution.py:246
  94.6 4.7 %collective-permute-start.11 = (f32[64,256]{1,0:T(8,128)S(1)}, f32[64,256]{1,0:T(8,128)S(1)}, u32[]{:S(2)}, u32[]{:S(2)}) collective-permute-start(f32[64,256]{1,0:T(8,128)S(1)} %get-tuple-element.20), channel_id=1, source_target_pairs={{0,384},{1,67},{64,448},{65,1},{2,386},{3,65},{66,450},{67,3},{128... | collective-permute-start | bytes 196616 | tf_op jit(solution)/shard_map/ppermute | solution.py:246
  99.3 1.9 %collective-permute-start.13 = (f32[64,256]{1,0:T(8,128)S(1)}, f32[64,256]{1,0:T(8,128)S(1)}, u32[]{:S(2)}, u32[]{:S(2)}) collective-permute-start(f32[64,256]{1,0:T(8,128)S(1)} %get-tuple-element.21), channel_id=1, source_target_pairs={{0,128},{1,65},{64,192},{65,3},{2,130},{3,67},{66,194},{67,1},{128... | collective-permute-start | bytes 196616 | tf_op jit(solution)/shard_map/ppermute | solution.py:246
  101.2 4.2 %collective-permute-start.12 = (f32[64,256]{1,0:T(8,128)S(1)}, f32[64,256]{1,0:T(8,128)S(1)}, u32[]{:S(2)}, u32[]{:S(2)}) collective-permute-start(f32[64,256]{1,0:T(8,128)S(1)} %get-tuple-element.22), channel_id=1, source_target_pairs={{0,256},{1,3},{64,320},{65,67},{2,258},{3,1},{66,322},{67,65},{128... | collective-permute-start | bytes 196616 | tf_op jit(solution)/shard_map/ppermute | solution.py:246
  105.4 1.2 %collective-permute-done.13 = f32[64,256]{1,0:T(8,128)S(1)} collective-permute-done((f32[64,256]{1,0:T(8,128)S(1)}, f32[64,256]{1,0:T(8,128)S(1)}, u32[]{:S(2)}, u32[]{:S(2)}) %collective-permute-start.13) | collective-permute-done | bytes 65568 | tf_op jit(solution)/shard_map/ppermute | solution.py:246
  106.6 2.2 %collective-permute-done.12 = f32[64,256]{1,0:T(8,128)S(1)} collective-permute-done((f32[64,256]{1,0:T(8,128)S(1)}, f32[64,256]{1,0:T(8,128)S(1)}, u32[]{:S(2)}, u32[]{:S(2)}) %collective-permute-start.12) | collective-permute-done | bytes 65568 | tf_op jit(solution)/shard_map/ppermute | solution.py:246
  108.9 0.6 fusion.5
  109.6 0.6 slice.120
  110.2 0.6 fusion.6
  (47 shorter events, 2.0 us)
Async XLA Ops:
  2.1 27.1 %copy-start = (bf16[80,512]{1,0:T(8,128)(2,1)S(1)}, bf16[80,512]{1,0:T(8,128)(2,1)}, u32[]{:S(2)}) copy-start(bf16[80,512]{1,0:T(8,128)(2,1)} %shard_map.94) | copy-start | bytes 245764
  2.1 27.3 %collective-permute-start.2 = (bf16[80,512]{1,0:T(8,128)(2,1)}, bf16[80,512]{1,0:T(8,128)(2,1)S(1)}, u32[]{:S(2)}, u32[]{:S(2)}) collective-permute-start(bf16[80,512]{1,0:T(8,128)(2,1)} %shard_map.94), channel_id=1, source_target_pairs={{0,384},{1,67},{64,448},{65,1},{2,386},{3,65},{66,450},{67,3},{128... | collective-permute-start | bytes 245768 | tf_op jit(solution)/shard_map/ppermute | solution.py:246
  6.8 22.5 %collective-permute-start.1 = (bf16[80,512]{1,0:T(8,128)(2,1)}, bf16[80,512]{1,0:T(8,128)(2,1)S(1)}, u32[]{:S(2)}, u32[]{:S(2)}) collective-permute-start(bf16[80,512]{1,0:T(8,128)(2,1)} %shard_map.94), channel_id=1, source_target_pairs={{0,256},{1,3},{64,320},{65,67},{2,258},{3,1},{66,322},{67,65},{128... | collective-permute-start | bytes 245768 | tf_op jit(solution)/shard_map/ppermute | solution.py:246
  9.6 19.8 %collective-permute-start = (bf16[80,512]{1,0:T(8,128)(2,1)}, bf16[80,512]{1,0:T(8,128)(2,1)S(1)}, u32[]{:S(2)}, u32[]{:S(2)}) collective-permute-start(bf16[80,512]{1,0:T(8,128)(2,1)} %shard_map.94), channel_id=1, source_target_pairs={{0,128},{1,65},{64,192},{65,3},{2,130},{3,67},{66,194},{67,1},{128... | collective-permute-start | bytes 245768 | tf_op jit(solution)/shard_map/ppermute | solution.py:246
  14.0 42.2 %all-to-all-start = ((bf16[16,64,256]{2,1,0:T(8,128)(2,1)}), bf16[16,64,256]{2,1,0:T(8,128)(2,1)S(1)}, u32[]{:S(2)}, u32[]{:S(2)}) async-start(bf16[16,64,256]{2,1,0:T(8,128)(2,1)} %broadcast_in_dim.84), calls=%async_computation | async-start | bytes 1048576 | tf_op jit(solution)/shard_map/all_to_all | solution.py:274
  29.5 10.1 %collective-permute-start.5 = (bf16[272,512]{1,0:T(8,128)(2,1)S(1)}, bf16[272,512]{1,0:T(8,128)(2,1)S(1)}, u32[]{:S(2)}, u32[]{:S(2)}) collective-permute-start(bf16[272,512]{1,0:T(8,128)(2,1)S(1)} %maximum_dynamic-update-slice_fusion), channel_id=1, source_target_pairs={{0,66},{1,385},{64,0},{65,449},{2,64},{3,387},{66,2},{67,451},{128... | collective-permute-start | bytes 835592 | tf_op jit(solution)/shard_map/ppermute | solution.py:246
  32.1 10.0 %collective-permute-start.4 = (bf16[272,512]{1,0:T(8,128)(2,1)S(1)}, bf16[272,512]{1,0:T(8,128)(2,1)S(1)}, u32[]{:S(2)}, u32[]{:S(2)}) collective-permute-start(bf16[272,512]{1,0:T(8,128)(2,1)S(1)} %maximum_dynamic-update-slice_fusion), channel_id=1, source_target_pairs={{0,2},{1,257},{64,66},{65,321},{2,0},{3,259},{66,64},{67,323},{128... | collective-permute-start | bytes 835592 | tf_op jit(solution)/shard_map/ppermute | solution.py:246
  35.0 9.9 %collective-permute-start.3 = (bf16[272,512]{1,0:T(8,128)(2,1)S(1)}, bf16[272,512]{1,0:T(8,128)(2,1)S(1)}, u32[]{:S(2)}, u32[]{:S(2)}) collective-permute-start(bf16[272,512]{1,0:T(8,128)(2,1)S(1)} %maximum_dynamic-update-slice_fusion), channel_id=1, source_target_pairs={{0,64},{1,129},{64,2},{65,193},{2,66},{3,131},{66,0},{67,195},{128... | collective-permute-start | bytes 835592 | tf_op jit(solution)/shard_map/ppermute | solution.py:246
  44.9 2.1 %copy-start.1 = (s32[1024]{0:T(1024)S(1)}, s32[1024]{0:T(1024)}, u32[]{:S(2)}) copy-start(s32[1024]{0:T(1024)} %param.13) | copy-start | bytes 12292
  45.0 4.8 %collective-permute-start.6 = (bf16[4,272,512]{2,1,0:T(8,128)(2,1)S(1)}, bf16[4,272,512]{2,1,0:T(8,128)(2,1)}, u32[]{:S(2)}, u32[]{:S(2)}) collective-permute-start(bf16[4,272,512]{2,1,0:T(8,128)(2,1)S(1)} %pad_maximum_fusion.refs_0_), channel_id=1, source_target_pairs={{0,1},{1,0},{2,3},{3,2},{4,5},{5,4},{6,7},{7,6},{8,9},{9,8},{10,11... | collective-permute-start | bytes 3342344 | tf_op jit(solution)/shard_map/ppermute | solution.py:254
  69.9 8.9 %collective-permute-start.7 = (f32[1024,256]{1,0:T(8,128)}, f32[1024,256]{1,0:T(8,128)S(1)}, u32[]{:S(2)}, u32[]{:S(2)}) collective-permute-start(f32[1024,256]{1,0:T(8,128)} %get-tuple-element.11), channel_id=1, source_target_pairs={{0,1},{1,0},{2,3},{3,2},{4,5},{5,4},{6,7},{7,6},{8,9},{9,8},{10,11... | collective-permute-start | bytes 3145736 | tf_op jit(solution)/shard_map/ppermute | solution.py:254
  71.8 37.7 %all-to-all-start.1 = ((bf16[16,64,256]{2,1,0:T(8,128)(2,1)}), bf16[16,64,256]{2,1,0:T(8,128)(2,1)S(1)}, u32[]{:S(2)}, u32[]{:S(2)}) async-start(bf16[16,64,256]{2,1,0:T(8,128)(2,1)} %bitcast.7), calls=%async_computation.1 | async-start | bytes 1048576 | tf_op jit(solution)/shard_map/all_to_all | solution.py:293
  79.1 10.1 %collective-permute-start.8 = (bf16[256,256]{1,0:T(8,128)(2,1)S(1)}, bf16[256,256]{1,0:T(8,128)(2,1)S(1)}, u32[]{:S(2)}, u32[]{:S(2)}) collective-permute-start(bf16[256,256]{1,0:T(8,128)(2,1)S(1)} %get-tuple-element.17), channel_id=1, source_target_pairs={{0,66},{1,385},{64,0},{65,449},{2,64},{3,387},{66,2},{67,451},{128... | collective-permute-start | bytes 393224 | tf_op jit(solution)/shard_map/ppermute | solution.py:246
  81.5 7.6 %collective-permute-start.10 = (bf16[256,256]{1,0:T(8,128)(2,1)S(1)}, bf16[256,256]{1,0:T(8,128)(2,1)S(1)}, u32[]{:S(2)}, u32[]{:S(2)}) collective-permute-start(bf16[256,256]{1,0:T(8,128)(2,1)S(1)} %get-tuple-element.18), channel_id=1, source_target_pairs={{0,64},{1,129},{64,2},{65,193},{2,66},{3,131},{66,0},{67,195},{128... | collective-permute-start | bytes 393224 | tf_op jit(solution)/shard_map/ppermute | solution.py:246
  86.1 8.4 %collective-permute-start.9 = (bf16[256,256]{1,0:T(8,128)(2,1)S(1)}, bf16[256,256]{1,0:T(8,128)(2,1)S(1)}, u32[]{:S(2)}, u32[]{:S(2)}) collective-permute-start(bf16[256,256]{1,0:T(8,128)(2,1)S(1)} %get-tuple-element.19), channel_id=1, source_target_pairs={{0,2},{1,257},{64,66},{65,321},{2,0},{3,259},{66,64},{67,323},{128... | collective-permute-start | bytes 393224 | tf_op jit(solution)/shard_map/ppermute | solution.py:246
  94.6 10.8 %collective-permute-start.11 = (f32[64,256]{1,0:T(8,128)S(1)}, f32[64,256]{1,0:T(8,128)S(1)}, u32[]{:S(2)}, u32[]{:S(2)}) collective-permute-start(f32[64,256]{1,0:T(8,128)S(1)} %get-tuple-element.20), channel_id=1, source_target_pairs={{0,384},{1,67},{64,448},{65,1},{2,386},{3,65},{66,450},{67,3},{128... | collective-permute-start | bytes 196616 | tf_op jit(solution)/shard_map/ppermute | solution.py:246
  99.3 7.4 %collective-permute-start.13 = (f32[64,256]{1,0:T(8,128)S(1)}, f32[64,256]{1,0:T(8,128)S(1)}, u32[]{:S(2)}, u32[]{:S(2)}) collective-permute-start(f32[64,256]{1,0:T(8,128)S(1)} %get-tuple-element.21), channel_id=1, source_target_pairs={{0,128},{1,65},{64,192},{65,3},{2,130},{3,67},{66,194},{67,1},{128... | collective-permute-start | bytes 196616 | tf_op jit(solution)/shard_map/ppermute | solution.py:246
  101.2 7.7 %collective-permute-start.12 = (f32[64,256]{1,0:T(8,128)S(1)}, f32[64,256]{1,0:T(8,128)S(1)}, u32[]{:S(2)}, u32[]{:S(2)}) collective-permute-start(f32[64,256]{1,0:T(8,128)S(1)} %get-tuple-element.22), channel_id=1, source_target_pairs={{0,256},{1,3},{64,320},{65,67},{2,258},{3,1},{66,322},{67,65},{128... | collective-permute-start | bytes 196616 | tf_op jit(solution)/shard_map/ppermute | solution.py:246

commit v10 on v9

--- a/solution.py
+++ b/solution.py
@@ -26,17 +26,13 @@
     return lax.dot_general(a, b, (((1,), (1,)), ((), ())), preferred_element_type=jnp.float32)
 
 
-def tile_kernel(rank_q, order_q, sorted_q, rank_k, sorted_k, *refs):
+def sort_q_kernel(rank_q, order_q, *refs):
     q_refs = refs[:2]
-    kv_ref, posq_ref, own_ref, sib_ref, dkv_ref = refs[2:7]
-    qs, gs, stats, rows, ks, vs, kt, dqt, dqn, dk, dv, todo = refs[7:]
+    qs, gs, rows, stats = refs[2:]
     n_q = qs.shape[0]
-    n_k = ks.shape[0]
     per_q = QT // HALF
-    per_k = KT // HALF
     lines = q_refs[0].shape[0]
     part_q = (q_refs[0].shape[1] - STATS) // HALF
-    part_k = kv_ref.shape[0] // HALF
 
     for a in range(2):
         for n in range(lines):
@@ -49,14 +45,6 @@
                     qs[j, pl.ds(h * QT + r, HALF), :] = q_refs[a][n, cut, h * HD:(h + 1) * HD]
                     gs[j, pl.ds(h * QT + r, HALF), :] = q_refs[a][n, cut, (HEADS + h) * HD:(HEADS + h + 1) * HD]
             stats[a * lines + n] = q_refs[a][n, part_q * HALF:, :].astype(jnp.float32)
-    for b in range(part_k):
-        place = rank_k[b]
-        i = place // per_k
-        r = pl.multiple_of(place % per_k * HALF, HALF)
-        cut = slice(b * HALF, (b + 1) * HALF)
-        ks[i, pl.ds(r, HALF), :] = kv_ref[cut, :HD]
-        vs[i, pl.ds(r, HALF), :] = kv_ref[cut, HD:]
-
     quarter = lax.broadcasted_iota(jnp.int32, (STATS, 128), 1) // HALF
     for t in range(n_q * QT // 128):
         line = jnp.zeros((STATS, 128), jnp.float32)
@@ -74,6 +62,39 @@
             rows[j, 0:1, cut] = stat[h:h + 1] * LOG2E
             rows[j, 1:2, cut] = stat[HEADS + h:HEADS + h + 1]
 
+
+def sort_q(q_parts, lists_q):
+    lines, part, width = q_parts[0].shape
+    n_q = 2 * lines * (part - STATS) // QT
+    bf, f32 = jnp.bfloat16, jnp.float32
+    tiles = jax.ShapeDtypeStruct((n_q, HEADS * QT, HD), bf)
+    return pl.pallas_call(
+        sort_q_kernel,
+        out_shape=(tiles, tiles, jax.ShapeDtypeStruct((n_q, 8, HEADS * QT), f32)),
+        in_specs=[SMEM] * 2 + [VMEM] * 2,
+        out_specs=(VMEM,) * 3,
+        scratch_shapes=[pltpu.VMEM((2 * lines, STATS, width), f32)],
+    )(lists_q[0], lists_q[1], *q_parts)
+
+
+def tile_kernel(rank_q, order_q, sorted_q, rank_k, sorted_k, *refs):
+    qs, gs, rows, kv_ref, posq_ref, own_ref, sib_ref, dkv_ref = refs[:8]
+    ks, vs, kt, dqt, dqn, dk, dv, todo = refs[8:]
+    n_q = qs.shape[0]
+    n_k = ks.shape[0]
+    per_q = QT // HALF
+    per_k = KT // HALF
+    half_q = own_ref.shape[0] // HALF
+    part_k = kv_ref.shape[0] // HALF
+
+    for b in range(part_k):
+        place = rank_k[b]
+        i = place // per_k
+        r = pl.multiple_of(place % per_k * HALF, HALF)
+        cut = slice(b * HALF, (b + 1) * HALF)
+        ks[i, pl.ds(r, HALF), :] = kv_ref[cut, :HD]
+        vs[i, pl.ds(r, HALF), :] = kv_ref[cut, HD:]
+
     for i in range(n_k):
         kt[i] = ks[i].astype(jnp.float32).T.astype(jnp.bfloat16)
 
@@ -126,8 +147,8 @@
             cut = slice(h * QT, (h + 1) * QT)
             dqn[j, cut, :] = dqt[j, :, cut].T
     for a, out in enumerate((own_ref, sib_ref)):
-        for b in range(lines * part_q):
-            place = rank_q[a * lines * part_q + b]
+        for b in range(half_q):
+            place = rank_q[a * half_q + b]
             j = place // per_q
             r = pl.multiple_of(place % per_q * HALF, HALF)
             cut = slice(b * HALF, (b + 1) * HALF)
@@ -142,9 +163,8 @@
         dkv_ref[cut, HD:] = dv[i, pl.ds(r, HALF), :].astype(jnp.bfloat16)
 
 
-def tile_grads(q_parts, kv, lists_q, lists_k):
-    lines, part = q_parts[0].shape[:2]
-    rows_q = 2 * lines * (part - STATS)
+def tile_grads(q_sorted, kv, lists_q, lists_k):
+    rows_q = q_sorted[0].shape[0] * QT
     rows_k = kv.shape[0]
     n_q, n_k = rows_q // QT, rows_k // KT
     rank_q, order_q, sorted_q = lists_q
@@ -159,13 +179,9 @@
             jax.ShapeDtypeStruct((rows_q // 2, HEADS * HD), f32),
             jax.ShapeDtypeStruct((rows_k, 2 * HD), bf),
         ),
-        in_specs=[SMEM] * 5 + [VMEM] * 4,
+        in_specs=[SMEM] * 5 + [VMEM] * 5,
         out_specs=(VMEM,) * 3,
         scratch_shapes=[
-            pltpu.VMEM((n_q, HEADS * QT, HD), bf),
-            pltpu.VMEM((n_q, HEADS * QT, HD), bf),
-            pltpu.VMEM((2 * lines, STATS, 512), f32),
-            pltpu.VMEM((n_q, 8, HEADS * QT), f32),
             pltpu.VMEM((n_k, KT, HD), bf),
             pltpu.VMEM((n_k, KT, HD), bf),
             pltpu.VMEM((n_k, HD, KT), bf),
@@ -181,7 +197,7 @@
             bytes_accessed=4 * 1024 * 1024,
             transcendentals=rows_q * HEADS * rows_k // 2,
         ),
-    )(rank_q, order_q, sorted_q, rank_k, sorted_k, *q_parts, kv, posq)
+    )(rank_q, order_q, sorted_q, rank_k, sorted_k, *q_sorted, kv, posq)
 
 
 def in_order(entries):
@@ -270,8 +286,8 @@
     ix, iyl, iz, iyh, ic = (lax.axis_index(a) for a in ("x", "yl", "z", "yh", "core"))
     iy = iyh * nyl + iyl
 
-    kv = jnp.concatenate([keys, values], axis=1)
-    kv = lax.all_to_all(jnp.broadcast_to(kv[None], (nz,) + kv.shape), "z", split_axis=0, concat_axis=0, tiled=True)
+    kv = jnp.concatenate([jnp.broadcast_to(x[None], (nz,) + x.shape) for x in (keys, values)], axis=2)
+    kv = lax.all_to_all(kv, "z", split_axis=0, concat_axis=0, tiled=True)
     kv = kv.reshape(nz * rows, 2 * HD)
     packed = pack_q(queries, out_grad, log_sum, delta)
     line = join([packed] + [from_offset(packed, 0, d) for d in (1, 2, 3)])
@@ -288,7 +304,7 @@
         at.append(((x * nyl + y % nyl) * nz + iz) * nyh * nc + y // nyl * nc + c)
     lists_q = in_order(look_up(table, both_blocks(jnp.concatenate(at))))
 
-    dq, dq_sib, dkv = tile_grads([q_own, q_sib], kv, lists_q, lists_k)
+    dq, dq_sib, dkv = tile_grads(sort_q([q_own, q_sib], lists_q), kv, lists_q, lists_k)
 
     dkv = lax.all_to_all(dkv.reshape(nz, rows, 2 * HD), "z", split_axis=0, concat_axis=0, tiled=True)
     dq = dq + other_core(dq_sib)

time: 112 us -> 121 us (1.080)
  the two profiles are of different devices: /device:TPU:24 before, /device:TPU:38 now
where the time goes in v10:
time: 121 us; the launch traced here: 120 us
  starting transfers between devices  70.6 us (58%)
  waiting for transfers between devices  18.7 us (15%)
  Pallas kernels  16.3 us (13%)
  local copies, waits for them, and re-layouts  6.75 us (6%)
  other arithmetic  6.62 us (5%)
    ppermute x12, starting transfers between devices, from_offset(): return lax.ppermute(x, ('x', 'yl', 'yh', 'core'), pairs)  38.6 us
    ppermute x12, waiting for transfers between devices, from_offset(): return lax.ppermute(x, ('x', 'yl', 'yh', 'core'), pairs)  17.5 us
    all_to_all x1, starting transfers between devices, local(): kv = lax.all_to_all(kv, 'z', split_axis=0, concat_axis=0, tiled=True)  15.2 us
    all_to_all x1, starting transfers between devices, local(): lax.all_to_all(dkv.reshape(nz, rows, 2 * HD), 'z', split_axis=0, concat_a...  12 us
    pallas_call x1, Pallas kernels, tile_grads(): pl.pallas_call(tile_kernel, out_shape=(jax.ShapeDtypeStruct((rows_q // 2,...  10.3 us
    ppermute x2, starting transfers between devices, other_core(): return lax.ppermute(x, 'core', [(0, 1), (1, 0)])  4.78 us
    pallas_call x1, Pallas kernels, sort_q(): pl.pallas_call(sort_q_kernel, out_shape=(tiles, tiles, jax.ShapeDtypeStru...  4.56 us
    unnamed x20, local copies, waits for them, and re-layouts  4.05 us
  transfers between devices with their start and end apart: 16, of which 6 were waited for; matrix products, arithmetic and copies ran while one was open for 7% of the time, Pallas kernels for 4%

profile of v10, /device:TPU:38, one launch (start us, length us, event | category | flops | bytes accessed | tf_op | source)
XLA Modules:
  0.0 120.1 jit_solution(2934338647799307761)
XLA Ops:
  0.6 1.4 %shard_map.94 = bf16[80,512]{1,0:T(8,128)(2,1)} custom-call(bf16[64,256]{1,0:T(8,128)(2,1)} %q_ref.1, bf16[64,256]{1,0:T(8,128)(2,1)} %g_ref.1, f32[2,64]{1,0:T(2,128)} %bitcast.13, f32[2,64]{1,0:T(2,128)} %bitcast.14), custom_call_target="tpu_custom_call" | custom-call | tf_op jit(solution)/shard_map/pallas_call | solution.py:240
  2.1 2.7 %collective-permute-start.2 = (bf16[80,512]{1,0:T(8,128)(2,1)}, bf16[80,512]{1,0:T(8,128)(2,1)S(1)}, u32[]{:S(2)}, u32[]{:S(2)}) collective-permute-start(bf16[80,512]{1,0:T(8,128)(2,1)} %shard_map.94), channel_id=1, source_target_pairs={{0,384},{1,67},{64,448},{65,1},{2,386},{3,65},{66,450},{67,3},{128... | collective-permute-start | bytes 245768 | tf_op jit(solution)/shard_map/ppermute | solution.py:262
  4.8 3.0 %collective-permute-start.1 = (bf16[80,512]{1,0:T(8,128)(2,1)}, bf16[80,512]{1,0:T(8,128)(2,1)S(1)}, u32[]{:S(2)}, u32[]{:S(2)}) collective-permute-start(bf16[80,512]{1,0:T(8,128)(2,1)} %shard_map.94), channel_id=1, source_target_pairs={{0,256},{1,3},{64,320},{65,67},{2,258},{3,1},{66,322},{67,65},{128... | collective-permute-start | bytes 245768 | tf_op jit(solution)/shard_map/ppermute | solution.py:262
  7.8 4.0 %collective-permute-start = (bf16[80,512]{1,0:T(8,128)(2,1)}, bf16[80,512]{1,0:T(8,128)(2,1)S(1)}, u32[]{:S(2)}, u32[]{:S(2)}) collective-permute-start(bf16[80,512]{1,0:T(8,128)(2,1)} %shard_map.94), channel_id=1, source_target_pairs={{0,128},{1,65},{64,192},{65,3},{2,130},{3,67},{66,194},{67,1},{128... | collective-permute-start | bytes 245768 | tf_op jit(solution)/shard_map/ppermute | solution.py:262
  11.8 0.8 broadcast_in_dim.90
  13.4 0.9 pad_maximum_fusion.1
  14.2 15.2 %all-to-all-start = ((bf16[16,64,256]{2,1,0:T(8,128)(2,1)}), bf16[16,64,256]{2,1,0:T(8,128)(2,1)S(1)}, u32[]{:S(2)}, u32[]{:S(2)}) async-start(bf16[16,64,256]{2,1,0:T(8,128)(2,1)} %pad_maximum_fusion.1), calls=%async_computation | async-start | bytes 1048576 | tf_op jit(solution)/shard_map/all_to_all | solution.py:290
  29.8 4.9 %collective-permute-start.5 = (bf16[272,512]{1,0:T(8,128)(2,1)S(1)}, bf16[272,512]{1,0:T(8,128)(2,1)S(1)}, u32[]{:S(2)}, u32[]{:S(2)}) collective-permute-start(bf16[272,512]{1,0:T(8,128)(2,1)S(1)} %maximum_dynamic-update-slice_fusion), channel_id=1, source_target_pairs={{0,66},{1,385},{64,0},{65,449},{2,64},{3,387},{66,2},{67,451},{128... | collective-permute-start | bytes 835592 | tf_op jit(solution)/shard_map/ppermute | solution.py:262
  34.7 2.5 %collective-permute-start.4 = (bf16[272,512]{1,0:T(8,128)(2,1)S(1)}, bf16[272,512]{1,0:T(8,128)(2,1)S(1)}, u32[]{:S(2)}, u32[]{:S(2)}) collective-permute-start(bf16[272,512]{1,0:T(8,128)(2,1)S(1)} %maximum_dynamic-update-slice_fusion), channel_id=1, source_target_pairs={{0,2},{1,257},{64,66},{65,321},{2,0},{3,259},{66,64},{67,323},{128... | collective-permute-start | bytes 835592 | tf_op jit(solution)/shard_map/ppermute | solution.py:262
  37.2 2.9 %collective-permute-start.3 = (bf16[272,512]{1,0:T(8,128)(2,1)S(1)}, bf16[272,512]{1,0:T(8,128)(2,1)S(1)}, u32[]{:S(2)}, u32[]{:S(2)}) collective-permute-start(bf16[272,512]{1,0:T(8,128)(2,1)S(1)} %maximum_dynamic-update-slice_fusion), channel_id=1, source_target_pairs={{0,64},{1,129},{64,2},{65,193},{2,66},{3,131},{66,0},{67,195},{128... | collective-permute-start | bytes 835592 | tf_op jit(solution)/shard_map/ppermute | solution.py:262
  40.6 4.1 %collective-permute-done.4 = bf16[272,512]{1,0:T(8,128)(2,1)S(1)} collective-permute-done((bf16[272,512]{1,0:T(8,128)(2,1)S(1)}, bf16[272,512]{1,0:T(8,128)(2,1)S(1)}, u32[]{:S(2)}, u32[]{:S(2)}) %collective-permute-start.4) | collective-permute-done | bytes 278560 | tf_op jit(solution)/shard_map/ppermute | solution.py:262
  44.7 2.9 %collective-permute-done.3 = bf16[272,512]{1,0:T(8,128)(2,1)S(1)} collective-permute-done((bf16[272,512]{1,0:T(8,128)(2,1)S(1)}, bf16[272,512]{1,0:T(8,128)(2,1)S(1)}, u32[]{:S(2)}, u32[]{:S(2)}) %collective-permute-start.3) | collective-permute-done | bytes 278560 | tf_op jit(solution)/shard_map/ppermute | solution.py:262
  47.6 1.1 pad_maximum_fusion.refs_0_
  48.8 1.9 %collective-permute-start.6 = (bf16[4,272,512]{2,1,0:T(8,128)(2,1)}, bf16[4,272,512]{2,1,0:T(8,128)(2,1)}, u32[]{:S(2)}, u32[]{:S(2)}) collective-permute-start(bf16[4,272,512]{2,1,0:T(8,128)(2,1)} %pad_maximum_fusion.refs_0_), channel_id=1, source_target_pairs={{0,1},{1,0},{2,3},{3,2},{4,5},{5,4},{6,7},{7,6},{8,9},{9,8},{10,11... | collective-permute-start | bytes 3342344 | tf_op jit(solution)/shard_map/ppermute | solution.py:270
  52.5 1.3 %collective-permute-done.6.refs_1_ = bf16[4,272,512]{2,1,0:T(8,128)(2,1)} collective-permute-done((bf16[4,272,512]{2,1,0:T(8,128)(2,1)}, bf16[4,272,512]{2,1,0:T(8,128)(2,1)}, u32[]{:S(2)}, u32[]{:S(2)}) %collective-permute-start.6) | collective-permute-done | bytes 1114144 | tf_op jit(solution)/shard_map/ppermute | solution.py:270
  53.7 4.6 %shard_map.95 = (bf16[8,512,128]{2,1,0:T(8,128)(2,1)}, bf16[8,512,128]{2,1,0:T(8,128)(2,1)}, f32[8,8,512]{2,1,0:T(8,128)}) custom-call(s32[64]{0:T(128)} %copy-done, s32[64]{0:T(128)} %get-tuple-element.20.order_q, bf16[4,272,512]{2,1,0:T(8,128)(2,1)} %pad_maximum_fusion.refs_0_, bf16[4,272,512]{2,1,0:T(8,128)(2,1)} %collective-permute-done.6.refs_1_), custom_call_target="tpu_custom_call" | custom-call | tf_op jit(solution)/shard_map/pallas_call | solution.py:71
  59.0 1.2 %copy-done.3 = bf16[8,512,128]{2,1,0:T(8,128)(2,1)S(1)} copy-done((bf16[8,512,128]{2,1,0:T(8,128)(2,1)S(1)}, bf16[8,512,128]{2,1,0:T(8,128)(2,1)}, u32[]{:S(2)}) %copy-start.3) | copy-done | bytes 1048600
  60.2 1.2 %copy-done.4 = bf16[8,512,128]{2,1,0:T(8,128)(2,1)S(1)} copy-done((bf16[8,512,128]{2,1,0:T(8,128)(2,1)S(1)}, bf16[8,512,128]{2,1,0:T(8,128)(2,1)}, u32[]{:S(2)}) %copy-start.4) | copy-done | bytes 1048600
  61.4 0.9 copy-done.5
  62.3 10.3 %shard_map.96 = (f32[1024,256]{1,0:T(8,128)S(1)}, f32[1024,256]{1,0:T(8,128)S(1)}, bf16[1024,256]{1,0:T(8,128)(2,1)}) custom-call(s32[64]{0:T(128)S(1)} %copy-done.1, s32[64]{0:T(128)S(1)} %copy-done.2, s32[64]{0:T(128)S(1)} %get-tuple-element.19.sorted_q, s32[32]{0:T(128)S(1)} %convert_reduce_fusion.2.rank_k, s32[32]{0:T(128)S(1)} %select_reduce_fusion.4.sorted_k, ...), custom_call_target="tpu_custom_call" | custom-call | flops 2684354560 | bytes 4194304 | tf_op jit(solution)/shard_map/pallas_call | solution.py:175
  72.7 2.9 %collective-permute-start.7 = (f32[1024,256]{1,0:T(8,128)S(1)}, f32[1024,256]{1,0:T(8,128)}, u32[]{:S(2)}, u32[]{:S(2)}) collective-permute-start(f32[1024,256]{1,0:T(8,128)S(1)} %get-tuple-element.17), channel_id=1, source_target_pairs={{0,1},{1,0},{2,3},{3,2},{4,5},{5,4},{6,7},{7,6},{8,9},{9,8},{10,11... | collective-permute-start | bytes 3145736 | tf_op jit(solution)/shard_map/ppermute | solution.py:270
  75.5 12.0 %all-to-all-start.1 = ((bf16[16,64,256]{2,1,0:T(8,128)(2,1)}), bf16[16,64,256]{2,1,0:T(8,128)(2,1)S(1)}, u32[]{:S(2)}, u32[]{:S(2)}) async-start(bf16[16,64,256]{2,1,0:T(8,128)(2,1)} %bitcast.7), calls=%async_computation.1 | async-start | bytes 1048576 | tf_op jit(solution)/shard_map/all_to_all | solution.py:309
  87.6 1.4 %fusion.19 = (bf16[1024,256]{1,0:T(8,128)(2,1)S(1)}, f32[1024,256]{1,0:T(8,128)S(1)}) fusion(f32[1024,256]{1,0:T(8,128)S(1)} %get-tuple-element.16, f32[1024,256]{1,0:T(8,128)} %collective-permute-done.7), kind=kLoop, calls=%fused_computation.82 | loop fusion | flops 524288 | bytes 3670016 | tf_op jit(solution)/shard_map/convert_element_type | solution.py:311
  89.1 2.5 %collective-permute-start.8 = (bf16[256,256]{1,0:T(8,128)(2,1)S(1)}, bf16[256,256]{1,0:T(8,128)(2,1)S(1)}, u32[]{:S(2)}, u32[]{:S(2)}) collective-permute-start(bf16[256,256]{1,0:T(8,128)(2,1)S(1)} %get-tuple-element.23), channel_id=1, source_target_pairs={{0,66},{1,385},{64,0},{65,449},{2,64},{3,387},{66,2},{67,451},{128... | collective-permute-start | bytes 393224 | tf_op jit(solution)/shard_map/ppermute | solution.py:262
  91.6 3.4 %collective-permute-start.10 = (bf16[256,256]{1,0:T(8,128)(2,1)S(1)}, bf16[256,256]{1,0:T(8,128)(2,1)S(1)}, u32[]{:S(2)}, u32[]{:S(2)}) collective-permute-start(bf16[256,256]{1,0:T(8,128)(2,1)S(1)} %get-tuple-element.24), channel_id=1, source_target_pairs={{0,64},{1,129},{64,2},{65,193},{2,66},{3,131},{66,0},{67,195},{128... | collective-permute-start | bytes 393224 | tf_op jit(solution)/shard_map/ppermute | solution.py:262
  94.9 2.9 %collective-permute-start.9 = (bf16[256,256]{1,0:T(8,128)(2,1)S(1)}, bf16[256,256]{1,0:T(8,128)(2,1)S(1)}, u32[]{:S(2)}, u32[]{:S(2)}) collective-permute-start(bf16[256,256]{1,0:T(8,128)(2,1)S(1)} %get-tuple-element.25), channel_id=1, source_target_pairs={{0,2},{1,257},{64,66},{65,321},{2,0},{3,259},{66,64},{67,323},{128... | collective-permute-start | bytes 393224 | tf_op jit(solution)/shard_map/ppermute | solution.py:262
  97.8 1.8 %collective-permute-done.10 = bf16[256,256]{1,0:T(8,128)(2,1)S(1)} collective-permute-done((bf16[256,256]{1,0:T(8,128)(2,1)S(1)}, bf16[256,256]{1,0:T(8,128)(2,1)S(1)}, u32[]{:S(2)}, u32[]{:S(2)}) %collective-permute-start.10) | collective-permute-done | bytes 131104 | tf_op jit(solution)/shard_map/ppermute | solution.py:262
  99.6 3.7 %collective-permute-done.9 = bf16[256,256]{1,0:T(8,128)(2,1)S(1)} collective-permute-done((bf16[256,256]{1,0:T(8,128)(2,1)S(1)}, bf16[256,256]{1,0:T(8,128)(2,1)S(1)}, u32[]{:S(2)}, u32[]{:S(2)}) %collective-permute-start.9) | collective-permute-done | bytes 131104 | tf_op jit(solution)/shard_map/ppermute | solution.py:262
  103.4 1.9 %collective-permute-start.11 = (f32[64,256]{1,0:T(8,128)S(1)}, f32[64,256]{1,0:T(8,128)S(1)}, u32[]{:S(2)}, u32[]{:S(2)}) collective-permute-start(f32[64,256]{1,0:T(8,128)S(1)} %get-tuple-element.26), channel_id=1, source_target_pairs={{0,384},{1,67},{64,448},{65,1},{2,386},{3,65},{66,450},{67,3},{128... | collective-permute-start | bytes 196616 | tf_op jit(solution)/shard_map/ppermute | solution.py:262
  105.3 5.1 %collective-permute-start.13 = (f32[64,256]{1,0:T(8,128)S(1)}, f32[64,256]{1,0:T(8,128)S(1)}, u32[]{:S(2)}, u32[]{:S(2)}) collective-permute-start(f32[64,256]{1,0:T(8,128)S(1)} %get-tuple-element.27), channel_id=1, source_target_pairs={{0,128},{1,65},{64,192},{65,3},{2,130},{3,67},{66,194},{67,1},{128... | collective-permute-start | bytes 196616 | tf_op jit(solution)/shard_map/ppermute | solution.py:262
  110.5 2.7 %collective-permute-start.12 = (f32[64,256]{1,0:T(8,128)S(1)}, f32[64,256]{1,0:T(8,128)S(1)}, u32[]{:S(2)}, u32[]{:S(2)}) collective-permute-start(f32[64,256]{1,0:T(8,128)S(1)} %get-tuple-element.28), channel_id=1, source_target_pairs={{0,256},{1,3},{64,320},{65,67},{2,258},{3,1},{66,322},{67,65},{128... | collective-permute-start | bytes 196616 | tf_op jit(solution)/shard_map/ppermute | solution.py:262
  113.2 4.9 %collective-permute-done.12 = f32[64,256]{1,0:T(8,128)S(1)} collective-permute-done((f32[64,256]{1,0:T(8,128)S(1)}, f32[64,256]{1,0:T(8,128)S(1)}, u32[]{:S(2)}, u32[]{:S(2)}) %collective-permute-start.12) | collective-permute-done | bytes 65568 | tf_op jit(solution)/shard_map/ppermute | solution.py:262
  (61 shorter events, 5.8 us)
Async XLA Ops:
  2.1 27.6 %collective-permute-start.2 = (bf16[80,512]{1,0:T(8,128)(2,1)}, bf16[80,512]{1,0:T(8,128)(2,1)S(1)}, u32[]{:S(2)}, u32[]{:S(2)}) collective-permute-start(bf16[80,512]{1,0:T(8,128)(2,1)} %shard_map.94), channel_id=1, source_target_pairs={{0,384},{1,67},{64,448},{65,1},{2,386},{3,65},{66,450},{67,3},{128... | collective-permute-start | bytes 245768 | tf_op jit(solution)/shard_map/ppermute | solution.py:262
  4.8 24.9 %collective-permute-start.1 = (bf16[80,512]{1,0:T(8,128)(2,1)}, bf16[80,512]{1,0:T(8,128)(2,1)S(1)}, u32[]{:S(2)}, u32[]{:S(2)}) collective-permute-start(bf16[80,512]{1,0:T(8,128)(2,1)} %shard_map.94), channel_id=1, source_target_pairs={{0,256},{1,3},{64,320},{65,67},{2,258},{3,1},{66,322},{67,65},{128... | collective-permute-start | bytes 245768 | tf_op jit(solution)/shard_map/ppermute | solution.py:262
  7.8 21.9 %collective-permute-start = (bf16[80,512]{1,0:T(8,128)(2,1)}, bf16[80,512]{1,0:T(8,128)(2,1)S(1)}, u32[]{:S(2)}, u32[]{:S(2)}) collective-permute-start(bf16[80,512]{1,0:T(8,128)(2,1)} %shard_map.94), channel_id=1, source_target_pairs={{0,128},{1,65},{64,192},{65,3},{2,130},{3,67},{66,194},{67,1},{128... | collective-permute-start | bytes 245768 | tf_op jit(solution)/shard_map/ppermute | solution.py:262
  13.4 16.1 %copy-start.6 = (bf16[80,512]{1,0:T(8,128)(2,1)S(1)}, bf16[80,512]{1,0:T(8,128)(2,1)}, u32[]{:S(2)}) copy-start(bf16[80,512]{1,0:T(8,128)(2,1)} %shard_map.94) | copy-start | bytes 245764
  14.2 44.1 %all-to-all-start = ((bf16[16,64,256]{2,1,0:T(8,128)(2,1)}), bf16[16,64,256]{2,1,0:T(8,128)(2,1)S(1)}, u32[]{:S(2)}, u32[]{:S(2)}) async-start(bf16[16,64,256]{2,1,0:T(8,128)(2,1)} %pad_maximum_fusion.1), calls=%async_computation | async-start | bytes 1048576 | tf_op jit(solution)/shard_map/all_to_all | solution.py:290
  29.8 10.8 %collective-permute-start.5 = (bf16[272,512]{1,0:T(8,128)(2,1)S(1)}, bf16[272,512]{1,0:T(8,128)(2,1)S(1)}, u32[]{:S(2)}, u32[]{:S(2)}) collective-permute-start(bf16[272,512]{1,0:T(8,128)(2,1)S(1)} %maximum_dynamic-update-slice_fusion), channel_id=1, source_target_pairs={{0,66},{1,385},{64,0},{65,449},{2,64},{3,387},{66,2},{67,451},{128... | collective-permute-start | bytes 835592 | tf_op jit(solution)/shard_map/ppermute | solution.py:262
  34.7 10.0 %collective-permute-start.4 = (bf16[272,512]{1,0:T(8,128)(2,1)S(1)}, bf16[272,512]{1,0:T(8,128)(2,1)S(1)}, u32[]{:S(2)}, u32[]{:S(2)}) collective-permute-start(bf16[272,512]{1,0:T(8,128)(2,1)S(1)} %maximum_dynamic-update-slice_fusion), channel_id=1, source_target_pairs={{0,2},{1,257},{64,66},{65,321},{2,0},{3,259},{66,64},{67,323},{128... | collective-permute-start | bytes 835592 | tf_op jit(solution)/shard_map/ppermute | solution.py:262
  37.2 10.4 %collective-permute-start.3 = (bf16[272,512]{1,0:T(8,128)(2,1)S(1)}, bf16[272,512]{1,0:T(8,128)(2,1)S(1)}, u32[]{:S(2)}, u32[]{:S(2)}) collective-permute-start(bf16[272,512]{1,0:T(8,128)(2,1)S(1)} %maximum_dynamic-update-slice_fusion), channel_id=1, source_target_pairs={{0,64},{1,129},{64,2},{65,193},{2,66},{3,131},{66,0},{67,195},{128... | collective-permute-start | bytes 835592 | tf_op jit(solution)/shard_map/ppermute | solution.py:262
  47.6 3.1 %copy-start.7 = (s32[1024]{0:T(1024)S(1)}, s32[1024]{0:T(1024)}, u32[]{:S(2)}) copy-start(s32[1024]{0:T(1024)} %param.13) | copy-start | bytes 12292
  48.8 5.0 %collective-permute-start.6 = (bf16[4,272,512]{2,1,0:T(8,128)(2,1)}, bf16[4,272,512]{2,1,0:T(8,128)(2,1)}, u32[]{:S(2)}, u32[]{:S(2)}) collective-permute-start(bf16[4,272,512]{2,1,0:T(8,128)(2,1)} %pad_maximum_fusion.refs_0_), channel_id=1, source_target_pairs={{0,1},{1,0},{2,3},{3,2},{4,5},{5,4},{6,7},{7,6},{8,9},{9,8},{10,11... | collective-permute-start | bytes 3342344 | tf_op jit(solution)/shard_map/ppermute | solution.py:270
  51.1 2.7 %copy-start = (s32[64]{0:T(128)}, s32[64]{0:T(128)S(1)}, u32[]{:S(2)}) copy-start(s32[64]{0:T(128)S(1)} %convert_reduce_fusion.1.rank_q) | copy-start | bytes 772
  53.7 4.6 %copy-start.2 = (s32[64]{0:T(128)S(1)}, s32[64]{0:T(128)}, u32[]{:S(2)}) copy-start(s32[64]{0:T(128)} %get-tuple-element.20.order_q) | copy-start | bytes 772
  58.3 0.7 copy-start.1
  59.0 1.2 %copy-start.3 = (bf16[8,512,128]{2,1,0:T(8,128)(2,1)S(1)}, bf16[8,512,128]{2,1,0:T(8,128)(2,1)}, u32[]{:S(2)}) copy-start(bf16[8,512,128]{2,1,0:T(8,128)(2,1)} %get-tuple-element.13.refs_0_) | copy-start | bytes 3145732
  60.2 1.2 %copy-start.4 = (bf16[8,512,128]{2,1,0:T(8,128)(2,1)S(1)}, bf16[8,512,128]{2,1,0:T(8,128)(2,1)}, u32[]{:S(2)}) copy-start(bf16[8,512,128]{2,1,0:T(8,128)(2,1)} %get-tuple-element.14.refs_1_) | copy-start | bytes 3145732
  61.4 0.9 copy-start.5
  72.7 14.9 %collective-permute-start.7 = (f32[1024,256]{1,0:T(8,128)S(1)}, f32[1024,256]{1,0:T(8,128)}, u32[]{:S(2)}, u32[]{:S(2)}) collective-permute-start(f32[1024,256]{1,0:T(8,128)S(1)} %get-tuple-element.17), channel_id=1, source_target_pairs={{0,1},{1,0},{2,3},{3,2},{4,5},{5,4},{6,7},{7,6},{8,9},{9,8},{10,11... | collective-permute-start | bytes 3145736 | tf_op jit(solution)/shard_map/ppermute | solution.py:270
  75.5 43.2 %all-to-all-start.1 = ((bf16[16,64,256]{2,1,0:T(8,128)(2,1)}), bf16[16,64,256]{2,1,0:T(8,128)(2,1)S(1)}, u32[]{:S(2)}, u32[]{:S(2)}) async-start(bf16[16,64,256]{2,1,0:T(8,128)(2,1)} %bitcast.7), calls=%async_computation.1 | async-start | bytes 1048576 | tf_op jit(solution)/shard_map/all_to_all | solution.py:309
  89.1 8.7 %collective-permute-start.8 = (bf16[256,256]{1,0:T(8,128)(2,1)S(1)}, bf16[256,256]{1,0:T(8,128)(2,1)S(1)}, u32[]{:S(2)}, u32[]{:S(2)}) collective-permute-start(bf16[256,256]{1,0:T(8,128)(2,1)S(1)} %get-tuple-element.23), channel_id=1, source_target_pairs={{0,66},{1,385},{64,0},{65,449},{2,64},{3,387},{66,2},{67,451},{128... | collective-permute-start | bytes 393224 | tf_op jit(solution)/shard_map/ppermute | solution.py:262
  91.6 8.1 %collective-permute-start.10 = (bf16[256,256]{1,0:T(8,128)(2,1)S(1)}, bf16[256,256]{1,0:T(8,128)(2,1)S(1)}, u32[]{:S(2)}, u32[]{:S(2)}) collective-permute-start(bf16[256,256]{1,0:T(8,128)(2,1)S(1)} %get-tuple-element.24), channel_id=1, source_target_pairs={{0,64},{1,129},{64,2},{65,193},{2,66},{3,131},{66,0},{67,195},{128... | collective-permute-start | bytes 393224 | tf_op jit(solution)/shard_map/ppermute | solution.py:262
  94.9 8.4 %collective-permute-start.9 = (bf16[256,256]{1,0:T(8,128)(2,1)S(1)}, bf16[256,256]{1,0:T(8,128)(2,1)S(1)}, u32[]{:S(2)}, u32[]{:S(2)}) collective-permute-start(bf16[256,256]{1,0:T(8,128)(2,1)S(1)} %get-tuple-element.25), channel_id=1, source_target_pairs={{0,2},{1,257},{64,66},{65,321},{2,0},{3,259},{66,64},{67,323},{128... | collective-permute-start | bytes 393224 | tf_op jit(solution)/shard_map/ppermute | solution.py:262
  103.4 9.8 %collective-permute-start.11 = (f32[64,256]{1,0:T(8,128)S(1)}, f32[64,256]{1,0:T(8,128)S(1)}, u32[]{:S(2)}, u32[]{:S(2)}) collective-permute-start(f32[64,256]{1,0:T(8,128)S(1)} %get-tuple-element.26), channel_id=1, source_target_pairs={{0,384},{1,67},{64,448},{65,1},{2,386},{3,65},{66,450},{67,3},{128... | collective-permute-start | bytes 196616 | tf_op jit(solution)/shard_map/ppermute | solution.py:262
  105.3 7.9 %collective-permute-start.13 = (f32[64,256]{1,0:T(8,128)S(1)}, f32[64,256]{1,0:T(8,128)S(1)}, u32[]{:S(2)}, u32[]{:S(2)}) collective-permute-start(f32[64,256]{1,0:T(8,128)S(1)} %get-tuple-element.27), channel_id=1, source_target_pairs={{0,128},{1,65},{64,192},{65,3},{2,130},{3,67},{66,194},{67,1},{128... | collective-permute-start | bytes 196616 | tf_op jit(solution)/shard_map/ppermute | solution.py:262
  110.5 7.7 %collective-permute-start.12 = (f32[64,256]{1,0:T(8,128)S(1)}, f32[64,256]{1,0:T(8,128)S(1)}, u32[]{:S(2)}, u32[]{:S(2)}) collective-permute-start(f32[64,256]{1,0:T(8,128)S(1)} %get-tuple-element.28), channel_id=1, source_target_pairs={{0,256},{1,3},{64,320},{65,67},{2,258},{3,1},{66,322},{67,65},{128... | collective-permute-start | bytes 196616 | tf_op jit(solution)/shard_map/ppermute | solution.py:262

commit v11 on v9

--- a/solution.py
+++ b/solution.py
@@ -132,7 +132,7 @@
             r = pl.multiple_of(place % per_q * HALF, HALF)
             cut = slice(b * HALF, (b + 1) * HALF)
             for h in range(HEADS):
-                out[cut, h * HD:(h + 1) * HD] = dqn[j, pl.ds(h * QT + r, HALF), :]
+                out[cut, h * HD:(h + 1) * HD] = dqn[j, pl.ds(h * QT + r, HALF), :].astype(out.dtype)
     for b in range(part_k):
         place = rank_k[b]
         i = place // per_k
@@ -156,7 +156,7 @@
         tile_kernel,
         out_shape=(
             jax.ShapeDtypeStruct((rows_q // 2, HEADS * HD), f32),
-            jax.ShapeDtypeStruct((rows_q // 2, HEADS * HD), f32),
+            jax.ShapeDtypeStruct((rows_q // 2, HEADS * HD), bf),
             jax.ShapeDtypeStruct((rows_k, 2 * HD), bf),
         ),
         in_specs=[SMEM] * 5 + [VMEM] * 4,
@@ -291,7 +291,7 @@
     dq, dq_sib, dkv = tile_grads([q_own, q_sib], kv, lists_q, lists_k)
 
     dkv = lax.all_to_all(dkv.reshape(nz, rows, 2 * HD), "z", split_axis=0, concat_axis=0, tiled=True)
-    dq = dq + other_core(dq_sib)
+    dq = dq + other_core(dq_sib).astype(jnp.float32)
     near, far = dq[:4 * rows], dq.astype(jnp.bfloat16)
     far = far.reshape(4, 4 * rows, width)
     for d in (1, 2, 3):

time: 112 us -> 112 us (level)
  no operation moved by 1% of the time
where the time goes in v11:
time: 112 us; the launch traced here: 110 us
  starting transfers between devices  66.7 us (60%)
  waiting for transfers between devices  22.1 us (20%)
  Pallas kernels  14.8 us (13%)
  other arithmetic  3.67 us (3%)
  local copies, waits for them, and re-layouts  2.07 us (2%)
    ppermute x12, starting transfers between devices, from_offset(): return lax.ppermute(x, ('x', 'yl', 'yh', 'core'), pairs)  40.7 us
    all_to_all x1, starting transfers between devices, local(): lax.all_to_all(jnp.broadcast_to(kv[None], (nz,) + kv.shape), 'z', split_a...  15.2 us
    ppermute x12, waiting for transfers between devices, from_offset(): return lax.ppermute(x, ('x', 'yl', 'yh', 'core'), pairs)  14.2 us
    pallas_call x1, Pallas kernels, tile_grads(): pl.pallas_call(tile_kernel, out_shape=(jax.ShapeDtypeStruct((rows_q // 2,...  13.3 us
    all_to_all x1, starting transfers between devices, local(): lax.all_to_all(dkv.reshape(nz, rows, 2 * HD), 'z', split_axis=0, concat_a...  6.98 us
    all_to_all x1, waiting for transfers between devices, local(): lax.all_to_all(jnp.broadcast_to(kv[None], (nz,) + kv.shape), 'z', split_a...  6.36 us
    ppermute x2, starting transfers between devices, other_core(): return lax.ppermute(x, 'core', [(0, 1), (1, 0)])  3.83 us
  transfers between devices with their start and end apart: 16, of which 7 were waited for; matrix products, arithmetic and copies ran while one was open for 4% of the time, Pallas kernels for 0%

profile of v11, /device:TPU:24, one launch (start us, length us, event | category | flops | bytes accessed | tf_op | source)
XLA Modules:
  0.0 110.3 jit_solution(3007574880541127778)
XLA Ops:
  0.6 1.4 %shard_map.94 = bf16[80,512]{1,0:T(8,128)(2,1)} custom-call(bf16[64,256]{1,0:T(8,128)(2,1)} %q_ref.1, bf16[64,256]{1,0:T(8,128)(2,1)} %g_ref.1, f32[2,64]{1,0:T(2,128)} %bitcast.13, f32[2,64]{1,0:T(2,128)} %bitcast.14), custom_call_target="tpu_custom_call" | custom-call | tf_op jit(solution)/shard_map/pallas_call | solution.py:224
  2.1 4.8 %collective-permute-start.2 = (bf16[80,512]{1,0:T(8,128)(2,1)}, bf16[80,512]{1,0:T(8,128)(2,1)S(1)}, u32[]{:S(2)}, u32[]{:S(2)}) collective-permute-start(bf16[80,512]{1,0:T(8,128)(2,1)} %shard_map.94), channel_id=1, source_target_pairs={{0,384},{1,67},{64,448},{65,1},{2,386},{3,65},{66,450},{67,3},{128... | collective-permute-start | bytes 245768 | tf_op jit(solution)/shard_map/ppermute | solution.py:246
  6.8 2.7 %collective-permute-start.1 = (bf16[80,512]{1,0:T(8,128)(2,1)}, bf16[80,512]{1,0:T(8,128)(2,1)S(1)}, u32[]{:S(2)}, u32[]{:S(2)}) collective-permute-start(bf16[80,512]{1,0:T(8,128)(2,1)} %shard_map.94), channel_id=1, source_target_pairs={{0,256},{1,3},{64,320},{65,67},{2,258},{3,1},{66,322},{67,65},{128... | collective-permute-start | bytes 245768 | tf_op jit(solution)/shard_map/ppermute | solution.py:246
  9.6 2.8 %collective-permute-start = (bf16[80,512]{1,0:T(8,128)(2,1)}, bf16[80,512]{1,0:T(8,128)(2,1)S(1)}, u32[]{:S(2)}, u32[]{:S(2)}) collective-permute-start(bf16[80,512]{1,0:T(8,128)(2,1)} %shard_map.94), channel_id=1, source_target_pairs={{0,128},{1,65},{64,192},{65,3},{2,130},{3,67},{66,194},{67,1},{128... | collective-permute-start | bytes 245768 | tf_op jit(solution)/shard_map/ppermute | solution.py:246
  12.4 0.7 pad_maximum_fusion.1
  13.1 0.9 broadcast_in_dim.84
  14.0 15.2 %all-to-all-start = ((bf16[16,64,256]{2,1,0:T(8,128)(2,1)}), bf16[16,64,256]{2,1,0:T(8,128)(2,1)S(1)}, u32[]{:S(2)}, u32[]{:S(2)}) async-start(bf16[16,64,256]{2,1,0:T(8,128)(2,1)} %broadcast_in_dim.84), calls=%async_computation | async-start | bytes 1048576 | tf_op jit(solution)/shard_map/all_to_all | solution.py:274
  29.5 2.7 %collective-permute-start.5 = (bf16[272,512]{1,0:T(8,128)(2,1)S(1)}, bf16[272,512]{1,0:T(8,128)(2,1)S(1)}, u32[]{:S(2)}, u32[]{:S(2)}) collective-permute-start(bf16[272,512]{1,0:T(8,128)(2,1)S(1)} %maximum_dynamic-update-slice_fusion), channel_id=1, source_target_pairs={{0,66},{1,385},{64,0},{65,449},{2,64},{3,387},{66,2},{67,451},{128... | collective-permute-start | bytes 835592 | tf_op jit(solution)/shard_map/ppermute | solution.py:246
  32.1 2.8 %collective-permute-start.4 = (bf16[272,512]{1,0:T(8,128)(2,1)S(1)}, bf16[272,512]{1,0:T(8,128)(2,1)S(1)}, u32[]{:S(2)}, u32[]{:S(2)}) collective-permute-start(bf16[272,512]{1,0:T(8,128)(2,1)S(1)} %maximum_dynamic-update-slice_fusion), channel_id=1, source_target_pairs={{0,2},{1,257},{64,66},{65,321},{2,0},{3,259},{66,64},{67,323},{128... | collective-permute-start | bytes 835592 | tf_op jit(solution)/shard_map/ppermute | solution.py:246
  35.0 4.1 %collective-permute-start.3 = (bf16[272,512]{1,0:T(8,128)(2,1)S(1)}, bf16[272,512]{1,0:T(8,128)(2,1)S(1)}, u32[]{:S(2)}, u32[]{:S(2)}) collective-permute-start(bf16[272,512]{1,0:T(8,128)(2,1)S(1)} %maximum_dynamic-update-slice_fusion), channel_id=1, source_target_pairs={{0,64},{1,129},{64,2},{65,193},{2,66},{3,131},{66,0},{67,195},{128... | collective-permute-start | bytes 835592 | tf_op jit(solution)/shard_map/ppermute | solution.py:246
  39.5 2.6 %collective-permute-done.4 = bf16[272,512]{1,0:T(8,128)(2,1)S(1)} collective-permute-done((bf16[272,512]{1,0:T(8,128)(2,1)S(1)}, bf16[272,512]{1,0:T(8,128)(2,1)S(1)}, u32[]{:S(2)}, u32[]{:S(2)}) %collective-permute-start.4) | collective-permute-done | bytes 278560 | tf_op jit(solution)/shard_map/ppermute | solution.py:246
  42.1 2.8 %collective-permute-done.3 = bf16[272,512]{1,0:T(8,128)(2,1)S(1)} collective-permute-done((bf16[272,512]{1,0:T(8,128)(2,1)S(1)}, bf16[272,512]{1,0:T(8,128)(2,1)S(1)}, u32[]{:S(2)}, u32[]{:S(2)}) %collective-permute-start.3) | collective-permute-done | bytes 278560 | tf_op jit(solution)/shard_map/ppermute | solution.py:246
  45.0 1.9 %collective-permute-start.6 = (bf16[4,272,512]{2,1,0:T(8,128)(2,1)S(1)}, bf16[4,272,512]{2,1,0:T(8,128)(2,1)}, u32[]{:S(2)}, u32[]{:S(2)}) collective-permute-start(bf16[4,272,512]{2,1,0:T(8,128)(2,1)S(1)} %pad_maximum_fusion.refs_0_), channel_id=1, source_target_pairs={{0,1},{1,0},{2,3},{3,2},{4,5},{5,4},{6,7},{7,6},{8,9},{9,8},{10,11... | collective-permute-start | bytes 3342344 | tf_op jit(solution)/shard_map/ppermute | solution.py:254
  47.0 0.2 select_reduce_fusion
  47.8 0.2 select_reduce_fusion.1
  48.3 1.6 %collective-permute-done.6.refs_1_ = bf16[4,272,512]{2,1,0:T(8,128)(2,1)} collective-permute-done((bf16[4,272,512]{2,1,0:T(8,128)(2,1)S(1)}, bf16[4,272,512]{2,1,0:T(8,128)(2,1)}, u32[]{:S(2)}, u32[]{:S(2)}) %collective-permute-start.6) | collective-permute-done | bytes 1114144 | tf_op jit(solution)/shard_map/ppermute | solution.py:254
  49.8 6.4 %all-to-all-done = bf16[16,64,256]{2,1,0:T(8,128)(2,1)S(1)} async-done(((bf16[16,64,256]{2,1,0:T(8,128)(2,1)}), bf16[16,64,256]{2,1,0:T(8,128)(2,1)S(1)}, u32[]{:S(2)}, u32[]{:S(2)}) %all-to-all-start) | async-done | bytes 524320 | tf_op jit(solution)/shard_map/all_to_all | solution.py:274
  56.2 13.3 %shard_map.95 = (f32[1024,256]{1,0:T(8,128)S(1)}, bf16[1024,256]{1,0:T(8,128)(2,1)S(1)}, bf16[1024,256]{1,0:T(8,128)(2,1)}) custom-call(s32[64]{0:T(128)S(1)} %convert_reduce_fusion.1.rank_q, s32[64]{0:T(128)S(1)} %get-tuple-element.14.order_q, s32[64]{0:T(128)S(1)} %get-tuple-element.13.sorted_q, s32[32]{0:T(128)S(1)} %convert_reduce_fusion.2.rank_k, ...), custom_call_target="tpu_custom_call" | custom-call | flops 2684354560 | bytes 4194304 | tf_op jit(solution)/shard_map/pallas_call | solution.py:155
  69.5 1.9 %collective-permute-start.7 = (bf16[1024,256]{1,0:T(8,128)(2,1)S(1)}, bf16[1024,256]{1,0:T(8,128)(2,1)S(1)}, u32[]{:S(2)}, u32[]{:S(2)}) collective-permute-start(bf16[1024,256]{1,0:T(8,128)(2,1)S(1)} %get-tuple-element.11), channel_id=1, source_target_pairs={{0,1},{1,0},{2,3},{3,2},{4,5},{5,4},{6,7},{7,6},{8,9},{9,8},{10,11... | collective-permute-start | bytes 1572872 | tf_op jit(solution)/shard_map/ppermute | solution.py:254
  71.4 7.0 %all-to-all-start.1 = ((bf16[16,64,256]{2,1,0:T(8,128)(2,1)}), bf16[16,64,256]{2,1,0:T(8,128)(2,1)S(1)}, u32[]{:S(2)}, u32[]{:S(2)}) async-start(bf16[16,64,256]{2,1,0:T(8,128)(2,1)} %bitcast.7), calls=%async_computation.1 | async-start | bytes 1048576 | tf_op jit(solution)/shard_map/all_to_all | solution.py:293
  78.6 2.4 %collective-permute-start.8 = (bf16[256,256]{1,0:T(8,128)(2,1)S(1)}, bf16[256,256]{1,0:T(8,128)(2,1)S(1)}, u32[]{:S(2)}, u32[]{:S(2)}) collective-permute-start(bf16[256,256]{1,0:T(8,128)(2,1)S(1)} %get-tuple-element.17), channel_id=1, source_target_pairs={{0,66},{1,385},{64,0},{65,449},{2,64},{3,387},{66,2},{67,451},{128... | collective-permute-start | bytes 393224 | tf_op jit(solution)/shard_map/ppermute | solution.py:246
  81.0 4.6 %collective-permute-start.10 = (bf16[256,256]{1,0:T(8,128)(2,1)S(1)}, bf16[256,256]{1,0:T(8,128)(2,1)S(1)}, u32[]{:S(2)}, u32[]{:S(2)}) collective-permute-start(bf16[256,256]{1,0:T(8,128)(2,1)S(1)} %get-tuple-element.18), channel_id=1, source_target_pairs={{0,64},{1,129},{64,2},{65,193},{2,66},{3,131},{66,0},{67,195},{128... | collective-permute-start | bytes 393224 | tf_op jit(solution)/shard_map/ppermute | solution.py:246
  85.7 3.0 %collective-permute-start.9 = (bf16[256,256]{1,0:T(8,128)(2,1)S(1)}, bf16[256,256]{1,0:T(8,128)(2,1)S(1)}, u32[]{:S(2)}, u32[]{:S(2)}) collective-permute-start(bf16[256,256]{1,0:T(8,128)(2,1)S(1)} %get-tuple-element.19), channel_id=1, source_target_pairs={{0,2},{1,257},{64,66},{65,321},{2,0},{3,259},{66,64},{67,323},{128... | collective-permute-start | bytes 393224 | tf_op jit(solution)/shard_map/ppermute | solution.py:246
  88.7 5.3 %collective-permute-done.9 = bf16[256,256]{1,0:T(8,128)(2,1)S(1)} collective-permute-done((bf16[256,256]{1,0:T(8,128)(2,1)S(1)}, bf16[256,256]{1,0:T(8,128)(2,1)S(1)}, u32[]{:S(2)}, u32[]{:S(2)}) %collective-permute-start.9) | collective-permute-done | bytes 131104 | tf_op jit(solution)/shard_map/ppermute | solution.py:246
  94.1 4.7 %collective-permute-start.11 = (f32[64,256]{1,0:T(8,128)S(1)}, f32[64,256]{1,0:T(8,128)S(1)}, u32[]{:S(2)}, u32[]{:S(2)}) collective-permute-start(f32[64,256]{1,0:T(8,128)S(1)} %get-tuple-element.20), channel_id=1, source_target_pairs={{0,384},{1,67},{64,448},{65,1},{2,386},{3,65},{66,450},{67,3},{128... | collective-permute-start | bytes 196616 | tf_op jit(solution)/shard_map/ppermute | solution.py:246
  98.8 1.9 %collective-permute-start.13 = (f32[64,256]{1,0:T(8,128)S(1)}, f32[64,256]{1,0:T(8,128)S(1)}, u32[]{:S(2)}, u32[]{:S(2)}) collective-permute-start(f32[64,256]{1,0:T(8,128)S(1)} %get-tuple-element.21), channel_id=1, source_target_pairs={{0,128},{1,65},{64,192},{65,3},{2,130},{3,67},{66,194},{67,1},{128... | collective-permute-start | bytes 196616 | tf_op jit(solution)/shard_map/ppermute | solution.py:246
  100.7 4.2 %collective-permute-start.12 = (f32[64,256]{1,0:T(8,128)S(1)}, f32[64,256]{1,0:T(8,128)S(1)}, u32[]{:S(2)}, u32[]{:S(2)}) collective-permute-start(f32[64,256]{1,0:T(8,128)S(1)} %get-tuple-element.22), channel_id=1, source_target_pairs={{0,256},{1,3},{64,320},{65,67},{2,258},{3,1},{66,322},{67,65},{128... | collective-permute-start | bytes 196616 | tf_op jit(solution)/shard_map/ppermute | solution.py:246
  104.9 1.2 %collective-permute-done.13 = f32[64,256]{1,0:T(8,128)S(1)} collective-permute-done((f32[64,256]{1,0:T(8,128)S(1)}, f32[64,256]{1,0:T(8,128)S(1)}, u32[]{:S(2)}, u32[]{:S(2)}) %collective-permute-start.13) | collective-permute-done | bytes 65568 | tf_op jit(solution)/shard_map/ppermute | solution.py:246
  106.2 2.2 %collective-permute-done.12 = f32[64,256]{1,0:T(8,128)S(1)} collective-permute-done((f32[64,256]{1,0:T(8,128)S(1)}, f32[64,256]{1,0:T(8,128)S(1)}, u32[]{:S(2)}, u32[]{:S(2)}) %collective-permute-start.12) | collective-permute-done | bytes 65568 | tf_op jit(solution)/shard_map/ppermute | solution.py:246
  108.4 0.6 fusion.5
  109.1 0.6 slice.120
  109.7 0.6 fusion.6
  (47 shorter events, 1.9 us)
Async XLA Ops:
  2.1 27.1 %copy-start = (bf16[80,512]{1,0:T(8,128)(2,1)S(1)}, bf16[80,512]{1,0:T(8,128)(2,1)}, u32[]{:S(2)}) copy-start(bf16[80,512]{1,0:T(8,128)(2,1)} %shard_map.94) | copy-start | bytes 245764
  2.1 27.3 %collective-permute-start.2 = (bf16[80,512]{1,0:T(8,128)(2,1)}, bf16[80,512]{1,0:T(8,128)(2,1)S(1)}, u32[]{:S(2)}, u32[]{:S(2)}) collective-permute-start(bf16[80,512]{1,0:T(8,128)(2,1)} %shard_map.94), channel_id=1, source_target_pairs={{0,384},{1,67},{64,448},{65,1},{2,386},{3,65},{66,450},{67,3},{128... | collective-permute-start | bytes 245768 | tf_op jit(solution)/shard_map/ppermute | solution.py:246
  6.8 22.5 %collective-permute-start.1 = (bf16[80,512]{1,0:T(8,128)(2,1)}, bf16[80,512]{1,0:T(8,128)(2,1)S(1)}, u32[]{:S(2)}, u32[]{:S(2)}) collective-permute-start(bf16[80,512]{1,0:T(8,128)(2,1)} %shard_map.94), channel_id=1, source_target_pairs={{0,256},{1,3},{64,320},{65,67},{2,258},{3,1},{66,322},{67,65},{128... | collective-permute-start | bytes 245768 | tf_op jit(solution)/shard_map/ppermute | solution.py:246
  9.6 19.8 %collective-permute-start = (bf16[80,512]{1,0:T(8,128)(2,1)}, bf16[80,512]{1,0:T(8,128)(2,1)S(1)}, u32[]{:S(2)}, u32[]{:S(2)}) collective-permute-start(bf16[80,512]{1,0:T(8,128)(2,1)} %shard_map.94), channel_id=1, source_target_pairs={{0,128},{1,65},{64,192},{65,3},{2,130},{3,67},{66,194},{67,1},{128... | collective-permute-start | bytes 245768 | tf_op jit(solution)/shard_map/ppermute | solution.py:246
  14.0 42.2 %all-to-all-start = ((bf16[16,64,256]{2,1,0:T(8,128)(2,1)}), bf16[16,64,256]{2,1,0:T(8,128)(2,1)S(1)}, u32[]{:S(2)}, u32[]{:S(2)}) async-start(bf16[16,64,256]{2,1,0:T(8,128)(2,1)} %broadcast_in_dim.84), calls=%async_computation | async-start | bytes 1048576 | tf_op jit(solution)/shard_map/all_to_all | solution.py:274
  29.5 10.1 %collective-permute-start.5 = (bf16[272,512]{1,0:T(8,128)(2,1)S(1)}, bf16[272,512]{1,0:T(8,128)(2,1)S(1)}, u32[]{:S(2)}, u32[]{:S(2)}) collective-permute-start(bf16[272,512]{1,0:T(8,128)(2,1)S(1)} %maximum_dynamic-update-slice_fusion), channel_id=1, source_target_pairs={{0,66},{1,385},{64,0},{65,449},{2,64},{3,387},{66,2},{67,451},{128... | collective-permute-start | bytes 835592 | tf_op jit(solution)/shard_map/ppermute | solution.py:246
  32.1 10.0 %collective-permute-start.4 = (bf16[272,512]{1,0:T(8,128)(2,1)S(1)}, bf16[272,512]{1,0:T(8,128)(2,1)S(1)}, u32[]{:S(2)}, u32[]{:S(2)}) collective-permute-start(bf16[272,512]{1,0:T(8,128)(2,1)S(1)} %maximum_dynamic-update-slice_fusion), channel_id=1, source_target_pairs={{0,2},{1,257},{64,66},{65,321},{2,0},{3,259},{66,64},{67,323},{128... | collective-permute-start | bytes 835592 | tf_op jit(solution)/shard_map/ppermute | solution.py:246
  35.0 9.9 %collective-permute-start.3 = (bf16[272,512]{1,0:T(8,128)(2,1)S(1)}, bf16[272,512]{1,0:T(8,128)(2,1)S(1)}, u32[]{:S(2)}, u32[]{:S(2)}) collective-permute-start(bf16[272,512]{1,0:T(8,128)(2,1)S(1)} %maximum_dynamic-update-slice_fusion), channel_id=1, source_target_pairs={{0,64},{1,129},{64,2},{65,193},{2,66},{3,131},{66,0},{67,195},{128... | collective-permute-start | bytes 835592 | tf_op jit(solution)/shard_map/ppermute | solution.py:246
  44.9 2.1 %copy-start.1 = (s32[1024]{0:T(1024)S(1)}, s32[1024]{0:T(1024)}, u32[]{:S(2)}) copy-start(s32[1024]{0:T(1024)} %param.13) | copy-start | bytes 12292
  45.0 4.8 %collective-permute-start.6 = (bf16[4,272,512]{2,1,0:T(8,128)(2,1)S(1)}, bf16[4,272,512]{2,1,0:T(8,128)(2,1)}, u32[]{:S(2)}, u32[]{:S(2)}) collective-permute-start(bf16[4,272,512]{2,1,0:T(8,128)(2,1)S(1)} %pad_maximum_fusion.refs_0_), channel_id=1, source_target_pairs={{0,1},{1,0},{2,3},{3,2},{4,5},{5,4},{6,7},{7,6},{8,9},{9,8},{10,11... | collective-permute-start | bytes 3342344 | tf_op jit(solution)/shard_map/ppermute | solution.py:254
  69.5 8.9 %collective-permute-start.7 = (bf16[1024,256]{1,0:T(8,128)(2,1)S(1)}, bf16[1024,256]{1,0:T(8,128)(2,1)S(1)}, u32[]{:S(2)}, u32[]{:S(2)}) collective-permute-start(bf16[1024,256]{1,0:T(8,128)(2,1)S(1)} %get-tuple-element.11), channel_id=1, source_target_pairs={{0,1},{1,0},{2,3},{3,2},{4,5},{5,4},{6,7},{7,6},{8,9},{9,8},{10,11... | collective-permute-start | bytes 1572872 | tf_op jit(solution)/shard_map/ppermute | solution.py:254
  71.4 37.6 %all-to-all-start.1 = ((bf16[16,64,256]{2,1,0:T(8,128)(2,1)}), bf16[16,64,256]{2,1,0:T(8,128)(2,1)S(1)}, u32[]{:S(2)}, u32[]{:S(2)}) async-start(bf16[16,64,256]{2,1,0:T(8,128)(2,1)} %bitcast.7), calls=%async_computation.1 | async-start | bytes 1048576 | tf_op jit(solution)/shard_map/all_to_all | solution.py:293
  78.6 10.1 %collective-permute-start.8 = (bf16[256,256]{1,0:T(8,128)(2,1)S(1)}, bf16[256,256]{1,0:T(8,128)(2,1)S(1)}, u32[]{:S(2)}, u32[]{:S(2)}) collective-permute-start(bf16[256,256]{1,0:T(8,128)(2,1)S(1)} %get-tuple-element.17), channel_id=1, source_target_pairs={{0,66},{1,385},{64,0},{65,449},{2,64},{3,387},{66,2},{67,451},{128... | collective-permute-start | bytes 393224 | tf_op jit(solution)/shard_map/ppermute | solution.py:246
  81.0 7.6 %collective-permute-start.10 = (bf16[256,256]{1,0:T(8,128)(2,1)S(1)}, bf16[256,256]{1,0:T(8,128)(2,1)S(1)}, u32[]{:S(2)}, u32[]{:S(2)}) collective-permute-start(bf16[256,256]{1,0:T(8,128)(2,1)S(1)} %get-tuple-element.18), channel_id=1, source_target_pairs={{0,64},{1,129},{64,2},{65,193},{2,66},{3,131},{66,0},{67,195},{128... | collective-permute-start | bytes 393224 | tf_op jit(solution)/shard_map/ppermute | solution.py:246
  85.7 8.4 %collective-permute-start.9 = (bf16[256,256]{1,0:T(8,128)(2,1)S(1)}, bf16[256,256]{1,0:T(8,128)(2,1)S(1)}, u32[]{:S(2)}, u32[]{:S(2)}) collective-permute-start(bf16[256,256]{1,0:T(8,128)(2,1)S(1)} %get-tuple-element.19), channel_id=1, source_target_pairs={{0,2},{1,257},{64,66},{65,321},{2,0},{3,259},{66,64},{67,323},{128... | collective-permute-start | bytes 393224 | tf_op jit(solution)/shard_map/ppermute | solution.py:246
  94.1 10.8 %collective-permute-start.11 = (f32[64,256]{1,0:T(8,128)S(1)}, f32[64,256]{1,0:T(8,128)S(1)}, u32[]{:S(2)}, u32[]{:S(2)}) collective-permute-start(f32[64,256]{1,0:T(8,128)S(1)} %get-tuple-element.20), channel_id=1, source_target_pairs={{0,384},{1,67},{64,448},{65,1},{2,386},{3,65},{66,450},{67,3},{128... | collective-permute-start | bytes 196616 | tf_op jit(solution)/shard_map/ppermute | solution.py:246
  98.8 7.4 %collective-permute-start.13 = (f32[64,256]{1,0:T(8,128)S(1)}, f32[64,256]{1,0:T(8,128)S(1)}, u32[]{:S(2)}, u32[]{:S(2)}) collective-permute-start(f32[64,256]{1,0:T(8,128)S(1)} %get-tuple-element.21), channel_id=1, source_target_pairs={{0,128},{1,65},{64,192},{65,3},{2,130},{3,67},{66,194},{67,1},{128... | collective-permute-start | bytes 196616 | tf_op jit(solution)/shard_map/ppermute | solution.py:246
  100.7 7.7 %collective-permute-start.12 = (f32[64,256]{1,0:T(8,128)S(1)}, f32[64,256]{1,0:T(8,128)S(1)}, u32[]{:S(2)}, u32[]{:S(2)}) collective-permute-start(f32[64,256]{1,0:T(8,128)S(1)} %get-tuple-element.22), channel_id=1, source_target_pairs={{0,256},{1,3},{64,320},{65,67},{2,258},{3,1},{66,322},{67,65},{128... | collective-permute-start | bytes 196616 | tf_op jit(solution)/shard_map/ppermute | solution.py:246

commit v12 on v11

--- a/solution.py
+++ b/solution.py
@@ -299,7 +299,7 @@
     near = near.reshape(4, rows, width)
     total = near[0]
     for d in (1, 2, 3):
-        total = total + from_offset(near[d], 0, 4 - d)
+        total = total + from_offset(near[d].astype(jnp.bfloat16), 0, 4 - d).astype(jnp.float32)
     q_grad = (total * SCALE).astype(jnp.bfloat16)
     dkv = jnp.sum(dkv.astype(jnp.float32), axis=0)
     k_grad = (dkv[:, :HD] * SCALE).astype(jnp.bfloat16)

time: 112 us -> 113 us (level)
  waiting for transfers between devices: 22.1 us -> 23.6 us
    ppermute x2, waiting for transfers between devices: 1.55 us -> 3.43 us  [other_core(): return lax.ppermute(x, 'core', [(0, 1), (1, 0)])]
  transfers between devices with their start and end apart: 16 -> 16, of which waited for: 7 -> 8; matrix products, arithmetic and copies ran while one was open for 4% -> 4% of each run, Pallas kernels for 0% -> 0%
where the time goes in v12:
time: 113 us; the launch traced here: 112 us
  starting transfers between devices  66.7 us (59%)
  waiting for transfers between devices  23.6 us (21%)
  Pallas kernels  14.8 us (13%)
  other arithmetic  3.68 us (3%)
  local copies, waits for them, and re-layouts  2.08 us (2%)
    ppermute x12, starting transfers between devices, from_offset(): return lax.ppermute(x, ('x', 'yl', 'yh', 'core'), pairs)  40.7 us
    all_to_all x1, starting transfers between devices, local(): lax.all_to_all(jnp.broadcast_to(kv[None], (nz,) + kv.shape), 'z', split_a...  15.2 us
    ppermute x12, waiting for transfers between devices, from_offset(): return lax.ppermute(x, ('x', 'yl', 'yh', 'core'), pairs)  13.8 us
    pallas_call x1, Pallas kernels, tile_grads(): pl.pallas_call(tile_kernel, out_shape=(jax.ShapeDtypeStruct((rows_q // 2,...  13.4 us
    all_to_all x1, starting transfers between devices, local(): lax.all_to_all(dkv.reshape(nz, rows, 2 * HD), 'z', split_axis=0, concat_a...  6.96 us
    all_to_all x1, waiting for transfers between devices, local(): lax.all_to_all(jnp.broadcast_to(kv[None], (nz,) + kv.shape), 'z', split_a...  6.36 us
    ppermute x2, starting transfers between devices, other_core(): return lax.ppermute(x, 'core', [(0, 1), (1, 0)])  3.84 us
    ppermute x2, waiting for transfers between devices, other_core(): return lax.ppermute(x, 'core', [(0, 1), (1, 0)])  3.43 us
  transfers between devices with their start and end apart: 16, of which 8 were waited for; matrix products, arithmetic and copies ran while one was open for 4% of the time, Pallas kernels for 0%

profile of v12, /device:TPU:24, one launch (start us, length us, event | category | flops | bytes accessed | tf_op | source)
XLA Modules:
  0.0 111.9 jit_solution(9468338660107291635)
XLA Ops:
  0.6 1.4 %shard_map.94 = bf16[80,512]{1,0:T(8,128)(2,1)} custom-call(bf16[64,256]{1,0:T(8,128)(2,1)} %q_ref.1, bf16[64,256]{1,0:T(8,128)(2,1)} %g_ref.1, f32[2,64]{1,0:T(2,128)} %bitcast.13, f32[2,64]{1,0:T(2,128)} %bitcast.14), custom_call_target="tpu_custom_call" | custom-call | tf_op jit(solution)/shard_map/pallas_call | solution.py:224
  2.1 4.8 %collective-permute-start.2 = (bf16[80,512]{1,0:T(8,128)(2,1)}, bf16[80,512]{1,0:T(8,128)(2,1)S(1)}, u32[]{:S(2)}, u32[]{:S(2)}) collective-permute-start(bf16[80,512]{1,0:T(8,128)(2,1)} %shard_map.94), channel_id=1, source_target_pairs={{0,384},{1,67},{64,448},{65,1},{2,386},{3,65},{66,450},{67,3},{128... | collective-permute-start | bytes 245768 | tf_op jit(solution)/shard_map/ppermute | solution.py:246
  6.9 2.7 %collective-permute-start.1 = (bf16[80,512]{1,0:T(8,128)(2,1)}, bf16[80,512]{1,0:T(8,128)(2,1)S(1)}, u32[]{:S(2)}, u32[]{:S(2)}) collective-permute-start(bf16[80,512]{1,0:T(8,128)(2,1)} %shard_map.94), channel_id=1, source_target_pairs={{0,256},{1,3},{64,320},{65,67},{2,258},{3,1},{66,322},{67,65},{128... | collective-permute-start | bytes 245768 | tf_op jit(solution)/shard_map/ppermute | solution.py:246
  9.6 2.8 %collective-permute-start = (bf16[80,512]{1,0:T(8,128)(2,1)}, bf16[80,512]{1,0:T(8,128)(2,1)S(1)}, u32[]{:S(2)}, u32[]{:S(2)}) collective-permute-start(bf16[80,512]{1,0:T(8,128)(2,1)} %shard_map.94), channel_id=1, source_target_pairs={{0,128},{1,65},{64,192},{65,3},{2,130},{3,67},{66,194},{67,1},{128... | collective-permute-start | bytes 245768 | tf_op jit(solution)/shard_map/ppermute | solution.py:246
  12.4 0.7 pad_maximum_fusion.1
  13.1 0.9 broadcast_in_dim.84
  14.0 15.2 %all-to-all-start = ((bf16[16,64,256]{2,1,0:T(8,128)(2,1)}), bf16[16,64,256]{2,1,0:T(8,128)(2,1)S(1)}, u32[]{:S(2)}, u32[]{:S(2)}) async-start(bf16[16,64,256]{2,1,0:T(8,128)(2,1)} %broadcast_in_dim.84), calls=%async_computation | async-start | bytes 1048576 | tf_op jit(solution)/shard_map/all_to_all | solution.py:274
  29.5 2.7 %collective-permute-start.5 = (bf16[272,512]{1,0:T(8,128)(2,1)S(1)}, bf16[272,512]{1,0:T(8,128)(2,1)S(1)}, u32[]{:S(2)}, u32[]{:S(2)}) collective-permute-start(bf16[272,512]{1,0:T(8,128)(2,1)S(1)} %maximum_dynamic-update-slice_fusion), channel_id=1, source_target_pairs={{0,66},{1,385},{64,0},{65,449},{2,64},{3,387},{66,2},{67,451},{128... | collective-permute-start | bytes 835592 | tf_op jit(solution)/shard_map/ppermute | solution.py:246
  32.1 2.8 %collective-permute-start.4 = (bf16[272,512]{1,0:T(8,128)(2,1)S(1)}, bf16[272,512]{1,0:T(8,128)(2,1)S(1)}, u32[]{:S(2)}, u32[]{:S(2)}) collective-permute-start(bf16[272,512]{1,0:T(8,128)(2,1)S(1)} %maximum_dynamic-update-slice_fusion), channel_id=1, source_target_pairs={{0,2},{1,257},{64,66},{65,321},{2,0},{3,259},{66,64},{67,323},{128... | collective-permute-start | bytes 835592 | tf_op jit(solution)/shard_map/ppermute | solution.py:246
  35.0 4.1 %collective-permute-start.3 = (bf16[272,512]{1,0:T(8,128)(2,1)S(1)}, bf16[272,512]{1,0:T(8,128)(2,1)S(1)}, u32[]{:S(2)}, u32[]{:S(2)}) collective-permute-start(bf16[272,512]{1,0:T(8,128)(2,1)S(1)} %maximum_dynamic-update-slice_fusion), channel_id=1, source_target_pairs={{0,64},{1,129},{64,2},{65,193},{2,66},{3,131},{66,0},{67,195},{128... | collective-permute-start | bytes 835592 | tf_op jit(solution)/shard_map/ppermute | solution.py:246
  39.5 2.6 %collective-permute-done.4 = bf16[272,512]{1,0:T(8,128)(2,1)S(1)} collective-permute-done((bf16[272,512]{1,0:T(8,128)(2,1)S(1)}, bf16[272,512]{1,0:T(8,128)(2,1)S(1)}, u32[]{:S(2)}, u32[]{:S(2)}) %collective-permute-start.4) | collective-permute-done | bytes 278560 | tf_op jit(solution)/shard_map/ppermute | solution.py:246
  42.1 2.8 %collective-permute-done.3 = bf16[272,512]{1,0:T(8,128)(2,1)S(1)} collective-permute-done((bf16[272,512]{1,0:T(8,128)(2,1)S(1)}, bf16[272,512]{1,0:T(8,128)(2,1)S(1)}, u32[]{:S(2)}, u32[]{:S(2)}) %collective-permute-start.3) | collective-permute-done | bytes 278560 | tf_op jit(solution)/shard_map/ppermute | solution.py:246
  45.0 1.9 %collective-permute-start.6 = (bf16[4,272,512]{2,1,0:T(8,128)(2,1)S(1)}, bf16[4,272,512]{2,1,0:T(8,128)(2,1)}, u32[]{:S(2)}, u32[]{:S(2)}) collective-permute-start(bf16[4,272,512]{2,1,0:T(8,128)(2,1)S(1)} %pad_maximum_fusion.refs_0_), channel_id=1, source_target_pairs={{0,1},{1,0},{2,3},{3,2},{4,5},{5,4},{6,7},{7,6},{8,9},{9,8},{10,11... | collective-permute-start | bytes 3342344 | tf_op jit(solution)/shard_map/ppermute | solution.py:254
  47.0 0.2 select_reduce_fusion
  48.3 1.6 %collective-permute-done.6.refs_1_ = bf16[4,272,512]{2,1,0:T(8,128)(2,1)} collective-permute-done((bf16[4,272,512]{2,1,0:T(8,128)(2,1)S(1)}, bf16[4,272,512]{2,1,0:T(8,128)(2,1)}, u32[]{:S(2)}, u32[]{:S(2)}) %collective-permute-start.6) | collective-permute-done | bytes 1114144 | tf_op jit(solution)/shard_map/ppermute | solution.py:254
  49.8 6.4 %all-to-all-done = bf16[16,64,256]{2,1,0:T(8,128)(2,1)S(1)} async-done(((bf16[16,64,256]{2,1,0:T(8,128)(2,1)}), bf16[16,64,256]{2,1,0:T(8,128)(2,1)S(1)}, u32[]{:S(2)}, u32[]{:S(2)}) %all-to-all-start) | async-done | bytes 524320 | tf_op jit(solution)/shard_map/all_to_all | solution.py:274
  56.2 13.4 %shard_map.95 = (f32[1024,256]{1,0:T(8,128)S(1)}, bf16[1024,256]{1,0:T(8,128)(2,1)S(1)}, bf16[1024,256]{1,0:T(8,128)(2,1)}) custom-call(s32[64]{0:T(128)S(1)} %convert_reduce_fusion.1.rank_q, s32[64]{0:T(128)S(1)} %get-tuple-element.14.order_q, s32[64]{0:T(128)S(1)} %get-tuple-element.13.sorted_q, s32[32]{0:T(128)S(1)} %convert_reduce_fusion.2.rank_k, ...), custom_call_target="tpu_custom_call" | custom-call | flops 2684354560 | bytes 4194304 | tf_op jit(solution)/shard_map/pallas_call | solution.py:155
  69.5 7.0 %all-to-all-start.1 = ((bf16[16,64,256]{2,1,0:T(8,128)(2,1)}), bf16[16,64,256]{2,1,0:T(8,128)(2,1)S(1)}, u32[]{:S(2)}, u32[]{:S(2)}) async-start(bf16[16,64,256]{2,1,0:T(8,128)(2,1)} %bitcast.7), calls=%async_computation.1 | async-start | bytes 1048576 | tf_op jit(solution)/shard_map/all_to_all | solution.py:293
  76.5 1.9 %collective-permute-start.7 = (bf16[1024,256]{1,0:T(8,128)(2,1)S(1)}, bf16[1024,256]{1,0:T(8,128)(2,1)S(1)}, u32[]{:S(2)}, u32[]{:S(2)}) collective-permute-start(bf16[1024,256]{1,0:T(8,128)(2,1)S(1)} %get-tuple-element.11), channel_id=1, source_target_pairs={{0,1},{1,0},{2,3},{3,2},{4,5},{5,4},{6,7},{7,6},{8,9},{9,8},{10,11... | collective-permute-start | bytes 1572872 | tf_op jit(solution)/shard_map/ppermute | solution.py:254
  78.4 1.9 %collective-permute-done.7 = bf16[1024,256]{1,0:T(8,128)(2,1)S(1)} collective-permute-done((bf16[1024,256]{1,0:T(8,128)(2,1)S(1)}, bf16[1024,256]{1,0:T(8,128)(2,1)S(1)}, u32[]{:S(2)}, u32[]{:S(2)}) %collective-permute-start.7) | collective-permute-done | bytes 524320 | tf_op jit(solution)/shard_map/ppermute | solution.py:254
  80.5 2.4 %collective-permute-start.8 = (bf16[256,256]{1,0:T(8,128)(2,1)S(1)}, bf16[256,256]{1,0:T(8,128)(2,1)S(1)}, u32[]{:S(2)}, u32[]{:S(2)}) collective-permute-start(bf16[256,256]{1,0:T(8,128)(2,1)S(1)} %get-tuple-element.19), channel_id=1, source_target_pairs={{0,66},{1,385},{64,0},{65,449},{2,64},{3,387},{66,2},{67,451},{128... | collective-permute-start | bytes 393224 | tf_op jit(solution)/shard_map/ppermute | solution.py:246
  82.9 4.6 %collective-permute-start.10 = (bf16[256,256]{1,0:T(8,128)(2,1)S(1)}, bf16[256,256]{1,0:T(8,128)(2,1)S(1)}, u32[]{:S(2)}, u32[]{:S(2)}) collective-permute-start(bf16[256,256]{1,0:T(8,128)(2,1)S(1)} %get-tuple-element.20), channel_id=1, source_target_pairs={{0,64},{1,129},{64,2},{65,193},{2,66},{3,131},{66,0},{67,195},{128... | collective-permute-start | bytes 393224 | tf_op jit(solution)/shard_map/ppermute | solution.py:246
  87.6 3.0 %collective-permute-start.9 = (bf16[256,256]{1,0:T(8,128)(2,1)S(1)}, bf16[256,256]{1,0:T(8,128)(2,1)S(1)}, u32[]{:S(2)}, u32[]{:S(2)}) collective-permute-start(bf16[256,256]{1,0:T(8,128)(2,1)S(1)} %get-tuple-element.21), channel_id=1, source_target_pairs={{0,2},{1,257},{64,66},{65,321},{2,0},{3,259},{66,64},{67,323},{128... | collective-permute-start | bytes 393224 | tf_op jit(solution)/shard_map/ppermute | solution.py:246
  90.6 5.3 %collective-permute-done.9 = bf16[256,256]{1,0:T(8,128)(2,1)S(1)} collective-permute-done((bf16[256,256]{1,0:T(8,128)(2,1)S(1)}, bf16[256,256]{1,0:T(8,128)(2,1)S(1)}, u32[]{:S(2)}, u32[]{:S(2)}) %collective-permute-start.9) | collective-permute-done | bytes 131104 | tf_op jit(solution)/shard_map/ppermute | solution.py:246
  96.0 4.7 %collective-permute-start.11 = (bf16[64,256]{1,0:T(8,128)(2,1)S(1)}, bf16[64,256]{1,0:T(8,128)(2,1)S(1)}, u32[]{:S(2)}, u32[]{:S(2)}) collective-permute-start(bf16[64,256]{1,0:T(8,128)(2,1)S(1)} %get-tuple-element.22), channel_id=1, source_target_pairs={{0,384},{1,67},{64,448},{65,1},{2,386},{3,65},{66,450},{67,3},{128... | collective-permute-start | bytes 98312 | tf_op jit(solution)/shard_map/ppermute | solution.py:246
  100.7 1.9 %collective-permute-start.13 = (bf16[64,256]{1,0:T(8,128)(2,1)S(1)}, bf16[64,256]{1,0:T(8,128)(2,1)S(1)}, u32[]{:S(2)}, u32[]{:S(2)}) collective-permute-start(bf16[64,256]{1,0:T(8,128)(2,1)S(1)} %get-tuple-element.23), channel_id=1, source_target_pairs={{0,128},{1,65},{64,192},{65,3},{2,130},{3,67},{66,194},{67,1},{128... | collective-permute-start | bytes 98312 | tf_op jit(solution)/shard_map/ppermute | solution.py:246
  102.6 4.2 %collective-permute-start.12 = (bf16[64,256]{1,0:T(8,128)(2,1)S(1)}, bf16[64,256]{1,0:T(8,128)(2,1)S(1)}, u32[]{:S(2)}, u32[]{:S(2)}) collective-permute-start(bf16[64,256]{1,0:T(8,128)(2,1)S(1)} %get-tuple-element.24), channel_id=1, source_target_pairs={{0,256},{1,3},{64,320},{65,67},{2,258},{3,1},{66,322},{67,65},{128... | collective-permute-start | bytes 98312 | tf_op jit(solution)/shard_map/ppermute | solution.py:246
  106.8 0.9 collective-permute-done.13
  107.7 2.2 %collective-permute-done.12 = bf16[64,256]{1,0:T(8,128)(2,1)S(1)} collective-permute-done((bf16[64,256]{1,0:T(8,128)(2,1)S(1)}, bf16[64,256]{1,0:T(8,128)(2,1)S(1)}, u32[]{:S(2)}, u32[]{:S(2)}) %collective-permute-start.12) | collective-permute-done | bytes 32800 | tf_op jit(solution)/shard_map/ppermute | solution.py:246
  109.9 0.6 fusion.5
  110.6 0.6 slice.123
  111.3 0.6 fusion.6
  (47 shorter events, 2.1 us)
Async XLA Ops:
  2.1 27.1 %copy-start = (bf16[80,512]{1,0:T(8,128)(2,1)S(1)}, bf16[80,512]{1,0:T(8,128)(2,1)}, u32[]{:S(2)}) copy-start(bf16[80,512]{1,0:T(8,128)(2,1)} %shard_map.94) | copy-start | bytes 245764
  2.1 27.3 %collective-permute-start.2 = (bf16[80,512]{1,0:T(8,128)(2,1)}, bf16[80,512]{1,0:T(8,128)(2,1)S(1)}, u32[]{:S(2)}, u32[]{:S(2)}) collective-permute-start(bf16[80,512]{1,0:T(8,128)(2,1)} %shard_map.94), channel_id=1, source_target_pairs={{0,384},{1,67},{64,448},{65,1},{2,386},{3,65},{66,450},{67,3},{128... | collective-permute-start | bytes 245768 | tf_op jit(solution)/shard_map/ppermute | solution.py:246
  6.9 22.5 %collective-permute-start.1 = (bf16[80,512]{1,0:T(8,128)(2,1)}, bf16[80,512]{1,0:T(8,128)(2,1)S(1)}, u32[]{:S(2)}, u32[]{:S(2)}) collective-permute-start(bf16[80,512]{1,0:T(8,128)(2,1)} %shard_map.94), channel_id=1, source_target_pairs={{0,256},{1,3},{64,320},{65,67},{2,258},{3,1},{66,322},{67,65},{128... | collective-permute-start | bytes 245768 | tf_op jit(solution)/shard_map/ppermute | solution.py:246
  9.6 19.8 %collective-permute-start = (bf16[80,512]{1,0:T(8,128)(2,1)}, bf16[80,512]{1,0:T(8,128)(2,1)S(1)}, u32[]{:S(2)}, u32[]{:S(2)}) collective-permute-start(bf16[80,512]{1,0:T(8,128)(2,1)} %shard_map.94), channel_id=1, source_target_pairs={{0,128},{1,65},{64,192},{65,3},{2,130},{3,67},{66,194},{67,1},{128... | collective-permute-start | bytes 245768 | tf_op jit(solution)/shard_map/ppermute | solution.py:246
  14.0 42.2 %all-to-all-start = ((bf16[16,64,256]{2,1,0:T(8,128)(2,1)}), bf16[16,64,256]{2,1,0:T(8,128)(2,1)S(1)}, u32[]{:S(2)}, u32[]{:S(2)}) async-start(bf16[16,64,256]{2,1,0:T(8,128)(2,1)} %broadcast_in_dim.84), calls=%async_computation | async-start | bytes 1048576 | tf_op jit(solution)/shard_map/all_to_all | solution.py:274
  29.5 10.1 %collective-permute-start.5 = (bf16[272,512]{1,0:T(8,128)(2,1)S(1)}, bf16[272,512]{1,0:T(8,128)(2,1)S(1)}, u32[]{:S(2)}, u32[]{:S(2)}) collective-permute-start(bf16[272,512]{1,0:T(8,128)(2,1)S(1)} %maximum_dynamic-update-slice_fusion), channel_id=1, source_target_pairs={{0,66},{1,385},{64,0},{65,449},{2,64},{3,387},{66,2},{67,451},{128... | collective-permute-start | bytes 835592 | tf_op jit(solution)/shard_map/ppermute | solution.py:246
  32.1 10.0 %collective-permute-start.4 = (bf16[272,512]{1,0:T(8,128)(2,1)S(1)}, bf16[272,512]{1,0:T(8,128)(2,1)S(1)}, u32[]{:S(2)}, u32[]{:S(2)}) collective-permute-start(bf16[272,512]{1,0:T(8,128)(2,1)S(1)} %maximum_dynamic-update-slice_fusion), channel_id=1, source_target_pairs={{0,2},{1,257},{64,66},{65,321},{2,0},{3,259},{66,64},{67,323},{128... | collective-permute-start | bytes 835592 | tf_op jit(solution)/shard_map/ppermute | solution.py:246
  35.0 9.9 %collective-permute-start.3 = (bf16[272,512]{1,0:T(8,128)(2,1)S(1)}, bf16[272,512]{1,0:T(8,128)(2,1)S(1)}, u32[]{:S(2)}, u32[]{:S(2)}) collective-permute-start(bf16[272,512]{1,0:T(8,128)(2,1)S(1)} %maximum_dynamic-update-slice_fusion), channel_id=1, source_target_pairs={{0,64},{1,129},{64,2},{65,193},{2,66},{3,131},{66,0},{67,195},{128... | collective-permute-start | bytes 835592 | tf_op jit(solution)/shard_map/ppermute | solution.py:246
  44.9 2.1 %copy-start.1 = (s32[1024]{0:T(1024)S(1)}, s32[1024]{0:T(1024)}, u32[]{:S(2)}) copy-start(s32[1024]{0:T(1024)} %param.13) | copy-start | bytes 12292
  45.0 4.8 %collective-permute-start.6 = (bf16[4,272,512]{2,1,0:T(8,128)(2,1)S(1)}, bf16[4,272,512]{2,1,0:T(8,128)(2,1)}, u32[]{:S(2)}, u32[]{:S(2)}) collective-permute-start(bf16[4,272,512]{2,1,0:T(8,128)(2,1)S(1)} %pad_maximum_fusion.refs_0_), channel_id=1, source_target_pairs={{0,1},{1,0},{2,3},{3,2},{4,5},{5,4},{6,7},{7,6},{8,9},{9,8},{10,11... | collective-permute-start | bytes 3342344 | tf_op jit(solution)/shard_map/ppermute | solution.py:254
  69.5 41.0 %all-to-all-start.1 = ((bf16[16,64,256]{2,1,0:T(8,128)(2,1)}), bf16[16,64,256]{2,1,0:T(8,128)(2,1)S(1)}, u32[]{:S(2)}, u32[]{:S(2)}) async-start(bf16[16,64,256]{2,1,0:T(8,128)(2,1)} %bitcast.7), calls=%async_computation.1 | async-start | bytes 1048576 | tf_op jit(solution)/shard_map/all_to_all | solution.py:293
  76.5 3.8 %collective-permute-start.7 = (bf16[1024,256]{1,0:T(8,128)(2,1)S(1)}, bf16[1024,256]{1,0:T(8,128)(2,1)S(1)}, u32[]{:S(2)}, u32[]{:S(2)}) collective-permute-start(bf16[1024,256]{1,0:T(8,128)(2,1)S(1)} %get-tuple-element.11), channel_id=1, source_target_pairs={{0,1},{1,0},{2,3},{3,2},{4,5},{5,4},{6,7},{7,6},{8,9},{9,8},{10,11... | collective-permute-start | bytes 1572872 | tf_op jit(solution)/shard_map/ppermute | solution.py:254
  80.5 10.1 %collective-permute-start.8 = (bf16[256,256]{1,0:T(8,128)(2,1)S(1)}, bf16[256,256]{1,0:T(8,128)(2,1)S(1)}, u32[]{:S(2)}, u32[]{:S(2)}) collective-permute-start(bf16[256,256]{1,0:T(8,128)(2,1)S(1)} %get-tuple-element.19), channel_id=1, source_target_pairs={{0,66},{1,385},{64,0},{65,449},{2,64},{3,387},{66,2},{67,451},{128... | collective-permute-start | bytes 393224 | tf_op jit(solution)/shard_map/ppermute | solution.py:246
  82.9 7.7 %collective-permute-start.10 = (bf16[256,256]{1,0:T(8,128)(2,1)S(1)}, bf16[256,256]{1,0:T(8,128)(2,1)S(1)}, u32[]{:S(2)}, u32[]{:S(2)}) collective-permute-start(bf16[256,256]{1,0:T(8,128)(2,1)S(1)} %get-tuple-element.20), channel_id=1, source_target_pairs={{0,64},{1,129},{64,2},{65,193},{2,66},{3,131},{66,0},{67,195},{128... | collective-permute-start | bytes 393224 | tf_op jit(solution)/shard_map/ppermute | solution.py:246
  87.6 8.4 %collective-permute-start.9 = (bf16[256,256]{1,0:T(8,128)(2,1)S(1)}, bf16[256,256]{1,0:T(8,128)(2,1)S(1)}, u32[]{:S(2)}, u32[]{:S(2)}) collective-permute-start(bf16[256,256]{1,0:T(8,128)(2,1)S(1)} %get-tuple-element.21), channel_id=1, source_target_pairs={{0,2},{1,257},{64,66},{65,321},{2,0},{3,259},{66,64},{67,323},{128... | collective-permute-start | bytes 393224 | tf_op jit(solution)/shard_map/ppermute | solution.py:246
  96.0 10.8 %collective-permute-start.11 = (bf16[64,256]{1,0:T(8,128)(2,1)S(1)}, bf16[64,256]{1,0:T(8,128)(2,1)S(1)}, u32[]{:S(2)}, u32[]{:S(2)}) collective-permute-start(bf16[64,256]{1,0:T(8,128)(2,1)S(1)} %get-tuple-element.22), channel_id=1, source_target_pairs={{0,384},{1,67},{64,448},{65,1},{2,386},{3,65},{66,450},{67,3},{128... | collective-permute-start | bytes 98312 | tf_op jit(solution)/shard_map/ppermute | solution.py:246
  100.7 7.0 %collective-permute-start.13 = (bf16[64,256]{1,0:T(8,128)(2,1)S(1)}, bf16[64,256]{1,0:T(8,128)(2,1)S(1)}, u32[]{:S(2)}, u32[]{:S(2)}) collective-permute-start(bf16[64,256]{1,0:T(8,128)(2,1)S(1)} %get-tuple-element.23), channel_id=1, source_target_pairs={{0,128},{1,65},{64,192},{65,3},{2,130},{3,67},{66,194},{67,1},{128... | collective-permute-start | bytes 98312 | tf_op jit(solution)/shard_map/ppermute | solution.py:246
  102.6 7.3 %collective-permute-start.12 = (bf16[64,256]{1,0:T(8,128)(2,1)S(1)}, bf16[64,256]{1,0:T(8,128)(2,1)S(1)}, u32[]{:S(2)}, u32[]{:S(2)}) collective-permute-start(bf16[64,256]{1,0:T(8,128)(2,1)S(1)} %get-tuple-element.24), channel_id=1, source_target_pairs={{0,256},{1,3},{64,320},{65,67},{2,258},{3,1},{66,322},{67,65},{128... | collective-permute-start | bytes 98312 | tf_op jit(solution)/shard_map/ppermute | solution.py:246
